TPU v7x, 256 devices: a whole 4x4x8 slice. The times are simulated.
256 devices in a mesh: segment: 4 (over x), dom: 64 (over z, y, core).
Axes of the slice: x: 4, y: 4, z: 8, core: 2. Of those that a mesh axis runs over, the one named last changes fastest.
Arguments:
- samples: bfloat16 [4, 32768, 512], P(None, 'dom'), may hold values from -6 to 6
- w_source: bfloat16 [4, 1, 512, 512], P('segment'), may hold values from -0.25 to 0.25
- w_self: bfloat16 [4, 1, 512, 512], P('segment'), may hold values from -0.25 to 0.25
- w_message: bfloat16 [4, 1, 512, 512], P('segment'), may hold values from -0.25 to 0.25
- w_output: bfloat16 [4, 1, 512, 512], P('segment'), may hold values from -0.25 to 0.25
- norm_gain: float32 [4, 1, 512], P('segment'), may hold values from 0.1 to 1.9
- tile_source: int32 [4, 256, 6], P('segment', 'dom'), may hold values from 0 to 255, as said below
- tile_count: int32 [4, 256], P('segment', 'dom'), may hold values from 3 to 6, as said below
- tile_value: bfloat16 [4, 256, 6, 128, 128], P('segment', 'dom'), may hold values from -0.21875 to 0.21875
Outputs:
- final: bfloat16 [4, 32768, 512], P('segment', 'dom')
Inputs may be any that keep to these rules, and one draw needn't show every extreme that they name: `tile_source`: each entry for destination block b names a block among the 4 blocks that hold b's dom index (blocks (b // 4) * 4 .. + 4 - 1) or the 1 block on either side of them, counted cyclically over 256. `tile_count`: slots at or beyond the count are unused; the first block of every dom index uses all 6 slots.
All inputs are finite; a program needn't handle non-finite values.
Results may differ from a plain program's by a relative error of at most 0.013.
Values may be sent and summed in bfloat16 or wider, within the bound.
No kernel may reach another device: no remote copies, remote signals or barrier semaphores. Data moves between devices by JAX's collectives and lax.ppermute only.
A program may use at most 64 MiB of HBM per device.

v0:
```python
import jax
import jax.numpy as jnp
from jax import lax
from jax.sharding import PartitionSpec as P


def passed_along(block, axis, distance):
    devices = range(lax.axis_size(axis))
    route = [((i - distance) % len(devices), i) for i in devices]
    return lax.ppermute(block, axis, route)


def from_behind(shard, axis, by):
    count = lax.axis_size(axis)
    pairs = [(i, i + by) for i in range(count) if 0 <= i + by < count]
    return lax.ppermute(shard, axis, pairs)


def run_layer(h, w_source, w_self, w_message, w_output, norm_gain, sources, counts, tiles):
    blocks = sources.shape[0]
    block_rows = tiles.shape[-1]
    width = h.shape[1]
    dom_index = lax.axis_index("dom")
    total_blocks = blocks * lax.axis_size("dom")
    sender = jax.nn.silu(jnp.dot(h, w_source, preferred_element_type=jnp.float32)).astype(
        jnp.bfloat16
    )
    below = passed_along(sender, "dom", 1)
    above = passed_along(sender, "dom", -1)
    padded = jnp.concatenate([below, sender, above], axis=0)
    first_block = dom_index * blocks - blocks
    local_index = jnp.mod(sources - first_block, total_blocks)
    padded_blocks = padded.reshape(padded.shape[0] // block_rows, block_rows, width)
    picked = padded_blocks[local_index]
    keep = (jnp.arange(sources.shape[1], dtype=jnp.int32)[None, :] < counts[:, None]).astype(
        jnp.bfloat16
    )
    weights = tiles * keep[:, :, None, None]
    gathered = jnp.einsum("bkij,bkjd->bid", weights, picked, preferred_element_type=jnp.float32)
    gathered = gathered.reshape(blocks * block_rows, width).astype(jnp.bfloat16)
    mixed = jnp.dot(h, w_self, preferred_element_type=jnp.float32) + jnp.dot(
        gathered, w_message, preferred_element_type=jnp.float32
    )
    scaled = mixed / jnp.sqrt(jnp.mean(mixed * mixed, axis=-1, keepdims=True) + 1e-05) * norm_gain
    update = jax.nn.silu(scaled).astype(jnp.bfloat16)
    return (
        h.astype(jnp.float32) + jnp.dot(update, w_output, preferred_element_type=jnp.float32)
    ).astype(jnp.bfloat16)


def shards(
    samples, w_source, w_self, w_message, w_output, norm_gain, tile_source, tile_count, tile_value
):
    sections = lax.axis_size("segment")
    segment_index = lax.axis_index("segment")
    sample_total = samples.shape[0]
    incoming = samples[0]
    finished = []
    for step in range(sample_total + sections - 1):
        entering = samples[min(step, sample_total - 1)]
        h = jnp.where(segment_index == 0, entering, incoming)
        h = run_layer(
            h,
            w_source[0, 0],
            w_self[0, 0],
            w_message[0, 0],
            w_output[0, 0],
            norm_gain[0, 0],
            tile_source[0],
            tile_count[0],
            tile_value[0],
        )
        if step >= sections - 1:
            finished.append(h)
        incoming = from_behind(h, "segment", 1)
    stacked = jnp.stack(finished)
    kept = jnp.where(segment_index == sections - 1, stacked, jnp.zeros_like(stacked))
    moved = lax.all_to_all(kept, "segment", split_axis=0, concat_axis=0, tiled=True)
    moved = moved.reshape(sections, sample_total // sections, moved.shape[1], moved.shape[2])
    return jnp.sum(moved.astype(jnp.float32), axis=0).astype(jnp.bfloat16)


def solution(mesh):
    return jax.shard_map(
        shards,
        mesh=mesh,
        in_specs=(
            P(None, "dom", None),
            P("segment", None, None, None),
            P("segment", None, None, None),
            P("segment", None, None, None),
            P("segment", None, None, None),
            P("segment", None, None),
            P("segment", "dom", None),
            P("segment", "dom"),
            P("segment", "dom", None, None, None),
        ),
        out_specs=P("segment", "dom", None),
        check_vma=False,
    )
```

profile of v0, /device:TPU:6, one launch (start us, length us, event | category | flops | bytes accessed | tf_op | source)
XLA Modules:
  0.0 278.3 jit_solution(2550854002434492739)
XLA Ops:
  0.0 1.9 multiply_convert_fusion.13
  1.9 7.8 %collective-permute-start.1 = (bf16[512,512]{0,1:T(8,128)(2,1)S(1)}, bf16[512,512]{0,1:T(8,128)(2,1)S(1)}, u32[]{:S(2)}, u32[]{:S(2)}) collective-permute-start(bf16[512,512]{0,1:T(8,128)(2,1)S(1)} %multiply_convert_fusion.13), channel_id=1, source_target_pairs={{1,0},{2,1},{3,2},{4,3},{5,4},{6,5},{7,6},{8,7},{9,8},{10,9},{11,1... | collective-permute-start | bytes 1572872 | tf_op jit(solution)/shard_map/ppermute | solution.py:10
  9.9 2.5 fusion.81
  12.5 4.0 %collective-permute-done.1 = bf16[512,512]{0,1:T(8,128)(2,1)S(1)} collective-permute-done((bf16[512,512]{0,1:T(8,128)(2,1)S(1)}, bf16[512,512]{0,1:T(8,128)(2,1)S(1)}, u32[]{:S(2)}, u32[]{:S(2)}) %collective-permute-start.1) | collective-permute-done | bytes 524320 | tf_op jit(solution)/shard_map/ppermute | solution.py:10
  16.4 5.2 %collective-permute-done = bf16[512,512]{0,1:T(8,128)(2,1)S(1)} collective-permute-done((bf16[512,512]{0,1:T(8,128)(2,1)S(1)}, bf16[512,512]{0,1:T(8,128)(2,1)S(1)}, u32[]{:S(2)}, u32[]{:S(2)}) %collective-permute-start) | collective-permute-done | bytes 524320 | tf_op jit(solution)/shard_map/ppermute | solution.py:10
  21.7 1.3 pad_maximum_fusion
  22.9 1.7 copy.33
  24.7 2.5 gather_fusion
  27.2 2.7 fusion
  30.4 2.7 fusion.7
  33.1 1.3 collective-permute-start.2
  34.4 10.0 %collective-permute-done.2 = bf16[512,512]{1,0:T(8,128)(2,1)S(1)} collective-permute-done((bf16[512,512]{1,0:T(8,128)(2,1)}, bf16[512,512]{1,0:T(8,128)(2,1)S(1)}, u32[]{:S(2)}, u32[]{:S(2)}) %collective-permute-start.2) | collective-permute-done | bytes 524320 | tf_op jit(solution)/shard_map/ppermute | solution.py:16
  46.9 2.5 collective-permute-start.4
  49.5 6.7 %collective-permute-done.4 = bf16[512,512]{0,1:T(8,128)(2,1)S(1)} collective-permute-done((bf16[512,512]{0,1:T(8,128)(2,1)S(1)}, bf16[512,512]{0,1:T(8,128)(2,1)S(1)}, u32[]{:S(2)}, u32[]{:S(2)}) %collective-permute-start.4) | collective-permute-done | bytes 524320 | tf_op jit(solution)/shard_map/ppermute | solution.py:10
  56.2 5.2 %collective-permute-done.3 = bf16[512,512]{0,1:T(8,128)(2,1)S(1)} collective-permute-done((bf16[512,512]{0,1:T(8,128)(2,1)S(1)}, bf16[512,512]{0,1:T(8,128)(2,1)S(1)}, u32[]{:S(2)}, u32[]{:S(2)}) %collective-permute-start.3) | collective-permute-done | bytes 524320 | tf_op jit(solution)/shard_map/ppermute | solution.py:10
  61.4 1.3 pad_maximum_fusion.1
  62.7 1.7 copy.36
  64.4 2.5 gather_fusion.1
  66.9 2.6 fusion.1
  71.3 1.3 collective-permute-start.5
  72.6 9.8 %collective-permute-done.5 = bf16[512,512]{1,0:T(8,128)(2,1)S(1)} collective-permute-done((bf16[512,512]{1,0:T(8,128)(2,1)S(1)}, bf16[512,512]{1,0:T(8,128)(2,1)S(1)}, u32[]{:S(2)}, u32[]{:S(2)}) %collective-permute-start.5) | collective-permute-done | bytes 524320 | tf_op jit(solution)/shard_map/ppermute | solution.py:16
  85.8 6.7 %collective-permute-done.7 = bf16[512,512]{0,1:T(8,128)(2,1)S(1)} collective-permute-done((bf16[512,512]{0,1:T(8,128)(2,1)S(1)}, bf16[512,512]{0,1:T(8,128)(2,1)S(1)}, u32[]{:S(2)}, u32[]{:S(2)}) %collective-permute-start.7) | collective-permute-done | bytes 524320 | tf_op jit(solution)/shard_map/ppermute | solution.py:10
  92.5 5.2 %collective-permute-done.6 = bf16[512,512]{0,1:T(8,128)(2,1)S(1)} collective-permute-done((bf16[512,512]{0,1:T(8,128)(2,1)S(1)}, bf16[512,512]{0,1:T(8,128)(2,1)S(1)}, u32[]{:S(2)}, u32[]{:S(2)}) %collective-permute-start.6) | collective-permute-done | bytes 524320 | tf_op jit(solution)/shard_map/ppermute | solution.py:10
  97.8 1.3 pad_maximum_fusion.2
  99.0 1.7 copy.39
  100.8 2.5 gather_fusion.2
  103.3 2.6 fusion.2
  107.7 1.3 collective-permute-start.8
  109.0 9.8 %collective-permute-done.8 = bf16[512,512]{1,0:T(8,128)(2,1)S(1)} collective-permute-done((bf16[512,512]{1,0:T(8,128)(2,1)S(1)}, bf16[512,512]{1,0:T(8,128)(2,1)S(1)}, u32[]{:S(2)}, u32[]{:S(2)}) %collective-permute-start.8) | collective-permute-done | bytes 524320 | tf_op jit(solution)/shard_map/ppermute | solution.py:16
  118.8 1.1 bitcast_select_fusion.5
  121.9 6.6 %collective-permute-done.10 = bf16[512,512]{0,1:T(8,128)(2,1)S(1)} collective-permute-done((bf16[512,512]{0,1:T(8,128)(2,1)S(1)}, bf16[512,512]{0,1:T(8,128)(2,1)S(1)}, u32[]{:S(2)}, u32[]{:S(2)}) %collective-permute-start.10) | collective-permute-done | bytes 524320 | tf_op jit(solution)/shard_map/ppermute | solution.py:10
  128.5 5.2 %collective-permute-done.9 = bf16[512,512]{0,1:T(8,128)(2,1)S(1)} collective-permute-done((bf16[512,512]{0,1:T(8,128)(2,1)S(1)}, bf16[512,512]{0,1:T(8,128)(2,1)S(1)}, u32[]{:S(2)}, u32[]{:S(2)}) %collective-permute-start.9) | collective-permute-done | bytes 524320 | tf_op jit(solution)/shard_map/ppermute | solution.py:10
  133.7 1.3 pad_maximum_fusion.3
  135.0 1.7 copy.42
  136.7 2.5 gather_fusion.3
  139.2 2.6 fusion.3
  143.7 1.3 collective-permute-start.11
  145.0 9.8 %collective-permute-done.11 = bf16[512,512]{1,0:T(8,128)(2,1)S(1)} collective-permute-done((bf16[512,512]{1,0:T(8,128)(2,1)S(1)}, bf16[512,512]{1,0:T(8,128)(2,1)S(1)}, u32[]{:S(2)}, u32[]{:S(2)}) %collective-permute-start.11) | collective-permute-done | bytes 524320 | tf_op jit(solution)/shard_map/ppermute | solution.py:16
  154.7 1.1 bitcast_select_fusion.4
  157.9 6.3 %collective-permute-done.13 = bf16[512,512]{0,1:T(8,128)(2,1)S(1)} collective-permute-done((bf16[512,512]{0,1:T(8,128)(2,1)S(1)}, bf16[512,512]{0,1:T(8,128)(2,1)S(1)}, u32[]{:S(2)}, u32[]{:S(2)}) %collective-permute-start.13) | collective-permute-done | bytes 524320 | tf_op jit(solution)/shard_map/ppermute | solution.py:10
  164.2 5.4 %collective-permute-done.12 = bf16[512,512]{0,1:T(8,128)(2,1)S(1)} collective-permute-done((bf16[512,512]{0,1:T(8,128)(2,1)S(1)}, bf16[512,512]{0,1:T(8,128)(2,1)S(1)}, u32[]{:S(2)}, u32[]{:S(2)}) %collective-permute-start.12) | collective-permute-done | bytes 524320 | tf_op jit(solution)/shard_map/ppermute | solution.py:10
  169.6 1.3 pad_maximum_fusion.4
  170.9 1.7 copy.45
  172.6 2.5 gather_fusion.4
  175.1 2.6 fusion.4
  179.6 1.3 collective-permute-start.14
  180.9 9.8 %collective-permute-done.14 = bf16[512,512]{1,0:T(8,128)(2,1)S(1)} collective-permute-done((bf16[512,512]{1,0:T(8,128)(2,1)S(1)}, bf16[512,512]{1,0:T(8,128)(2,1)S(1)}, u32[]{:S(2)}, u32[]{:S(2)}) %collective-permute-start.14) | collective-permute-done | bytes 524320 | tf_op jit(solution)/shard_map/ppermute | solution.py:16
  190.6 1.1 bitcast_select_fusion.3
  193.8 6.2 %collective-permute-done.16 = bf16[512,512]{0,1:T(8,128)(2,1)S(1)} collective-permute-done((bf16[512,512]{0,1:T(8,128)(2,1)S(1)}, bf16[512,512]{0,1:T(8,128)(2,1)S(1)}, u32[]{:S(2)}, u32[]{:S(2)}) %collective-permute-start.16) | collective-permute-done | bytes 524320 | tf_op jit(solution)/shard_map/ppermute | solution.py:10
  200.0 5.3 %collective-permute-done.15 = bf16[512,512]{0,1:T(8,128)(2,1)S(1)} collective-permute-done((bf16[512,512]{0,1:T(8,128)(2,1)S(1)}, bf16[512,512]{0,1:T(8,128)(2,1)S(1)}, u32[]{:S(2)}, u32[]{:S(2)}) %collective-permute-start.15) | collective-permute-done | bytes 524320 | tf_op jit(solution)/shard_map/ppermute | solution.py:10
  205.3 1.3 pad_maximum_fusion.5
  206.6 1.7 copy.48
  208.3 2.5 gather_fusion.5
  210.8 2.6 fusion.5
  215.2 1.3 collective-permute-start.17
  216.5 9.8 %collective-permute-done.17 = bf16[512,512]{1,0:T(8,128)(2,1)S(1)} collective-permute-done((bf16[512,512]{1,0:T(8,128)(2,1)S(1)}, bf16[512,512]{1,0:T(8,128)(2,1)S(1)}, u32[]{:S(2)}, u32[]{:S(2)}) %collective-permute-start.17) | collective-permute-done | bytes 524320 | tf_op jit(solution)/shard_map/ppermute | solution.py:16
  229.4 6.2 %collective-permute-done.19 = bf16[512,512]{0,1:T(8,128)(2,1)S(1)} collective-permute-done((bf16[512,512]{0,1:T(8,128)(2,1)S(1)}, bf16[512,512]{0,1:T(8,128)(2,1)S(1)}, u32[]{:S(2)}, u32[]{:S(2)}) %collective-permute-start.19) | collective-permute-done | bytes 524320 | tf_op jit(solution)/shard_map/ppermute | solution.py:10
  235.6 5.6 %collective-permute-done.18 = bf16[512,512]{0,1:T(8,128)(2,1)S(1)} collective-permute-done((bf16[512,512]{0,1:T(8,128)(2,1)S(1)}, bf16[512,512]{0,1:T(8,128)(2,1)S(1)}, u32[]{:S(2)}, u32[]{:S(2)}) %collective-permute-start.18) | collective-permute-done | bytes 524320 | tf_op jit(solution)/shard_map/ppermute | solution.py:10
  241.2 1.3 pad_maximum_fusion.6
  242.5 1.7 copy.51
  244.2 2.5 gather_fusion.6
  246.7 2.6 fusion.6
  252.0 23.4 %all_to_all.5 = bf16[4,512,512]{2,1,0:T(8,128)(2,1)} all-to-all(bf16[4,512,512]{2,1,0:T(8,128)(2,1)S(1)} %maximum_select_fusion), channel_id=1, replica_groups=mesh['segment'=4,'dom'=64] {'segment'}, dimensions={0} | all-to-all | bytes 4194304 | tf_op jit(solution)/shard_map/all_to_all | solution.py:78
  275.4 2.9 %reduce_sum.84 = bf16[512,512]{1,0:T(8,128)(2,1)} reduce(bf16[4,512,512]{2,1,0:T(8,128)(2,1)} %all_to_all.5, bf16[]{:T(256)} %constant.83.clone.1), dimensions={0}, to_apply=%region_7.8 | reduce | flops 786432 | bytes 2621442 | tf_op jit(solution)/shard_map/reduce_sum | solution.py:80
  (128 shorter events, 27.5 us)
Async XLA Ops:
  0.0 9.9 %copy-start = (bf16[1,1,512,512]{3,2,1,0:T(8,128)(2,1)S(1)}, bf16[1,1,512,512]{3,2,1,0:T(8,128)(2,1)}, u32[]{:S(2)}) copy-start(bf16[1,1,512,512]{3,2,1,0:T(8,128)(2,1)} %param.11) | copy-start | bytes 1572868
  0.0 9.7 %copy-start.22 = (s32[1,4,6]{2,1,0:T(4,128)S(1)}, s32[1,4,6]{2,1,0:T(4,128)}, u32[]{:S(2)}) copy-start(s32[1,4,6]{2,1,0:T(4,128)} %param.15) | copy-start | bytes 292
  0.0 9.8 %copy-start.37 = (s32[1,4]{1,0:T(1,128)S(1)}, s32[1,4]{1,0:T(1,128)}, u32[]{:S(2)}) copy-start(s32[1,4]{1,0:T(1,128)} %param.16) | copy-start | bytes 52
  1.9 14.5 %collective-permute-start.1 = (bf16[512,512]{0,1:T(8,128)(2,1)S(1)}, bf16[512,512]{0,1:T(8,128)(2,1)S(1)}, u32[]{:S(2)}, u32[]{:S(2)}) collective-permute-start(bf16[512,512]{0,1:T(8,128)(2,1)S(1)} %multiply_convert_fusion.13), channel_id=1, source_target_pairs={{1,0},{2,1},{3,2},{4,3},{5,4},{6,5},{7,6},{8,7},{9,8},{10,9},{11,1... | collective-permute-start | bytes 1572872 | tf_op jit(solution)/shard_map/ppermute | solution.py:10
  9.7 11.9 %collective-permute-start = (bf16[512,512]{0,1:T(8,128)(2,1)S(1)}, bf16[512,512]{0,1:T(8,128)(2,1)S(1)}, u32[]{:S(2)}, u32[]{:S(2)}) collective-permute-start(bf16[512,512]{0,1:T(8,128)(2,1)S(1)} %multiply_convert_fusion.13), channel_id=1, source_target_pairs={{63,0},{0,1},{1,2},{2,3},{3,4},{4,5},{5,6},{6,7},{7,8},{8,9},{9,10... | collective-permute-start | bytes 1572872 | tf_op jit(solution)/shard_map/ppermute | solution.py:10
  24.7 2.5 copy-start.1
  27.2 2.7 copy-start.2
  27.2 2.7 copy-start.3
  27.2 3.2 %copy-start.29 = (bf16[1,1,512,512]{3,2,1,0:T(8,128)(2,1)S(1)}, bf16[1,1,512,512]{3,2,1,0:T(8,128)(2,1)}, u32[]{:S(2)}) copy-start(bf16[1,1,512,512]{3,2,1,0:T(8,128)(2,1)} %param.13) | copy-start | bytes 1572868
  27.2 3.2 %copy-start.36 = (f32[1,1,512]{2,1,0:T(1,128)S(1)}, f32[1,1,512]{2,1,0:T(1,128)}, u32[]{:S(2)}) copy-start(f32[1,1,512]{2,1,0:T(1,128)} %param.14) | copy-start | bytes 6148
  30.4 15.9 %copy-start.23 = (bf16[1,1,512,512]{3,2,1,0:T(8,128)(2,1)S(1)}, bf16[1,1,512,512]{3,2,1,0:T(8,128)(2,1)}, u32[]{:S(2)}) copy-start(bf16[1,1,512,512]{3,2,1,0:T(8,128)(2,1)} %param.10) | copy-start | bytes 1572868
  33.1 11.3 %collective-permute-start.2 = (bf16[512,512]{1,0:T(8,128)(2,1)}, bf16[512,512]{1,0:T(8,128)(2,1)S(1)}, u32[]{:S(2)}, u32[]{:S(2)}) collective-permute-start(bf16[512,512]{1,0:T(8,128)(2,1)} %fusion.7), channel_id=1, source_target_pairs={{0,64},{64,128},{128,192},{1,65},{65,129},{129,193},{2,66},{66,130... | collective-permute-start | bytes 1572872 | tf_op jit(solution)/shard_map/ppermute | solution.py:16
  45.5 0.8 copy-start.6
  46.9 9.2 %collective-permute-start.4 = (bf16[512,512]{0,1:T(8,128)(2,1)S(1)}, bf16[512,512]{0,1:T(8,128)(2,1)S(1)}, u32[]{:S(2)}, u32[]{:S(2)}) collective-permute-start(bf16[512,512]{0,1:T(8,128)(2,1)S(1)} %multiply_convert_fusion.11), channel_id=1, source_target_pairs={{1,0},{2,1},{3,2},{4,3},{5,4},{6,5},{7,6},{8,7},{9,8},{10,9},{11,1... | collective-permute-start | bytes 1572872 | tf_op jit(solution)/shard_map/ppermute | solution.py:10
  49.5 11.9 %collective-permute-start.3 = (bf16[512,512]{0,1:T(8,128)(2,1)S(1)}, bf16[512,512]{0,1:T(8,128)(2,1)S(1)}, u32[]{:S(2)}, u32[]{:S(2)}) collective-permute-start(bf16[512,512]{0,1:T(8,128)(2,1)S(1)} %multiply_convert_fusion.11), channel_id=1, source_target_pairs={{63,0},{0,1},{1,2},{2,3},{3,4},{4,5},{5,6},{6,7},{7,8},{8,9},{9,10... | collective-permute-start | bytes 1572872 | tf_op jit(solution)/shard_map/ppermute | solution.py:10
  66.9 3.1 %copy-start.7 = (bf16[512,512]{1,0:T(8,128)(2,1)S(1)}, bf16[512,512]{1,0:T(8,128)(2,1)}, u32[]{:S(2)}) copy-start(bf16[512,512]{1,0:T(8,128)(2,1)} %copy-done.6) | copy-start | bytes 1572868
  69.5 1.0 copy-start.30
  70.5 13.8 %copy-start.24 = (bf16[1,1,512,512]{3,2,1,0:T(8,128)(2,1)S(1)}, bf16[1,1,512,512]{3,2,1,0:T(8,128)(2,1)}, u32[]{:S(2)}) copy-start(bf16[1,1,512,512]{3,2,1,0:T(8,128)(2,1)} %param.10) | copy-start | bytes 1572868
  71.3 11.1 %collective-permute-start.5 = (bf16[512,512]{1,0:T(8,128)(2,1)S(1)}, bf16[512,512]{1,0:T(8,128)(2,1)S(1)}, u32[]{:S(2)}, u32[]{:S(2)}) collective-permute-start(bf16[512,512]{1,0:T(8,128)(2,1)S(1)} %add_convert_fusion.5), channel_id=1, source_target_pairs={{0,64},{64,128},{128,192},{1,65},{65,129},{129,193},{2,66},{66,130... | collective-permute-start | bytes 1572872 | tf_op jit(solution)/shard_map/ppermute | solution.py:16
  83.5 0.8 copy-start.8
  84.9 7.6 %collective-permute-start.7 = (bf16[512,512]{0,1:T(8,128)(2,1)S(1)}, bf16[512,512]{0,1:T(8,128)(2,1)S(1)}, u32[]{:S(2)}, u32[]{:S(2)}) collective-permute-start(bf16[512,512]{0,1:T(8,128)(2,1)S(1)} %multiply_convert_fusion.9), channel_id=1, source_target_pairs={{1,0},{2,1},{3,2},{4,3},{5,4},{6,5},{7,6},{8,7},{9,8},{10,9},{11,1... | collective-permute-start | bytes 1572872 | tf_op jit(solution)/shard_map/ppermute | solution.py:10
  85.8 11.9 %collective-permute-start.6 = (bf16[512,512]{0,1:T(8,128)(2,1)S(1)}, bf16[512,512]{0,1:T(8,128)(2,1)S(1)}, u32[]{:S(2)}, u32[]{:S(2)}) collective-permute-start(bf16[512,512]{0,1:T(8,128)(2,1)S(1)} %multiply_convert_fusion.9), channel_id=1, source_target_pairs={{63,0},{0,1},{1,2},{2,3},{3,4},{4,5},{5,6},{6,7},{7,8},{8,9},{9,10... | collective-permute-start | bytes 1572872 | tf_op jit(solution)/shard_map/ppermute | solution.py:10
  103.3 3.1 %copy-start.9 = (bf16[512,512]{1,0:T(8,128)(2,1)S(1)}, bf16[512,512]{1,0:T(8,128)(2,1)}, u32[]{:S(2)}) copy-start(bf16[512,512]{1,0:T(8,128)(2,1)} %copy-done.8) | copy-start | bytes 1572868
  105.8 1.0 copy-start.31
  106.9 13.8 %copy-start.25 = (bf16[1,1,512,512]{3,2,1,0:T(8,128)(2,1)S(1)}, bf16[1,1,512,512]{3,2,1,0:T(8,128)(2,1)}, u32[]{:S(2)}) copy-start(bf16[1,1,512,512]{3,2,1,0:T(8,128)(2,1)} %param.10) | copy-start | bytes 1572868
  107.7 11.1 %collective-permute-start.8 = (bf16[512,512]{1,0:T(8,128)(2,1)S(1)}, bf16[512,512]{1,0:T(8,128)(2,1)S(1)}, u32[]{:S(2)}, u32[]{:S(2)}) collective-permute-start(bf16[512,512]{1,0:T(8,128)(2,1)S(1)} %add_convert_fusion.4), channel_id=1, source_target_pairs={{0,64},{64,128},{128,192},{1,65},{65,129},{129,193},{2,66},{66,130... | collective-permute-start | bytes 1572872 | tf_op jit(solution)/shard_map/ppermute | solution.py:16
  119.9 0.8 copy-start.10
  121.3 7.2 %collective-permute-start.10 = (bf16[512,512]{0,1:T(8,128)(2,1)S(1)}, bf16[512,512]{0,1:T(8,128)(2,1)S(1)}, u32[]{:S(2)}, u32[]{:S(2)}) collective-permute-start(bf16[512,512]{0,1:T(8,128)(2,1)S(1)} %multiply_convert_fusion.7), channel_id=1, source_target_pairs={{1,0},{2,1},{3,2},{4,3},{5,4},{6,5},{7,6},{8,7},{9,8},{10,9},{11,1... | collective-permute-start | bytes 1572872 | tf_op jit(solution)/shard_map/ppermute | solution.py:10
  121.8 11.9 %collective-permute-start.9 = (bf16[512,512]{0,1:T(8,128)(2,1)S(1)}, bf16[512,512]{0,1:T(8,128)(2,1)S(1)}, u32[]{:S(2)}, u32[]{:S(2)}) collective-permute-start(bf16[512,512]{0,1:T(8,128)(2,1)S(1)} %multiply_convert_fusion.7), channel_id=1, source_target_pairs={{63,0},{0,1},{1,2},{2,3},{3,4},{4,5},{5,6},{6,7},{7,8},{8,9},{9,10... | collective-permute-start | bytes 1572872 | tf_op jit(solution)/shard_map/ppermute | solution.py:10
  139.2 3.1 %copy-start.11 = (bf16[512,512]{1,0:T(8,128)(2,1)S(1)}, bf16[512,512]{1,0:T(8,128)(2,1)}, u32[]{:S(2)}) copy-start(bf16[512,512]{1,0:T(8,128)(2,1)} %copy-done.10) | copy-start | bytes 1572868
  141.8 1.0 copy-start.32
  142.8 13.8 %copy-start.26 = (bf16[1,1,512,512]{3,2,1,0:T(8,128)(2,1)S(1)}, bf16[1,1,512,512]{3,2,1,0:T(8,128)(2,1)}, u32[]{:S(2)}) copy-start(bf16[1,1,512,512]{3,2,1,0:T(8,128)(2,1)} %param.10) | copy-start | bytes 1572868
  143.7 13.6 %copy-start.16 = (bf16[512,512]{1,0:T(8,128)(2,1)}, bf16[512,512]{1,0:T(8,128)(2,1)S(1)}, u32[]{:S(2)}) copy-start(bf16[512,512]{1,0:T(8,128)(2,1)S(1)} %add_convert_fusion.3) | copy-start | bytes 1572868
  143.7 11.1 %collective-permute-start.11 = (bf16[512,512]{1,0:T(8,128)(2,1)S(1)}, bf16[512,512]{1,0:T(8,128)(2,1)S(1)}, u32[]{:S(2)}, u32[]{:S(2)}) collective-permute-start(bf16[512,512]{1,0:T(8,128)(2,1)S(1)} %add_convert_fusion.3), channel_id=1, source_target_pairs={{0,64},{64,128},{128,192},{1,65},{65,129},{129,193},{2,66},{66,130... | collective-permute-start | bytes 1572872 | tf_op jit(solution)/shard_map/ppermute | solution.py:16
  155.8 0.8 copy-start.12
  157.3 6.9 %collective-permute-start.13 = (bf16[512,512]{0,1:T(8,128)(2,1)S(1)}, bf16[512,512]{0,1:T(8,128)(2,1)S(1)}, u32[]{:S(2)}, u32[]{:S(2)}) collective-permute-start(bf16[512,512]{0,1:T(8,128)(2,1)S(1)} %multiply_convert_fusion.5), channel_id=1, source_target_pairs={{1,0},{2,1},{3,2},{4,3},{5,4},{6,5},{7,6},{8,7},{9,8},{10,9},{11,1... | collective-permute-start | bytes 1572872 | tf_op jit(solution)/shard_map/ppermute | solution.py:10
  157.5 12.1 %collective-permute-start.12 = (bf16[512,512]{0,1:T(8,128)(2,1)S(1)}, bf16[512,512]{0,1:T(8,128)(2,1)S(1)}, u32[]{:S(2)}, u32[]{:S(2)}) collective-permute-start(bf16[512,512]{0,1:T(8,128)(2,1)S(1)} %multiply_convert_fusion.5), channel_id=1, source_target_pairs={{63,0},{0,1},{1,2},{2,3},{3,4},{4,5},{5,6},{6,7},{7,8},{8,9},{9,10... | collective-permute-start | bytes 1572872 | tf_op jit(solution)/shard_map/ppermute | solution.py:10
  175.1 3.1 %copy-start.13 = (bf16[512,512]{1,0:T(8,128)(2,1)S(1)}, bf16[512,512]{1,0:T(8,128)(2,1)}, u32[]{:S(2)}) copy-start(bf16[512,512]{1,0:T(8,128)(2,1)} %copy-done.12) | copy-start | bytes 1572868
  177.7 1.0 copy-start.33
  178.7 13.8 %copy-start.27 = (bf16[1,1,512,512]{3,2,1,0:T(8,128)(2,1)S(1)}, bf16[1,1,512,512]{3,2,1,0:T(8,128)(2,1)}, u32[]{:S(2)}) copy-start(bf16[1,1,512,512]{3,2,1,0:T(8,128)(2,1)} %param.10) | copy-start | bytes 1572868
  179.6 13.6 %copy-start.18 = (bf16[512,512]{1,0:T(8,128)(2,1)}, bf16[512,512]{1,0:T(8,128)(2,1)S(1)}, u32[]{:S(2)}) copy-start(bf16[512,512]{1,0:T(8,128)(2,1)S(1)} %add_convert_fusion.2) | copy-start | bytes 1572868
  179.6 11.1 %collective-permute-start.14 = (bf16[512,512]{1,0:T(8,128)(2,1)S(1)}, bf16[512,512]{1,0:T(8,128)(2,1)S(1)}, u32[]{:S(2)}, u32[]{:S(2)}) collective-permute-start(bf16[512,512]{1,0:T(8,128)(2,1)S(1)} %add_convert_fusion.2), channel_id=1, source_target_pairs={{0,64},{64,128},{128,192},{1,65},{65,129},{129,193},{2,66},{66,130... | collective-permute-start | bytes 1572872 | tf_op jit(solution)/shard_map/ppermute | solution.py:16
  191.7 0.8 copy-start.14
  193.2 6.8 %collective-permute-start.16 = (bf16[512,512]{0,1:T(8,128)(2,1)S(1)}, bf16[512,512]{0,1:T(8,128)(2,1)S(1)}, u32[]{:S(2)}, u32[]{:S(2)}) collective-permute-start(bf16[512,512]{0,1:T(8,128)(2,1)S(1)} %multiply_convert_fusion.3), channel_id=1, source_target_pairs={{1,0},{2,1},{3,2},{4,3},{5,4},{6,5},{7,6},{8,7},{9,8},{10,9},{11,1... | collective-permute-start | bytes 1572872 | tf_op jit(solution)/shard_map/ppermute | solution.py:10
  193.3 12.0 %collective-permute-start.15 = (bf16[512,512]{0,1:T(8,128)(2,1)S(1)}, bf16[512,512]{0,1:T(8,128)(2,1)S(1)}, u32[]{:S(2)}, u32[]{:S(2)}) collective-permute-start(bf16[512,512]{0,1:T(8,128)(2,1)S(1)} %multiply_convert_fusion.3), channel_id=1, source_target_pairs={{63,0},{0,1},{1,2},{2,3},{3,4},{4,5},{5,6},{6,7},{7,8},{8,9},{9,10... | collective-permute-start | bytes 1572872 | tf_op jit(solution)/shard_map/ppermute | solution.py:10
  210.8 3.1 %copy-start.15 = (bf16[512,512]{1,0:T(8,128)(2,1)S(1)}, bf16[512,512]{1,0:T(8,128)(2,1)}, u32[]{:S(2)}) copy-start(bf16[512,512]{1,0:T(8,128)(2,1)} %copy-done.14) | copy-start | bytes 1572868
  213.4 1.0 copy-start.34
  214.4 13.8 %copy-start.28 = (bf16[1,1,512,512]{3,2,1,0:T(8,128)(2,1)S(1)}, bf16[1,1,512,512]{3,2,1,0:T(8,128)(2,1)}, u32[]{:S(2)}) copy-start(bf16[1,1,512,512]{3,2,1,0:T(8,128)(2,1)} %param.10) | copy-start | bytes 1572868
  215.2 13.6 %copy-start.20 = (bf16[512,512]{1,0:T(8,128)(2,1)}, bf16[512,512]{1,0:T(8,128)(2,1)S(1)}, u32[]{:S(2)}) copy-start(bf16[512,512]{1,0:T(8,128)(2,1)S(1)} %add_convert_fusion.1) | copy-start | bytes 1572868
  215.2 11.1 %collective-permute-start.17 = (bf16[512,512]{1,0:T(8,128)(2,1)S(1)}, bf16[512,512]{1,0:T(8,128)(2,1)S(1)}, u32[]{:S(2)}, u32[]{:S(2)}) collective-permute-start(bf16[512,512]{1,0:T(8,128)(2,1)S(1)} %add_convert_fusion.1), channel_id=1, source_target_pairs={{0,64},{64,128},{128,192},{1,65},{65,129},{129,193},{2,66},{66,130... | collective-permute-start | bytes 1572872 | tf_op jit(solution)/shard_map/ppermute | solution.py:16
  227.4 0.8 copy-start.4
  228.9 6.8 %collective-permute-start.19 = (bf16[512,512]{0,1:T(8,128)(2,1)S(1)}, bf16[512,512]{0,1:T(8,128)(2,1)S(1)}, u32[]{:S(2)}, u32[]{:S(2)}) collective-permute-start(bf16[512,512]{0,1:T(8,128)(2,1)S(1)} %multiply_convert_fusion.1), channel_id=1, source_target_pairs={{1,0},{2,1},{3,2},{4,3},{5,4},{6,5},{7,6},{8,7},{9,8},{10,9},{11,1... | collective-permute-start | bytes 1572872 | tf_op jit(solution)/shard_map/ppermute | solution.py:10
  228.9 12.3 %collective-permute-start.18 = (bf16[512,512]{0,1:T(8,128)(2,1)S(1)}, bf16[512,512]{0,1:T(8,128)(2,1)S(1)}, u32[]{:S(2)}, u32[]{:S(2)}) collective-permute-start(bf16[512,512]{0,1:T(8,128)(2,1)S(1)} %multiply_convert_fusion.1), channel_id=1, source_target_pairs={{63,0},{0,1},{1,2},{2,3},{3,4},{4,5},{5,6},{6,7},{7,8},{8,9},{9,10... | collective-permute-start | bytes 1572872 | tf_op jit(solution)/shard_map/ppermute | solution.py:10
  246.7 3.1 %copy-start.5 = (bf16[512,512]{1,0:T(8,128)(2,1)S(1)}, bf16[512,512]{1,0:T(8,128)(2,1)}, u32[]{:S(2)}) copy-start(bf16[512,512]{1,0:T(8,128)(2,1)} %copy-done.4) | copy-start | bytes 1572868
  249.3 1.0 copy-start.35
  250.3 1.0 copy-start.17
  250.3 1.2 copy-start.19
  250.3 1.3 copy-start.21
where the time goes:
time: 280 us; the launch traced here: 278 us
  waiting for transfers between devices  139 us (50%)
  matrix products  40.2 us (14%)
  local copies, waits for them, and re-layouts  35 us (12%)
  blocking collectives  23.4 us (8%)
  starting transfers between devices  21.3 us (8%)
  other arithmetic  18.9 us (7%)
    ppermute x14, waiting for transfers between devices, passed_along(): return lax.ppermute(block, axis, route)  79.9 us
    ppermute x6, waiting for transfers between devices, from_behind(): return lax.ppermute(shard, axis, pairs)  58.9 us
    all_to_all x1, blocking collectives, shards(): lax.all_to_all(kept, 'segment', split_axis=0, concat_axis=0, tiled=True)  23.4 us
    dot_general x7, matrix products, run_layer(): jnp.einsum('bkij,bkjd->bid', weights, picked, preferred_element_type=jnp....  18.1 us
    gather x7, local copies, waits for them, and re-layouts, run_layer(): picked = padded_blocks[local_index]  17.4 us
    ppermute x14, starting transfers between devices, passed_along(): return lax.ppermute(block, axis, route)  13.6 us
    concatenate x7, local copies, waits for them, and re-layouts, run_layer(): padded = jnp.concatenate([below, sender, above], axis=0)  12 us
    concatenate x7, other arithmetic, run_layer(): padded = jnp.concatenate([below, sender, above], axis=0)  8.99 us
  transfers between devices with their start and end apart: 20, of which 20 were waited for; matrix products, arithmetic and copies ran while one was open for 1% of the time, Pallas kernels for 0%

commit v1 on v0

v1 whole, which is shorter than its diff:
```python
import functools

import jax
import jax.numpy as jnp
from jax import lax
from jax.experimental import pallas as pl
from jax.experimental.pallas import tpu as pltpu
from jax.sharding import PartitionSpec as P

D = 512
BLK = 128
BD = 4
K = 6
SEG = 4
Y, Z = 4, 8
HALF = D // 2
META = 16
BF = jnp.bfloat16
F32 = jnp.float32
ANY = pl.BlockSpec(memory_space=pl.ANY)
SMEM = pl.BlockSpec(memory_space=pltpu.SMEM)
VMEM = pl.BlockSpec(memory_space=pltpu.VMEM)


def silu(v):
    return (0.5 * v) * (1.0 + jnp.tanh(0.5 * v))


def params(mib):
    return pltpu.CompilerParams(vmem_limit_bytes=mib * 2**20)


def by_segment(x):
    return [(i, i ^ x) for i in range(SEG)]


def shifted(by):
    return [(i, (i + by) % SEG) for i in range(SEG)]


def dom_pairs(move):
    out = []
    for d in range(Z * Y * 2):
        z, y, c = move(d // (2 * Y), d // 2 % Y, d % 2)
        out.append((d, ((z % Z) * Y + y % Y) * 2 + c % 2))
    return out


def along_y(by):
    return dom_pairs(lambda z, y, c: (z, y + by, c))


def along_z(by):
    return dom_pairs(lambda z, y, c: (z + by, y, c))


def to_dom(by):
    n = Z * Y * 2
    return [(i, (i + by) % n) for i in range(n)]


OTHER_CORE = dom_pairs(lambda z, y, c: (z, y, c + 1))


def pack_kernel(scal, src, cnt, gain, w0, w1, w2, w3, out, buf, sem):
    y, zpar, c, dom = scal[1], scal[2], scal[3], scal[8]
    for m, w in enumerate((w0, w1, w2, w3)):

        @pl.when(y == m)
        def _():
            pltpu.make_async_copy(
                w.at[
                    0,
                    0,
                    pl.ds(pl.multiple_of(zpar * HALF, HALF), HALF),
                    pl.ds(pl.multiple_of(c * HALF, HALF), HALF),
                ],
                buf,
                sem,
            ).start()

    row = lax.broadcasted_iota(jnp.int32, (META, HALF), 0)
    col = lax.broadcasted_iota(jnp.int32, (META, HALF), 1)
    meta = jnp.zeros((META, HALF), F32)
    for b in range(BD):
        for k in range(K):
            rel = (src[0, b, k] - (dom * BD - 1) + 512) & 255
            code = jnp.where(k < cnt[0, b], rel, 7).astype(F32)
            meta = jnp.where((row == 0) & (col == b * K + k), code, meta)
    left = gain[0]
    for part in range(3):
        piece = left.astype(BF).astype(F32)
        left = left - piece
        for half in range(2):
            meta = jnp.where(
                row == 2 + 2 * part + half, piece[:, half * HALF : (half + 1) * HALF], meta
            )
    out[HALF:, :] = meta.astype(BF)
    pltpu.make_async_copy(out.at[:HALF], buf, sem).wait()
    out[:HALF, :] = buf[...]


def pack(scal, src, cnt, gain, ws):
    return pl.pallas_call(
        pack_kernel,
        out_shape=jax.ShapeDtypeStruct((HALF + META, HALF), BF),
        in_specs=[SMEM, SMEM, SMEM, VMEM] + [ANY] * 4,
        out_specs=VMEM,
        scratch_shapes=[pltpu.VMEM((HALF, HALF), BF), pltpu.SemaphoreType.DMA],
        compiler_params=params(4),
        name="pack",
    )(scal, src, cnt, gain, *ws)


def start_weights(scal, section, own, stages, mats, wbuf, wsem):
    p, zpar, c = scal[0], scal[2], scal[3]

    @pl.when(p == section)
    def _():
        for i, m in enumerate(mats):
            pltpu.make_async_copy(own[i].at[0, 0], wbuf.at[i], wsem.at[i]).start()

    by_stage = {}
    for q in range(SEG):
        if q != section:
            by_stage.setdefault(section - (1 if section > q else 0), []).append(q)
    for j, holders in by_stage.items():
        cond = functools.reduce(jnp.logical_or, [p == q for q in holders])

        @pl.when(cond)
        def _():
            for i, m in enumerate(mats):
                r = scal[4 + m]
                for core in range(2):
                    for zrel in range(2):
                        rows = pl.multiple_of(((zpar + zrel) & 1) * HALF, HALF)
                        cols = pl.multiple_of(((c + core) & 1) * HALF, HALF)
                        pltpu.make_async_copy(
                            stages[j][core].at[zrel * 4 + r],
                            wbuf.at[i, pl.ds(rows, HALF), pl.ds(cols, HALF)],
                            wsem.at[i],
                        ).start()


def wait_weight(own, i, wbuf, wsem):
    pltpu.make_async_copy(own[i].at[0, 0], wbuf.at[i], wsem.at[i]).wait()


def tile_halves(section, p):
    k = (p - section) % SEG
    if k == 0:
        return "ownA", "ownB"
    if k == 1:
        return "r1p", ("r2p" if p == 1 else "r3p")
    if k == 2:
        return ("r3p" if p == 1 else "r2p"), ("r3m" if p == 3 else "r2m")
    return ("r2m" if p == 3 else "r3m"), "r1m"


def start_tiles(scal, section, own, moved, tbuf, tsem):
    for q in range(SEG):

        @pl.when(scal[0] == q)
        def _():
            for half, name in enumerate(tile_halves(section, q)):
                src = own.at[0, pl.ds(2 * half, 2)] if name.startswith("own") else moved[name]
                pltpu.make_async_copy(src, tbuf.at[pl.ds(2 * half, 2)], tsem.at[half]).start()


def section_kernel(section, names, n_stage, scal, ints, meta, h, below, above, *rest):
    first = section == 0
    mats = (0, 1, 2, 3) if first else (1, 2, 3)
    n = len(mats)
    rest = list(rest)
    if not first:
        sender = rest.pop(0)
    own, rest = rest[:n], rest[n:]
    stages, rest = [rest[2 * j : 2 * j + 2] for j in range(n_stage)], rest[2 * n_stage :]
    tiles = rest.pop(0)
    moved = dict(zip(names, rest))
    rest = rest[len(names) :]
    out, wbuf, tbuf, sbuf, gbuf, hbuf, wsem, tsem, hsem = rest

    start_weights(scal, section, own, stages, mats, wbuf, wsem)
    if first:
        pltpu.make_async_copy(h.at[scal[0]], hbuf, hsem).start()
    else:
        pltpu.make_async_copy(h, hbuf, hsem).start()
    start_tiles(scal, section, tiles, moved, tbuf, tsem)
    x = scal[0] ^ section
    if first:
        pltpu.make_async_copy(h.at[0], hbuf, hsem).wait()
        wait_weight(own, 0, wbuf, wsem)
        w = wbuf[0]
        for rows, src in ((0, below), (5 * BLK, above)):
            s = silu(jnp.dot(src[...], w, preferred_element_type=F32)).astype(BF)
            sbuf[rows : rows + BLK, :] = s
        for i in range(2):
            s = jnp.dot(hbuf[i * HALF : (i + 1) * HALF, :], w, preferred_element_type=F32)
            sbuf[BLK + i * HALF : BLK + (i + 1) * HALF, :] = silu(s).astype(BF)
    else:
        sbuf[:BLK, :] = below[...]
        sbuf[BLK : 5 * BLK, :] = sender[...]
        sbuf[5 * BLK :, :] = above[...]
        pltpu.make_async_copy(h, hbuf, hsem).wait()
    for half in range(2):
        pltpu.make_async_copy(
            tiles.at[0, pl.ds(2 * half, 2)], tbuf.at[pl.ds(2 * half, 2)], tsem.at[half]
        ).wait()
    for b in range(BD):
        left, right = [], []
        for k in range(K):
            code = ints[x, b * K + k]
            used = code < 7
            at = pl.multiple_of(jnp.where(used, code, 0) * BLK, BLK)
            tile = tbuf[b, k]
            left.append(jnp.where(used, tile, jnp.zeros_like(tile)))
            right.append(sbuf[pl.ds(at, BLK), :])
        got = jnp.dot(
            jnp.concatenate(left, axis=1),
            jnp.concatenate(right, axis=0),
            preferred_element_type=F32,
        )
        gbuf[b * BLK : (b + 1) * BLK, :] = got.astype(BF)
    for i in range(n - 3, n):
        wait_weight(own, i, wbuf, wsem)
    m = meta[x].astype(F32)
    gain = jnp.concatenate(
        [m[2 + h : 3 + h, :] + (m[4 + h : 5 + h, :] + m[6 + h : 7 + h, :]) for h in range(2)],
        axis=1,
    )
    for i in range(2):
        rows = slice(i * HALF, (i + 1) * HALF)
        mixed = jnp.dot(hbuf[rows, :], wbuf[n - 3], preferred_element_type=F32)
        mixed = mixed + jnp.dot(gbuf[rows, :], wbuf[n - 2], preferred_element_type=F32)
        mean = jnp.mean(mixed * mixed, axis=-1, keepdims=True)
        scaled = mixed * lax.rsqrt(mean + 1e-05) * gain
        update = silu(scaled).astype(BF)
        new = hbuf[rows, :].astype(F32) + jnp.dot(
            update, wbuf[n - 1], preferred_element_type=F32
        )
        out[rows, :] = new.astype(BF)


def section_call(section, scal, ints, meta, h, below, above, sender, own, stages, tiles, moved):
    first = section == 0
    mats = (0, 1, 2, 3) if first else (1, 2, 3)
    own = [own[m] for m in mats]
    flat = [a for pair in stages for a in pair]
    args = [scal, ints, meta, h, below, above]
    specs = [SMEM, SMEM, VMEM, ANY, VMEM, VMEM]
    if not first:
        args.append(sender)
        specs.append(VMEM)
    args += own + flat + [tiles] + list(moved.values())
    specs += [ANY] * (len(args) - len(specs))
    n = len(mats)
    return pl.pallas_call(
        functools.partial(section_kernel, section, list(moved), len(stages)),
        out_shape=jax.ShapeDtypeStruct((BD * BLK, D), BF),
        in_specs=specs,
        out_specs=VMEM,
        scratch_shapes=[
            pltpu.VMEM((n, D, D), BF),
            pltpu.VMEM((BD, K, BLK, BLK), BF),
            pltpu.VMEM(((BD + 2) * BLK, D), BF),
            pltpu.VMEM((BD * BLK, D), BF),
            pltpu.VMEM((BD * BLK, D), BF),
            pltpu.SemaphoreType.DMA((4,)),
            pltpu.SemaphoreType.DMA((2,)),
            pltpu.SemaphoreType.DMA,
        ],
        compiler_params=params(24),
        cost_estimate=pl.CostEstimate(
            flops=1_500_000_000, bytes_accessed=4_000_000, transcendentals=262144
        ),
        name=f"section{section}",
    )(*args)


def sender_kernel(section, n_stage, scal, h, own, *rest):
    stages = [rest[2 * j : 2 * j + 2] for j in range(n_stage)]
    full, head, tail, wbuf, wsem = rest[2 * n_stage :]
    start_weights(scal, section, [own], stages, (0,), wbuf, wsem)
    wait_weight([own], 0, wbuf, wsem)
    w = wbuf[0]
    for i in range(2):
        rows = slice(i * HALF, (i + 1) * HALF)
        s = silu(jnp.dot(h[rows, :], w, preferred_element_type=F32)).astype(BF)
        full[rows, :] = s
        if i == 0:
            head[...] = s[:BLK, :]
        else:
            tail[...] = s[HALF - BLK :, :]


def sender_call(section, scal, h, own, stages):
    flat = [a for pair in stages for a in pair]
    return pl.pallas_call(
        functools.partial(sender_kernel, section, len(stages)),
        out_shape=[
            jax.ShapeDtypeStruct((BD * BLK, D), BF),
            jax.ShapeDtypeStruct((BLK, D), BF),
            jax.ShapeDtypeStruct((BLK, D), BF),
        ],
        in_specs=[SMEM, VMEM, ANY] + [ANY] * len(flat),
        out_specs=[VMEM] * 3,
        scratch_shapes=[pltpu.VMEM((1, D, D), BF), pltpu.SemaphoreType.DMA((1,))],
        compiler_params=params(8),
        cost_estimate=pl.CostEstimate(
            flops=270_000_000, bytes_accessed=1_500_000, transcendentals=262144
        ),
        name=f"sender{section}",
    )(scal, h, own, *flat)


def gather_stage(pieces):
    n = pieces.shape[0]
    ring = [pieces] + [lax.ppermute(pieces, "dom", along_y(by)) for by in (1, -1, 2)]
    mine = jnp.stack(ring, axis=1)
    upper = lax.ppermute(mine[:, :, :BLK, :], "dom", along_z(1))
    lower = lax.ppermute(mine[:, :, BLK:, :], "dom", along_z(-1))
    mine = jnp.concatenate([mine, jnp.concatenate([upper, lower], axis=2)], axis=1)
    other = lax.ppermute(mine, "dom", OTHER_CORE)
    return [(mine[i], other[i]) for i in range(n)]


def shards(samples, w_source, w_self, w_message, w_output, norm_gain, tile_source, tile_count, tile_value):
    p = lax.axis_index("segment")
    dom = lax.axis_index("dom")
    c, y, zpar = dom % 2, dom // 2 % Y, dom // (2 * Y) % 2
    steps = jnp.array([0, 2, 3, 1], jnp.int32)
    scal = jnp.stack(
        [p, y, zpar, c] + [steps[(m - y) % Y] for m in range(4)] + [dom]
    ).astype(jnp.int32)
    ws = [w_source, w_self, w_message, w_output]
    packed = pack(scal, tile_source, tile_count, norm_gain, ws)
    crossed = [packed] + [lax.ppermute(packed, "segment", by_segment(x)) for x in (1, 2, 3)]

    h = lax.dynamic_index_in_dim(samples, p, 0, keepdims=False)
    below = lax.ppermute(h[(BD - 1) * BLK :], "dom", to_dom(1))
    above = lax.ppermute(h[:BLK], "dom", to_dom(-1))

    half_a, half_b = tile_value[0, :2], tile_value[0, 2:]
    root = p == 0
    moved = {}
    moved["r1p"] = lax.ppermute(half_a, "segment", shifted(1))
    moved["r1m"] = lax.ppermute(half_b, "segment", shifted(-1))
    moved["r2p"] = lax.ppermute(jnp.where(root, half_b, moved["r1p"]), "segment", shifted(1))
    moved["r2m"] = lax.ppermute(jnp.where(root, half_a, moved["r1m"]), "segment", shifted(-1))
    early = dict(moved)
    moved["r3p"] = lax.ppermute(jnp.where(root, moved["r1p"], half_b), "segment", shifted(1))
    moved["r3m"] = lax.ppermute(jnp.where(root, moved["r1m"], half_a), "segment", shifted(-1))

    meta = jnp.stack([a[HALF:] for a in crossed])
    ints = meta[:, 0, :BLK].astype(jnp.int32)
    need = jnp.array([[1, 2, 3], [1, 3, 2], [2, 3, 1], [3, 2, 1]], jnp.int32)[p]
    parts = jnp.stack([a[:HALF] for a in crossed[1:]])
    stage = [lax.dynamic_index_in_dim(parts, need[j] - 1, 0, keepdims=True) for j in range(3)]
    stages = gather_stage(stage[0])
    stages += gather_stage(jnp.concatenate(stage[1:], axis=0))

    h = section_call(0, scal, ints, meta, samples, below, above, None, ws, stages[:1], tile_value, early)
    for section in range(1, SEG):
        sender, head, tail = sender_call(section, scal, h, w_source, stages)
        below = lax.ppermute(tail, "dom", to_dom(1))
        above = lax.ppermute(head, "dom", to_dom(-1))
        h = section_call(section, scal, ints, meta, h, below, above, sender, ws, stages, tile_value, moved)
    return h[None]


def solution(mesh):
    return jax.shard_map(
        shards,
        mesh=mesh,
        in_specs=(
            P(None, "dom", None),
            P("segment", None, None, None),
            P("segment", None, None, None),
            P("segment", None, None, None),
            P("segment", None, None, None),
            P("segment", None, None),
            P("segment", "dom", None),
            P("segment", "dom"),
            P("segment", "dom", None, None, None),
        ),
        out_specs=P("segment", "dom", None),
        check_vma=False,
    )
```

time: 280 us -> 127 us (0.45)
  waiting for transfers between devices: 139 us -> 40.7 us
  matrix products: 40.2 us -> 0 us
  starting transfers between devices: 21.3 us -> 48.1 us
  blocking collectives: 23.4 us -> 0 us
  local copies, waits for them, and re-layouts: 35 us -> 13.2 us
  Pallas kernels: 0 us -> 18.5 us
  other arithmetic: 18.9 us -> 0.53 us
  between operations: 0.75 us -> 4.44 us
    ppermute x20 -> x29, waiting for transfers between devices: 139 us -> 40.7 us  [the longest x2 12.1 us: gather_stage(): upper = lax.ppermute(mine[:, :, :BLK, :], 'dom', along_z(1))]
    dot_general x35 -> x0, matrix products: 40.2 us -> none  [the longest x7 18.1 us: run_layer(): jnp.einsum('bkij,bkjd->bid', weights, picked, preferred_element_type=jnp....]
    ppermute x20 -> x29, starting transfers between devices: 21.3 us -> 48.1 us  [the longest x3 15.4 us: shards(): above = lax.ppermute(head, 'dom', to_dom(-1))]
    all_to_all x1 -> x0, blocking collectives: 23.4 us -> none  [shards(): lax.all_to_all(kept, 'segment', split_axis=0, concat_axis=0, tiled=True)]
    pallas_call x0 -> x8, Pallas kernels: none -> 18.5 us  [the longest x4 14.4 us: section_call(): pl.pallas_call(functools.partial(section_kernel, section, list(moved), le...]
    gather x7 -> x0, local copies, waits for them, and re-layouts: 17.4 us -> none  [run_layer(): picked = padded_blocks[local_index]]
    concatenate x7 -> x0, local copies, waits for them, and re-layouts: 12 us -> none  [run_layer(): padded = jnp.concatenate([below, sender, above], axis=0)]
    concatenate x7 -> x2, other arithmetic: 8.99 us -> 0.1 us  [gather_stage(): jnp.concatenate([mine, jnp.concatenate([upper, lower], axis=2)], axis=1)]
  transfers between devices with their start and end apart: 20 -> 29, of which waited for: 20 -> 12; matrix products, arithmetic and copies ran while one was open for 1% -> 3% of each run, Pallas kernels for 0% -> 4%
where the time goes in v1:
time: 127 us; the launch traced here: 126 us
  starting transfers between devices  48.1 us (38%)
  waiting for transfers between devices  40.7 us (32%)
  Pallas kernels  18.5 us (15%)
  local copies, waits for them, and re-layouts  13.2 us (10%)
  between operations  4.44 us (3%)
    ppermute x3, starting transfers between devices, shards(): above = lax.ppermute(head, 'dom', to_dom(-1))  15.4 us
    pallas_call x4, Pallas kernels, section_call(): pl.pallas_call(functools.partial(section_kernel, section, list(moved), le...  14.4 us
    ppermute x2, waiting for transfers between devices, gather_stage(): upper = lax.ppermute(mine[:, :, :BLK, :], 'dom', along_z(1))  12.1 us
    ppermute x6, waiting for transfers between devices, gather_stage(): lax.ppermute(pieces, 'dom', along_y(by))  10.6 us
    ppermute x6, starting transfers between devices, gather_stage(): lax.ppermute(pieces, 'dom', along_y(by))  10 us
    ppermute x3, waiting for transfers between devices, shards(): below = lax.ppermute(tail, 'dom', to_dom(1))  7.77 us
    unnamed x33, local copies, waits for them, and re-layouts  6.33 us
    ppermute x2, starting transfers between devices, gather_stage(): lower = lax.ppermute(mine[:, :, BLK:, :], 'dom', along_z(-1))  5.77 us
  transfers between devices with their start and end apart: 29, of which 12 were waited for; matrix products, arithmetic and copies ran while one was open for 3% of the time, Pallas kernels for 4%

profile of v1, /device:TPU:6, one launch (start us, length us, event | category | flops | bytes accessed | tf_op | source)
XLA Modules:
  0.0 125.6 jit_solution(4298647847416145117)
XLA Ops:
  0.0 1.5 %fusion.4 = (s32[1]{0:T(128)}, s32[1]{0:T(128)}, s32[1]{0:T(128)}, s32[1]{0:T(128)}) fusion(s32[4]{0:T(128)} %constant.106.clone, s32[]{:T(128)S(6)} %select_n.97, s32[]{:T(128)S(6)} %select_n.93, s32[]{:T(128)S(6)} %select_n.91, s32[]{:T(128)S(6)} %select_n.95), kind=kLoop, calls=%fused_computation.43 | loop fusion | bytes 48 | tf_op jit(solution)/shard_map/dynamic_slice | solution.py:334
  1.5 2.6 %stack.80.scal = s32[9]{0:T(128)S(1)} concatenate(s32[1]{0:T(128)} %bitcast, s32[1]{0:T(128)} %bitcast.1, s32[1]{0:T(128)} %bitcast.2, s32[1]{0:T(128)} %bitcast.3, s32[1]{0:T(128)} %get-tuple-element.52, s32[1]{0:T(128)} %get-tuple-element.51, s32[1]{0:T(128)} %get-tuple-element.53, s32[1]{0:T(128)} %get-tuple-element.50, s32[1]{0:T(128)} %bitcast.4), dimensions={0} | concatenate | bytes 72 | tf_op jit(solution)/shard_map/stack | solution.py:333
  4.1 1.0 copy-done.1
  5.1 1.0 copy-done.3
  6.1 1.0 copy-done.5
  7.2 1.0 copy-done.7
  8.2 0.7 copy-done.10
  8.9 0.7 copy-done.11
  9.6 0.7 copy-done.12
  10.2 0.7 pack.1
  10.9 2.3 %collective-permute-start.2 = (bf16[272,256]{1,0:T(8,128)(2,1)S(1)}, bf16[272,256]{1,0:T(8,128)(2,1)S(1)}, u32[]{:S(2)}, u32[]{:S(2)}) collective-permute-start(bf16[272,256]{1,0:T(8,128)(2,1)S(1)} %pack.1), channel_id=1, source_target_pairs={{0,192},{64,128},{128,64},{192,0},{1,193},{65,129},{129,65},{193,1... | collective-permute-start | bytes 417800 | tf_op jit(solution)/shard_map/ppermute | solution.py:338
  13.2 0.7 collective-permute-start.1
  13.9 1.2 collective-permute-start
  15.2 2.3 %collective-permute-start.11 = (bf16[2,6,128,128]{3,2,1,0:T(8,128)(2,1)S(1)}, bf16[2,6,128,128]{3,2,1,0:T(8,128)(2,1)S(1)}, u32[]{:S(2)}, u32[]{:S(2)}) collective-permute-start(bf16[2,6,128,128]{3,2,1,0:T(8,128)(2,1)S(1)} %get-tuple-element.40), channel_id=1, source_target_pairs={{0,64},{64,128},{128,192},{192,0},{1,65},{65,129},{129,193},{193,1... | collective-permute-start | bytes 1179656 | tf_op jit(solution)/shard_map/ppermute | solution.py:347
  17.5 0.7 constant_dynamic-slice_fusion.3
  18.2 0.7 fusion.3
  22.7 1.0 dynamic-slice_bitcast_fusion
  23.8 1.5 %collective-permute-start.5 = (bf16[1,256,256]{2,1,0:T(8,128)(2,1)S(1)}, bf16[1,256,256]{2,1,0:T(8,128)(2,1)S(1)}, u32[]{:S(2)}, u32[]{:S(2)}) collective-permute-start(bf16[1,256,256]{2,1,0:T(8,128)(2,1)S(1)} %get-tuple-element.24), channel_id=1, source_target_pairs={{0,2},{1,3},{2,4},{3,5},{4,6},{5,7},{6,0},{7,1},{8,10},{9,11},{10,... | collective-permute-start | bytes 393224 | tf_op jit(solution)/shard_map/ppermute | solution.py:319
  25.3 1.9 %collective-permute-start.6 = (bf16[1,256,256]{2,1,0:T(8,128)(2,1)S(1)}, bf16[1,256,256]{2,1,0:T(8,128)(2,1)S(1)}, u32[]{:S(2)}, u32[]{:S(2)}) collective-permute-start(bf16[1,256,256]{2,1,0:T(8,128)(2,1)S(1)} %get-tuple-element.24), channel_id=1, source_target_pairs={{0,6},{1,7},{2,0},{3,1},{4,2},{5,3},{6,4},{7,5},{8,14},{9,15},{10,... | collective-permute-start | bytes 393224 | tf_op jit(solution)/shard_map/ppermute | solution.py:319
  27.1 1.8 %collective-permute-start.7 = (bf16[1,256,256]{2,1,0:T(8,128)(2,1)S(1)}, bf16[1,256,256]{2,1,0:T(8,128)(2,1)S(1)}, u32[]{:S(2)}, u32[]{:S(2)}) collective-permute-start(bf16[1,256,256]{2,1,0:T(8,128)(2,1)S(1)} %get-tuple-element.24), channel_id=1, source_target_pairs={{0,4},{1,5},{2,6},{3,7},{4,0},{5,1},{6,2},{7,3},{8,12},{9,13},{10,... | collective-permute-start | bytes 393224 | tf_op jit(solution)/shard_map/ppermute | solution.py:319
  29.1 2.5 %collective-permute-done.5 = bf16[1,256,256]{2,1,0:T(8,128)(2,1)S(1)} collective-permute-done((bf16[1,256,256]{2,1,0:T(8,128)(2,1)S(1)}, bf16[1,256,256]{2,1,0:T(8,128)(2,1)S(1)}, u32[]{:S(2)}, u32[]{:S(2)}) %collective-permute-start.5) | collective-permute-done | bytes 131104 | tf_op jit(solution)/shard_map/ppermute | solution.py:319
  31.6 3.2 %collective-permute-start.16 = (bf16[2,256,256]{2,1,0:T(8,128)(2,1)S(1)}, bf16[2,256,256]{2,1,0:T(8,128)(2,1)S(1)}, u32[]{:S(2)}, u32[]{:S(2)}) collective-permute-start(bf16[2,256,256]{2,1,0:T(8,128)(2,1)S(1)} %get-tuple-element.46), channel_id=1, source_target_pairs={{0,6},{1,7},{2,0},{3,1},{4,2},{5,3},{6,4},{7,5},{8,14},{9,15},{10,... | collective-permute-start | bytes 786440 | tf_op jit(solution)/shard_map/ppermute | solution.py:319
  34.8 0.4 collective-permute-done.7
  35.2 1.7 %collective-permute-start.17 = (bf16[2,256,256]{2,1,0:T(8,128)(2,1)S(1)}, bf16[2,256,256]{2,1,0:T(8,128)(2,1)S(1)}, u32[]{:S(2)}, u32[]{:S(2)}) collective-permute-start(bf16[2,256,256]{2,1,0:T(8,128)(2,1)S(1)} %get-tuple-element.46), channel_id=1, source_target_pairs={{0,4},{1,5},{2,6},{3,7},{4,0},{5,1},{6,2},{7,3},{8,12},{9,13},{10,... | collective-permute-start | bytes 786440 | tf_op jit(solution)/shard_map/ppermute | solution.py:319
  37.0 7.7 %collective-permute-done.15 = bf16[2,256,256]{2,1,0:T(8,128)(2,1)S(1)} collective-permute-done((bf16[2,256,256]{2,1,0:T(8,128)(2,1)S(1)}, bf16[2,256,256]{2,1,0:T(8,128)(2,1)S(1)}, u32[]{:S(2)}, u32[]{:S(2)}) %collective-permute-start.15) | collective-permute-done | bytes 262176 | tf_op jit(solution)/shard_map/ppermute | solution.py:319
  44.7 0.1 pad_maximum_fusion
  44.8 0.1 fusion.1
  44.9 1.8 %collective-permute-start.18 = (bf16[2,4,128,256]{3,2,1,0:T(8,128)(2,1)S(1)}, bf16[2,4,128,256]{3,2,1,0:T(8,128)(2,1)S(1)}, u32[]{:S(2)}, u32[]{:S(2)}) collective-permute-start(bf16[2,4,128,256]{3,2,1,0:T(8,128)(2,1)S(1)} %get-tuple-element.35), channel_id=1, source_target_pairs={{0,8},{1,9},{2,10},{3,11},{4,12},{5,13},{6,14},{7,15},{8,16},{9,17... | collective-permute-start | bytes 1572872 | tf_op jit(solution)/shard_map/ppermute | solution.py:321
  46.7 4.0 %collective-permute-start.19 = (bf16[2,4,128,256]{3,2,1,0:T(8,128)(2,1)S(1)}, bf16[2,4,128,256]{3,2,1,0:T(8,128)(2,1)S(1)}, u32[]{:S(2)}, u32[]{:S(2)}) collective-permute-start(bf16[2,4,128,256]{3,2,1,0:T(8,128)(2,1)S(1)} %get-tuple-element.36), channel_id=1, source_target_pairs={{0,56},{1,57},{2,58},{3,59},{4,60},{5,61},{6,62},{7,63},{8,0},{9,1... | collective-permute-start | bytes 1572872 | tf_op jit(solution)/shard_map/ppermute | solution.py:322
  50.9 12.1 %collective-permute-done.18 = bf16[2,4,128,256]{3,2,1,0:T(8,128)(2,1)S(1)} collective-permute-done((bf16[2,4,128,256]{3,2,1,0:T(8,128)(2,1)S(1)}, bf16[2,4,128,256]{3,2,1,0:T(8,128)(2,1)S(1)}, u32[]{:S(2)}, u32[]{:S(2)}) %collective-permute-start.18) | collective-permute-done | bytes 524320 | tf_op jit(solution)/shard_map/ppermute | solution.py:321
  63.0 1.7 %collective-permute-start.9 = (bf16[1,4,128,256]{3,2,1,0:T(8,128)(2,1)S(1)}, bf16[1,4,128,256]{3,2,1,0:T(8,128)(2,1)S(1)}, u32[]{:S(2)}, u32[]{:S(2)}) collective-permute-start(bf16[1,4,128,256]{3,2,1,0:T(8,128)(2,1)S(1)} %get-tuple-element.42), channel_id=1, source_target_pairs={{0,56},{1,57},{2,58},{3,59},{4,60},{5,61},{6,62},{7,63},{8,0},{9,1... | collective-permute-start | bytes 786440 | tf_op jit(solution)/shard_map/ppermute | solution.py:322
  64.7 0.1 maximum_dynamic-update-slice_fusion
  64.8 0.3 collective-permute-start.20
  65.1 0.6 collective-permute-start.3
  65.7 3.6 %collective-permute-done.9 = bf16[1,4,128,256]{3,2,1,0:T(8,128)(2,1)S(1)} collective-permute-done((bf16[1,4,128,256]{3,2,1,0:T(8,128)(2,1)S(1)}, bf16[1,4,128,256]{3,2,1,0:T(8,128)(2,1)S(1)}, u32[]{:S(2)}, u32[]{:S(2)}) %collective-permute-start.9) | collective-permute-done | bytes 262176 | tf_op jit(solution)/shard_map/ppermute | solution.py:322
  69.4 0.1 collective-permute-start.10
  69.5 0.1 broadcast_select_fusion
  69.6 1.8 %collective-permute-start.13 = (bf16[2,6,128,128]{3,2,1,0:T(8,128)(2,1)S(1)}, bf16[2,6,128,128]{3,2,1,0:T(8,128)(2,1)S(1)}, u32[]{:S(2)}, u32[]{:S(2)}) collective-permute-start(bf16[2,6,128,128]{3,2,1,0:T(8,128)(2,1)S(1)} %get-tuple-element.37), channel_id=1, source_target_pairs={{0,64},{64,128},{128,192},{192,0},{1,65},{65,129},{129,193},{193,1... | collective-permute-start | bytes 1179656 | tf_op jit(solution)/shard_map/ppermute | solution.py:349
  71.4 0.3 collective-permute-start.14
  71.8 1.2 collective-permute-done.3.below
  72.9 1.6 %collective-permute-start.4 = (bf16[128,512]{1,0:T(8,128)(2,1)S(1)}, bf16[128,512]{1,0:T(8,128)(2,1)S(1)}, u32[]{:S(2)}, u32[]{:S(2)}) collective-permute-start(bf16[128,512]{1,0:T(8,128)(2,1)S(1)} %get-tuple-element.29), channel_id=1, source_target_pairs={{0,63},{1,0},{2,1},{3,2},{4,3},{5,4},{6,5},{7,6},{8,7},{9,8},{10,9... | collective-permute-start | bytes 393224 | tf_op jit(solution)/shard_map/ppermute | solution.py:342
  74.5 0.1 slice_bitcast_fusion.1
  74.7 2.4 %collective-permute-done.4.above = bf16[128,512]{1,0:T(8,128)(2,1)S(1)} collective-permute-done((bf16[128,512]{1,0:T(8,128)(2,1)S(1)}, bf16[128,512]{1,0:T(8,128)(2,1)S(1)}, u32[]{:S(2)}, u32[]{:S(2)}) %collective-permute-start.4) | collective-permute-done | bytes 131104 | tf_op jit(solution)/shard_map/ppermute | solution.py:342
  77.1 2.9 %collective-permute-start.23 = (bf16[2,6,128,128]{3,2,1,0:T(8,128)(2,1)S(1)}, bf16[2,6,128,128]{3,2,1,0:T(8,128)(2,1)S(1)}, u32[]{:S(2)}, u32[]{:S(2)}) collective-permute-start(bf16[2,6,128,128]{3,2,1,0:T(8,128)(2,1)S(1)} %get-tuple-element.38), channel_id=1, source_target_pairs={{0,64},{64,128},{128,192},{192,0},{1,65},{65,129},{129,193},{193,1... | collective-permute-start | bytes 1179656 | tf_op jit(solution)/shard_map/ppermute | solution.py:352
  80.0 1.7 %collective-permute-done.13.rest_9_.rest_13_ = bf16[2,6,128,128]{3,2,1,0:T(8,128)(2,1)S(1)} collective-permute-done((bf16[2,6,128,128]{3,2,1,0:T(8,128)(2,1)S(1)}, bf16[2,6,128,128]{3,2,1,0:T(8,128)(2,1)S(1)}, u32[]{:S(2)}, u32[]{:S(2)}) %collective-permute-start.13) | collective-permute-done | bytes 393248 | tf_op jit(solution)/shard_map/ppermute | solution.py:349
  81.6 0.8 collective-permute-start.24
  82.5 1.4 %collective-permute-done.14.rest_10_.rest_14_ = bf16[2,6,128,128]{3,2,1,0:T(8,128)(2,1)S(1)} collective-permute-done((bf16[2,6,128,128]{3,2,1,0:T(8,128)(2,1)S(1)}, bf16[2,6,128,128]{3,2,1,0:T(8,128)(2,1)S(1)}, u32[]{:S(2)}, u32[]{:S(2)}) %collective-permute-start.14) | collective-permute-done | bytes 393248 | tf_op jit(solution)/shard_map/ppermute | solution.py:350
  83.9 3.8 %section0.1.h = bf16[512,512]{1,0:T(8,128)(2,1)S(1)} custom-call(s32[9]{0:T(128)S(1)} %stack.80.scal, s32[4,128]{1,0:T(4,128)S(1)} %bitcast.90, bf16[4,16,256]{2,1,0:T(8,128)(2,1)S(1)} %pad_maximum_fusion.4.meta, bf16[4,512,512]{2,1,0:T(8,128)(2,1)S(1)} %copy-done.9, bf16[128,512]{1,0:T(8,128)(2,1)S(1)} %collective-permute-done.3.below, ...), custom_call_target="tpu_custom_call" | custom-call | flops 1500000000 | bytes 4000000 | tf_op jit(solution)/shard_map/section0/pallas_call | solution.py:258
  87.7 0.1 slice_bitcast_fusion
  87.9 1.1 sender1.1
  89.0 0.1 collective-permute-start.21
  89.1 5.1 %collective-permute-start.22 = (bf16[128,512]{1,0:T(8,128)(2,1)S(1)}, bf16[128,512]{1,0:T(8,128)(2,1)S(1)}, u32[]{:S(2)}, u32[]{:S(2)}) collective-permute-start(bf16[128,512]{1,0:T(8,128)(2,1)S(1)} %get-tuple-element.15), channel_id=1, source_target_pairs={{0,63},{1,0},{2,1},{3,2},{4,3},{5,4},{6,5},{7,6},{8,7},{9,8},{10,9... | collective-permute-start | bytes 393224 | tf_op jit(solution)/shard_map/ppermute | solution.py:367
  94.1 2.6 %collective-permute-done.21.below = bf16[128,512]{1,0:T(8,128)(2,1)S(1)} collective-permute-done((bf16[128,512]{1,0:T(8,128)(2,1)S(1)}, bf16[128,512]{1,0:T(8,128)(2,1)S(1)}, u32[]{:S(2)}, u32[]{:S(2)}) %collective-permute-start.21) | collective-permute-done | bytes 131104 | tf_op jit(solution)/shard_map/ppermute | solution.py:366
  96.8 3.3 %section1.1.h = bf16[512,512]{1,0:T(8,128)(2,1)S(1)} custom-call(s32[9]{0:T(128)S(1)} %stack.80.scal, s32[4,128]{1,0:T(4,128)S(1)} %bitcast.91, bf16[4,16,256]{2,1,0:T(8,128)(2,1)S(1)} %pad_maximum_fusion.4.meta, bf16[512,512]{1,0:T(8,128)(2,1)S(1)} %section0.1.h, bf16[128,512]{1,0:T(8,128)(2,1)S(1)} %collective-permute-done.21.below, ...), custom_call_target="tpu_custom_call" | custom-call | flops 1500000000 | bytes 4000000 | tf_op jit(solution)/shard_map/section1/pallas_call | solution.py:258
  100.0 1.3 %sender2.1 = (bf16[512,512]{1,0:T(8,128)(2,1)S(1)}, bf16[128,512]{1,0:T(8,128)(2,1)S(1)}, bf16[128,512]{1,0:T(8,128)(2,1)S(1)}) custom-call(s32[9]{0:T(128)S(1)} %stack.80.scal, bf16[512,512]{1,0:T(8,128)(2,1)S(1)} %section1.1.h, bf16[1,1,512,512]{3,2,1,0:T(8,128)(2,1)S(1)} %copy-done.8, bf16[8,256,256]{2,1,0:T(8,128)(2,1)S(1)} %bitcast.79, ...), custom_call_target="tpu_custom_call" | custom-call | flops 270000000 | bytes 1500000 | tf_op jit(solution)/shard_map/sender2/pallas_call | solution.py:299
  101.4 0.1 collective-permute-start.25
  101.5 5.1 %collective-permute-start.26 = (bf16[128,512]{1,0:T(8,128)(2,1)S(1)}, bf16[128,512]{1,0:T(8,128)(2,1)S(1)}, u32[]{:S(2)}, u32[]{:S(2)}) collective-permute-start(bf16[128,512]{1,0:T(8,128)(2,1)S(1)} %get-tuple-element.18), channel_id=1, source_target_pairs={{0,63},{1,0},{2,1},{3,2},{4,3},{5,4},{6,5},{7,6},{8,7},{9,8},{10,9... | collective-permute-start | bytes 393224 | tf_op jit(solution)/shard_map/ppermute | solution.py:367
  106.6 2.6 %collective-permute-done.25.below = bf16[128,512]{1,0:T(8,128)(2,1)S(1)} collective-permute-done((bf16[128,512]{1,0:T(8,128)(2,1)S(1)}, bf16[128,512]{1,0:T(8,128)(2,1)S(1)}, u32[]{:S(2)}, u32[]{:S(2)}) %collective-permute-start.25) | collective-permute-done | bytes 131104 | tf_op jit(solution)/shard_map/ppermute | solution.py:366
  109.2 3.3 %section2.1.h = bf16[512,512]{1,0:T(8,128)(2,1)S(1)} custom-call(s32[9]{0:T(128)S(1)} %stack.80.scal, s32[4,128]{1,0:T(4,128)S(1)} %bitcast.92, bf16[4,16,256]{2,1,0:T(8,128)(2,1)S(1)} %pad_maximum_fusion.4.meta, bf16[512,512]{1,0:T(8,128)(2,1)S(1)} %section1.1.h, bf16[128,512]{1,0:T(8,128)(2,1)S(1)} %collective-permute-done.25.below, ...), custom_call_target="tpu_custom_call" | custom-call | flops 1500000000 | bytes 4000000 | tf_op jit(solution)/shard_map/section2/pallas_call | solution.py:258
  112.5 1.1 sender3.1
  113.5 0.1 collective-permute-start.27
  113.6 5.2 %collective-permute-start.28 = (bf16[128,512]{1,0:T(8,128)(2,1)S(1)}, bf16[128,512]{1,0:T(8,128)(2,1)S(1)}, u32[]{:S(2)}, u32[]{:S(2)}) collective-permute-start(bf16[128,512]{1,0:T(8,128)(2,1)S(1)} %get-tuple-element.21), channel_id=1, source_target_pairs={{0,63},{1,0},{2,1},{3,2},{4,3},{5,4},{6,5},{7,6},{8,7},{9,8},{10,9... | collective-permute-start | bytes 393224 | tf_op jit(solution)/shard_map/ppermute | solution.py:367
  118.9 2.6 %collective-permute-done.27.below = bf16[128,512]{1,0:T(8,128)(2,1)S(1)} collective-permute-done((bf16[128,512]{1,0:T(8,128)(2,1)S(1)}, bf16[128,512]{1,0:T(8,128)(2,1)S(1)}, u32[]{:S(2)}, u32[]{:S(2)}) %collective-permute-start.27) | collective-permute-done | bytes 131104 | tf_op jit(solution)/shard_map/ppermute | solution.py:366
  121.4 4.0 %section3.1 = bf16[512,512]{1,0:T(8,128)(2,1)} custom-call(s32[9]{0:T(128)S(1)} %stack.80.scal, s32[4,128]{1,0:T(4,128)S(1)} %bitcast.93, bf16[4,16,256]{2,1,0:T(8,128)(2,1)S(1)} %pad_maximum_fusion.4.meta, bf16[512,512]{1,0:T(8,128)(2,1)S(1)} %section2.1.h, bf16[128,512]{1,0:T(8,128)(2,1)S(1)} %collective-permute-done.27.below, ...), custom_call_target="tpu_custom_call" | custom-call | flops 1500000000 | bytes 4000000 | tf_op jit(solution)/shard_map/section3/pallas_call | solution.py:258
  (63 shorter events, 0.6 us)
Async XLA Ops:
  0.0 15.1 %copy-start = (bf16[1,4,6,128,128]{4,3,2,1,0:T(8,128)(2,1)S(1)}, bf16[1,4,6,128,128]{4,3,2,1,0:T(8,128)(2,1)}, u32[]{:S(2)}) copy-start(bf16[1,4,6,128,128]{4,3,2,1,0:T(8,128)(2,1)} %rest_10_.5) | copy-start | bytes 2359300
  4.0 1.0 copy-start.1
  5.1 1.0 copy-start.3
  6.1 1.0 copy-start.5
  7.2 1.0 copy-start.7
  8.2 0.7 copy-start.10
  8.9 0.7 copy-start.11
  9.6 0.7 copy-start.12
  10.9 12.7 %collective-permute-start.2 = (bf16[272,256]{1,0:T(8,128)(2,1)S(1)}, bf16[272,256]{1,0:T(8,128)(2,1)S(1)}, u32[]{:S(2)}, u32[]{:S(2)}) collective-permute-start(bf16[272,256]{1,0:T(8,128)(2,1)S(1)} %pack.1), channel_id=1, source_target_pairs={{0,192},{64,128},{128,64},{192,0},{1,193},{65,129},{129,65},{193,1... | collective-permute-start | bytes 417800 | tf_op jit(solution)/shard_map/ppermute | solution.py:338
  13.2 10.5 %collective-permute-start.1 = (bf16[272,256]{1,0:T(8,128)(2,1)S(1)}, bf16[272,256]{1,0:T(8,128)(2,1)S(1)}, u32[]{:S(2)}, u32[]{:S(2)}) collective-permute-start(bf16[272,256]{1,0:T(8,128)(2,1)S(1)} %pack.1), channel_id=1, source_target_pairs={{0,128},{64,192},{128,0},{192,64},{1,129},{65,193},{129,1},{193,65... | collective-permute-start | bytes 417800 | tf_op jit(solution)/shard_map/ppermute | solution.py:338
  13.9 9.8 %collective-permute-start = (bf16[272,256]{1,0:T(8,128)(2,1)S(1)}, bf16[272,256]{1,0:T(8,128)(2,1)S(1)}, u32[]{:S(2)}, u32[]{:S(2)}) collective-permute-start(bf16[272,256]{1,0:T(8,128)(2,1)S(1)} %pack.1), channel_id=1, source_target_pairs={{0,64},{64,0},{128,192},{192,128},{1,65},{65,1},{129,193},{193,129... | collective-permute-start | bytes 417800 | tf_op jit(solution)/shard_map/ppermute | solution.py:338
  15.2 54.3 %collective-permute-start.11 = (bf16[2,6,128,128]{3,2,1,0:T(8,128)(2,1)S(1)}, bf16[2,6,128,128]{3,2,1,0:T(8,128)(2,1)S(1)}, u32[]{:S(2)}, u32[]{:S(2)}) collective-permute-start(bf16[2,6,128,128]{3,2,1,0:T(8,128)(2,1)S(1)} %get-tuple-element.40), channel_id=1, source_target_pairs={{0,64},{64,128},{128,192},{192,0},{1,65},{65,129},{129,193},{193,1... | collective-permute-start | bytes 1179656 | tf_op jit(solution)/shard_map/ppermute | solution.py:347
  17.5 52.0 %collective-permute-start.12 = (bf16[2,6,128,128]{3,2,1,0:T(8,128)(2,1)S(1)}, bf16[2,6,128,128]{3,2,1,0:T(8,128)(2,1)S(1)}, u32[]{:S(2)}, u32[]{:S(2)}) collective-permute-start(bf16[2,6,128,128]{3,2,1,0:T(8,128)(2,1)S(1)} %get-tuple-element.39), channel_id=1, source_target_pairs={{0,192},{64,0},{128,64},{192,128},{1,193},{65,1},{129,65},{193,129... | collective-permute-start | bytes 1179656 | tf_op jit(solution)/shard_map/ppermute | solution.py:348
  23.8 7.7 %collective-permute-start.5 = (bf16[1,256,256]{2,1,0:T(8,128)(2,1)S(1)}, bf16[1,256,256]{2,1,0:T(8,128)(2,1)S(1)}, u32[]{:S(2)}, u32[]{:S(2)}) collective-permute-start(bf16[1,256,256]{2,1,0:T(8,128)(2,1)S(1)} %get-tuple-element.24), channel_id=1, source_target_pairs={{0,2},{1,3},{2,4},{3,5},{4,6},{5,7},{6,0},{7,1},{8,10},{9,11},{10,... | collective-permute-start | bytes 393224 | tf_op jit(solution)/shard_map/ppermute | solution.py:319
  25.3 6.3 %collective-permute-start.6 = (bf16[1,256,256]{2,1,0:T(8,128)(2,1)S(1)}, bf16[1,256,256]{2,1,0:T(8,128)(2,1)S(1)}, u32[]{:S(2)}, u32[]{:S(2)}) collective-permute-start(bf16[1,256,256]{2,1,0:T(8,128)(2,1)S(1)} %get-tuple-element.24), channel_id=1, source_target_pairs={{0,6},{1,7},{2,0},{3,1},{4,2},{5,3},{6,4},{7,5},{8,14},{9,15},{10,... | collective-permute-start | bytes 393224 | tf_op jit(solution)/shard_map/ppermute | solution.py:319
  27.1 8.1 %collective-permute-start.7 = (bf16[1,256,256]{2,1,0:T(8,128)(2,1)S(1)}, bf16[1,256,256]{2,1,0:T(8,128)(2,1)S(1)}, u32[]{:S(2)}, u32[]{:S(2)}) collective-permute-start(bf16[1,256,256]{2,1,0:T(8,128)(2,1)S(1)} %get-tuple-element.24), channel_id=1, source_target_pairs={{0,4},{1,5},{2,6},{3,7},{4,0},{5,1},{6,2},{7,3},{8,12},{9,13},{10,... | collective-permute-start | bytes 393224 | tf_op jit(solution)/shard_map/ppermute | solution.py:319
  31.6 13.1 %collective-permute-start.15 = (bf16[2,256,256]{2,1,0:T(8,128)(2,1)S(1)}, bf16[2,256,256]{2,1,0:T(8,128)(2,1)S(1)}, u32[]{:S(2)}, u32[]{:S(2)}) collective-permute-start(bf16[2,256,256]{2,1,0:T(8,128)(2,1)S(1)} %get-tuple-element.46), channel_id=1, source_target_pairs={{0,2},{1,3},{2,4},{3,5},{4,6},{5,7},{6,0},{7,1},{8,10},{9,11},{10,... | collective-permute-start | bytes 786440 | tf_op jit(solution)/shard_map/ppermute | solution.py:319
  31.6 13.1 %collective-permute-start.16 = (bf16[2,256,256]{2,1,0:T(8,128)(2,1)S(1)}, bf16[2,256,256]{2,1,0:T(8,128)(2,1)S(1)}, u32[]{:S(2)}, u32[]{:S(2)}) collective-permute-start(bf16[2,256,256]{2,1,0:T(8,128)(2,1)S(1)} %get-tuple-element.46), channel_id=1, source_target_pairs={{0,6},{1,7},{2,0},{3,1},{4,2},{5,3},{6,4},{7,5},{8,14},{9,15},{10,... | collective-permute-start | bytes 786440 | tf_op jit(solution)/shard_map/ppermute | solution.py:319
  35.2 9.5 %collective-permute-start.17 = (bf16[2,256,256]{2,1,0:T(8,128)(2,1)S(1)}, bf16[2,256,256]{2,1,0:T(8,128)(2,1)S(1)}, u32[]{:S(2)}, u32[]{:S(2)}) collective-permute-start(bf16[2,256,256]{2,1,0:T(8,128)(2,1)S(1)} %get-tuple-element.46), channel_id=1, source_target_pairs={{0,4},{1,5},{2,6},{3,7},{4,0},{5,1},{6,2},{7,3},{8,12},{9,13},{10,... | collective-permute-start | bytes 786440 | tf_op jit(solution)/shard_map/ppermute | solution.py:319
  44.7 20.4 %collective-permute-start.8 = (bf16[1,4,128,256]{3,2,1,0:T(8,128)(2,1)S(1)}, bf16[1,4,128,256]{3,2,1,0:T(8,128)(2,1)S(1)}, u32[]{:S(2)}, u32[]{:S(2)}) collective-permute-start(bf16[1,4,128,256]{3,2,1,0:T(8,128)(2,1)S(1)} %get-tuple-element.41), channel_id=1, source_target_pairs={{0,8},{1,9},{2,10},{3,11},{4,12},{5,13},{6,14},{7,15},{8,16},{9,17... | collective-permute-start | bytes 786440 | tf_op jit(solution)/shard_map/ppermute | solution.py:321
  44.9 18.0 %collective-permute-start.18 = (bf16[2,4,128,256]{3,2,1,0:T(8,128)(2,1)S(1)}, bf16[2,4,128,256]{3,2,1,0:T(8,128)(2,1)S(1)}, u32[]{:S(2)}, u32[]{:S(2)}) collective-permute-start(bf16[2,4,128,256]{3,2,1,0:T(8,128)(2,1)S(1)} %get-tuple-element.35), channel_id=1, source_target_pairs={{0,8},{1,9},{2,10},{3,11},{4,12},{5,13},{6,14},{7,15},{8,16},{9,17... | collective-permute-start | bytes 1572872 | tf_op jit(solution)/shard_map/ppermute | solution.py:321
  46.7 18.0 %collective-permute-start.19 = (bf16[2,4,128,256]{3,2,1,0:T(8,128)(2,1)S(1)}, bf16[2,4,128,256]{3,2,1,0:T(8,128)(2,1)S(1)}, u32[]{:S(2)}, u32[]{:S(2)}) collective-permute-start(bf16[2,4,128,256]{3,2,1,0:T(8,128)(2,1)S(1)} %get-tuple-element.36), channel_id=1, source_target_pairs={{0,56},{1,57},{2,58},{3,59},{4,60},{5,61},{6,62},{7,63},{8,0},{9,1... | collective-permute-start | bytes 1572872 | tf_op jit(solution)/shard_map/ppermute | solution.py:322
  63.0 6.4 %collective-permute-start.9 = (bf16[1,4,128,256]{3,2,1,0:T(8,128)(2,1)S(1)}, bf16[1,4,128,256]{3,2,1,0:T(8,128)(2,1)S(1)}, u32[]{:S(2)}, u32[]{:S(2)}) collective-permute-start(bf16[1,4,128,256]{3,2,1,0:T(8,128)(2,1)S(1)} %get-tuple-element.42), channel_id=1, source_target_pairs={{0,56},{1,57},{2,58},{3,59},{4,60},{5,61},{6,62},{7,63},{8,0},{9,1... | collective-permute-start | bytes 786440 | tf_op jit(solution)/shard_map/ppermute | solution.py:322
  64.8 22.9 %collective-permute-start.20 = (bf16[2,8,256,256]{3,2,1,0:T(8,128)(2,1)S(1)}, bf16[2,8,256,256]{3,2,1,0:T(8,128)(2,1)S(1)}, u32[]{:S(2)}, u32[]{:S(2)}) collective-permute-start(bf16[2,8,256,256]{3,2,1,0:T(8,128)(2,1)S(1)} %maximum_dynamic-update-slice_fusion), channel_id=1, source_target_pairs={{0,1},{1,0},{2,3},{3,2},{4,5},{5,4},{6,7},{7,6},{8,9},{9,8},{10,11... | collective-permute-start | bytes 6291464 | tf_op jit(solution)/shard_map/ppermute | solution.py:324
  65.1 7.8 %collective-permute-start.3 = (bf16[128,512]{1,0:T(8,128)(2,1)S(1)}, bf16[128,512]{1,0:T(8,128)(2,1)S(1)}, u32[]{:S(2)}, u32[]{:S(2)}) collective-permute-start(bf16[128,512]{1,0:T(8,128)(2,1)S(1)} %get-tuple-element.30), channel_id=1, source_target_pairs={{0,1},{1,2},{2,3},{3,4},{4,5},{5,6},{6,7},{7,8},{8,9},{9,10},{10,1... | collective-permute-start | bytes 393224 | tf_op jit(solution)/shard_map/ppermute | solution.py:341
  69.4 14.5 %collective-permute-start.10 = (bf16[1,8,256,256]{3,2,1,0:T(8,128)(2,1)S(1)}, bf16[1,8,256,256]{3,2,1,0:T(8,128)(2,1)S(1)}, u32[]{:S(2)}, u32[]{:S(2)}) collective-permute-start(bf16[1,8,256,256]{3,2,1,0:T(8,128)(2,1)S(1)} %maximum_dynamic-update-slice_fusion.1), channel_id=1, source_target_pairs={{0,1},{1,0},{2,3},{3,2},{4,5},{5,4},{6,7},{7,6},{8,9},{9,8},{10,11... | collective-permute-start | bytes 3145736 | tf_op jit(solution)/shard_map/ppermute | solution.py:324
  69.6 12.0 %collective-permute-start.13 = (bf16[2,6,128,128]{3,2,1,0:T(8,128)(2,1)S(1)}, bf16[2,6,128,128]{3,2,1,0:T(8,128)(2,1)S(1)}, u32[]{:S(2)}, u32[]{:S(2)}) collective-permute-start(bf16[2,6,128,128]{3,2,1,0:T(8,128)(2,1)S(1)} %get-tuple-element.37), channel_id=1, source_target_pairs={{0,64},{64,128},{128,192},{192,0},{1,65},{65,129},{129,193},{193,1... | collective-permute-start | bytes 1179656 | tf_op jit(solution)/shard_map/ppermute | solution.py:349
  71.4 12.4 %collective-permute-start.14 = (bf16[2,6,128,128]{3,2,1,0:T(8,128)(2,1)S(1)}, bf16[2,6,128,128]{3,2,1,0:T(8,128)(2,1)S(1)}, u32[]{:S(2)}, u32[]{:S(2)}) collective-permute-start(bf16[2,6,128,128]{3,2,1,0:T(8,128)(2,1)S(1)} %get-tuple-element.32), channel_id=1, source_target_pairs={{0,192},{64,0},{128,64},{192,128},{1,193},{65,1},{129,65},{193,129... | collective-permute-start | bytes 1179656 | tf_op jit(solution)/shard_map/ppermute | solution.py:350
  72.9 10.9 %copy-start.2 = (bf16[1,1,512,512]{3,2,1,0:T(8,128)(2,1)S(1)}, bf16[1,1,512,512]{3,2,1,0:T(8,128)(2,1)}, u32[]{:S(2)}) copy-start(bf16[1,1,512,512]{3,2,1,0:T(8,128)(2,1)} %rest_1_.7) | copy-start | bytes 1572868
  72.9 10.9 %copy-start.4 = (bf16[1,1,512,512]{3,2,1,0:T(8,128)(2,1)S(1)}, bf16[1,1,512,512]{3,2,1,0:T(8,128)(2,1)}, u32[]{:S(2)}) copy-start(bf16[1,1,512,512]{3,2,1,0:T(8,128)(2,1)} %rest_2_.7) | copy-start | bytes 1572868
  72.9 10.9 %copy-start.6 = (bf16[1,1,512,512]{3,2,1,0:T(8,128)(2,1)S(1)}, bf16[1,1,512,512]{3,2,1,0:T(8,128)(2,1)}, u32[]{:S(2)}) copy-start(bf16[1,1,512,512]{3,2,1,0:T(8,128)(2,1)} %rest_3_.7) | copy-start | bytes 1572868
  72.9 10.9 %copy-start.8 = (bf16[1,1,512,512]{3,2,1,0:T(8,128)(2,1)S(1)}, bf16[1,1,512,512]{3,2,1,0:T(8,128)(2,1)}, u32[]{:S(2)}) copy-start(bf16[1,1,512,512]{3,2,1,0:T(8,128)(2,1)} %own.5) | copy-start | bytes 1572868
  72.9 10.9 %copy-start.9 = (bf16[4,512,512]{2,1,0:T(8,128)(2,1)S(1)}, bf16[4,512,512]{2,1,0:T(8,128)(2,1)}, u32[]{:S(2)}) copy-start(bf16[4,512,512]{2,1,0:T(8,128)(2,1)} %h.1) | copy-start | bytes 6291460
  72.9 4.1 %collective-permute-start.4 = (bf16[128,512]{1,0:T(8,128)(2,1)S(1)}, bf16[128,512]{1,0:T(8,128)(2,1)S(1)}, u32[]{:S(2)}, u32[]{:S(2)}) collective-permute-start(bf16[128,512]{1,0:T(8,128)(2,1)S(1)} %get-tuple-element.29), channel_id=1, source_target_pairs={{0,63},{1,0},{2,1},{3,2},{4,3},{5,4},{6,5},{7,6},{8,7},{9,8},{10,9... | collective-permute-start | bytes 393224 | tf_op jit(solution)/shard_map/ppermute | solution.py:342
  77.1 17.1 %collective-permute-start.23 = (bf16[2,6,128,128]{3,2,1,0:T(8,128)(2,1)S(1)}, bf16[2,6,128,128]{3,2,1,0:T(8,128)(2,1)S(1)}, u32[]{:S(2)}, u32[]{:S(2)}) collective-permute-start(bf16[2,6,128,128]{3,2,1,0:T(8,128)(2,1)S(1)} %get-tuple-element.38), channel_id=1, source_target_pairs={{0,64},{64,128},{128,192},{192,0},{1,65},{65,129},{129,193},{193,1... | collective-permute-start | bytes 1179656 | tf_op jit(solution)/shard_map/ppermute | solution.py:352
  81.6 12.5 %collective-permute-start.24 = (bf16[2,6,128,128]{3,2,1,0:T(8,128)(2,1)S(1)}, bf16[2,6,128,128]{3,2,1,0:T(8,128)(2,1)S(1)}, u32[]{:S(2)}, u32[]{:S(2)}) collective-permute-start(bf16[2,6,128,128]{3,2,1,0:T(8,128)(2,1)S(1)} %get-tuple-element.31), channel_id=1, source_target_pairs={{0,192},{64,0},{128,64},{192,128},{1,193},{65,1},{129,65},{193,129... | collective-permute-start | bytes 1179656 | tf_op jit(solution)/shard_map/ppermute | solution.py:353
  89.0 7.8 %collective-permute-start.21 = (bf16[128,512]{1,0:T(8,128)(2,1)S(1)}, bf16[128,512]{1,0:T(8,128)(2,1)S(1)}, u32[]{:S(2)}, u32[]{:S(2)}) collective-permute-start(bf16[128,512]{1,0:T(8,128)(2,1)S(1)} %get-tuple-element.14), channel_id=1, source_target_pairs={{0,1},{1,2},{2,3},{3,4},{4,5},{5,6},{6,7},{7,8},{8,9},{9,10},{10,1... | collective-permute-start | bytes 393224 | tf_op jit(solution)/shard_map/ppermute | solution.py:366
  89.1 7.7 %collective-permute-start.22 = (bf16[128,512]{1,0:T(8,128)(2,1)S(1)}, bf16[128,512]{1,0:T(8,128)(2,1)S(1)}, u32[]{:S(2)}, u32[]{:S(2)}) collective-permute-start(bf16[128,512]{1,0:T(8,128)(2,1)S(1)} %get-tuple-element.15), channel_id=1, source_target_pairs={{0,63},{1,0},{2,1},{3,2},{4,3},{5,4},{6,5},{7,6},{8,7},{9,8},{10,9... | collective-permute-start | bytes 393224 | tf_op jit(solution)/shard_map/ppermute | solution.py:367
  101.4 7.8 %collective-permute-start.25 = (bf16[128,512]{1,0:T(8,128)(2,1)S(1)}, bf16[128,512]{1,0:T(8,128)(2,1)S(1)}, u32[]{:S(2)}, u32[]{:S(2)}) collective-permute-start(bf16[128,512]{1,0:T(8,128)(2,1)S(1)} %get-tuple-element.17), channel_id=1, source_target_pairs={{0,1},{1,2},{2,3},{3,4},{4,5},{5,6},{6,7},{7,8},{8,9},{9,10},{10,1... | collective-permute-start | bytes 393224 | tf_op jit(solution)/shard_map/ppermute | solution.py:366
  101.5 7.7 %collective-permute-start.26 = (bf16[128,512]{1,0:T(8,128)(2,1)S(1)}, bf16[128,512]{1,0:T(8,128)(2,1)S(1)}, u32[]{:S(2)}, u32[]{:S(2)}) collective-permute-start(bf16[128,512]{1,0:T(8,128)(2,1)S(1)} %get-tuple-element.18), channel_id=1, source_target_pairs={{0,63},{1,0},{2,1},{3,2},{4,3},{5,4},{6,5},{7,6},{8,7},{9,8},{10,9... | collective-permute-start | bytes 393224 | tf_op jit(solution)/shard_map/ppermute | solution.py:367
  113.5 7.9 %collective-permute-start.27 = (bf16[128,512]{1,0:T(8,128)(2,1)S(1)}, bf16[128,512]{1,0:T(8,128)(2,1)S(1)}, u32[]{:S(2)}, u32[]{:S(2)}) collective-permute-start(bf16[128,512]{1,0:T(8,128)(2,1)S(1)} %get-tuple-element.20), channel_id=1, source_target_pairs={{0,1},{1,2},{2,3},{3,4},{4,5},{5,6},{6,7},{7,8},{8,9},{9,10},{10,1... | collective-permute-start | bytes 393224 | tf_op jit(solution)/shard_map/ppermute | solution.py:366
  113.6 7.8 %collective-permute-start.28 = (bf16[128,512]{1,0:T(8,128)(2,1)S(1)}, bf16[128,512]{1,0:T(8,128)(2,1)S(1)}, u32[]{:S(2)}, u32[]{:S(2)}) collective-permute-start(bf16[128,512]{1,0:T(8,128)(2,1)S(1)} %get-tuple-element.21), channel_id=1, source_target_pairs={{0,63},{1,0},{2,1},{3,2},{4,3},{5,4},{6,5},{7,6},{8,7},{9,8},{10,9... | collective-permute-start | bytes 393224 | tf_op jit(solution)/shard_map/ppermute | solution.py:367

commit v2 on v0

v2 whole, which is shorter than its diff:
```python
import functools

import jax
import jax.numpy as jnp
from jax import lax
from jax.experimental import pallas as pl
from jax.experimental.pallas import tpu as pltpu
from jax.sharding import PartitionSpec as P

D = 512
BLK = 128
BD = 4
K = 6
SEG = 4
Y, Z = 4, 8
HALF = D // 2
META = 16
ROWS = 2 * K * BLK
BF = jnp.bfloat16
F32 = jnp.float32
ANY = pl.BlockSpec(memory_space=pl.ANY)
HBM = pl.BlockSpec(memory_space=pltpu.HBM)
SMEM = pl.BlockSpec(memory_space=pltpu.SMEM)
VMEM = pl.BlockSpec(memory_space=pltpu.VMEM)


def silu(v):
    return (0.5 * v) * (1.0 + jnp.tanh(0.5 * v))


def params(mib):
    return pltpu.CompilerParams(vmem_limit_bytes=mib * 2**20)


def by_segment(x):
    return [(i, i ^ x) for i in range(SEG)]


def dom_pairs(move):
    out = []
    for d in range(Z * Y * 2):
        z, y, c = move(d // (2 * Y), d // 2 % Y, d % 2)
        out.append((d, ((z % Z) * Y + y % Y) * 2 + c % 2))
    return out


def by_y(x):
    return dom_pairs(lambda z, y, c: (z, y ^ x, c))


Z_EVEN = dom_pairs(lambda z, y, c: (z ^ 1, y, c))
Z_ODD = dom_pairs(lambda z, y, c: (((z + 1) ^ 1) - 1, y, c))
OTHER_CORE = dom_pairs(lambda z, y, c: (z, y, c ^ 1))
NEXT_CHIP = [(d, (((d + 1) ^ 1) - 1) % (2 * Y * Z)) for d in range(2 * Y * Z)]


def place():
    p, dom = lax.axis_index("segment"), lax.axis_index("dom")
    return p, dom, (dom >> 1) & 3, (dom >> 3) & 1, dom & 1


def meta_kernel(src, cnt, gain, out):
    dom = place()[1]
    row = lax.broadcasted_iota(jnp.int32, (META, BLK), 0)
    col = lax.broadcasted_iota(jnp.int32, (META, BLK), 1)
    meta = jnp.zeros((META, BLK), F32)
    for b in range(BD):
        for k in range(K):
            rel = (src[0, b, k] - (dom * BD - 1) + 512) & 255
            code = jnp.where(k < cnt[0, b], rel, 7).astype(F32)
            meta = jnp.where((row == 0) & (col == b * K + k), code, meta)
    left = gain[0]
    for part in range(3):
        piece = left.astype(BF).astype(F32)
        left = left - piece
        for i in range(4):
            meta = jnp.where(row == 1 + 4 * part + i, piece[:, i * BLK : (i + 1) * BLK], meta)
    out[...] = meta.astype(BF)


def meta_call(src, cnt, gain):
    return pl.pallas_call(
        meta_kernel,
        out_shape=jax.ShapeDtypeStruct((META, BLK), BF),
        in_specs=[SMEM, SMEM, VMEM],
        out_specs=VMEM,
        compiler_params=params(4),
        name="meta",
    )(src, cnt, gain)


def copies(kernel_name, plan, shapes, *args):
    def kernel(*refs):
        ins, outs, sem = refs[: len(args)], refs[len(args) : -1], refs[-1]
        moves = [
            pltpu.make_async_copy(a, b, sem.at[i]) for i, (a, b) in enumerate(plan(ins, outs))
        ]
        for m in moves:
            m.start()
        for m in moves:
            m.wait()

    return pl.pallas_call(
        kernel,
        out_shape=[jax.ShapeDtypeStruct(shape, BF) for shape in shapes],
        in_specs=[ANY] * len(args),
        out_specs=[ANY] * len(shapes),
        scratch_shapes=[pltpu.SemaphoreType.DMA((12,))],
        compiler_params=params(4),
        cost_estimate=pl.CostEstimate(flops=0, bytes_accessed=2_000_000, transcendentals=0),
        name=kernel_name,
    )(*args)


def z_halves(ring):
    def plan(ins, outs):
        return [
            (ins[r].at[pl.ds(i * BLK, BLK)], outs[i].at[r]) for r in range(4) for i in range(2)
        ]

    return copies("halves", plan, [(4, BLK, HALF)] * 2, *ring)


def joined(ring, halves):
    def plan(ins, outs):
        return [(ins[r], outs[0].at[r]) for r in range(4)] + [
            (ins[4 + i], outs[0].at[pl.ds(4, 4), pl.ds(i * BLK, BLK)]) for i in range(2)
        ]

    return copies("joined", plan, [(8, HALF, HALF)], *ring, *halves)[0]


def weights_kernel(section, holders, n_stage, *refs):
    own, stages = refs[:4], [refs[4 + 2 * j : 6 + 2 * j] for j in range(n_stage)]
    out, sem = refs[-2:]
    p, _, y, zpar, c = place()

    @pl.when(p == section)
    def _():
        for m in range(4):
            pltpu.make_async_copy(own[m].at[0, 0], out.at[m], sem.at[m]).start()

    for (first, second), held_by in zip(stages, holders):

        @pl.when(functools.reduce(jnp.logical_or, [p == q for q in held_by]))
        def _():
            for m in range(4):
                for core, stage in enumerate((first, second)):
                    for zrel in range(2):
                        rows = pl.multiple_of((zpar ^ zrel) * HALF, HALF)
                        cols = pl.multiple_of((c ^ core) * HALF, HALF)
                        pltpu.make_async_copy(
                            stage.at[zrel * 4 + (y ^ m)],
                            out.at[m, pl.ds(rows, HALF), pl.ds(cols, HALF)],
                            sem.at[m],
                        ).start()

    for m in range(4):
        pltpu.make_async_copy(own[m].at[0, 0], out.at[m], sem.at[m]).wait()


def weights_call(section, own, stages):
    by_stage = {}
    for q in range(SEG):
        if q != section:
            by_stage.setdefault(section - (1 if section > q else 0), []).append(q)
    flat = [a for j in by_stage for a in stages[j]]
    return pl.pallas_call(
        functools.partial(weights_kernel, section, list(by_stage.values()), len(by_stage)),
        out_shape=jax.ShapeDtypeStruct((4, D, D), BF),
        in_specs=[ANY] * (4 + len(flat)),
        out_specs=VMEM,
        scratch_shapes=[pltpu.SemaphoreType.DMA((4,))],
        compiler_params=params(4),
        cost_estimate=pl.CostEstimate(flops=0, bytes_accessed=4_000_000, transcendentals=0),
        name=f"weights{section}",
    )(*own, *flat)


def tile_halves(section, p):
    x = p ^ section
    if x == 0:
        return "own_a", "own_b"
    if x == 1:
        return "r1a", ("r2a" if p == 1 else "r3a")
    if x == 2:
        return ("r3c" if p == 3 else "r2c"), ("r3a" if p == 1 else "r2a")
    return ("r2c" if p == 3 else "r3c"), "r1c"


def tiles_kernel(section, names, *refs):
    ins = dict(zip(names, refs))
    tiles, codes, gain, meta, sem = refs[len(names) :]
    for q in range(SEG):

        @pl.when(lax.axis_index("segment") == q)
        def _():
            a, b = (ins[name] for name in tile_halves(section, q))
            for i in range(2 * K):
                rows = pl.ds(i * BLK, BLK)
                pltpu.make_async_copy(a.at[rows], tiles.at[i], sem.at[0]).start()
                pltpu.make_async_copy(b.at[rows], tiles.at[2 * K + i], sem.at[1]).start()
            pltpu.make_async_copy(a.at[pl.ds(ROWS, META)], meta, sem.at[2]).start()

    pltpu.make_async_copy(ins["own_a"].at[pl.ds(ROWS, META)], meta, sem.at[2]).wait()
    for half in range(2):
        there = tiles.at[pl.ds(half * 2 * K, 2 * K)]
        pltpu.make_async_copy(there, there, sem.at[half]).wait()
    m = meta[...].astype(F32)
    code = m[:8]
    codes[...] = jnp.where(code < 7.0, code, 0.0).astype(jnp.int32)
    gain[...] = jnp.concatenate(
        [m[1 + i : 2 + i] + (m[5 + i : 6 + i] + m[9 + i : 10 + i]) for i in range(4)], axis=1
    )
    for i in range(BD * K):
        used = jnp.broadcast_to(m[0:1, i : i + 1], (BLK, BLK)) < 7.0
        tiles[i] = jnp.where(used, tiles[i].astype(F32), 0.0).astype(BF)


def tiles_call(section, arrays):
    return pl.pallas_call(
        functools.partial(tiles_kernel, section, list(arrays)),
        out_shape=[
            jax.ShapeDtypeStruct((BD * K, BLK, BLK), BF),
            jax.ShapeDtypeStruct((8, BLK), jnp.int32),
            jax.ShapeDtypeStruct((1, D), F32),
        ],
        in_specs=[ANY] * len(arrays),
        out_specs=[VMEM] * 3,
        scratch_shapes=[pltpu.VMEM((META, BLK), BF), pltpu.SemaphoreType.DMA((3,))],
        compiler_params=params(4),
        cost_estimate=pl.CostEstimate(flops=0, bytes_accessed=2_000_000, transcendentals=0),
        name=f"tiles{section}",
    )(*arrays.values())


def section_kernel(section, codes, gain, tiles, w, h, inner, outer, *rest):
    sender = rest[0]
    out, sbuf, gbuf = rest[-3:]
    core = place()[4]
    at_inner = pl.multiple_of((1 - core) * (5 * BLK), BLK)
    at_outer = pl.multiple_of(core * (5 * BLK), BLK)
    if section == 0:
        for at, src in ((at_inner, inner), (at_outer, outer)):
            s = silu(jnp.dot(src[...], w[0], preferred_element_type=F32)).astype(BF)
            sbuf[pl.ds(at, BLK), :] = s
        for i in range(2):
            s = jnp.dot(h[i * HALF : (i + 1) * HALF, :], w[0], preferred_element_type=F32)
            sbuf[BLK + i * HALF : BLK + (i + 1) * HALF, :] = silu(s).astype(BF)
    else:
        sbuf[BLK : 5 * BLK, :] = sender[...]
        sbuf[pl.ds(at_inner, BLK), :] = inner[...]
        sbuf[pl.ds(at_outer, BLK), :] = outer[...]
    for b in range(BD):
        places = [pl.multiple_of(codes[0, b * K + k] * BLK, BLK) for k in range(K)]
        got = jnp.dot(
            jnp.concatenate([tiles[b * K + k] for k in range(K)], axis=1),
            jnp.concatenate([sbuf[pl.ds(at, BLK), :] for at in places], axis=0),
            preferred_element_type=F32,
        )
        gbuf[b * BLK : (b + 1) * BLK, :] = got.astype(BF)
    for i in range(2):
        rows = slice(i * HALF, (i + 1) * HALF)
        mixed = jnp.dot(h[rows, :], w[1], preferred_element_type=F32)
        mixed = mixed + jnp.dot(gbuf[rows, :], w[2], preferred_element_type=F32)
        mean = jnp.mean(mixed * mixed, axis=-1, keepdims=True)
        scaled = mixed * lax.rsqrt(mean + 1e-05) * gain[...]
        update = silu(scaled).astype(BF)
        new = h[rows, :].astype(F32) + jnp.dot(update, w[3], preferred_element_type=F32)
        out[rows, :] = new.astype(BF)


def section_call(section, codes, gain, tiles, w, h, inner, outer, *sender):
    return pl.pallas_call(
        functools.partial(section_kernel, section),
        out_shape=jax.ShapeDtypeStruct((BD * BLK, D), BF),
        in_specs=[SMEM] + [VMEM] * (6 + len(sender)),
        out_specs=VMEM,
        scratch_shapes=[
            pltpu.VMEM(((BD + 2) * BLK, D), BF),
            pltpu.VMEM((BD * BLK, D), BF),
        ],
        compiler_params=params(16),
        cost_estimate=pl.CostEstimate(
            flops=1_500_000_000, bytes_accessed=4_000_000, transcendentals=262144
        ),
        name=f"section{section}",
    )(codes, gain, tiles, w, h, inner, outer, *sender)


def sender_kernel(h, w, full, inner, outer):
    core = place()[4]
    for i in range(2):
        rows = slice(i * HALF, (i + 1) * HALF)
        s = silu(jnp.dot(h[rows, :], w[0], preferred_element_type=F32)).astype(BF)
        full[rows, :] = s
    inner[...] = full[pl.ds(pl.multiple_of((1 - core) * 3 * BLK, BLK), BLK), :]
    outer[...] = full[pl.ds(pl.multiple_of(core * 3 * BLK, BLK), BLK), :]


def sender_call(section, h, w):
    return pl.pallas_call(
        sender_kernel,
        out_shape=[
            jax.ShapeDtypeStruct((BD * BLK, D), BF),
            jax.ShapeDtypeStruct((BLK, D), BF),
            jax.ShapeDtypeStruct((BLK, D), BF),
        ],
        in_specs=[VMEM, VMEM],
        out_specs=[VMEM] * 3,
        compiler_params=params(8),
        cost_estimate=pl.CostEstimate(
            flops=270_000_000, bytes_accessed=1_500_000, transcendentals=262144
        ),
        name=f"sender{section}",
    )(h, w)


def after(values, *others):
    return lax.optimization_barrier((values, others))[0]


def over_segments(value, x):
    return lax.ppermute(value, "segment", by_segment(x))


def over_dom(value, pairs):
    return lax.ppermute(value, "dom", pairs)


def exchange(inner, outer):
    return over_dom(inner, OTHER_CORE), over_dom(outer, NEXT_CHIP)


def shards(samples, w_source, w_self, w_message, w_output, norm_gain, tile_source, tile_count, tile_value):
    p, _, y, zpar, core = place()
    ws = [w_source, w_self, w_message, w_output]
    piece = [lax.dynamic_slice(w[0, 0], (zpar * HALF, core * HALF), (HALF, HALF)) for w in ws]
    piece = jnp.where(
        y < 2, jnp.where(y == 0, piece[0], piece[1]), jnp.where(y == 2, piece[2], piece[3])
    )
    x1, x3 = over_segments(piece, 1), over_segments(piece, 3)
    x2 = over_segments(piece, 2)

    h = lax.dynamic_index_in_dim(samples, p, 0, keepdims=False)
    edge = [h[:BLK], h[(BD - 1) * BLK :]]
    inner, outer = exchange(
        jnp.where(core == 0, edge[1], edge[0]), jnp.where(core == 0, edge[0], edge[1])
    )

    root = p == 0
    half_a, half_b = tile_value[0, :2].reshape(ROWS, BLK), tile_value[0, 2:].reshape(ROWS, BLK)
    half_a = jnp.concatenate([half_a, meta_call(tile_source, tile_count, norm_gain)])
    arrays = {"own_a": half_a, "own_b": half_b}
    half_a, half_b = after((half_a, half_b), x1, x3, inner, outer)
    arrays["r1a"], arrays["r1c"] = over_segments(half_a, 1), over_segments(half_b, 3)
    second = (jnp.where(root, half_b, arrays["r1c"]), jnp.where(root, half_a, arrays["r1a"]))
    arrays["r2a"], arrays["r2c"] = over_segments(second[0], 1), over_segments(second[1], 3)
    early = dict(arrays)
    half_a, half_b = after((half_a, half_b), arrays["r2a"], arrays["r2c"])
    third = (jnp.where(root, arrays["r1c"], half_b), jnp.where(root, arrays["r1a"], half_a))
    arrays["r3a"], arrays["r3c"] = over_segments(third[0], 1), over_segments(third[1], 3)

    pieces = [
        jnp.where(p == 2, x2, jnp.where(p == 3, x3, x1)),
        jnp.where((p == 0) | (p == 3), x2, x3),
        jnp.where(p == 0, x3, jnp.where(p == 1, x2, x1)),
    ]

    def over_y(own):
        a, b = over_dom(own, by_y(1)), over_dom(own, by_y(3))
        return [own, a, over_dom(own, by_y(2)), b]

    def over_z(halves):
        return over_dom(halves[0], Z_EVEN), over_dom(halves[1], Z_ODD)

    def both(pieces):
        return pieces, over_dom(pieces, OTHER_CORE)

    ring0 = over_y(pieces[0])
    z0 = over_z(z_halves(ring0))
    ring1 = over_y(after(pieces[1], ring0, arrays["r1a"], arrays["r1c"]))
    stage0 = both(after(joined(ring0, z0), second))
    z1 = over_z(after(z_halves(ring1), z0))
    w = weights_call(0, ws, [stage0])
    tiles, codes, gain = tiles_call(0, early)
    h = section_call(0, codes, gain, tiles, w, h, inner, outer)
    stage1 = both(after(joined(ring1, z1), third))
    ring2 = over_y(after(pieces[2], z1))
    z2 = over_z(z_halves(after(ring2, h)))
    stage2 = both(joined(ring2, z2))
    stages = [stage0, stage1, stage2]
    for section in range(1, SEG):
        w = weights_call(section, ws, stages)
        tiles, codes, gain = tiles_call(section, arrays)
        sender, inner, outer = sender_call(section, h, w)
        inner, outer = exchange(inner, outer)
        h = section_call(section, codes, gain, tiles, w, h, inner, outer, sender)
    return h[None]


def solution(mesh):
    return jax.shard_map(
        shards,
        mesh=mesh,
        in_specs=(
            P(None, "dom", None),
            P("segment", None, None, None),
            P("segment", None, None, None),
            P("segment", None, None, None),
            P("segment", None, None, None),
            P("segment", None, None),
            P("segment", "dom", None),
            P("segment", "dom"),
            P("segment", "dom", None, None, None),
        ),
        out_specs=P("segment", "dom", None),
        check_vma=False,
    )
```

time: 280 us -> 117 us (0.42)
  waiting for transfers between devices: 139 us -> 29.2 us
  matrix products: 40.2 us -> 0 us
  starting transfers between devices: 21.3 us -> 57.9 us
  local copies, waits for them, and re-layouts: 35 us -> 2.28 us
  Pallas kernels: 0 us -> 24.1 us
  blocking collectives: 23.4 us -> 0 us
  other arithmetic: 18.9 us -> 2.46 us
    ppermute x20 -> x35, waiting for transfers between devices: 139 us -> 29.2 us  [the longest x26 23.2 us: over_dom(): return lax.ppermute(value, 'dom', pairs)]
    dot_general x35 -> x0, matrix products: 40.2 us -> none  [the longest x7 18.1 us: run_layer(): jnp.einsum('bkij,bkjd->bid', weights, picked, preferred_element_type=jnp....]
    ppermute x20 -> x35, starting transfers between devices: 21.3 us -> 57.9 us  [the longest x26 47 us: over_dom(): return lax.ppermute(value, 'dom', pairs)]
    pallas_call x0 -> x22, Pallas kernels: none -> 24.1 us  [the longest x4 11 us: section_call(): pl.pallas_call(functools.partial(section_kernel, section), out_shape=jax....]
    all_to_all x1 -> x0, blocking collectives: 23.4 us -> none  [shards(): lax.all_to_all(kept, 'segment', split_axis=0, concat_axis=0, tiled=True)]
    gather x7 -> x0, local copies, waits for them, and re-layouts: 17.4 us -> none  [run_layer(): picked = padded_blocks[local_index]]
    concatenate x7 -> x0, local copies, waits for them, and re-layouts: 12 us -> none  [run_layer(): padded = jnp.concatenate([below, sender, above], axis=0)]
    concatenate x7 -> x1, other arithmetic: 8.99 us -> 0.03 us  [shards(): jnp.concatenate([half_a, meta_call(tile_source, tile_count, norm_gain)])]
  transfers between devices with their start and end apart: 20 -> 35, of which waited for: 20 -> 14; matrix products, arithmetic and copies ran while one was open for 1% -> 3% of each run, Pallas kernels for 0% -> 15%
where the time goes in v2:
time: 117 us; the launch traced here: 116 us
  starting transfers between devices  57.9 us (49%)
  waiting for transfers between devices  29.2 us (25%)
  Pallas kernels  24.1 us (21%)
  other arithmetic  2.46 us (2%)
  local copies, waits for them, and re-layouts  2.28 us (2%)
    ppermute x26, starting transfers between devices, over_dom(): return lax.ppermute(value, 'dom', pairs)  47 us
    ppermute x26, waiting for transfers between devices, over_dom(): return lax.ppermute(value, 'dom', pairs)  23.2 us
    pallas_call x4, Pallas kernels, section_call(): pl.pallas_call(functools.partial(section_kernel, section), out_shape=jax....  11 us
    ppermute x9, starting transfers between devices, over_segments(): return lax.ppermute(value, 'segment', by_segment(x))  10.9 us
    ppermute x9, waiting for transfers between devices, over_segments(): return lax.ppermute(value, 'segment', by_segment(x))  5.99 us
    pallas_call x4, Pallas kernels, tiles_call(): pl.pallas_call(functools.partial(tiles_kernel, section, list(arrays)), ou...  5.1 us
    pallas_call x6, Pallas kernels, copies(): pl.pallas_call(kernel, out_shape=[jax.ShapeDtypeStruct(shape, BF) for sha...  4.69 us
  transfers between devices with their start and end apart: 35, of which 14 were waited for; matrix products, arithmetic and copies ran while one was open for 3% of the time, Pallas kernels for 15%

profile of v2, /device:TPU:6, one launch (start us, length us, event | category | flops | bytes accessed | tf_op | source)
XLA Modules:
  0.0 116.4 jit_solution(14868172069785605863)
XLA Ops:
  0.0 1.2 %select_bitcast_fusion.2 = bf16[256,256]{1,0:T(8,128)(2,1)S(1)} fusion(bf16[1,1,512,512]{3,2,1,0:T(8,128)(2,1)} %refs_3_.7, s32[]{:T(128)S(6)} %select_n.115, s32[]{:T(128)S(6)} %select_n.116, bf16[1,1,512,512]{3,2,1,0:T(8,128)(2,1)} %refs_2_.7, bf16[1,1,512,512]{3,2,1,0:T(8,128)(2,1)} %refs_1_.7, bf16[1,1,512,512]{3,2,1,0:T(8,128)(2,1)} %refs_0_.7, ...), kind=kLoop, calls=%fused_computation.10 | loop fusion | flops 196608 | bytes 655371 | tf_op jit(solution)/shard_map/jit(_where)/select_n | solution.py:339
  1.2 0.9 collective-permute-start
  2.1 1.5 %collective-permute-start.1 = (bf16[256,256]{1,0:T(8,128)(2,1)S(1)}, bf16[256,256]{1,0:T(8,128)(2,1)S(1)}, u32[]{:S(2)}, u32[]{:S(2)}) collective-permute-start(bf16[256,256]{1,0:T(8,128)(2,1)S(1)} %select_bitcast_fusion.2), channel_id=1, source_target_pairs={{0,192},{64,128},{128,64},{192,0},{1,193},{65,129},{129,65},{193,1... | collective-permute-start | bytes 393224 | tf_op jit(solution)/shard_map/ppermute | solution.py:324
  3.6 1.8 %collective-permute-start.10 = (bf16[256,256]{1,0:T(8,128)(2,1)S(1)}, bf16[256,256]{1,0:T(8,128)(2,1)S(1)}, u32[]{:S(2)}, u32[]{:S(2)}) collective-permute-start(bf16[256,256]{1,0:T(8,128)(2,1)S(1)} %select_bitcast_fusion.2), channel_id=1, source_target_pairs={{0,128},{64,192},{128,0},{192,64},{1,129},{65,193},{129,1},{193,65... | collective-permute-start | bytes 393224 | tf_op jit(solution)/shard_map/ppermute | solution.py:324
  5.4 1.0 select_bitcast_fusion
  6.5 8.4 %collective-permute-start.3 = (bf16[128,512]{1,0:T(8,128)(2,1)S(1)}, bf16[128,512]{1,0:T(8,128)(2,1)S(1)}, u32[]{:S(2)}, u32[]{:S(2)}) collective-permute-start(bf16[128,512]{1,0:T(8,128)(2,1)S(1)} %get-tuple-element.87), channel_id=1, source_target_pairs={{0,63},{1,2},{2,1},{3,4},{4,3},{5,6},{6,5},{7,8},{8,7},{9,10},{10,... | collective-permute-start | bytes 393224 | tf_op jit(solution)/shard_map/ppermute | solution.py:328
  14.9 1.2 %fusion = (bf16[1,2,6,128,128]{4,3,2,1,0:T(8,128)(2,1)S(1)}, bf16[1,2,6,128,128]{4,3,2,1,0:T(8,128)(2,1)S(1)}) fusion(bf16[1,4,6,128,128]{4,3,2,1,0:T(8,128)(2,1)} %param.17), kind=kLoop, calls=%fused_computation.12 | loop fusion | bytes 1572864 | tf_op jit(solution)/shard_map/slice | solution.py:352
  16.1 0.6 meta.1
  16.8 0.7 collective-permute-done.3.outer
  17.6 0.8 collective-permute-start.4
  18.4 1.1 collective-permute-start.5
  19.8 4.6 %collective-permute-start.13 = (bf16[256,256]{1,0:T(8,128)(2,1)S(1)}, bf16[256,256]{1,0:T(8,128)(2,1)S(1)}, u32[]{:S(2)}, u32[]{:S(2)}) collective-permute-start(bf16[256,256]{1,0:T(8,128)(2,1)S(1)} %get-tuple-element.91.refs_0_), channel_id=1, source_target_pairs={{0,6},{1,7},{2,4},{3,5},{4,2},{5,3},{6,0},{7,1},{8,14},{9,15},{10,... | collective-permute-start | bytes 393224 | tf_op jit(solution)/shard_map/ppermute | solution.py:328
  24.4 0.3 collective-permute-done.11.refs_1_
  24.6 1.6 %collective-permute-done.12.refs_2_ = bf16[256,256]{1,0:T(8,128)(2,1)S(1)} collective-permute-done((bf16[256,256]{1,0:T(8,128)(2,1)S(1)}, bf16[256,256]{1,0:T(8,128)(2,1)S(1)}, u32[]{:S(2)}, u32[]{:S(2)}) %collective-permute-start.12) | collective-permute-done | bytes 131104 | tf_op jit(solution)/shard_map/ppermute | solution.py:328
  26.3 1.4 %collective-permute-done.13.refs_3_ = bf16[256,256]{1,0:T(8,128)(2,1)S(1)} collective-permute-done((bf16[256,256]{1,0:T(8,128)(2,1)S(1)}, bf16[256,256]{1,0:T(8,128)(2,1)S(1)}, u32[]{:S(2)}, u32[]{:S(2)}) %collective-permute-start.13) | collective-permute-done | bytes 131104 | tf_op jit(solution)/shard_map/ppermute | solution.py:328
  27.6 0.8 halves.4
  28.4 1.4 %collective-permute-start.17 = (bf16[4,128,256]{2,1,0:T(8,128)(2,1)S(1)}, bf16[4,128,256]{2,1,0:T(8,128)(2,1)S(1)}, u32[]{:S(2)}, u32[]{:S(2)}) collective-permute-start(bf16[4,128,256]{2,1,0:T(8,128)(2,1)S(1)} %get-tuple-element.56), channel_id=1, source_target_pairs={{0,8},{1,9},{2,10},{3,11},{4,12},{5,13},{6,14},{7,15},{8,0},{9,1},... | collective-permute-start | bytes 786440 | tf_op jit(solution)/shard_map/ppermute | solution.py:328
  29.8 4.9 %collective-permute-start.18 = (bf16[4,128,256]{2,1,0:T(8,128)(2,1)S(1)}, bf16[4,128,256]{2,1,0:T(8,128)(2,1)S(1)}, u32[]{:S(2)}, u32[]{:S(2)}) collective-permute-start(bf16[4,128,256]{2,1,0:T(8,128)(2,1)S(1)} %get-tuple-element.57), channel_id=1, source_target_pairs={{0,56},{1,57},{2,58},{3,59},{4,60},{5,61},{6,62},{7,63},{8,16},{9,... | collective-permute-start | bytes 786440 | tf_op jit(solution)/shard_map/ppermute | solution.py:328
  34.8 2.7 %collective-permute-start.15 = (bf16[256,256]{1,0:T(8,128)(2,1)S(1)}, bf16[256,256]{1,0:T(8,128)(2,1)S(1)}, u32[]{:S(2)}, u32[]{:S(2)}) collective-permute-start(bf16[256,256]{1,0:T(8,128)(2,1)S(1)} %get-tuple-element.53.refs_0_), channel_id=1, source_target_pairs={{0,4},{1,5},{2,6},{3,7},{4,0},{5,1},{6,2},{7,3},{8,12},{9,13},{10,... | collective-permute-start | bytes 393224 | tf_op jit(solution)/shard_map/ppermute | solution.py:328
  37.5 2.0 %collective-permute-start.16 = (bf16[256,256]{1,0:T(8,128)(2,1)S(1)}, bf16[256,256]{1,0:T(8,128)(2,1)S(1)}, u32[]{:S(2)}, u32[]{:S(2)}) collective-permute-start(bf16[256,256]{1,0:T(8,128)(2,1)S(1)} %get-tuple-element.53.refs_0_), channel_id=1, source_target_pairs={{0,6},{1,7},{2,4},{3,5},{4,2},{5,3},{6,0},{7,1},{8,14},{9,15},{10,... | collective-permute-start | bytes 393224 | tf_op jit(solution)/shard_map/ppermute | solution.py:328
  39.5 1.6 %collective-permute-done.14.refs_1_ = bf16[256,256]{1,0:T(8,128)(2,1)S(1)} collective-permute-done((bf16[256,256]{1,0:T(8,128)(2,1)S(1)}, bf16[256,256]{1,0:T(8,128)(2,1)S(1)}, u32[]{:S(2)}, u32[]{:S(2)}) %collective-permute-start.14) | collective-permute-done | bytes 131104 | tf_op jit(solution)/shard_map/ppermute | solution.py:328
  41.1 2.1 %collective-permute-start.7 = (bf16[1552,128]{1,0:T(8,128)(2,1)S(1)}, bf16[1552,128]{1,0:T(8,128)(2,1)S(1)}, u32[]{:S(2)}, u32[]{:S(2)}) collective-permute-start(bf16[1552,128]{1,0:T(8,128)(2,1)S(1)} %broadcast_select_fusion.1), channel_id=1, source_target_pairs={{0,192},{64,128},{128,64},{192,0},{1,193},{65,129},{129,65},{193,1... | collective-permute-start | bytes 1191944 | tf_op jit(solution)/shard_map/ppermute | solution.py:324
  43.3 0.3 collective-permute-start.6
  43.6 1.1 collective-permute-done.16.refs_3_
  44.8 0.8 halves.3
  45.5 0.1 collective-permute-start.19
  45.7 2.3 %collective-permute-start.20 = (bf16[4,128,256]{2,1,0:T(8,128)(2,1)S(1)}, bf16[4,128,256]{2,1,0:T(8,128)(2,1)S(1)}, u32[]{:S(2)}, u32[]{:S(2)}) collective-permute-start(bf16[4,128,256]{2,1,0:T(8,128)(2,1)S(1)} %get-tuple-element.59), channel_id=1, source_target_pairs={{0,56},{1,57},{2,58},{3,59},{4,60},{5,61},{6,62},{7,63},{8,16},{9,... | collective-permute-start | bytes 786440 | tf_op jit(solution)/shard_map/ppermute | solution.py:328
  47.9 0.8 joined.3.refs_4_
  48.8 1.1 dynamic-slice_bitcast_fusion.h
  49.9 2.9 %collective-permute-done.19.refs_4_ = bf16[4,128,256]{2,1,0:T(8,128)(2,1)S(1)} collective-permute-done((bf16[4,128,256]{2,1,0:T(8,128)(2,1)S(1)}, bf16[4,128,256]{2,1,0:T(8,128)(2,1)S(1)}, u32[]{:S(2)}, u32[]{:S(2)}) %collective-permute-start.19) | collective-permute-done | bytes 262176 | tf_op jit(solution)/shard_map/ppermute | solution.py:328
  52.8 1.3 %collective-permute-done.20.refs_5_ = bf16[4,128,256]{2,1,0:T(8,128)(2,1)S(1)} collective-permute-done((bf16[4,128,256]{2,1,0:T(8,128)(2,1)S(1)}, bf16[4,128,256]{2,1,0:T(8,128)(2,1)S(1)}, u32[]{:S(2)}, u32[]{:S(2)}) %collective-permute-start.20) | collective-permute-done | bytes 262176 | tf_op jit(solution)/shard_map/ppermute | solution.py:328
  54.2 4.1 %collective-permute-start.22 = (bf16[256,256]{1,0:T(8,128)(2,1)S(1)}, bf16[256,256]{1,0:T(8,128)(2,1)S(1)}, u32[]{:S(2)}, u32[]{:S(2)}) collective-permute-start(bf16[256,256]{1,0:T(8,128)(2,1)S(1)} %get-tuple-element.65.refs_0_), channel_id=1, source_target_pairs={{0,4},{1,5},{2,6},{3,7},{4,0},{5,1},{6,2},{7,3},{8,12},{9,13},{10,... | collective-permute-start | bytes 393224 | tf_op jit(solution)/shard_map/ppermute | solution.py:328
  58.2 0.8 joined.5.refs_4_.refs_6_
  59.1 0.7 collective-permute-start.23
  60.0 1.3 %tiles0.1 = (bf16[24,128,128]{2,1,0:T(8,128)(2,1)S(1)}, s32[8,128]{1,0:T(8,128)S(1)}, f32[1,512]{1,0:T(1,128)S(1)}) custom-call(bf16[1552,128]{1,0:T(8,128)(2,1)S(1)} %pad_maximum_fusion.refs_0_, bf16[1536,128]{1,0:T(8,128)(2,1)S(1)} %bitcast.14, bf16[1552,128]{1,0:T(8,128)(2,1)S(1)} %collective-permute-done.4.refs_2_, ...), custom_call_target="tpu_custom_call" | custom-call | bytes 2000000 | tf_op jit(solution)/shard_map/tiles0/pallas_call | solution.py:221
  61.4 0.2 weights0.1.w
  61.6 3.0 %section0.1.h = bf16[512,512]{1,0:T(8,128)(2,1)S(1)} custom-call(s32[8,128]{1,0:T(8,128)S(1)} %get-tuple-element.61.codes, f32[1,512]{1,0:T(1,128)S(1)} %get-tuple-element.62.gain, bf16[24,128,128]{2,1,0:T(8,128)(2,1)S(1)} %get-tuple-element.63.tiles, bf16[4,512,512]{2,1,0:T(8,128)(2,1)S(1)} %weights0.1.w, bf16[512,512]{1,0:T(8,128)(2,1)S(1)} %dynamic-slice_bitcast_fusion.h, ...), custom_call_target="tpu_custom_call" | custom-call | flops 1500000000 | bytes 4000000 | tf_op jit(solution)/shard_map/section0/pallas_call | solution.py:274
  64.6 0.7 collective-permute-done.23.refs_3_
  65.4 0.8 halves.5
  66.1 0.5 collective-permute-start.25
  66.7 1.8 %collective-permute-start.26 = (bf16[4,128,256]{2,1,0:T(8,128)(2,1)S(1)}, bf16[4,128,256]{2,1,0:T(8,128)(2,1)S(1)}, u32[]{:S(2)}, u32[]{:S(2)}) collective-permute-start(bf16[4,128,256]{2,1,0:T(8,128)(2,1)S(1)} %get-tuple-element.70), channel_id=1, source_target_pairs={{0,56},{1,57},{2,58},{3,59},{4,60},{5,61},{6,62},{7,63},{8,16},{9,... | collective-permute-start | bytes 786440 | tf_op jit(solution)/shard_map/ppermute | solution.py:328
  68.4 5.7 %collective-permute-done.25.refs_4_ = bf16[4,128,256]{2,1,0:T(8,128)(2,1)S(1)} collective-permute-done((bf16[4,128,256]{2,1,0:T(8,128)(2,1)S(1)}, bf16[4,128,256]{2,1,0:T(8,128)(2,1)S(1)}, u32[]{:S(2)}, u32[]{:S(2)}) %collective-permute-start.25) | collective-permute-done | bytes 262176 | tf_op jit(solution)/shard_map/ppermute | solution.py:328
  74.2 1.4 %collective-permute-done.26.refs_5_ = bf16[4,128,256]{2,1,0:T(8,128)(2,1)S(1)} collective-permute-done((bf16[4,128,256]{2,1,0:T(8,128)(2,1)S(1)}, bf16[4,128,256]{2,1,0:T(8,128)(2,1)S(1)}, u32[]{:S(2)}, u32[]{:S(2)}) %collective-permute-start.26) | collective-permute-done | bytes 262176 | tf_op jit(solution)/shard_map/ppermute | solution.py:328
  75.6 0.8 joined.4.refs_4_.refs_6_
  76.5 2.2 %collective-permute-start.9 = (bf16[1552,128]{1,0:T(8,128)(2,1)S(1)}, bf16[1552,128]{1,0:T(8,128)(2,1)S(1)}, u32[]{:S(2)}, u32[]{:S(2)}) collective-permute-start(bf16[1552,128]{1,0:T(8,128)(2,1)S(1)} %broadcast_select_fusion), channel_id=1, source_target_pairs={{0,192},{64,128},{128,64},{192,0},{1,193},{65,129},{129,65},{193,1... | collective-permute-start | bytes 1191944 | tf_op jit(solution)/shard_map/ppermute | solution.py:324
  78.6 0.2 collective-permute-start.8
  78.8 0.2 weights1.1.w
  79.0 0.5 sender1.1
  79.6 4.2 %collective-permute-start.30 = (bf16[128,512]{1,0:T(8,128)(2,1)S(1)}, bf16[128,512]{1,0:T(8,128)(2,1)S(1)}, u32[]{:S(2)}, u32[]{:S(2)}) collective-permute-start(bf16[128,512]{1,0:T(8,128)(2,1)S(1)} %get-tuple-element.79), channel_id=1, source_target_pairs={{0,63},{1,2},{2,1},{3,4},{4,3},{5,6},{6,5},{7,8},{8,7},{9,10},{10,... | collective-permute-start | bytes 393224 | tf_op jit(solution)/shard_map/ppermute | solution.py:328
  83.8 6.0 %collective-permute-done.8.refs_6_ = bf16[1536,128]{1,0:T(8,128)(2,1)S(1)} collective-permute-done((bf16[1536,128]{1,0:T(8,128)(2,1)S(1)}, bf16[1536,128]{1,0:T(8,128)(2,1)S(1)}, u32[]{:S(2)}, u32[]{:S(2)}) %collective-permute-start.8) | collective-permute-done | bytes 393248 | tf_op jit(solution)/shard_map/ppermute | solution.py:324
  89.8 1.3 %tiles1.1 = (bf16[24,128,128]{2,1,0:T(8,128)(2,1)S(1)}, s32[8,128]{1,0:T(8,128)S(1)}, f32[1,512]{1,0:T(1,128)S(1)}) custom-call(bf16[1552,128]{1,0:T(8,128)(2,1)S(1)} %pad_maximum_fusion.refs_0_, bf16[1536,128]{1,0:T(8,128)(2,1)S(1)} %bitcast.15, bf16[1552,128]{1,0:T(8,128)(2,1)S(1)} %collective-permute-done.4.refs_2_, ...), custom_call_target="tpu_custom_call" | custom-call | bytes 2000000 | tf_op jit(solution)/shard_map/tiles1/pallas_call | solution.py:221
  91.1 2.4 %section1.1.h = bf16[512,512]{1,0:T(8,128)(2,1)S(1)} custom-call(s32[8,128]{1,0:T(8,128)S(1)} %get-tuple-element.75.codes, f32[1,512]{1,0:T(1,128)S(1)} %get-tuple-element.76.gain, bf16[24,128,128]{2,1,0:T(8,128)(2,1)S(1)} %get-tuple-element.77.tiles, bf16[4,512,512]{2,1,0:T(8,128)(2,1)S(1)} %weights1.1.w, bf16[512,512]{1,0:T(8,128)(2,1)S(1)} %section0.1.h, ...), custom_call_target="tpu_custom_call" | custom-call | flops 1500000000 | bytes 4000000 | tf_op jit(solution)/shard_map/section1/pallas_call | solution.py:274
  93.5 0.5 weights2.1.w
  94.0 0.5 sender2.1
  94.6 4.2 %collective-permute-start.32 = (bf16[128,512]{1,0:T(8,128)(2,1)S(1)}, bf16[128,512]{1,0:T(8,128)(2,1)S(1)}, u32[]{:S(2)}, u32[]{:S(2)}) collective-permute-start(bf16[128,512]{1,0:T(8,128)(2,1)S(1)} %get-tuple-element.82), channel_id=1, source_target_pairs={{0,63},{1,2},{2,1},{3,4},{4,3},{5,6},{6,5},{7,8},{8,7},{9,10},{10,... | collective-permute-start | bytes 393224 | tf_op jit(solution)/shard_map/ppermute | solution.py:328
  98.9 1.3 %tiles2.1 = (bf16[24,128,128]{2,1,0:T(8,128)(2,1)S(1)}, s32[8,128]{1,0:T(8,128)S(1)}, f32[1,512]{1,0:T(1,128)S(1)}) custom-call(bf16[1552,128]{1,0:T(8,128)(2,1)S(1)} %pad_maximum_fusion.refs_0_, bf16[1536,128]{1,0:T(8,128)(2,1)S(1)} %bitcast.16, bf16[1552,128]{1,0:T(8,128)(2,1)S(1)} %collective-permute-done.4.refs_2_, ...), custom_call_target="tpu_custom_call" | custom-call | bytes 2000000 | tf_op jit(solution)/shard_map/tiles2/pallas_call | solution.py:221
  100.1 0.2 weights3.1.w
  100.3 2.1 %collective-permute-done.32.outer = bf16[128,512]{1,0:T(8,128)(2,1)S(1)} collective-permute-done((bf16[128,512]{1,0:T(8,128)(2,1)S(1)}, bf16[128,512]{1,0:T(8,128)(2,1)S(1)}, u32[]{:S(2)}, u32[]{:S(2)}) %collective-permute-start.32) | collective-permute-done | bytes 131104 | tf_op jit(solution)/shard_map/ppermute | solution.py:328
  102.4 2.4 %section2.1.h = bf16[512,512]{1,0:T(8,128)(2,1)S(1)} custom-call(s32[8,128]{1,0:T(8,128)S(1)} %get-tuple-element.71.codes, f32[1,512]{1,0:T(1,128)S(1)} %get-tuple-element.72.gain, bf16[24,128,128]{2,1,0:T(8,128)(2,1)S(1)} %get-tuple-element.73.tiles, bf16[4,512,512]{2,1,0:T(8,128)(2,1)S(1)} %weights2.1.w, bf16[512,512]{1,0:T(8,128)(2,1)S(1)} %section1.1.h, ...), custom_call_target="tpu_custom_call" | custom-call | flops 1500000000 | bytes 4000000 | tf_op jit(solution)/shard_map/section2/pallas_call | solution.py:274
  104.8 0.5 sender3.1
  105.4 4.3 %collective-permute-start.34 = (bf16[128,512]{1,0:T(8,128)(2,1)S(1)}, bf16[128,512]{1,0:T(8,128)(2,1)S(1)}, u32[]{:S(2)}, u32[]{:S(2)}) collective-permute-start(bf16[128,512]{1,0:T(8,128)(2,1)S(1)} %get-tuple-element.85), channel_id=1, source_target_pairs={{0,63},{1,2},{2,1},{3,4},{4,3},{5,6},{6,5},{7,8},{8,7},{9,10},{10,... | collective-permute-start | bytes 393224 | tf_op jit(solution)/shard_map/ppermute | solution.py:328
  109.7 1.3 %tiles3.1 = (bf16[24,128,128]{2,1,0:T(8,128)(2,1)S(1)}, s32[8,128]{1,0:T(8,128)S(1)}, f32[1,512]{1,0:T(1,128)S(1)}) custom-call(bf16[1552,128]{1,0:T(8,128)(2,1)S(1)} %pad_maximum_fusion.refs_0_, bf16[1536,128]{1,0:T(8,128)(2,1)S(1)} %bitcast.17, bf16[1552,128]{1,0:T(8,128)(2,1)S(1)} %collective-permute-done.4.refs_2_, ...), custom_call_target="tpu_custom_call" | custom-call | bytes 2000000 | tf_op jit(solution)/shard_map/tiles3/pallas_call | solution.py:221
  111.0 2.3 %collective-permute-done.34.outer = bf16[128,512]{1,0:T(8,128)(2,1)S(1)} collective-permute-done((bf16[128,512]{1,0:T(8,128)(2,1)S(1)}, bf16[128,512]{1,0:T(8,128)(2,1)S(1)}, u32[]{:S(2)}, u32[]{:S(2)}) %collective-permute-start.34) | collective-permute-done | bytes 131104 | tf_op jit(solution)/shard_map/ppermute | solution.py:328
  113.2 3.2 %section3.1 = bf16[512,512]{1,0:T(8,128)(2,1)} custom-call(s32[8,128]{1,0:T(8,128)S(1)} %get-tuple-element.50.codes, f32[1,512]{1,0:T(1,128)S(1)} %get-tuple-element.51.gain, bf16[24,128,128]{2,1,0:T(8,128)(2,1)S(1)} %get-tuple-element.52.tiles, bf16[4,512,512]{2,1,0:T(8,128)(2,1)S(1)} %weights3.1.w, bf16[512,512]{1,0:T(8,128)(2,1)S(1)} %section2.1.h, ...), custom_call_target="tpu_custom_call" | custom-call | flops 1500000000 | bytes 4000000 | tf_op jit(solution)/shard_map/section3/pallas_call | solution.py:274
  (52 shorter events, 1.2 us)
Async XLA Ops:
  0.0 16.1 %copy-start.5 = (f32[1,1,512]{2,1,0:T(1,128)S(1)}, f32[1,1,512]{2,1,0:T(1,128)}, u32[]{:S(2)}) copy-start(f32[1,1,512]{2,1,0:T(1,128)} %gain.1) | copy-start | bytes 6148
  0.0 16.1 %copy-start.4 = (s32[1,4,6]{2,1,0:T(4,128)S(1)}, s32[1,4,6]{2,1,0:T(4,128)}, u32[]{:S(2)}) copy-start(s32[1,4,6]{2,1,0:T(4,128)} %src.1) | copy-start | bytes 292
  0.0 16.1 %copy-start.6 = (s32[1,4]{1,0:T(1,128)S(1)}, s32[1,4]{1,0:T(1,128)}, u32[]{:S(2)}) copy-start(s32[1,4]{1,0:T(1,128)} %cnt.1) | copy-start | bytes 52
  1.2 15.6 %collective-permute-start = (bf16[256,256]{1,0:T(8,128)(2,1)S(1)}, bf16[256,256]{1,0:T(8,128)(2,1)S(1)}, u32[]{:S(2)}, u32[]{:S(2)}) collective-permute-start(bf16[256,256]{1,0:T(8,128)(2,1)S(1)} %select_bitcast_fusion.2), channel_id=1, source_target_pairs={{0,64},{64,0},{128,192},{192,128},{1,65},{65,1},{129,193},{193,129... | collective-permute-start | bytes 393224 | tf_op jit(solution)/shard_map/ppermute | solution.py:324
  2.1 14.7 %collective-permute-start.1 = (bf16[256,256]{1,0:T(8,128)(2,1)S(1)}, bf16[256,256]{1,0:T(8,128)(2,1)S(1)}, u32[]{:S(2)}, u32[]{:S(2)}) collective-permute-start(bf16[256,256]{1,0:T(8,128)(2,1)S(1)} %select_bitcast_fusion.2), channel_id=1, source_target_pairs={{0,192},{64,128},{128,64},{192,0},{1,193},{65,129},{129,65},{193,1... | collective-permute-start | bytes 393224 | tf_op jit(solution)/shard_map/ppermute | solution.py:324
  3.6 15.9 %collective-permute-start.10 = (bf16[256,256]{1,0:T(8,128)(2,1)S(1)}, bf16[256,256]{1,0:T(8,128)(2,1)S(1)}, u32[]{:S(2)}, u32[]{:S(2)}) collective-permute-start(bf16[256,256]{1,0:T(8,128)(2,1)S(1)} %select_bitcast_fusion.2), channel_id=1, source_target_pairs={{0,128},{64,192},{128,0},{192,64},{1,129},{65,193},{129,1},{193,65... | collective-permute-start | bytes 393224 | tf_op jit(solution)/shard_map/ppermute | solution.py:324
  6.4 10.4 %collective-permute-start.2 = (bf16[128,512]{1,0:T(8,128)(2,1)S(1)}, bf16[128,512]{1,0:T(8,128)(2,1)S(1)}, u32[]{:S(2)}, u32[]{:S(2)}) collective-permute-start(bf16[128,512]{1,0:T(8,128)(2,1)S(1)} %get-tuple-element.88), channel_id=1, source_target_pairs={{0,1},{1,0},{2,3},{3,2},{4,5},{5,4},{6,7},{7,6},{8,9},{9,8},{10,11... | collective-permute-start | bytes 393224 | tf_op jit(solution)/shard_map/ppermute | solution.py:328
  6.5 11.1 %collective-permute-start.3 = (bf16[128,512]{1,0:T(8,128)(2,1)S(1)}, bf16[128,512]{1,0:T(8,128)(2,1)S(1)}, u32[]{:S(2)}, u32[]{:S(2)}) collective-permute-start(bf16[128,512]{1,0:T(8,128)(2,1)S(1)} %get-tuple-element.87), channel_id=1, source_target_pairs={{0,63},{1,2},{2,1},{3,4},{4,3},{5,6},{6,5},{7,8},{8,7},{9,10},{10,... | collective-permute-start | bytes 393224 | tf_op jit(solution)/shard_map/ppermute | solution.py:328
  17.6 17.2 %collective-permute-start.4 = (bf16[1552,128]{1,0:T(8,128)(2,1)S(1)}, bf16[1552,128]{1,0:T(8,128)(2,1)S(1)}, u32[]{:S(2)}, u32[]{:S(2)}) collective-permute-start(bf16[1552,128]{1,0:T(8,128)(2,1)S(1)} %pad_maximum_fusion.refs_0_), channel_id=1, source_target_pairs={{0,64},{64,0},{128,192},{192,128},{1,65},{65,1},{129,193},{193,129... | collective-permute-start | bytes 1191944 | tf_op jit(solution)/shard_map/ppermute | solution.py:324
  18.4 16.4 %collective-permute-start.5 = (bf16[1536,128]{1,0:T(8,128)(2,1)S(1)}, bf16[1536,128]{1,0:T(8,128)(2,1)S(1)}, u32[]{:S(2)}, u32[]{:S(2)}) collective-permute-start(bf16[1536,128]{1,0:T(8,128)(2,1)S(1)} %bitcast.11), channel_id=1, source_target_pairs={{0,192},{64,128},{128,64},{192,0},{1,193},{65,129},{129,65},{193,1... | collective-permute-start | bytes 1179656 | tf_op jit(solution)/shard_map/ppermute | solution.py:324
  19.6 5.1 %collective-permute-start.11 = (bf16[256,256]{1,0:T(8,128)(2,1)S(1)}, bf16[256,256]{1,0:T(8,128)(2,1)S(1)}, u32[]{:S(2)}, u32[]{:S(2)}) collective-permute-start(bf16[256,256]{1,0:T(8,128)(2,1)S(1)} %get-tuple-element.91.refs_0_), channel_id=1, source_target_pairs={{0,2},{1,3},{2,0},{3,1},{4,6},{5,7},{6,4},{7,5},{8,10},{9,11},{10,... | collective-permute-start | bytes 393224 | tf_op jit(solution)/shard_map/ppermute | solution.py:328
  19.7 6.6 %collective-permute-start.12 = (bf16[256,256]{1,0:T(8,128)(2,1)S(1)}, bf16[256,256]{1,0:T(8,128)(2,1)S(1)}, u32[]{:S(2)}, u32[]{:S(2)}) collective-permute-start(bf16[256,256]{1,0:T(8,128)(2,1)S(1)} %get-tuple-element.91.refs_0_), channel_id=1, source_target_pairs={{0,4},{1,5},{2,6},{3,7},{4,0},{5,1},{6,2},{7,3},{8,12},{9,13},{10,... | collective-permute-start | bytes 393224 | tf_op jit(solution)/shard_map/ppermute | solution.py:328
  19.8 7.9 %collective-permute-start.13 = (bf16[256,256]{1,0:T(8,128)(2,1)S(1)}, bf16[256,256]{1,0:T(8,128)(2,1)S(1)}, u32[]{:S(2)}, u32[]{:S(2)}) collective-permute-start(bf16[256,256]{1,0:T(8,128)(2,1)S(1)} %get-tuple-element.91.refs_0_), channel_id=1, source_target_pairs={{0,6},{1,7},{2,4},{3,5},{4,2},{5,3},{6,0},{7,1},{8,14},{9,15},{10,... | collective-permute-start | bytes 393224 | tf_op jit(solution)/shard_map/ppermute | solution.py:328
  28.4 17.1 %collective-permute-start.17 = (bf16[4,128,256]{2,1,0:T(8,128)(2,1)S(1)}, bf16[4,128,256]{2,1,0:T(8,128)(2,1)S(1)}, u32[]{:S(2)}, u32[]{:S(2)}) collective-permute-start(bf16[4,128,256]{2,1,0:T(8,128)(2,1)S(1)} %get-tuple-element.56), channel_id=1, source_target_pairs={{0,8},{1,9},{2,10},{3,11},{4,12},{5,13},{6,14},{7,15},{8,0},{9,1},... | collective-permute-start | bytes 786440 | tf_op jit(solution)/shard_map/ppermute | solution.py:328
  29.8 15.7 %collective-permute-start.18 = (bf16[4,128,256]{2,1,0:T(8,128)(2,1)S(1)}, bf16[4,128,256]{2,1,0:T(8,128)(2,1)S(1)}, u32[]{:S(2)}, u32[]{:S(2)}) collective-permute-start(bf16[4,128,256]{2,1,0:T(8,128)(2,1)S(1)} %get-tuple-element.57), channel_id=1, source_target_pairs={{0,56},{1,57},{2,58},{3,59},{4,60},{5,61},{6,62},{7,63},{8,16},{9,... | collective-permute-start | bytes 786440 | tf_op jit(solution)/shard_map/ppermute | solution.py:328
  34.8 6.4 %collective-permute-start.14 = (bf16[256,256]{1,0:T(8,128)(2,1)S(1)}, bf16[256,256]{1,0:T(8,128)(2,1)S(1)}, u32[]{:S(2)}, u32[]{:S(2)}) collective-permute-start(bf16[256,256]{1,0:T(8,128)(2,1)S(1)} %get-tuple-element.53.refs_0_), channel_id=1, source_target_pairs={{0,2},{1,3},{2,0},{3,1},{4,6},{5,7},{6,4},{7,5},{8,10},{9,11},{10,... | collective-permute-start | bytes 393224 | tf_op jit(solution)/shard_map/ppermute | solution.py:328
  34.8 8.5 %collective-permute-start.15 = (bf16[256,256]{1,0:T(8,128)(2,1)S(1)}, bf16[256,256]{1,0:T(8,128)(2,1)S(1)}, u32[]{:S(2)}, u32[]{:S(2)}) collective-permute-start(bf16[256,256]{1,0:T(8,128)(2,1)S(1)} %get-tuple-element.53.refs_0_), channel_id=1, source_target_pairs={{0,4},{1,5},{2,6},{3,7},{4,0},{5,1},{6,2},{7,3},{8,12},{9,13},{10,... | collective-permute-start | bytes 393224 | tf_op jit(solution)/shard_map/ppermute | solution.py:328
  37.5 7.3 %collective-permute-start.16 = (bf16[256,256]{1,0:T(8,128)(2,1)S(1)}, bf16[256,256]{1,0:T(8,128)(2,1)S(1)}, u32[]{:S(2)}, u32[]{:S(2)}) collective-permute-start(bf16[256,256]{1,0:T(8,128)(2,1)S(1)} %get-tuple-element.53.refs_0_), channel_id=1, source_target_pairs={{0,6},{1,7},{2,4},{3,5},{4,2},{5,3},{6,0},{7,1},{8,14},{9,15},{10,... | collective-permute-start | bytes 393224 | tf_op jit(solution)/shard_map/ppermute | solution.py:328
  41.1 18.7 %collective-permute-start.7 = (bf16[1552,128]{1,0:T(8,128)(2,1)S(1)}, bf16[1552,128]{1,0:T(8,128)(2,1)S(1)}, u32[]{:S(2)}, u32[]{:S(2)}) collective-permute-start(bf16[1552,128]{1,0:T(8,128)(2,1)S(1)} %broadcast_select_fusion.1), channel_id=1, source_target_pairs={{0,192},{64,128},{128,64},{192,0},{1,193},{65,129},{129,65},{193,1... | collective-permute-start | bytes 1191944 | tf_op jit(solution)/shard_map/ppermute | solution.py:324
  43.3 15.8 %collective-permute-start.6 = (bf16[1536,128]{1,0:T(8,128)(2,1)S(1)}, bf16[1536,128]{1,0:T(8,128)(2,1)S(1)}, u32[]{:S(2)}, u32[]{:S(2)}) collective-permute-start(bf16[1536,128]{1,0:T(8,128)(2,1)S(1)} %broadcast_select_fusion.3), channel_id=1, source_target_pairs={{0,64},{64,0},{128,192},{192,128},{1,65},{65,1},{129,193},{193,129... | collective-permute-start | bytes 1179656 | tf_op jit(solution)/shard_map/ppermute | solution.py:324
  45.5 7.3 %collective-permute-start.19 = (bf16[4,128,256]{2,1,0:T(8,128)(2,1)S(1)}, bf16[4,128,256]{2,1,0:T(8,128)(2,1)S(1)}, u32[]{:S(2)}, u32[]{:S(2)}) collective-permute-start(bf16[4,128,256]{2,1,0:T(8,128)(2,1)S(1)} %get-tuple-element.58), channel_id=1, source_target_pairs={{0,8},{1,9},{2,10},{3,11},{4,12},{5,13},{6,14},{7,15},{8,0},{9,1},... | collective-permute-start | bytes 786440 | tf_op jit(solution)/shard_map/ppermute | solution.py:328
  45.7 8.5 %collective-permute-start.20 = (bf16[4,128,256]{2,1,0:T(8,128)(2,1)S(1)}, bf16[4,128,256]{2,1,0:T(8,128)(2,1)S(1)}, u32[]{:S(2)}, u32[]{:S(2)}) collective-permute-start(bf16[4,128,256]{2,1,0:T(8,128)(2,1)S(1)} %get-tuple-element.59), channel_id=1, source_target_pairs={{0,56},{1,57},{2,58},{3,59},{4,60},{5,61},{6,62},{7,63},{8,16},{9,... | collective-permute-start | bytes 786440 | tf_op jit(solution)/shard_map/ppermute | solution.py:328
  48.7 12.6 %collective-permute-start.24 = (bf16[8,256,256]{2,1,0:T(8,128)(2,1)S(1)}, bf16[8,256,256]{2,1,0:T(8,128)(2,1)S(1)}, u32[]{:S(2)}, u32[]{:S(2)}) collective-permute-start(bf16[8,256,256]{2,1,0:T(8,128)(2,1)S(1)} %joined.3.refs_4_), channel_id=1, source_target_pairs={{0,1},{1,0},{2,3},{3,2},{4,5},{5,4},{6,7},{7,6},{8,9},{9,8},{10,11... | collective-permute-start | bytes 3145736 | tf_op jit(solution)/shard_map/ppermute | solution.py:328
  54.2 10.5 %collective-permute-start.21 = (bf16[256,256]{1,0:T(8,128)(2,1)S(1)}, bf16[256,256]{1,0:T(8,128)(2,1)S(1)}, u32[]{:S(2)}, u32[]{:S(2)}) collective-permute-start(bf16[256,256]{1,0:T(8,128)(2,1)S(1)} %get-tuple-element.65.refs_0_), channel_id=1, source_target_pairs={{0,2},{1,3},{2,0},{3,1},{4,6},{5,7},{6,4},{7,5},{8,10},{9,11},{10,... | collective-permute-start | bytes 393224 | tf_op jit(solution)/shard_map/ppermute | solution.py:328
  54.2 10.5 %collective-permute-start.22 = (bf16[256,256]{1,0:T(8,128)(2,1)S(1)}, bf16[256,256]{1,0:T(8,128)(2,1)S(1)}, u32[]{:S(2)}, u32[]{:S(2)}) collective-permute-start(bf16[256,256]{1,0:T(8,128)(2,1)S(1)} %get-tuple-element.65.refs_0_), channel_id=1, source_target_pairs={{0,4},{1,5},{2,6},{3,7},{4,0},{5,1},{6,2},{7,3},{8,12},{9,13},{10,... | collective-permute-start | bytes 393224 | tf_op jit(solution)/shard_map/ppermute | solution.py:328
  59.0 2.3 %copy-start = (bf16[1,1,512,512]{3,2,1,0:T(8,128)(2,1)S(1)}, bf16[1,1,512,512]{3,2,1,0:T(8,128)(2,1)}, u32[]{:S(2)}) copy-start(bf16[1,1,512,512]{3,2,1,0:T(8,128)(2,1)} %refs_0_.7) | copy-start | bytes 1572868
  59.0 2.3 %copy-start.1 = (bf16[1,1,512,512]{3,2,1,0:T(8,128)(2,1)S(1)}, bf16[1,1,512,512]{3,2,1,0:T(8,128)(2,1)}, u32[]{:S(2)}) copy-start(bf16[1,1,512,512]{3,2,1,0:T(8,128)(2,1)} %refs_1_.7) | copy-start | bytes 1572868
  59.1 2.3 %copy-start.2 = (bf16[1,1,512,512]{3,2,1,0:T(8,128)(2,1)S(1)}, bf16[1,1,512,512]{3,2,1,0:T(8,128)(2,1)}, u32[]{:S(2)}) copy-start(bf16[1,1,512,512]{3,2,1,0:T(8,128)(2,1)} %refs_2_.7) | copy-start | bytes 1572868
  59.1 2.3 %copy-start.3 = (bf16[1,1,512,512]{3,2,1,0:T(8,128)(2,1)S(1)}, bf16[1,1,512,512]{3,2,1,0:T(8,128)(2,1)}, u32[]{:S(2)}) copy-start(bf16[1,1,512,512]{3,2,1,0:T(8,128)(2,1)} %refs_3_.7) | copy-start | bytes 1572868
  59.1 6.3 %collective-permute-start.23 = (bf16[256,256]{1,0:T(8,128)(2,1)S(1)}, bf16[256,256]{1,0:T(8,128)(2,1)S(1)}, u32[]{:S(2)}, u32[]{:S(2)}) collective-permute-start(bf16[256,256]{1,0:T(8,128)(2,1)S(1)} %get-tuple-element.65.refs_0_), channel_id=1, source_target_pairs={{0,6},{1,7},{2,4},{3,5},{4,2},{5,3},{6,0},{7,1},{8,14},{9,15},{10,... | collective-permute-start | bytes 393224 | tf_op jit(solution)/shard_map/ppermute | solution.py:328
  59.9 18.9 %collective-permute-start.28 = (bf16[8,256,256]{2,1,0:T(8,128)(2,1)S(1)}, bf16[8,256,256]{2,1,0:T(8,128)(2,1)S(1)}, u32[]{:S(2)}, u32[]{:S(2)}) collective-permute-start(bf16[8,256,256]{2,1,0:T(8,128)(2,1)S(1)} %joined.5.refs_4_.refs_6_), channel_id=1, source_target_pairs={{0,1},{1,0},{2,3},{3,2},{4,5},{5,4},{6,7},{7,6},{8,9},{9,8},{10,11... | collective-permute-start | bytes 3145736 | tf_op jit(solution)/shard_map/ppermute | solution.py:328
  66.1 8.0 %collective-permute-start.25 = (bf16[4,128,256]{2,1,0:T(8,128)(2,1)S(1)}, bf16[4,128,256]{2,1,0:T(8,128)(2,1)S(1)}, u32[]{:S(2)}, u32[]{:S(2)}) collective-permute-start(bf16[4,128,256]{2,1,0:T(8,128)(2,1)S(1)} %get-tuple-element.69), channel_id=1, source_target_pairs={{0,8},{1,9},{2,10},{3,11},{4,12},{5,13},{6,14},{7,15},{8,0},{9,1},... | collective-permute-start | bytes 786440 | tf_op jit(solution)/shard_map/ppermute | solution.py:328
  66.7 8.9 %collective-permute-start.26 = (bf16[4,128,256]{2,1,0:T(8,128)(2,1)S(1)}, bf16[4,128,256]{2,1,0:T(8,128)(2,1)S(1)}, u32[]{:S(2)}, u32[]{:S(2)}) collective-permute-start(bf16[4,128,256]{2,1,0:T(8,128)(2,1)S(1)} %get-tuple-element.70), channel_id=1, source_target_pairs={{0,56},{1,57},{2,58},{3,59},{4,60},{5,61},{6,62},{7,63},{8,16},{9,... | collective-permute-start | bytes 786440 | tf_op jit(solution)/shard_map/ppermute | solution.py:328
  76.4 17.2 %collective-permute-start.27 = (bf16[8,256,256]{2,1,0:T(8,128)(2,1)S(1)}, bf16[8,256,256]{2,1,0:T(8,128)(2,1)S(1)}, u32[]{:S(2)}, u32[]{:S(2)}) collective-permute-start(bf16[8,256,256]{2,1,0:T(8,128)(2,1)S(1)} %joined.4.refs_4_.refs_6_), channel_id=1, source_target_pairs={{0,1},{1,0},{2,3},{3,2},{4,5},{5,4},{6,7},{7,6},{8,9},{9,8},{10,11... | collective-permute-start | bytes 3145736 | tf_op jit(solution)/shard_map/ppermute | solution.py:328
  76.5 13.3 %collective-permute-start.9 = (bf16[1552,128]{1,0:T(8,128)(2,1)S(1)}, bf16[1552,128]{1,0:T(8,128)(2,1)S(1)}, u32[]{:S(2)}, u32[]{:S(2)}) collective-permute-start(bf16[1552,128]{1,0:T(8,128)(2,1)S(1)} %broadcast_select_fusion), channel_id=1, source_target_pairs={{0,192},{64,128},{128,64},{192,0},{1,193},{65,129},{129,65},{193,1... | collective-permute-start | bytes 1191944 | tf_op jit(solution)/shard_map/ppermute | solution.py:324
  78.6 11.2 %collective-permute-start.8 = (bf16[1536,128]{1,0:T(8,128)(2,1)S(1)}, bf16[1536,128]{1,0:T(8,128)(2,1)S(1)}, u32[]{:S(2)}, u32[]{:S(2)}) collective-permute-start(bf16[1536,128]{1,0:T(8,128)(2,1)S(1)} %broadcast_select_fusion.2), channel_id=1, source_target_pairs={{0,64},{64,0},{128,192},{192,128},{1,65},{65,1},{129,193},{193,129... | collective-permute-start | bytes 1179656 | tf_op jit(solution)/shard_map/ppermute | solution.py:324
  79.5 11.6 %collective-permute-start.29 = (bf16[128,512]{1,0:T(8,128)(2,1)S(1)}, bf16[128,512]{1,0:T(8,128)(2,1)S(1)}, u32[]{:S(2)}, u32[]{:S(2)}) collective-permute-start(bf16[128,512]{1,0:T(8,128)(2,1)S(1)} %get-tuple-element.78), channel_id=1, source_target_pairs={{0,1},{1,0},{2,3},{3,2},{4,5},{5,4},{6,7},{7,6},{8,9},{9,8},{10,11... | collective-permute-start | bytes 393224 | tf_op jit(solution)/shard_map/ppermute | solution.py:328
  79.6 11.5 %collective-permute-start.30 = (bf16[128,512]{1,0:T(8,128)(2,1)S(1)}, bf16[128,512]{1,0:T(8,128)(2,1)S(1)}, u32[]{:S(2)}, u32[]{:S(2)}) collective-permute-start(bf16[128,512]{1,0:T(8,128)(2,1)S(1)} %get-tuple-element.79), channel_id=1, source_target_pairs={{0,63},{1,2},{2,1},{3,4},{4,3},{5,6},{6,5},{7,8},{8,7},{9,10},{10,... | collective-permute-start | bytes 393224 | tf_op jit(solution)/shard_map/ppermute | solution.py:328
  94.5 5.8 %collective-permute-start.31 = (bf16[128,512]{1,0:T(8,128)(2,1)S(1)}, bf16[128,512]{1,0:T(8,128)(2,1)S(1)}, u32[]{:S(2)}, u32[]{:S(2)}) collective-permute-start(bf16[128,512]{1,0:T(8,128)(2,1)S(1)} %get-tuple-element.81), channel_id=1, source_target_pairs={{0,1},{1,0},{2,3},{3,2},{4,5},{5,4},{6,7},{7,6},{8,9},{9,8},{10,11... | collective-permute-start | bytes 393224 | tf_op jit(solution)/shard_map/ppermute | solution.py:328
  94.6 7.8 %collective-permute-start.32 = (bf16[128,512]{1,0:T(8,128)(2,1)S(1)}, bf16[128,512]{1,0:T(8,128)(2,1)S(1)}, u32[]{:S(2)}, u32[]{:S(2)}) collective-permute-start(bf16[128,512]{1,0:T(8,128)(2,1)S(1)} %get-tuple-element.82), channel_id=1, source_target_pairs={{0,63},{1,2},{2,1},{3,4},{4,3},{5,6},{6,5},{7,8},{8,7},{9,10},{10,... | collective-permute-start | bytes 393224 | tf_op jit(solution)/shard_map/ppermute | solution.py:328
  105.3 5.6 %collective-permute-start.33 = (bf16[128,512]{1,0:T(8,128)(2,1)S(1)}, bf16[128,512]{1,0:T(8,128)(2,1)S(1)}, u32[]{:S(2)}, u32[]{:S(2)}) collective-permute-start(bf16[128,512]{1,0:T(8,128)(2,1)S(1)} %get-tuple-element.84), channel_id=1, source_target_pairs={{0,1},{1,0},{2,3},{3,2},{4,5},{5,4},{6,7},{7,6},{8,9},{9,8},{10,11... | collective-permute-start | bytes 393224 | tf_op jit(solution)/shard_map/ppermute | solution.py:328
  105.4 7.8 %collective-permute-start.34 = (bf16[128,512]{1,0:T(8,128)(2,1)S(1)}, bf16[128,512]{1,0:T(8,128)(2,1)S(1)}, u32[]{:S(2)}, u32[]{:S(2)}) collective-permute-start(bf16[128,512]{1,0:T(8,128)(2,1)S(1)} %get-tuple-element.85), channel_id=1, source_target_pairs={{0,63},{1,2},{2,1},{3,4},{4,3},{5,6},{6,5},{7,8},{8,7},{9,10},{10,... | collective-permute-start | bytes 393224 | tf_op jit(solution)/shard_map/ppermute | solution.py:328

commit v3 on v2

v3 whole, which is shorter than its diff:
```python
import functools

import jax
import jax.numpy as jnp
from jax import lax
from jax.experimental import pallas as pl
from jax.experimental.pallas import tpu as pltpu
from jax.sharding import PartitionSpec as P

D = 512
BLK = 128
BD = 4
K = 6
SEG = 4
Y, Z = 4, 8
HALF = D // 2
META = 16
ROWS = 2 * K * BLK
BF = jnp.bfloat16
F32 = jnp.float32
ANY = pl.BlockSpec(memory_space=pl.ANY)
HBM = pl.BlockSpec(memory_space=pltpu.HBM)
SMEM = pl.BlockSpec(memory_space=pltpu.SMEM)
VMEM = pl.BlockSpec(memory_space=pltpu.VMEM)


def silu(v):
    return (0.5 * v) * (1.0 + jnp.tanh(0.5 * v))


def params(mib):
    return pltpu.CompilerParams(vmem_limit_bytes=mib * 2**20)


def by_segment(x):
    return [(i, i ^ x) for i in range(SEG)]


def dom_pairs(move):
    out = []
    for d in range(Z * Y * 2):
        z, y, c = move(d // (2 * Y), d // 2 % Y, d % 2)
        out.append((d, ((z % Z) * Y + y % Y) * 2 + c % 2))
    return out


def by_y(x):
    return dom_pairs(lambda z, y, c: (z, y ^ x, c))


Z_FAR = dom_pairs(lambda z, y, c: (z ^ 2, y, c))
Z_EVEN = dom_pairs(lambda z, y, c: (z ^ 1, y, c))
Z_ODD = dom_pairs(lambda z, y, c: (((z + 1) ^ 1) - 1, y, c))
OTHER_CORE = dom_pairs(lambda z, y, c: (z, y, c ^ 1))
NEXT_CHIP = [(d, (((d + 1) ^ 1) - 1) % (2 * Y * Z)) for d in range(2 * Y * Z)]


def place():
    p, dom = lax.axis_index("segment"), lax.axis_index("dom")
    return p, dom, (dom >> 1) & 3, (dom >> 3) & 1, dom & 1


def sender_rows(rows, w):
    return silu(jnp.dot(rows, w, preferred_element_type=F32)).astype(BF)


def halo_places():
    core = place()[4]
    return pl.multiple_of((1 - core) * (5 * BLK), BLK), pl.multiple_of(core * (5 * BLK), BLK)


def gather(tile, code, sbuf, gbuf):
    for b in range(BD):
        slots = range(b * K, (b + 1) * K)
        places = [pl.multiple_of(code(i) * BLK, BLK) for i in slots]
        got = jnp.dot(
            jnp.concatenate([tile(i) for i in slots], axis=1),
            jnp.concatenate([sbuf[pl.ds(at, BLK), :] for at in places], axis=0),
            preferred_element_type=F32,
        )
        gbuf[b * BLK : (b + 1) * BLK, :] = got.astype(BF)


def update_rows(h, gathered, w, gain):
    mixed = jnp.dot(h, w[1], preferred_element_type=F32)
    mixed = mixed + jnp.dot(gathered, w[2], preferred_element_type=F32)
    mean = jnp.mean(mixed * mixed, axis=-1, keepdims=True)
    update = silu(mixed * lax.rsqrt(mean + 1e-05) * gain).astype(BF)
    return (h.astype(F32) + jnp.dot(update, w[3], preferred_element_type=F32)).astype(BF)


def own_small(src, cnt, gain):
    dom = place()[1]
    row = lax.broadcasted_iota(jnp.int32, (META, BLK), 0)
    col = lax.broadcasted_iota(jnp.int32, (META, BLK), 1)
    meta = jnp.zeros((META, BLK), F32)
    for i in range(BD * K):
        used, code = own_slot(src, cnt, dom, i)
        meta = jnp.where((row == 0) & (col == i), jnp.where(used, code, 7).astype(F32), meta)
    left = gain[0]
    for part in range(3):
        piece = left.astype(BF).astype(F32)
        left = left - piece
        for i in range(4):
            meta = jnp.where(row == 1 + 4 * part + i, piece[:, i * BLK : (i + 1) * BLK], meta)
    return meta.astype(BF)


def own_slot(src, cnt, dom, i):
    b, k = divmod(i, K)
    return k < cnt[0, b], (src[0, b, k] - (dom * BD - 1) + 512) & 255


def first_kernel(order, src, cnt, gain, inner, outer, samples, w0, w1, w2, w3, tiles, *rest):
    outs, (wbuf, tbuf, sbuf, gbuf, hbuf, ibuf, obuf, wsem, tsem, hsem, esem) = rest[:-11], rest[-11:]
    p, dom, _, _, _ = place()

    @pl.when(p == 0)
    def _():
        for m, w in enumerate((w0, w1, w2, w3)):
            pltpu.make_async_copy(w.at[0, 0], wbuf.at[m], wsem.at[m]).start()
        for n, sample in enumerate(order):
            pltpu.make_async_copy(samples.at[sample], hbuf.at[n], hsem.at[n]).start()
            pltpu.make_async_copy(inner.at[sample], ibuf.at[n], esem.at[0, n]).start()
            pltpu.make_async_copy(outer.at[sample], obuf.at[n], esem.at[1, n]).start()
        pltpu.make_async_copy(tiles.at[0], tbuf, tsem).start()
        in_place = halo_places()

        def tile(i):
            b, k = divmod(i, K)
            used, _ = own_slot(src, cnt, dom, i)
            t = tbuf[b, k]
            return jnp.where(used, t, jnp.zeros_like(t))

        def code(i):
            used, at = own_slot(src, cnt, dom, i)
            return jnp.where(used, at, 0)

        for n, sample in enumerate(order):
            if n == 0:
                pltpu.make_async_copy(w0.at[0, 0], wbuf.at[0], wsem.at[0]).wait()
            pltpu.make_async_copy(samples.at[sample], hbuf.at[n], hsem.at[n]).wait()
            pltpu.make_async_copy(inner.at[sample], ibuf.at[n], esem.at[0, n]).wait()
            pltpu.make_async_copy(outer.at[sample], obuf.at[n], esem.at[1, n]).wait()
            for at, block in zip(in_place, (ibuf, obuf)):
                sbuf[pl.ds(at, BLK), :] = sender_rows(block[n], wbuf[0])
            for i in range(2):
                rows = slice(i * HALF, (i + 1) * HALF)
                sbuf[BLK + i * HALF : BLK + (i + 1) * HALF, :] = sender_rows(hbuf[n, rows, :], wbuf[0])
            if n == 0:
                pltpu.make_async_copy(tiles.at[0], tbuf, tsem).wait()
                for m, w in ((1, w1), (2, w2), (3, w3)):
                    pltpu.make_async_copy(w.at[0, 0], wbuf.at[m], wsem.at[m]).wait()
            gather(tile, code, sbuf, gbuf)
            for i in range(2):
                rows = slice(i * HALF, (i + 1) * HALF)
                new = update_rows(hbuf[n, rows, :], gbuf[rows, :], wbuf, gain[0])
                if sample == 0:
                    outs[0][rows, :] = new
                    continue
                for j in range(4):
                    which, at = layout(sample, j)
                    outs[which][at + i * HALF : at + (i + 1) * HALF, :] = new[:, j * BLK : (j + 1) * BLK]

    if 0 not in order:

        @pl.when(p != 0)
        def _():
            moves = [
                pltpu.make_async_copy(
                    tiles.at[0, b, k], out.at[pl.ds((b * K + k) * BLK, BLK)], wsem.at[n]
                )
                for n, out in enumerate(outs)
                for b in range(BD)
                for k in range(K)
            ]
            for m in moves:
                m.start()
            small = own_small(src, cnt, gain)
            for n, out in enumerate(outs):
                out[2 * ROWS :, :] = small
                there = out.at[pl.ds(0, 2 * ROWS)]
                pltpu.make_async_copy(there, there, wsem.at[n]).wait()


def layout(sample, j):
    if sample == 1:
        return 0, 2 * D + j * D
    if sample == 3:
        return 1, j * D
    return (0, j * D) if j < 2 else (1, 4 * D + (j - 2) * D)


def first_call(order, src, cnt, gain, inner, outer, samples, ws, tiles):
    n = len(order)
    shape = (D, D) if 0 in order else (2 * ROWS + META, BLK)
    return pl.pallas_call(
        functools.partial(first_kernel, order),
        out_shape=[jax.ShapeDtypeStruct(shape, BF)] * (1 if 0 in order else 2),
        in_specs=[SMEM, SMEM, VMEM] + [ANY] * 8,
        out_specs=[VMEM] * (1 if 0 in order else 2),
        scratch_shapes=[
            pltpu.VMEM((4, D, D), BF),
            pltpu.VMEM((BD, K, BLK, BLK), BF),
            pltpu.VMEM(((BD + 2) * BLK, D), BF),
            pltpu.VMEM((BD * BLK, D), BF),
            pltpu.VMEM((n, D, D), BF),
            pltpu.VMEM((n, BLK, D), BF),
            pltpu.VMEM((n, BLK, D), BF),
            pltpu.SemaphoreType.DMA((4,)),
            pltpu.SemaphoreType.DMA,
            pltpu.SemaphoreType.DMA((n,)),
            pltpu.SemaphoreType.DMA((2, n)),
        ],
        compiler_params=params(20 if 0 in order else 60),
        cost_estimate=pl.CostEstimate(
            flops=2_000_000_000 * n, bytes_accessed=4_000_000, transcendentals=262144 * n
        ),
        name=f"first{n}",
    )(src, cnt, gain, inner, outer, samples, *ws, tiles)


def arrived_kernel(h0, near, far, mixed_a, mixed_b, out, sem):
    p = lax.axis_index("segment")

    @pl.when(p == 0)
    def _():
        pltpu.make_async_copy(h0, out, sem).start()

    for q in (1, 2, 3):

        @pl.when(p == q)
        def _():
            for j in range(4):
                which, at = layout(q, j)
                src = (near, far)[which]
                if q == 2:
                    src, at = (mixed_a, at) if which == 0 else (mixed_b, at - ROWS)
                pltpu.make_async_copy(
                    src.at[pl.ds(at, D)], out.at[:, pl.ds(j * BLK, BLK)], sem
                ).start()

    pltpu.make_async_copy(h0, out, sem).wait()


def arrived_call(*args):
    return pl.pallas_call(
        arrived_kernel,
        out_shape=jax.ShapeDtypeStruct((D, D), BF),
        in_specs=[ANY] * 5,
        out_specs=VMEM,
        scratch_shapes=[pltpu.SemaphoreType.DMA],
        compiler_params=params(4),
        name="arrived",
    )(*args)


def copies(kernel_name, plan, shapes, *args):
    def kernel(*refs):
        ins, outs, sem = refs[: len(args)], refs[len(args) : -1], refs[-1]
        moves = [
            pltpu.make_async_copy(a, b, sem.at[i]) for i, (a, b) in enumerate(plan(ins, outs))
        ]
        for m in moves:
            m.start()
        for m in moves:
            m.wait()

    return pl.pallas_call(
        kernel,
        out_shape=[jax.ShapeDtypeStruct(shape, BF) for shape in shapes],
        in_specs=[ANY] * len(args),
        out_specs=[ANY] * len(shapes),
        scratch_shapes=[pltpu.SemaphoreType.DMA((12,))],
        compiler_params=params(4),
        cost_estimate=pl.CostEstimate(flops=0, bytes_accessed=2_000_000, transcendentals=0),
        name=kernel_name,
    )(*args)


def joined(ring):
    def plan(ins, outs):
        return [(ins[r], outs[0].at[r]) for r in range(4)]

    return copies("joined", plan, [(4, D, HALF)], *ring)[0]


STAGE_BY_Y = {1: True, 2: False, 3: True}


def weights_kernel(section, *refs):
    own, stage = refs[:4], refs[4:6]
    out, sem = refs[-2:]
    p, dom, y, _, c = place()

    @pl.when(p == section)
    def _():
        for m in range(4):
            pltpu.make_async_copy(own[m].at[0, 0], out.at[m], sem.at[m]).start()

    @pl.when(p != section)
    def _():
        first = y if STAGE_BY_Y[section] else (dom >> 3) & 3
        for m in range(4):
            for core in range(2):
                cols = pl.multiple_of((c ^ core) * HALF, HALF)
                pltpu.make_async_copy(
                    stage[core].at[first ^ m], out.at[m, :, pl.ds(cols, HALF)], sem.at[m]
                ).start()

    for m in range(4):
        pltpu.make_async_copy(own[m].at[0, 0], out.at[m], sem.at[m]).wait()


def weights_call(section, own, stage):
    return pl.pallas_call(
        functools.partial(weights_kernel, section),
        out_shape=jax.ShapeDtypeStruct((4, D, D), BF),
        in_specs=[ANY] * 6,
        out_specs=VMEM,
        scratch_shapes=[pltpu.SemaphoreType.DMA((4,))],
        compiler_params=params(4),
        cost_estimate=pl.CostEstimate(flops=0, bytes_accessed=4_000_000, transcendentals=0),
        name=f"weights{section}",
    )(*own, *stage)


def tiles_kernel(section, own, near, far, mixed_a, mixed_b, tiles, codes, gain, meta, sem):
    for q in range(SEG):

        @pl.when(lax.axis_index("segment") == q)
        def _():
            x = q ^ section
            if x == 2:
                first, second, small = mixed_a, mixed_b, mixed_b.at[pl.ds(ROWS, META)]
            else:
                whole = {0: own, 1: near, 3: far}[x]
                first, second = whole, whole.at[pl.ds(ROWS, ROWS)]
                small = whole.at[pl.ds(2 * ROWS, META)]
            for i in range(2 * K):
                rows = pl.ds(i * BLK, BLK)
                pltpu.make_async_copy(first.at[rows], tiles.at[i], sem.at[0]).start()
                pltpu.make_async_copy(second.at[rows], tiles.at[2 * K + i], sem.at[1]).start()
            pltpu.make_async_copy(small, meta, sem.at[2]).start()

    pltpu.make_async_copy(own.at[pl.ds(2 * ROWS, META)], meta, sem.at[2]).wait()
    for half in range(2):
        there = tiles.at[pl.ds(half * 2 * K, 2 * K)]
        pltpu.make_async_copy(there, there, sem.at[half]).wait()
    m = meta[...].astype(F32)
    code = m[:8]
    codes[...] = jnp.where(code < 7.0, code, 0.0).astype(jnp.int32)
    gain[...] = jnp.concatenate(
        [m[1 + i : 2 + i] + (m[5 + i : 6 + i] + m[9 + i : 10 + i]) for i in range(4)], axis=1
    )
    for i in range(BD * K):
        used = jnp.broadcast_to(m[0:1, i : i + 1], (BLK, BLK)) < 7.0
        tiles[i] = jnp.where(used, tiles[i].astype(F32), 0.0).astype(BF)


def tiles_call(section, arrays):
    return pl.pallas_call(
        functools.partial(tiles_kernel, section),
        out_shape=[
            jax.ShapeDtypeStruct((BD * K, BLK, BLK), BF),
            jax.ShapeDtypeStruct((8, BLK), jnp.int32),
            jax.ShapeDtypeStruct((1, D), F32),
        ],
        in_specs=[ANY] * len(arrays),
        out_specs=[VMEM] * 3,
        scratch_shapes=[pltpu.VMEM((META, BLK), BF), pltpu.SemaphoreType.DMA((3,))],
        compiler_params=params(4),
        cost_estimate=pl.CostEstimate(flops=0, bytes_accessed=2_000_000, transcendentals=0),
        name=f"tiles{section}",
    )(*arrays)


def section_kernel(codes, gain, tiles, w, h, inner, outer, sender, out, sbuf, gbuf):
    sbuf[BLK : 5 * BLK, :] = sender[...]
    for at, block in zip(halo_places(), (inner, outer)):
        sbuf[pl.ds(at, BLK), :] = block[...]
    gather(lambda i: tiles[i], lambda i: codes[0, i], sbuf, gbuf)
    for i in range(2):
        rows = slice(i * HALF, (i + 1) * HALF)
        out[rows, :] = update_rows(h[rows, :], gbuf[rows, :], w, gain[...])


def section_call(section, codes, gain, tiles, w, h, inner, outer, sender):
    return pl.pallas_call(
        section_kernel,
        out_shape=jax.ShapeDtypeStruct((BD * BLK, D), BF),
        in_specs=[SMEM] + [VMEM] * 7,
        out_specs=VMEM,
        scratch_shapes=[
            pltpu.VMEM(((BD + 2) * BLK, D), BF),
            pltpu.VMEM((BD * BLK, D), BF),
        ],
        compiler_params=params(16),
        cost_estimate=pl.CostEstimate(
            flops=1_500_000_000, bytes_accessed=4_000_000, transcendentals=262144
        ),
        name=f"section{section}",
    )(codes, gain, tiles, w, h, inner, outer, sender)


def sender_kernel(h, w, full, inner, outer):
    core = place()[4]
    for i in range(2):
        rows = slice(i * HALF, (i + 1) * HALF)
        full[rows, :] = sender_rows(h[rows, :], w[0])
    inner[...] = full[pl.ds(pl.multiple_of((1 - core) * 3 * BLK, BLK), BLK), :]
    outer[...] = full[pl.ds(pl.multiple_of(core * 3 * BLK, BLK), BLK), :]


def sender_call(section, h, w):
    return pl.pallas_call(
        sender_kernel,
        out_shape=[
            jax.ShapeDtypeStruct((BD * BLK, D), BF),
            jax.ShapeDtypeStruct((BLK, D), BF),
            jax.ShapeDtypeStruct((BLK, D), BF),
        ],
        in_specs=[VMEM, VMEM],
        out_specs=[VMEM] * 3,
        compiler_params=params(8),
        cost_estimate=pl.CostEstimate(
            flops=270_000_000, bytes_accessed=1_500_000, transcendentals=262144
        ),
        name=f"sender{section}",
    )(h, w)


def after(values, *others):
    return lax.optimization_barrier((values, others))[0]


def over_segments(value, x):
    return lax.ppermute(value, "segment", by_segment(x))


def over_dom(value, pairs):
    return lax.ppermute(value, "dom", pairs)


def exchange(inner, outer):
    return over_dom(inner, OTHER_CORE), over_dom(outer, NEXT_CHIP)


def shards(samples, w_source, w_self, w_message, w_output, norm_gain, tile_source, tile_count, tile_value):
    p, dom, y, _, core = place()
    ws = [w_source, w_self, w_message, w_output]
    edge = [samples[:, :BLK], samples[:, (BD - 1) * BLK :]]
    edge = [jnp.where(core == 0, edge[1], edge[0]), jnp.where(core == 0, edge[0], edge[1])]
    inner, outer = exchange(*edge)

    m = jnp.where(p == 2, (dom >> 3) & 3, y)
    a, b, c, d = (lax.dynamic_slice(w[0, 0], (0, core * HALF), (D, HALF)) for w in ws)
    piece = jnp.where(m < 2, jnp.where(m == 0, a, b), jnp.where(m == 2, c, d))
    piece = after(piece, edge)
    x1, x3, x2 = over_segments(piece, 1), over_segments(piece, 3), over_segments(piece, 2)

    small = (tile_source, tile_count, norm_gain, inner, outer, samples, ws, tile_value)
    own, own_far = first_call((2, 1, 3), *small)
    near, far = over_segments(own, 1), over_segments(own_far, 3)
    (h0,) = first_call((0,), *small)
    mixed_b, mixed_a = over_segments(far[ROWS:], 1), over_segments(near[:ROWS], 3)
    arrays = [own, near, far, mixed_a, mixed_b]

    def ring(own, routes, *waits):
        a, c = over_dom(own, routes[0]), over_dom(own, routes[2])
        b = over_dom(after(own, a, c, waits), routes[1])
        return [own, a, b, c]

    def both(pieces):
        return pieces, over_dom(pieces, OTHER_CORE)

    over_y, over_z = [by_y(x) for x in (1, 2, 3)], [Z_EVEN, Z_FAR, Z_ODD]
    x1, x2, x3 = after((x1, x2, x3), own, own_far)
    ring1 = ring(jnp.where(p == 2, x3, jnp.where(p == 3, x2, x1)), over_y)
    then = jnp.where(p == 0, x2, jnp.where(p == 1, x3, x1))
    last = jnp.where(p == 0, x3, jnp.where(p == 1, x2, x1))
    then, last = after((then, last), near, far, ring1)
    ring2, ring3 = ring(then, over_z), ring(last, over_y)
    stages = {1: both(joined(ring1)), 2: both(joined(ring2))}
    h = arrived_call(h0, near, far, mixed_a, mixed_b)
    for section in range(1, SEG):
        if section == 2:
            stages[3] = both(joined(after(ring3, h)))
        w = weights_call(section, ws, stages[section])
        tiles, codes, gain = tiles_call(section, arrays)
        sender, inner, outer = sender_call(section, h, w)
        inner, outer = exchange(inner, outer)
        h = section_call(section, codes, gain, tiles, w, h, inner, outer, sender)
    return h[None]


def solution(mesh):
    return jax.shard_map(
        shards,
        mesh=mesh,
        in_specs=(
            P(None, "dom", None),
            P("segment", None, None, None),
            P("segment", None, None, None),
            P("segment", None, None, None),
            P("segment", None, None, None),
            P("segment", None, None),
            P("segment", "dom", None),
            P("segment", "dom"),
            P("segment", "dom", None, None, None),
        ),
        out_specs=P("segment", "dom", None),
        check_vma=False,
    )
```

time: 117 us -> 114 us (0.974)
  waiting for transfers between devices: 29.2 us -> 50.5 us
  starting transfers between devices: 57.9 us -> 37.6 us
  Pallas kernels: 24.1 us -> 18.8 us
  local copies, waits for them, and re-layouts: 2.28 us -> 3.78 us
    ppermute x26 -> x20, waiting for transfers between devices: 23.2 us -> 44.2 us  [over_dom(): return lax.ppermute(value, 'dom', pairs)]
    ppermute x26 -> x20, starting transfers between devices: 47 us -> 26 us  [over_dom(): return lax.ppermute(value, 'dom', pairs)]
    pallas_call x6 -> x3, Pallas kernels: 4.69 us -> 0.56 us  [copies(): pl.pallas_call(kernel, out_shape=[jax.ShapeDtypeStruct(shape, BF) for sha...]
    unnamed x14 -> x36, local copies, waits for them, and re-layouts: 0.04 us -> 3.73 us
    select_n x1, other arithmetic: 1.01 us -> 2.39 us  [shards(): jnp.where(core == 0, edge[0], edge[1])]
    select_n x6 -> x2, other arithmetic: 1.42 us -> 0.22 us  [the longest x1 0.15 us: shards(): piece = jnp.where(m < 2, jnp.where(m == 0, a, b), jnp.where(m == 2, c, d))]
    pallas_call x13 -> x12, Pallas kernels: 17.9 us -> 16.7 us  [the longest x3 8.14 us: section_call(): pl.pallas_call(section_kernel, out_shape=jax.ShapeDtypeStruct((BD * BLK,...]
    ppermute x9 -> x7, starting transfers between devices: 10.9 us -> 11.6 us  [over_segments(): return lax.ppermute(value, 'segment', by_segment(x))]
  transfers between devices with their start and end apart: 35 -> 27, of which waited for: 14 -> 13; matrix products, arithmetic and copies ran while one was open for 3% -> 0% of each run, Pallas kernels for 15% -> 13%
where the time goes in v3:
time: 114 us
  waiting for transfers between devices  50.5 us (44%)
  starting transfers between devices  37.6 us (33%)
  Pallas kernels  18.8 us (16%)
  local copies, waits for them, and re-layouts  3.78 us (3%)
  other arithmetic  2.61 us (2%)
    ppermute x20, waiting for transfers between devices, over_dom(): return lax.ppermute(value, 'dom', pairs)  44.2 us
    ppermute x20, starting transfers between devices, over_dom(): return lax.ppermute(value, 'dom', pairs)  26 us
    ppermute x7, starting transfers between devices, over_segments(): return lax.ppermute(value, 'segment', by_segment(x))  11.6 us
    pallas_call x3, Pallas kernels, section_call(): pl.pallas_call(section_kernel, out_shape=jax.ShapeDtypeStruct((BD * BLK,...  8.14 us
    ppermute x7, waiting for transfers between devices, over_segments(): return lax.ppermute(value, 'segment', by_segment(x))  6.24 us
    pallas_call x2, Pallas kernels, first_call(): pl.pallas_call(functools.partial(first_kernel, order), out_shape=[jax.Sha...  4.04 us
    pallas_call x3, Pallas kernels, tiles_call(): pl.pallas_call(functools.partial(tiles_kernel, section), out_shape=[jax.S...  3.78 us
    unnamed x36, local copies, waits for them, and re-layouts  3.73 us
  transfers between devices with their start and end apart: 27, of which 13 were waited for; matrix products, arithmetic and copies ran while one was open for 0% of the time, Pallas kernels for 13%

profile of v3, /device:TPU:6, one launch (start us, length us, event | category | flops | bytes accessed | tf_op | source)
XLA Modules:
  0.0 113.7 jit_solution(14041292862316227551)
XLA Ops:
  0.0 0.0 copy-start.1
  0.0 2.4 %broadcast_select_fusion = (bf16[4,128,512]{2,1,0:T(8,128)(2,1)}, bf16[4,128,512]{2,1,0:T(8,128)(2,1)}) fusion(pred[]{:T(512)S(6)} %eq.25, bf16[4,512,512]{2,1,0:T(8,128)(2,1)} %samples.3), kind=kLoop, calls=%fused_computation | loop fusion | flops 524288 | bytes 2097153 | tf_op jit(solution)/shard_map/jit(_where)/select_n | solution.py:453
  2.4 7.7 %collective-permute-start.1 = (bf16[4,128,512]{2,1,0:T(8,128)(2,1)}, bf16[4,128,512]{2,1,0:T(8,128)(2,1)S(1)}, u32[]{:S(2)}, u32[]{:S(2)}) collective-permute-start(bf16[4,128,512]{2,1,0:T(8,128)(2,1)} %get-tuple-element.71), channel_id=1, source_target_pairs={{0,63},{1,2},{2,1},{3,4},{4,3},{5,6},{6,5},{7,8},{8,7},{9,10},{10,... | collective-permute-start | bytes 1572872 | tf_op jit(solution)/shard_map/ppermute | solution.py:442
  10.2 0.1 select_bitcast_fusion
  10.4 0.6 collective-permute-start.8
  10.9 2.4 %collective-permute-start.7 = (bf16[512,256]{1,0:T(8,128)(2,1)S(1)}, bf16[512,256]{1,0:T(8,128)(2,1)S(1)}, u32[]{:S(2)}, u32[]{:S(2)}) collective-permute-start(bf16[512,256]{1,0:T(8,128)(2,1)S(1)} %select_bitcast_fusion), channel_id=1, source_target_pairs={{0,128},{64,192},{128,0},{192,64},{1,129},{65,193},{129,1},{193,65... | collective-permute-start | bytes 786440 | tf_op jit(solution)/shard_map/ppermute | solution.py:438
  13.3 1.2 %collective-permute-start.6 = (bf16[512,256]{1,0:T(8,128)(2,1)S(1)}, bf16[512,256]{1,0:T(8,128)(2,1)S(1)}, u32[]{:S(2)}, u32[]{:S(2)}) collective-permute-start(bf16[512,256]{1,0:T(8,128)(2,1)S(1)} %select_bitcast_fusion), channel_id=1, source_target_pairs={{0,64},{64,0},{128,192},{192,128},{1,65},{65,1},{129,193},{193,129... | collective-permute-start | bytes 786440 | tf_op jit(solution)/shard_map/ppermute | solution.py:438
  14.5 2.7 %collective-permute-done.1.outer = bf16[4,128,512]{2,1,0:T(8,128)(2,1)S(1)} collective-permute-done((bf16[4,128,512]{2,1,0:T(8,128)(2,1)}, bf16[4,128,512]{2,1,0:T(8,128)(2,1)S(1)}, u32[]{:S(2)}, u32[]{:S(2)}) %collective-permute-start.1) | collective-permute-done | bytes 524320 | tf_op jit(solution)/shard_map/ppermute | solution.py:442
  17.2 0.8 copy-done.11
  18.0 0.8 copy-done.13
  18.8 3.4 %first3.1 = (bf16[3088,128]{1,0:T(8,128)(2,1)}, bf16[3088,128]{1,0:T(8,128)(2,1)}) custom-call(s32[1,4,6]{2,1,0:T(4,128)} %src.3, s32[1,4]{1,0:T(1,128)} %cnt.3, f32[1,1,512]{2,1,0:T(1,128)} %gain.3, bf16[4,128,512]{2,1,0:T(8,128)(2,1)} %copy-done.13, bf16[4,128,512]{2,1,0:T(8,128)(2,1)} %copy-done.11, bf16[4,512,512]{2,1,0:T(8,128)(2,1)} %samples.3, ...), custom_call_target="tpu_custom_call" | custom-call | flops 6000000000 | bytes 4000000 | tf_op jit(solution)/shard_map/first3/pallas_call | solution.py:197
  22.2 3.8 %collective-permute-done.8 = bf16[512,256]{1,0:T(8,128)(2,1)S(1)} collective-permute-done((bf16[512,256]{1,0:T(8,128)(2,1)S(1)}, bf16[512,256]{1,0:T(8,128)(2,1)S(1)}, u32[]{:S(2)}, u32[]{:S(2)}) %collective-permute-start.8) | collective-permute-done | bytes 262176 | tf_op jit(solution)/shard_map/ppermute | solution.py:438
  26.0 0.6 collective-permute-done.6
  26.6 0.1 select_select_fusion
  26.8 0.1 collective-permute-start.10
  26.9 0.1 collective-permute-start.9
  27.0 0.9 collective-permute-start.2
  27.9 3.1 %collective-permute-start.3 = (bf16[3088,128]{1,0:T(8,128)(2,1)}, bf16[3088,128]{1,0:T(8,128)(2,1)S(1)}, u32[]{:S(2)}, u32[]{:S(2)}) collective-permute-start(bf16[3088,128]{1,0:T(8,128)(2,1)} %get-tuple-element.39), channel_id=1, source_target_pairs={{0,192},{64,128},{128,64},{192,0},{1,193},{65,129},{129,65},{193,1... | collective-permute-start | bytes 2371592 | tf_op jit(solution)/shard_map/ppermute | solution.py:438
  31.0 4.7 %collective-permute-done.10.refs_3_ = bf16[512,256]{1,0:T(8,128)(2,1)S(1)} collective-permute-done((bf16[512,256]{1,0:T(8,128)(2,1)S(1)}, bf16[512,256]{1,0:T(8,128)(2,1)S(1)}, u32[]{:S(2)}, u32[]{:S(2)}) %collective-permute-start.10) | collective-permute-done | bytes 262176 | tf_op jit(solution)/shard_map/ppermute | solution.py:442
  35.7 1.5 %collective-permute-start.11 = (bf16[512,256]{1,0:T(8,128)(2,1)S(1)}, bf16[512,256]{1,0:T(8,128)(2,1)S(1)}, u32[]{:S(2)}, u32[]{:S(2)}) collective-permute-start(bf16[512,256]{1,0:T(8,128)(2,1)S(1)} %get-tuple-element.47.refs_0_), channel_id=1, source_target_pairs={{0,4},{1,5},{2,6},{3,7},{4,0},{5,1},{6,2},{7,3},{8,12},{9,13},{10,... | collective-permute-start | bytes 786440 | tf_op jit(solution)/shard_map/ppermute | solution.py:442
  37.1 6.7 %collective-permute-done.11.refs_2_ = bf16[512,256]{1,0:T(8,128)(2,1)S(1)} collective-permute-done((bf16[512,256]{1,0:T(8,128)(2,1)S(1)}, bf16[512,256]{1,0:T(8,128)(2,1)S(1)}, u32[]{:S(2)}, u32[]{:S(2)}) %collective-permute-start.11) | collective-permute-done | bytes 262176 | tf_op jit(solution)/shard_map/ppermute | solution.py:442
  43.9 0.2 joined.3.refs_4_
  44.1 0.3 collective-permute-start.15
  44.3 1.9 %collective-permute-done.2.near = bf16[3088,128]{1,0:T(8,128)(2,1)S(1)} collective-permute-done((bf16[3088,128]{1,0:T(8,128)(2,1)}, bf16[3088,128]{1,0:T(8,128)(2,1)S(1)}, u32[]{:S(2)}, u32[]{:S(2)}) %collective-permute-start.2) | collective-permute-done | bytes 790560 | tf_op jit(solution)/shard_map/ppermute | solution.py:438
  46.2 3.3 %collective-permute-start.4 = (bf16[1536,128]{1,0:T(8,128)(2,1)S(1)}, bf16[1536,128]{1,0:T(8,128)(2,1)S(1)}, u32[]{:S(2)}, u32[]{:S(2)}) collective-permute-start(bf16[1536,128]{1,0:T(8,128)(2,1)S(1)} %slice.16), channel_id=1, source_target_pairs={{0,192},{64,128},{128,64},{192,0},{1,193},{65,129},{129,65},{193,1... | collective-permute-start | bytes 1179656 | tf_op jit(solution)/shard_map/ppermute | solution.py:438
  49.5 4.0 %collective-permute-start.20 = (bf16[512,256]{1,0:T(8,128)(2,1)S(1)}, bf16[512,256]{1,0:T(8,128)(2,1)S(1)}, u32[]{:S(2)}, u32[]{:S(2)}) collective-permute-start(bf16[512,256]{1,0:T(8,128)(2,1)S(1)} %get-tuple-element.64.refs_0_), channel_id=1, source_target_pairs={{0,56},{1,57},{2,58},{3,59},{4,60},{5,61},{6,62},{7,63},{8,16},{9,... | collective-permute-start | bytes 786440 | tf_op jit(solution)/shard_map/ppermute | solution.py:442
  53.5 0.1 collective-permute-start.5
  53.6 6.9 %collective-permute-done.20.refs_3_ = bf16[512,256]{1,0:T(8,128)(2,1)S(1)} collective-permute-done((bf16[512,256]{1,0:T(8,128)(2,1)S(1)}, bf16[512,256]{1,0:T(8,128)(2,1)S(1)}, u32[]{:S(2)}, u32[]{:S(2)}) %collective-permute-start.20) | collective-permute-done | bytes 262176 | tf_op jit(solution)/shard_map/ppermute | solution.py:442
  60.5 1.5 %collective-permute-done.19.refs_1_ = bf16[512,256]{1,0:T(8,128)(2,1)S(1)} collective-permute-done((bf16[512,256]{1,0:T(8,128)(2,1)S(1)}, bf16[512,256]{1,0:T(8,128)(2,1)S(1)}, u32[]{:S(2)}, u32[]{:S(2)}) %collective-permute-start.19) | collective-permute-done | bytes 262176 | tf_op jit(solution)/shard_map/ppermute | solution.py:442
  62.0 1.4 %collective-permute-start.21 = (bf16[512,256]{1,0:T(8,128)(2,1)S(1)}, bf16[512,256]{1,0:T(8,128)(2,1)S(1)}, u32[]{:S(2)}, u32[]{:S(2)}) collective-permute-start(bf16[512,256]{1,0:T(8,128)(2,1)S(1)} %get-tuple-element.64.refs_0_), channel_id=1, source_target_pairs={{0,16},{1,17},{2,18},{3,19},{4,20},{5,21},{6,22},{7,23},{8,24},{9,... | collective-permute-start | bytes 786440 | tf_op jit(solution)/shard_map/ppermute | solution.py:442
  63.4 1.1 collective-permute-start.13
  64.5 0.8 collective-permute-start.12
  65.4 1.0 copy-done.12
  66.4 1.0 copy-done.14
  67.5 0.7 first1.1.h0
  68.1 0.1 arrived.1.h
  68.3 7.9 %collective-permute-done.21.refs_2_ = bf16[512,256]{1,0:T(8,128)(2,1)S(1)} collective-permute-done((bf16[512,256]{1,0:T(8,128)(2,1)S(1)}, bf16[512,256]{1,0:T(8,128)(2,1)S(1)}, u32[]{:S(2)}, u32[]{:S(2)}) %collective-permute-start.21) | collective-permute-done | bytes 262176 | tf_op jit(solution)/shard_map/ppermute | solution.py:442
  76.2 0.2 joined.5.refs_4_
  76.4 0.1 collective-permute-start.22
  76.5 0.2 weights1.1.w
  76.7 0.5 sender1.1
  77.2 0.6 collective-permute-start.16
  77.8 0.5 collective-permute-start.17
  78.3 3.3 %collective-permute-start.14 = (bf16[512,256]{1,0:T(8,128)(2,1)S(1)}, bf16[512,256]{1,0:T(8,128)(2,1)S(1)}, u32[]{:S(2)}, u32[]{:S(2)}) collective-permute-start(bf16[512,256]{1,0:T(8,128)(2,1)S(1)} %get-tuple-element.56.refs_0_), channel_id=1, source_target_pairs={{0,4},{1,5},{2,6},{3,7},{4,0},{5,1},{6,2},{7,3},{8,12},{9,13},{10,... | collective-permute-start | bytes 786440 | tf_op jit(solution)/shard_map/ppermute | solution.py:442
  81.6 1.3 %tiles1.1 = (bf16[24,128,128]{2,1,0:T(8,128)(2,1)S(1)}, s32[8,128]{1,0:T(8,128)S(1)}, f32[1,512]{1,0:T(1,128)S(1)}) custom-call(bf16[3088,128]{1,0:T(8,128)(2,1)S(1)} %copy-done, bf16[3088,128]{1,0:T(8,128)(2,1)S(1)} %collective-permute-done.2.near, bf16[3088,128]{1,0:T(8,128)(2,1)S(1)} %collective-permute-done.3.far, ...), custom_call_target="tpu_custom_call" | custom-call | bytes 2000000 | tf_op jit(solution)/shard_map/tiles1/pallas_call | solution.py:362
  82.8 3.9 %collective-permute-done.17.outer = bf16[128,512]{1,0:T(8,128)(2,1)S(1)} collective-permute-done((bf16[128,512]{1,0:T(8,128)(2,1)S(1)}, bf16[128,512]{1,0:T(8,128)(2,1)S(1)}, u32[]{:S(2)}, u32[]{:S(2)}) %collective-permute-start.17) | collective-permute-done | bytes 131104 | tf_op jit(solution)/shard_map/ppermute | solution.py:442
  86.7 2.4 %section1.1.h = bf16[512,512]{1,0:T(8,128)(2,1)S(1)} custom-call(s32[8,128]{1,0:T(8,128)S(1)} %get-tuple-element.50.codes, f32[1,512]{1,0:T(1,128)S(1)} %get-tuple-element.51.gain, bf16[24,128,128]{2,1,0:T(8,128)(2,1)S(1)} %get-tuple-element.52.tiles, bf16[4,512,512]{2,1,0:T(8,128)(2,1)S(1)} %weights1.1.w, bf16[512,512]{1,0:T(8,128)(2,1)S(1)} %arrived.1.h, ...), custom_call_target="tpu_custom_call" | custom-call | flops 1500000000 | bytes 4000000 | tf_op jit(solution)/shard_map/section1/pallas_call | solution.py:389
  89.1 0.7 collective-permute-done.14.refs_2_
  89.8 0.2 joined.4.refs_4_
  90.0 0.7 collective-permute-start.18
  90.7 0.2 weights2.1.w
  90.9 0.5 sender2.1
  91.4 0.2 collective-permute-start.23
  91.6 1.8 %collective-permute-start.24 = (bf16[128,512]{1,0:T(8,128)(2,1)S(1)}, bf16[128,512]{1,0:T(8,128)(2,1)S(1)}, u32[]{:S(2)}, u32[]{:S(2)}) collective-permute-start(bf16[128,512]{1,0:T(8,128)(2,1)S(1)} %get-tuple-element.66), channel_id=1, source_target_pairs={{0,63},{1,2},{2,1},{3,4},{4,3},{5,6},{6,5},{7,8},{8,7},{9,10},{10,... | collective-permute-start | bytes 393224 | tf_op jit(solution)/shard_map/ppermute | solution.py:442
  93.4 1.3 %tiles2.1 = (bf16[24,128,128]{2,1,0:T(8,128)(2,1)S(1)}, s32[8,128]{1,0:T(8,128)S(1)}, f32[1,512]{1,0:T(1,128)S(1)}) custom-call(bf16[3088,128]{1,0:T(8,128)(2,1)S(1)} %copy-done, bf16[3088,128]{1,0:T(8,128)(2,1)S(1)} %collective-permute-done.2.near, bf16[3088,128]{1,0:T(8,128)(2,1)S(1)} %collective-permute-done.3.far, ...), custom_call_target="tpu_custom_call" | custom-call | bytes 2000000 | tf_op jit(solution)/shard_map/tiles2/pallas_call | solution.py:362
  94.7 4.7 %collective-permute-done.24.outer = bf16[128,512]{1,0:T(8,128)(2,1)S(1)} collective-permute-done((bf16[128,512]{1,0:T(8,128)(2,1)S(1)}, bf16[128,512]{1,0:T(8,128)(2,1)S(1)}, u32[]{:S(2)}, u32[]{:S(2)}) %collective-permute-start.24) | collective-permute-done | bytes 131104 | tf_op jit(solution)/shard_map/ppermute | solution.py:442
  99.3 2.5 %section2.1.h = bf16[512,512]{1,0:T(8,128)(2,1)S(1)} custom-call(s32[8,128]{1,0:T(8,128)S(1)} %get-tuple-element.60.codes, f32[1,512]{1,0:T(1,128)S(1)} %get-tuple-element.61.gain, bf16[24,128,128]{2,1,0:T(8,128)(2,1)S(1)} %get-tuple-element.62.tiles, bf16[4,512,512]{2,1,0:T(8,128)(2,1)S(1)} %weights2.1.w, bf16[512,512]{1,0:T(8,128)(2,1)S(1)} %section1.1.h, ...), custom_call_target="tpu_custom_call" | custom-call | flops 1500000000 | bytes 4000000 | tf_op jit(solution)/shard_map/section2/pallas_call | solution.py:389
  101.8 0.2 weights3.1.w
  102.0 0.5 sender3.1
  102.5 0.1 collective-permute-start.25
  102.6 1.9 %collective-permute-start.26 = (bf16[128,512]{1,0:T(8,128)(2,1)S(1)}, bf16[128,512]{1,0:T(8,128)(2,1)S(1)}, u32[]{:S(2)}, u32[]{:S(2)}) collective-permute-start(bf16[128,512]{1,0:T(8,128)(2,1)S(1)} %get-tuple-element.69), channel_id=1, source_target_pairs={{0,63},{1,2},{2,1},{3,4},{4,3},{5,6},{6,5},{7,8},{8,7},{9,10},{10,... | collective-permute-start | bytes 393224 | tf_op jit(solution)/shard_map/ppermute | solution.py:442
  104.5 1.3 %tiles3.1 = (bf16[24,128,128]{2,1,0:T(8,128)(2,1)S(1)}, s32[8,128]{1,0:T(8,128)S(1)}, f32[1,512]{1,0:T(1,128)S(1)}) custom-call(bf16[3088,128]{1,0:T(8,128)(2,1)S(1)} %copy-done, bf16[3088,128]{1,0:T(8,128)(2,1)S(1)} %collective-permute-done.2.near, bf16[3088,128]{1,0:T(8,128)(2,1)S(1)} %collective-permute-done.3.far, ...), custom_call_target="tpu_custom_call" | custom-call | bytes 2000000 | tf_op jit(solution)/shard_map/tiles3/pallas_call | solution.py:362
  105.8 4.7 %collective-permute-done.26.outer = bf16[128,512]{1,0:T(8,128)(2,1)S(1)} collective-permute-done((bf16[128,512]{1,0:T(8,128)(2,1)S(1)}, bf16[128,512]{1,0:T(8,128)(2,1)S(1)}, u32[]{:S(2)}, u32[]{:S(2)}) %collective-permute-start.26) | collective-permute-done | bytes 131104 | tf_op jit(solution)/shard_map/ppermute | solution.py:442
  110.4 3.2 %section3.1 = bf16[512,512]{1,0:T(8,128)(2,1)} custom-call(s32[8,128]{1,0:T(8,128)S(1)} %get-tuple-element.40.codes, f32[1,512]{1,0:T(1,128)S(1)} %get-tuple-element.41.gain, bf16[24,128,128]{2,1,0:T(8,128)(2,1)S(1)} %get-tuple-element.42.tiles, bf16[4,512,512]{2,1,0:T(8,128)(2,1)S(1)} %weights3.1.w, bf16[512,512]{1,0:T(8,128)(2,1)S(1)} %section2.1.h, ...), custom_call_target="tpu_custom_call" | custom-call | flops 1500000000 | bytes 4000000 | tf_op jit(solution)/shard_map/section3/pallas_call | solution.py:389
  (49 shorter events, 0.2 us)
Async XLA Ops:
  0.0 10.2 %copy-start.7 = (bf16[1,1,512,512]{3,2,1,0:T(8,128)(2,1)S(1)}, bf16[1,1,512,512]{3,2,1,0:T(8,128)(2,1)}, u32[]{:S(2)}) copy-start(bf16[1,1,512,512]{3,2,1,0:T(8,128)(2,1)} %refs_3_.5) | copy-start | bytes 1572868
  0.0 10.2 %copy-start.5 = (bf16[1,1,512,512]{3,2,1,0:T(8,128)(2,1)S(1)}, bf16[1,1,512,512]{3,2,1,0:T(8,128)(2,1)}, u32[]{:S(2)}) copy-start(bf16[1,1,512,512]{3,2,1,0:T(8,128)(2,1)} %refs_2_.5) | copy-start | bytes 1572868
  0.0 10.2 %copy-start.3 = (bf16[1,1,512,512]{3,2,1,0:T(8,128)(2,1)S(1)}, bf16[1,1,512,512]{3,2,1,0:T(8,128)(2,1)}, u32[]{:S(2)}) copy-start(bf16[1,1,512,512]{3,2,1,0:T(8,128)(2,1)} %refs_1_.5) | copy-start | bytes 1572868
  0.0 10.2 %copy-start.1 = (bf16[1,1,512,512]{3,2,1,0:T(8,128)(2,1)S(1)}, bf16[1,1,512,512]{3,2,1,0:T(8,128)(2,1)}, u32[]{:S(2)}) copy-start(bf16[1,1,512,512]{3,2,1,0:T(8,128)(2,1)} %refs_0_.5) | copy-start | bytes 1572868
  2.4 14.8 %collective-permute-start.1 = (bf16[4,128,512]{2,1,0:T(8,128)(2,1)}, bf16[4,128,512]{2,1,0:T(8,128)(2,1)S(1)}, u32[]{:S(2)}, u32[]{:S(2)}) collective-permute-start(bf16[4,128,512]{2,1,0:T(8,128)(2,1)} %get-tuple-element.71), channel_id=1, source_target_pairs={{0,63},{1,2},{2,1},{3,4},{4,3},{5,6},{6,5},{7,8},{8,7},{9,10},{10,... | collective-permute-start | bytes 1572872 | tf_op jit(solution)/shard_map/ppermute | solution.py:442
  10.2 7.1 %collective-permute-start = (bf16[4,128,512]{2,1,0:T(8,128)(2,1)}, bf16[4,128,512]{2,1,0:T(8,128)(2,1)S(1)}, u32[]{:S(2)}, u32[]{:S(2)}) collective-permute-start(bf16[4,128,512]{2,1,0:T(8,128)(2,1)} %get-tuple-element.72), channel_id=1, source_target_pairs={{0,1},{1,0},{2,3},{3,2},{4,5},{5,4},{6,7},{7,6},{8,9},{9,8},{10,11... | collective-permute-start | bytes 1572872 | tf_op jit(solution)/shard_map/ppermute | solution.py:442
  10.4 15.6 %collective-permute-start.8 = (bf16[512,256]{1,0:T(8,128)(2,1)S(1)}, bf16[512,256]{1,0:T(8,128)(2,1)S(1)}, u32[]{:S(2)}, u32[]{:S(2)}) collective-permute-start(bf16[512,256]{1,0:T(8,128)(2,1)S(1)} %select_bitcast_fusion), channel_id=1, source_target_pairs={{0,192},{64,128},{128,64},{192,0},{1,193},{65,129},{129,65},{193,1... | collective-permute-start | bytes 786440 | tf_op jit(solution)/shard_map/ppermute | solution.py:438
  10.9 15.1 %collective-permute-start.7 = (bf16[512,256]{1,0:T(8,128)(2,1)S(1)}, bf16[512,256]{1,0:T(8,128)(2,1)S(1)}, u32[]{:S(2)}, u32[]{:S(2)}) collective-permute-start(bf16[512,256]{1,0:T(8,128)(2,1)S(1)} %select_bitcast_fusion), channel_id=1, source_target_pairs={{0,128},{64,192},{128,0},{192,64},{1,129},{65,193},{129,1},{193,65... | collective-permute-start | bytes 786440 | tf_op jit(solution)/shard_map/ppermute | solution.py:438
  13.3 13.3 %collective-permute-start.6 = (bf16[512,256]{1,0:T(8,128)(2,1)S(1)}, bf16[512,256]{1,0:T(8,128)(2,1)S(1)}, u32[]{:S(2)}, u32[]{:S(2)}) collective-permute-start(bf16[512,256]{1,0:T(8,128)(2,1)S(1)} %select_bitcast_fusion), channel_id=1, source_target_pairs={{0,64},{64,0},{128,192},{192,128},{1,65},{65,1},{129,193},{193,129... | collective-permute-start | bytes 786440 | tf_op jit(solution)/shard_map/ppermute | solution.py:438
  17.2 0.8 copy-start.11
  18.0 0.8 copy-start.13
  26.6 38.7 %copy-start.9 = (bf16[4,512,512]{2,1,0:T(8,128)(2,1)S(1)}, bf16[4,512,512]{2,1,0:T(8,128)(2,1)}, u32[]{:S(2)}) copy-start(bf16[4,512,512]{2,1,0:T(8,128)(2,1)} %samples.3) | copy-start | bytes 6291460
  26.7 38.6 %copy-start.2 = (bf16[1,1,512,512]{3,2,1,0:T(8,128)(2,1)S(1)}, bf16[1,1,512,512]{3,2,1,0:T(8,128)(2,1)}, u32[]{:S(2)}) copy-start(bf16[1,1,512,512]{3,2,1,0:T(8,128)(2,1)} %refs_0_.5) | copy-start | bytes 1572868
  26.7 38.6 %copy-start.4 = (bf16[1,1,512,512]{3,2,1,0:T(8,128)(2,1)S(1)}, bf16[1,1,512,512]{3,2,1,0:T(8,128)(2,1)}, u32[]{:S(2)}) copy-start(bf16[1,1,512,512]{3,2,1,0:T(8,128)(2,1)} %refs_1_.5) | copy-start | bytes 1572868
  26.7 38.6 %copy-start.6 = (bf16[1,1,512,512]{3,2,1,0:T(8,128)(2,1)S(1)}, bf16[1,1,512,512]{3,2,1,0:T(8,128)(2,1)}, u32[]{:S(2)}) copy-start(bf16[1,1,512,512]{3,2,1,0:T(8,128)(2,1)} %refs_2_.5) | copy-start | bytes 1572868
  26.7 38.6 %copy-start.8 = (bf16[1,1,512,512]{3,2,1,0:T(8,128)(2,1)S(1)}, bf16[1,1,512,512]{3,2,1,0:T(8,128)(2,1)}, u32[]{:S(2)}) copy-start(bf16[1,1,512,512]{3,2,1,0:T(8,128)(2,1)} %refs_3_.5) | copy-start | bytes 1572868
  26.7 38.6 %copy-start.10 = (bf16[1,4,6,128,128]{4,3,2,1,0:T(8,128)(2,1)S(1)}, bf16[1,4,6,128,128]{4,3,2,1,0:T(8,128)(2,1)}, u32[]{:S(2)}) copy-start(bf16[1,4,6,128,128]{4,3,2,1,0:T(8,128)(2,1)} %tiles.3) | copy-start | bytes 2359300
  26.7 38.6 %copy-start.15 = (s32[1,4,6]{2,1,0:T(4,128)S(1)}, s32[1,4,6]{2,1,0:T(4,128)}, u32[]{:S(2)}) copy-start(s32[1,4,6]{2,1,0:T(4,128)} %src.3) | copy-start | bytes 292
  26.7 38.6 %copy-start.16 = (f32[1,1,512]{2,1,0:T(1,128)S(1)}, f32[1,1,512]{2,1,0:T(1,128)}, u32[]{:S(2)}) copy-start(f32[1,1,512]{2,1,0:T(1,128)} %gain.3) | copy-start | bytes 6148
  26.8 38.6 %copy-start.17 = (s32[1,4]{1,0:T(1,128)S(1)}, s32[1,4]{1,0:T(1,128)}, u32[]{:S(2)}) copy-start(s32[1,4]{1,0:T(1,128)} %cnt.3) | copy-start | bytes 52
  26.8 8.9 %collective-permute-start.10 = (bf16[512,256]{1,0:T(8,128)(2,1)S(1)}, bf16[512,256]{1,0:T(8,128)(2,1)S(1)}, u32[]{:S(2)}, u32[]{:S(2)}) collective-permute-start(bf16[512,256]{1,0:T(8,128)(2,1)S(1)} %get-tuple-element.47.refs_0_), channel_id=1, source_target_pairs={{0,6},{1,7},{2,4},{3,5},{4,2},{5,3},{6,0},{7,1},{8,14},{9,15},{10,... | collective-permute-start | bytes 786440 | tf_op jit(solution)/shard_map/ppermute | solution.py:442
  26.9 8.8 %collective-permute-start.9 = (bf16[512,256]{1,0:T(8,128)(2,1)S(1)}, bf16[512,256]{1,0:T(8,128)(2,1)S(1)}, u32[]{:S(2)}, u32[]{:S(2)}) collective-permute-start(bf16[512,256]{1,0:T(8,128)(2,1)S(1)} %get-tuple-element.47.refs_0_), channel_id=1, source_target_pairs={{0,2},{1,3},{2,0},{3,1},{4,6},{5,7},{6,4},{7,5},{8,10},{9,11},{10,... | collective-permute-start | bytes 786440 | tf_op jit(solution)/shard_map/ppermute | solution.py:442
  27.0 19.2 %collective-permute-start.2 = (bf16[3088,128]{1,0:T(8,128)(2,1)}, bf16[3088,128]{1,0:T(8,128)(2,1)S(1)}, u32[]{:S(2)}, u32[]{:S(2)}) collective-permute-start(bf16[3088,128]{1,0:T(8,128)(2,1)} %get-tuple-element.38.own), channel_id=1, source_target_pairs={{0,64},{64,0},{128,192},{192,128},{1,65},{65,1},{129,193},{193,129... | collective-permute-start | bytes 2371592 | tf_op jit(solution)/shard_map/ppermute | solution.py:438
  27.9 21.6 %collective-permute-start.3 = (bf16[3088,128]{1,0:T(8,128)(2,1)}, bf16[3088,128]{1,0:T(8,128)(2,1)S(1)}, u32[]{:S(2)}, u32[]{:S(2)}) collective-permute-start(bf16[3088,128]{1,0:T(8,128)(2,1)} %get-tuple-element.39), channel_id=1, source_target_pairs={{0,192},{64,128},{128,64},{192,0},{1,193},{65,129},{129,65},{193,1... | collective-permute-start | bytes 2371592 | tf_op jit(solution)/shard_map/ppermute | solution.py:438
  35.7 8.2 %collective-permute-start.11 = (bf16[512,256]{1,0:T(8,128)(2,1)S(1)}, bf16[512,256]{1,0:T(8,128)(2,1)S(1)}, u32[]{:S(2)}, u32[]{:S(2)}) collective-permute-start(bf16[512,256]{1,0:T(8,128)(2,1)S(1)} %get-tuple-element.47.refs_0_), channel_id=1, source_target_pairs={{0,4},{1,5},{2,6},{3,7},{4,0},{5,1},{6,2},{7,3},{8,12},{9,13},{10,... | collective-permute-start | bytes 786440 | tf_op jit(solution)/shard_map/ppermute | solution.py:442
  44.1 32.4 %collective-permute-start.15 = (bf16[4,512,256]{2,1,0:T(8,128)(2,1)S(1)}, bf16[4,512,256]{2,1,0:T(8,128)(2,1)S(1)}, u32[]{:S(2)}, u32[]{:S(2)}) collective-permute-start(bf16[4,512,256]{2,1,0:T(8,128)(2,1)S(1)} %joined.3.refs_4_), channel_id=1, source_target_pairs={{0,1},{1,0},{2,3},{3,2},{4,5},{5,4},{6,7},{7,6},{8,9},{9,8},{10,11... | collective-permute-start | bytes 3145736 | tf_op jit(solution)/shard_map/ppermute | solution.py:442
  46.2 18.3 %collective-permute-start.4 = (bf16[1536,128]{1,0:T(8,128)(2,1)S(1)}, bf16[1536,128]{1,0:T(8,128)(2,1)S(1)}, u32[]{:S(2)}, u32[]{:S(2)}) collective-permute-start(bf16[1536,128]{1,0:T(8,128)(2,1)S(1)} %slice.16), channel_id=1, source_target_pairs={{0,192},{64,128},{128,64},{192,0},{1,193},{65,129},{129,65},{193,1... | collective-permute-start | bytes 1179656 | tf_op jit(solution)/shard_map/ppermute | solution.py:438
  49.5 11.0 %collective-permute-start.20 = (bf16[512,256]{1,0:T(8,128)(2,1)S(1)}, bf16[512,256]{1,0:T(8,128)(2,1)S(1)}, u32[]{:S(2)}, u32[]{:S(2)}) collective-permute-start(bf16[512,256]{1,0:T(8,128)(2,1)S(1)} %get-tuple-element.64.refs_0_), channel_id=1, source_target_pairs={{0,56},{1,57},{2,58},{3,59},{4,60},{5,61},{6,62},{7,63},{8,16},{9,... | collective-permute-start | bytes 786440 | tf_op jit(solution)/shard_map/ppermute | solution.py:442
  53.5 8.5 %collective-permute-start.19 = (bf16[512,256]{1,0:T(8,128)(2,1)S(1)}, bf16[512,256]{1,0:T(8,128)(2,1)S(1)}, u32[]{:S(2)}, u32[]{:S(2)}) collective-permute-start(bf16[512,256]{1,0:T(8,128)(2,1)S(1)} %get-tuple-element.64.refs_0_), channel_id=1, source_target_pairs={{0,8},{1,9},{2,10},{3,11},{4,12},{5,13},{6,14},{7,15},{8,0},{9,1},... | collective-permute-start | bytes 786440 | tf_op jit(solution)/shard_map/ppermute | solution.py:442
  53.5 14.6 %collective-permute-start.5 = (bf16[1552,128]{1,0:T(8,128)(2,1)S(1)}, bf16[1552,128]{1,0:T(8,128)(2,1)S(1)}, u32[]{:S(2)}, u32[]{:S(2)}) collective-permute-start(bf16[1552,128]{1,0:T(8,128)(2,1)S(1)} %slice.17), channel_id=1, source_target_pairs={{0,64},{64,0},{128,192},{192,128},{1,65},{65,1},{129,193},{193,129... | collective-permute-start | bytes 1191944 | tf_op jit(solution)/shard_map/ppermute | solution.py:438
  62.0 14.2 %collective-permute-start.21 = (bf16[512,256]{1,0:T(8,128)(2,1)S(1)}, bf16[512,256]{1,0:T(8,128)(2,1)S(1)}, u32[]{:S(2)}, u32[]{:S(2)}) collective-permute-start(bf16[512,256]{1,0:T(8,128)(2,1)S(1)} %get-tuple-element.64.refs_0_), channel_id=1, source_target_pairs={{0,16},{1,17},{2,18},{3,19},{4,20},{5,21},{6,22},{7,23},{8,24},{9,... | collective-permute-start | bytes 786440 | tf_op jit(solution)/shard_map/ppermute | solution.py:442
  63.4 14.9 %collective-permute-start.13 = (bf16[512,256]{1,0:T(8,128)(2,1)S(1)}, bf16[512,256]{1,0:T(8,128)(2,1)S(1)}, u32[]{:S(2)}, u32[]{:S(2)}) collective-permute-start(bf16[512,256]{1,0:T(8,128)(2,1)S(1)} %get-tuple-element.56.refs_0_), channel_id=1, source_target_pairs={{0,6},{1,7},{2,4},{3,5},{4,2},{5,3},{6,0},{7,1},{8,14},{9,15},{10,... | collective-permute-start | bytes 786440 | tf_op jit(solution)/shard_map/ppermute | solution.py:442
  64.5 13.8 %collective-permute-start.12 = (bf16[512,256]{1,0:T(8,128)(2,1)S(1)}, bf16[512,256]{1,0:T(8,128)(2,1)S(1)}, u32[]{:S(2)}, u32[]{:S(2)}) collective-permute-start(bf16[512,256]{1,0:T(8,128)(2,1)S(1)} %get-tuple-element.56.refs_0_), channel_id=1, source_target_pairs={{0,2},{1,3},{2,0},{3,1},{4,6},{5,7},{6,4},{7,5},{8,10},{9,11},{10,... | collective-permute-start | bytes 786440 | tf_op jit(solution)/shard_map/ppermute | solution.py:442
  65.4 1.0 copy-start.12
  66.4 1.0 copy-start.14
  76.4 14.4 %collective-permute-start.22 = (bf16[4,512,256]{2,1,0:T(8,128)(2,1)S(1)}, bf16[4,512,256]{2,1,0:T(8,128)(2,1)S(1)}, u32[]{:S(2)}, u32[]{:S(2)}) collective-permute-start(bf16[4,512,256]{2,1,0:T(8,128)(2,1)S(1)} %joined.5.refs_4_), channel_id=1, source_target_pairs={{0,1},{1,0},{2,3},{3,2},{4,5},{5,4},{6,7},{7,6},{8,9},{9,8},{10,11... | collective-permute-start | bytes 3145736 | tf_op jit(solution)/shard_map/ppermute | solution.py:442
  76.7 4.9 %copy-start = (bf16[3088,128]{1,0:T(8,128)(2,1)S(1)}, bf16[3088,128]{1,0:T(8,128)(2,1)}, u32[]{:S(2)}) copy-start(bf16[3088,128]{1,0:T(8,128)(2,1)} %get-tuple-element.38.own) | copy-start | bytes 2371588
  77.2 5.6 %collective-permute-start.16 = (bf16[128,512]{1,0:T(8,128)(2,1)S(1)}, bf16[128,512]{1,0:T(8,128)(2,1)S(1)}, u32[]{:S(2)}, u32[]{:S(2)}) collective-permute-start(bf16[128,512]{1,0:T(8,128)(2,1)S(1)} %get-tuple-element.53), channel_id=1, source_target_pairs={{0,1},{1,0},{2,3},{3,2},{4,5},{5,4},{6,7},{7,6},{8,9},{9,8},{10,11... | collective-permute-start | bytes 393224 | tf_op jit(solution)/shard_map/ppermute | solution.py:442
  77.8 8.9 %collective-permute-start.17 = (bf16[128,512]{1,0:T(8,128)(2,1)S(1)}, bf16[128,512]{1,0:T(8,128)(2,1)S(1)}, u32[]{:S(2)}, u32[]{:S(2)}) collective-permute-start(bf16[128,512]{1,0:T(8,128)(2,1)S(1)} %get-tuple-element.54), channel_id=1, source_target_pairs={{0,63},{1,2},{2,1},{3,4},{4,3},{5,6},{6,5},{7,8},{8,7},{9,10},{10,... | collective-permute-start | bytes 393224 | tf_op jit(solution)/shard_map/ppermute | solution.py:442
  78.3 11.5 %collective-permute-start.14 = (bf16[512,256]{1,0:T(8,128)(2,1)S(1)}, bf16[512,256]{1,0:T(8,128)(2,1)S(1)}, u32[]{:S(2)}, u32[]{:S(2)}) collective-permute-start(bf16[512,256]{1,0:T(8,128)(2,1)S(1)} %get-tuple-element.56.refs_0_), channel_id=1, source_target_pairs={{0,4},{1,5},{2,6},{3,7},{4,0},{5,1},{6,2},{7,3},{8,12},{9,13},{10,... | collective-permute-start | bytes 786440 | tf_op jit(solution)/shard_map/ppermute | solution.py:442
  90.0 11.8 %collective-permute-start.18 = (bf16[4,512,256]{2,1,0:T(8,128)(2,1)S(1)}, bf16[4,512,256]{2,1,0:T(8,128)(2,1)S(1)}, u32[]{:S(2)}, u32[]{:S(2)}) collective-permute-start(bf16[4,512,256]{2,1,0:T(8,128)(2,1)S(1)} %joined.4.refs_4_), channel_id=1, source_target_pairs={{0,1},{1,0},{2,3},{3,2},{4,5},{5,4},{6,7},{7,6},{8,9},{9,8},{10,11... | collective-permute-start | bytes 3145736 | tf_op jit(solution)/shard_map/ppermute | solution.py:442
  91.4 3.2 %collective-permute-start.23 = (bf16[128,512]{1,0:T(8,128)(2,1)S(1)}, bf16[128,512]{1,0:T(8,128)(2,1)S(1)}, u32[]{:S(2)}, u32[]{:S(2)}) collective-permute-start(bf16[128,512]{1,0:T(8,128)(2,1)S(1)} %get-tuple-element.65), channel_id=1, source_target_pairs={{0,1},{1,0},{2,3},{3,2},{4,5},{5,4},{6,7},{7,6},{8,9},{9,8},{10,11... | collective-permute-start | bytes 393224 | tf_op jit(solution)/shard_map/ppermute | solution.py:442
  91.6 7.7 %collective-permute-start.24 = (bf16[128,512]{1,0:T(8,128)(2,1)S(1)}, bf16[128,512]{1,0:T(8,128)(2,1)S(1)}, u32[]{:S(2)}, u32[]{:S(2)}) collective-permute-start(bf16[128,512]{1,0:T(8,128)(2,1)S(1)} %get-tuple-element.66), channel_id=1, source_target_pairs={{0,63},{1,2},{2,1},{3,4},{4,3},{5,6},{6,5},{7,8},{8,7},{9,10},{10,... | collective-permute-start | bytes 393224 | tf_op jit(solution)/shard_map/ppermute | solution.py:442
  102.5 3.2 %collective-permute-start.25 = (bf16[128,512]{1,0:T(8,128)(2,1)S(1)}, bf16[128,512]{1,0:T(8,128)(2,1)S(1)}, u32[]{:S(2)}, u32[]{:S(2)}) collective-permute-start(bf16[128,512]{1,0:T(8,128)(2,1)S(1)} %get-tuple-element.68), channel_id=1, source_target_pairs={{0,1},{1,0},{2,3},{3,2},{4,5},{5,4},{6,7},{7,6},{8,9},{9,8},{10,11... | collective-permute-start | bytes 393224 | tf_op jit(solution)/shard_map/ppermute | solution.py:442
  102.6 7.8 %collective-permute-start.26 = (bf16[128,512]{1,0:T(8,128)(2,1)S(1)}, bf16[128,512]{1,0:T(8,128)(2,1)S(1)}, u32[]{:S(2)}, u32[]{:S(2)}) collective-permute-start(bf16[128,512]{1,0:T(8,128)(2,1)S(1)} %get-tuple-element.69), channel_id=1, source_target_pairs={{0,63},{1,2},{2,1},{3,4},{4,3},{5,6},{6,5},{7,8},{8,7},{9,10},{10,... | collective-permute-start | bytes 393224 | tf_op jit(solution)/shard_map/ppermute | solution.py:442

commit v4 on v3

--- a/solution.py
+++ b/solution.py
@@ -255,7 +255,7 @@
     )(*args)
 
 
-def copies(kernel_name, plan, shapes, *args):
+def copies(kernel_name, plan, shapes, *args, mib=4):
     def kernel(*refs):
         ins, outs, sem = refs[: len(args)], refs[len(args) : -1], refs[-1]
         moves = [
@@ -271,13 +271,25 @@
         out_shape=[jax.ShapeDtypeStruct(shape, BF) for shape in shapes],
         in_specs=[ANY] * len(args),
         out_specs=[ANY] * len(shapes),
-        scratch_shapes=[pltpu.SemaphoreType.DMA((12,))],
-        compiler_params=params(4),
+        scratch_shapes=[pltpu.SemaphoreType.DMA((4,))],
+        compiler_params=params(mib),
         cost_estimate=pl.CostEstimate(flops=0, bytes_accessed=2_000_000, transcendentals=0),
         name=kernel_name,
     )(*args)
 
 
+def edges(samples):
+    def plan(ins, outs):
+        core = place()[4]
+        last = 3 * BLK
+        return [
+            (ins[0].at[:, pl.ds(pl.multiple_of((1 - core) * last, BLK), BLK)], outs[0]),
+            (ins[0].at[:, pl.ds(pl.multiple_of(core * last, BLK), BLK)], outs[1]),
+        ]
+
+    return copies("edges", plan, [(4, BLK, D)] * 2, samples, mib=60)
+
+
 def joined(ring):
     def plan(ins, outs):
         return [(ins[r], outs[0].at[r]) for r in range(4)]
@@ -285,7 +297,7 @@
     return copies("joined", plan, [(4, D, HALF)], *ring)[0]
 
 
-STAGE_BY_Y = {1: True, 2: False, 3: True}
+STAGE_BY_Y = {1: True, 2: True, 3: False}
 
 
 def weights_kernel(section, *refs):
@@ -449,11 +461,10 @@
 def shards(samples, w_source, w_self, w_message, w_output, norm_gain, tile_source, tile_count, tile_value):
     p, dom, y, _, core = place()
     ws = [w_source, w_self, w_message, w_output]
-    edge = [samples[:, :BLK], samples[:, (BD - 1) * BLK :]]
-    edge = [jnp.where(core == 0, edge[1], edge[0]), jnp.where(core == 0, edge[0], edge[1])]
+    edge = edges(samples)
     inner, outer = exchange(*edge)
 
-    m = jnp.where(p == 2, (dom >> 3) & 3, y)
+    m = jnp.where(p == 3, (dom >> 3) & 3, y)
     a, b, c, d = (lax.dynamic_slice(w[0, 0], (0, core * HALF), (D, HALF)) for w in ws)
     piece = jnp.where(m < 2, jnp.where(m == 0, a, b), jnp.where(m == 2, c, d))
     piece = after(piece, edge)
@@ -466,10 +477,8 @@
     mixed_b, mixed_a = over_segments(far[ROWS:], 1), over_segments(near[:ROWS], 3)
     arrays = [own, near, far, mixed_a, mixed_b]
 
-    def ring(own, routes, *waits):
-        a, c = over_dom(own, routes[0]), over_dom(own, routes[2])
-        b = over_dom(after(own, a, c, waits), routes[1])
-        return [own, a, b, c]
+    def ring(own, routes):
+        return [own] + [over_dom(own, route) for route in routes]
 
     def both(pieces):
         return pieces, over_dom(pieces, OTHER_CORE)
@@ -479,18 +488,18 @@
     ring1 = ring(jnp.where(p == 2, x3, jnp.where(p == 3, x2, x1)), over_y)
     then = jnp.where(p == 0, x2, jnp.where(p == 1, x3, x1))
     last = jnp.where(p == 0, x3, jnp.where(p == 1, x2, x1))
-    then, last = after((then, last), near, far, ring1)
-    ring2, ring3 = ring(then, over_z), ring(last, over_y)
+    ring2 = ring(after(then, ring1), over_y)
     stages = {1: both(joined(ring1)), 2: both(joined(ring2))}
-    h = arrived_call(h0, near, far, mixed_a, mixed_b)
+    ring3 = ring(after(last, near, far, stages[2]), over_z)
+    h = arrived_call(h0, near, far, after(mixed_a, stages[2][0]), mixed_b)
     for section in range(1, SEG):
-        if section == 2:
-            stages[3] = both(joined(after(ring3, h)))
         w = weights_call(section, ws, stages[section])
         tiles, codes, gain = tiles_call(section, arrays)
         sender, inner, outer = sender_call(section, h, w)
         inner, outer = exchange(inner, outer)
         h = section_call(section, codes, gain, tiles, w, h, inner, outer, sender)
+        if section == 1:
+            stages[3] = both(joined(after(ring3, h)))
     return h[None]
 
 

time: 114 us -> 155 us (1.36)
  Pallas kernels: 18.8 us -> 51.6 us
  starting transfers between devices: 37.6 us -> 51.4 us
  local copies, waits for them, and re-layouts: 3.78 us -> 0.93 us
  other arithmetic: 2.61 us -> 0.21 us
    pallas_call x3 -> x4, Pallas kernels: 0.56 us -> 33.3 us  [copies(): pl.pallas_call(kernel, out_shape=[jax.ShapeDtypeStruct(shape, BF) for sha...]
    ppermute x20, waiting for transfers between devices: 44.2 us -> 27.2 us  [over_dom(): return lax.ppermute(value, 'dom', pairs)]
    ppermute x7, waiting for transfers between devices: 6.24 us -> 22.6 us  [over_segments(): return lax.ppermute(value, 'segment', by_segment(x))]
    ppermute x20, starting transfers between devices: 26 us -> 40 us  [over_dom(): return lax.ppermute(value, 'dom', pairs)]
    unnamed x36, local copies, waits for them, and re-layouts: 3.73 us -> 0.88 us
    select_n x1 -> x0, other arithmetic: 2.39 us -> none  [shards(): jnp.where(core == 0, edge[0], edge[1])]
  transfers between devices with their start and end apart: 27 -> 27, of which waited for: 13 -> 13; matrix products, arithmetic and copies ran while one was open for 0% -> 0% of each run, Pallas kernels for 13% -> 10%
where the time goes in v4:
time: 155 us; the launch traced here: 154 us
  Pallas kernels  51.6 us (33%)
  starting transfers between devices  51.4 us (33%)
  waiting for transfers between devices  49.8 us (32%)
    ppermute x20, starting transfers between devices, over_dom(): return lax.ppermute(value, 'dom', pairs)  40 us
    pallas_call x4, Pallas kernels, copies(): pl.pallas_call(kernel, out_shape=[jax.ShapeDtypeStruct(shape, BF) for sha...  33.3 us
    ppermute x20, waiting for transfers between devices, over_dom(): return lax.ppermute(value, 'dom', pairs)  27.2 us
    ppermute x7, waiting for transfers between devices, over_segments(): return lax.ppermute(value, 'segment', by_segment(x))  22.6 us
    ppermute x7, starting transfers between devices, over_segments(): return lax.ppermute(value, 'segment', by_segment(x))  11.4 us
    pallas_call x3, Pallas kernels, section_call(): pl.pallas_call(section_kernel, out_shape=jax.ShapeDtypeStruct((BD * BLK,...  8.04 us
    pallas_call x2, Pallas kernels, first_call(): pl.pallas_call(functools.partial(first_kernel, order), out_shape=[jax.Sha...  4.05 us
    pallas_call x3, Pallas kernels, tiles_call(): pl.pallas_call(functools.partial(tiles_kernel, section), out_shape=[jax.S...  3.78 us
  transfers between devices with their start and end apart: 27, of which 13 were waited for; matrix products, arithmetic and copies ran while one was open for 0% of the time, Pallas kernels for 10%

profile of v4, /device:TPU:6, one launch (start us, length us, event | category | flops | bytes accessed | tf_op | source)
XLA Modules:
  0.0 154.4 jit_solution(1239892682199173855)
XLA Ops:
  0.0 0.0 copy-start.1
  0.0 32.9 %edges.1 = (bf16[4,128,512]{2,1,0:T(8,128)(2,1)}, bf16[4,128,512]{2,1,0:T(8,128)(2,1)}) custom-call(bf16[4,512,512]{2,1,0:T(8,128)(2,1)} %samples.3), custom_call_target="tpu_custom_call" | custom-call | bytes 2000000 | tf_op jit(solution)/shard_map/edges/pallas_call | solution.py:269
  32.9 0.1 collective-permute-start
  33.0 8.4 %collective-permute-start.1 = (bf16[4,128,512]{2,1,0:T(8,128)(2,1)}, bf16[4,128,512]{2,1,0:T(8,128)(2,1)S(1)}, u32[]{:S(2)}, u32[]{:S(2)}) collective-permute-start(bf16[4,128,512]{2,1,0:T(8,128)(2,1)} %get-tuple-element.39), channel_id=1, source_target_pairs={{0,63},{1,2},{2,1},{3,4},{4,3},{5,6},{6,5},{7,8},{8,7},{9,10},{10,... | collective-permute-start | bytes 1572872 | tf_op jit(solution)/shard_map/ppermute | solution.py:454
  41.5 0.1 select_bitcast_fusion
  41.6 0.6 collective-permute-start.8
  42.2 2.4 %collective-permute-start.7 = (bf16[512,256]{1,0:T(8,128)(2,1)S(1)}, bf16[512,256]{1,0:T(8,128)(2,1)S(1)}, u32[]{:S(2)}, u32[]{:S(2)}) collective-permute-start(bf16[512,256]{1,0:T(8,128)(2,1)S(1)} %select_bitcast_fusion), channel_id=1, source_target_pairs={{0,128},{64,192},{128,0},{192,64},{1,129},{65,193},{129,1},{193,65... | collective-permute-start | bytes 786440 | tf_op jit(solution)/shard_map/ppermute | solution.py:450
  44.6 1.2 collective-permute-start.6
  45.8 2.7 %collective-permute-done.1.outer = bf16[4,128,512]{2,1,0:T(8,128)(2,1)S(1)} collective-permute-done((bf16[4,128,512]{2,1,0:T(8,128)(2,1)}, bf16[4,128,512]{2,1,0:T(8,128)(2,1)S(1)}, u32[]{:S(2)}, u32[]{:S(2)}) %collective-permute-start.1) | collective-permute-done | bytes 524320 | tf_op jit(solution)/shard_map/ppermute | solution.py:454
  48.5 0.8 copy-done.13
  49.3 3.4 %first3.1 = (bf16[3088,128]{1,0:T(8,128)(2,1)}, bf16[3088,128]{1,0:T(8,128)(2,1)}) custom-call(s32[1,4,6]{2,1,0:T(4,128)} %src.3, s32[1,4]{1,0:T(1,128)} %cnt.3, f32[1,1,512]{2,1,0:T(1,128)} %gain.3, bf16[4,128,512]{2,1,0:T(8,128)(2,1)} %copy-done.11, bf16[4,128,512]{2,1,0:T(8,128)(2,1)} %copy-done.13, bf16[4,512,512]{2,1,0:T(8,128)(2,1)} %samples.3, ...), custom_call_target="tpu_custom_call" | custom-call | flops 6000000000 | bytes 4000000 | tf_op jit(solution)/shard_map/first3/pallas_call | solution.py:197
  52.7 0.2 collective-permute-done.6
  53.0 0.1 select_select_fusion
  53.0 0.9 collective-permute-start.11
  53.9 0.6 collective-permute-start.10
  54.5 2.7 %collective-permute-start.9 = (bf16[512,256]{1,0:T(8,128)(2,1)S(1)}, bf16[512,256]{1,0:T(8,128)(2,1)S(1)}, u32[]{:S(2)}, u32[]{:S(2)}) collective-permute-start(bf16[512,256]{1,0:T(8,128)(2,1)S(1)} %get-tuple-element.71.refs_0_), channel_id=1, source_target_pairs={{0,2},{1,3},{2,0},{3,1},{4,6},{5,7},{6,4},{7,5},{8,10},{9,11},{10,... | collective-permute-start | bytes 786440 | tf_op jit(solution)/shard_map/ppermute | solution.py:454
  57.2 8.7 %collective-permute-done.11.refs_3_ = bf16[512,256]{1,0:T(8,128)(2,1)S(1)} collective-permute-done((bf16[512,256]{1,0:T(8,128)(2,1)S(1)}, bf16[512,256]{1,0:T(8,128)(2,1)S(1)}, u32[]{:S(2)}, u32[]{:S(2)}) %collective-permute-start.11) | collective-permute-done | bytes 262176 | tf_op jit(solution)/shard_map/ppermute | solution.py:454
  66.0 0.6 collective-permute-done.9.refs_1_
  66.5 2.9 %collective-permute-start.14 = (bf16[512,256]{1,0:T(8,128)(2,1)S(1)}, bf16[512,256]{1,0:T(8,128)(2,1)S(1)}, u32[]{:S(2)}, u32[]{:S(2)}) collective-permute-start(bf16[512,256]{1,0:T(8,128)(2,1)S(1)} %get-tuple-element.49.refs_0_), channel_id=1, source_target_pairs={{0,6},{1,7},{2,4},{3,5},{4,2},{5,3},{6,0},{7,1},{8,14},{9,15},{10,... | collective-permute-start | bytes 786440 | tf_op jit(solution)/shard_map/ppermute | solution.py:454
  69.4 0.9 collective-permute-start.13
  70.3 0.3 collective-permute-start.12
  70.6 6.6 %collective-permute-start.3 = (bf16[3088,128]{1,0:T(8,128)(2,1)}, bf16[3088,128]{1,0:T(8,128)(2,1)S(1)}, u32[]{:S(2)}, u32[]{:S(2)}) collective-permute-start(bf16[3088,128]{1,0:T(8,128)(2,1)} %get-tuple-element.41), channel_id=1, source_target_pairs={{0,192},{64,128},{128,64},{192,0},{1,193},{65,129},{129,65},{193,1... | collective-permute-start | bytes 2371592 | tf_op jit(solution)/shard_map/ppermute | solution.py:450
  77.3 0.1 joined.4.refs_4_
  77.4 0.0 copy-start.4
  77.4 0.0 copy-start.6
  77.4 0.0 copy-start.12
  77.4 0.0 copy-start.15
  77.5 3.0 %collective-permute-done.14.refs_3_ = bf16[512,256]{1,0:T(8,128)(2,1)S(1)} collective-permute-done((bf16[512,256]{1,0:T(8,128)(2,1)S(1)}, bf16[512,256]{1,0:T(8,128)(2,1)S(1)}, u32[]{:S(2)}, u32[]{:S(2)}) %collective-permute-start.14) | collective-permute-done | bytes 262176 | tf_op jit(solution)/shard_map/ppermute | solution.py:454
  80.4 0.7 collective-permute-done.12.refs_1_
  81.2 0.1 joined.3.refs_4_
  81.3 0.1 collective-permute-start.15
  81.4 11.9 %collective-permute-done.3.far = bf16[3088,128]{1,0:T(8,128)(2,1)S(1)} collective-permute-done((bf16[3088,128]{1,0:T(8,128)(2,1)}, bf16[3088,128]{1,0:T(8,128)(2,1)S(1)}, u32[]{:S(2)}, u32[]{:S(2)}) %collective-permute-start.3) | collective-permute-done | bytes 790560 | tf_op jit(solution)/shard_map/ppermute | solution.py:450
  93.3 0.1 collective-permute-start.5
  93.4 2.6 %collective-permute-done.2.near = bf16[3088,128]{1,0:T(8,128)(2,1)S(1)} collective-permute-done((bf16[3088,128]{1,0:T(8,128)(2,1)}, bf16[3088,128]{1,0:T(8,128)(2,1)S(1)}, u32[]{:S(2)}, u32[]{:S(2)}) %collective-permute-start.2) | collective-permute-done | bytes 790560 | tf_op jit(solution)/shard_map/ppermute | solution.py:450
  96.1 0.5 collective-permute-start.4
  96.6 0.7 first1.1.h0
  97.3 7.9 %collective-permute-done.4.mixed_a = bf16[1536,128]{1,0:T(8,128)(2,1)S(1)} collective-permute-done((bf16[1536,128]{1,0:T(8,128)(2,1)S(1)}, bf16[1536,128]{1,0:T(8,128)(2,1)S(1)}, u32[]{:S(2)}, u32[]{:S(2)}) %collective-permute-start.4) | collective-permute-done | bytes 393248 | tf_op jit(solution)/shard_map/ppermute | solution.py:450
  105.1 0.1 arrived.1.h
  105.3 0.2 weights1.1.w
  105.5 0.5 sender1.1
  106.0 0.1 collective-permute-start.20
  106.1 8.8 %collective-permute-start.21 = (bf16[128,512]{1,0:T(8,128)(2,1)S(1)}, bf16[128,512]{1,0:T(8,128)(2,1)S(1)}, u32[]{:S(2)}, u32[]{:S(2)}) collective-permute-start(bf16[128,512]{1,0:T(8,128)(2,1)S(1)} %get-tuple-element.56), channel_id=1, source_target_pairs={{0,63},{1,2},{2,1},{3,4},{4,3},{5,6},{6,5},{7,8},{8,7},{9,10},{10,... | collective-permute-start | bytes 393224 | tf_op jit(solution)/shard_map/ppermute | solution.py:454
  114.9 0.9 collective-permute-start.18
  115.8 1.6 %collective-permute-start.16 = (bf16[512,256]{1,0:T(8,128)(2,1)S(1)}, bf16[512,256]{1,0:T(8,128)(2,1)S(1)}, u32[]{:S(2)}, u32[]{:S(2)}) collective-permute-start(bf16[512,256]{1,0:T(8,128)(2,1)S(1)} %get-tuple-element.58.refs_0_), channel_id=1, source_target_pairs={{0,8},{1,9},{2,10},{3,11},{4,12},{5,13},{6,14},{7,15},{8,0},{9,1},... | collective-permute-start | bytes 786440 | tf_op jit(solution)/shard_map/ppermute | solution.py:454
  117.4 1.3 tiles1.1
  118.7 2.4 %section1.1.h = bf16[512,512]{1,0:T(8,128)(2,1)S(1)} custom-call(s32[8,128]{1,0:T(8,128)S(1)} %get-tuple-element.51.codes, f32[1,512]{1,0:T(1,128)S(1)} %get-tuple-element.52.gain, bf16[24,128,128]{2,1,0:T(8,128)(2,1)S(1)} %get-tuple-element.53.tiles, bf16[4,512,512]{2,1,0:T(8,128)(2,1)S(1)} %weights1.1.w, bf16[512,512]{1,0:T(8,128)(2,1)S(1)} %arrived.1.h, ...), custom_call_target="tpu_custom_call" | custom-call | flops 1500000000 | bytes 4000000 | tf_op jit(solution)/shard_map/section1/pallas_call | solution.py:401
  121.1 1.3 collective-permute-done.18.refs_3_
  122.5 7.3 %collective-permute-done.17.refs_2_ = bf16[512,256]{1,0:T(8,128)(2,1)S(1)} collective-permute-done((bf16[512,256]{1,0:T(8,128)(2,1)S(1)}, bf16[512,256]{1,0:T(8,128)(2,1)S(1)}, u32[]{:S(2)}, u32[]{:S(2)}) %collective-permute-start.17) | collective-permute-done | bytes 262176 | tf_op jit(solution)/shard_map/ppermute | solution.py:454
  129.8 0.1 joined.5.refs_4_
  130.0 0.1 collective-permute-start.22
  130.1 0.4 weights2.1.w
  130.5 0.5 sender2.1
  131.0 0.3 collective-permute-start.23
  131.4 6.1 %collective-permute-start.24 = (bf16[128,512]{1,0:T(8,128)(2,1)S(1)}, bf16[128,512]{1,0:T(8,128)(2,1)S(1)}, u32[]{:S(2)}, u32[]{:S(2)}) collective-permute-start(bf16[128,512]{1,0:T(8,128)(2,1)S(1)} %get-tuple-element.66), channel_id=1, source_target_pairs={{0,63},{1,2},{2,1},{3,4},{4,3},{5,6},{6,5},{7,8},{8,7},{9,10},{10,... | collective-permute-start | bytes 393224 | tf_op jit(solution)/shard_map/ppermute | solution.py:454
  137.4 1.3 tiles2.1
  138.7 1.4 collective-permute-done.24.outer
  140.1 2.4 %section2.1.h = bf16[512,512]{1,0:T(8,128)(2,1)S(1)} custom-call(s32[8,128]{1,0:T(8,128)S(1)} %get-tuple-element.62.codes, f32[1,512]{1,0:T(1,128)S(1)} %get-tuple-element.63.gain, bf16[24,128,128]{2,1,0:T(8,128)(2,1)S(1)} %get-tuple-element.64.tiles, bf16[4,512,512]{2,1,0:T(8,128)(2,1)S(1)} %weights2.1.w, bf16[512,512]{1,0:T(8,128)(2,1)S(1)} %section1.1.h, ...), custom_call_target="tpu_custom_call" | custom-call | flops 1500000000 | bytes 4000000 | tf_op jit(solution)/shard_map/section2/pallas_call | solution.py:401
  142.5 0.2 weights3.1.w
  142.7 0.5 sender3.1
  143.2 0.1 collective-permute-start.25
  143.3 5.1 %collective-permute-start.26 = (bf16[128,512]{1,0:T(8,128)(2,1)S(1)}, bf16[128,512]{1,0:T(8,128)(2,1)S(1)}, u32[]{:S(2)}, u32[]{:S(2)}) collective-permute-start(bf16[128,512]{1,0:T(8,128)(2,1)S(1)} %get-tuple-element.69), channel_id=1, source_target_pairs={{0,63},{1,2},{2,1},{3,4},{4,3},{5,6},{6,5},{7,8},{8,7},{9,10},{10,... | collective-permute-start | bytes 393224 | tf_op jit(solution)/shard_map/ppermute | solution.py:454
  148.5 1.3 tiles3.1
  149.8 1.4 collective-permute-done.26.outer
  151.1 3.2 %section3.1 = bf16[512,512]{1,0:T(8,128)(2,1)} custom-call(s32[8,128]{1,0:T(8,128)S(1)} %get-tuple-element.42.codes, f32[1,512]{1,0:T(1,128)S(1)} %get-tuple-element.43.gain, bf16[24,128,128]{2,1,0:T(8,128)(2,1)S(1)} %get-tuple-element.44.tiles, bf16[4,512,512]{2,1,0:T(8,128)(2,1)S(1)} %weights3.1.w, bf16[512,512]{1,0:T(8,128)(2,1)S(1)} %section2.1.h, ...), custom_call_target="tpu_custom_call" | custom-call | flops 1500000000 | bytes 4000000 | tf_op jit(solution)/shard_map/section3/pallas_call | solution.py:401
  (49 shorter events, 0.2 us)
Async XLA Ops:
  0.0 41.5 %copy-start.7 = (bf16[1,1,512,512]{3,2,1,0:T(8,128)(2,1)S(1)}, bf16[1,1,512,512]{3,2,1,0:T(8,128)(2,1)}, u32[]{:S(2)}) copy-start(bf16[1,1,512,512]{3,2,1,0:T(8,128)(2,1)} %refs_3_.5) | copy-start | bytes 1572868
  0.0 41.5 %copy-start.5 = (bf16[1,1,512,512]{3,2,1,0:T(8,128)(2,1)S(1)}, bf16[1,1,512,512]{3,2,1,0:T(8,128)(2,1)}, u32[]{:S(2)}) copy-start(bf16[1,1,512,512]{3,2,1,0:T(8,128)(2,1)} %refs_2_.5) | copy-start | bytes 1572868
  0.0 41.5 %copy-start.3 = (bf16[1,1,512,512]{3,2,1,0:T(8,128)(2,1)S(1)}, bf16[1,1,512,512]{3,2,1,0:T(8,128)(2,1)}, u32[]{:S(2)}) copy-start(bf16[1,1,512,512]{3,2,1,0:T(8,128)(2,1)} %refs_1_.5) | copy-start | bytes 1572868
  0.0 41.4 %copy-start.1 = (bf16[1,1,512,512]{3,2,1,0:T(8,128)(2,1)S(1)}, bf16[1,1,512,512]{3,2,1,0:T(8,128)(2,1)}, u32[]{:S(2)}) copy-start(bf16[1,1,512,512]{3,2,1,0:T(8,128)(2,1)} %refs_0_.7) | copy-start | bytes 1572868
  32.9 12.9 %collective-permute-start = (bf16[4,128,512]{2,1,0:T(8,128)(2,1)}, bf16[4,128,512]{2,1,0:T(8,128)(2,1)S(1)}, u32[]{:S(2)}, u32[]{:S(2)}) collective-permute-start(bf16[4,128,512]{2,1,0:T(8,128)(2,1)} %get-tuple-element.38), channel_id=1, source_target_pairs={{0,1},{1,0},{2,3},{3,2},{4,5},{5,4},{6,7},{7,6},{8,9},{9,8},{10,11... | collective-permute-start | bytes 1572872 | tf_op jit(solution)/shard_map/ppermute | solution.py:454
  33.0 15.5 %collective-permute-start.1 = (bf16[4,128,512]{2,1,0:T(8,128)(2,1)}, bf16[4,128,512]{2,1,0:T(8,128)(2,1)S(1)}, u32[]{:S(2)}, u32[]{:S(2)}) collective-permute-start(bf16[4,128,512]{2,1,0:T(8,128)(2,1)} %get-tuple-element.39), channel_id=1, source_target_pairs={{0,63},{1,2},{2,1},{3,4},{4,3},{5,6},{6,5},{7,8},{8,7},{9,10},{10,... | collective-permute-start | bytes 1572872 | tf_op jit(solution)/shard_map/ppermute | solution.py:454
  41.6 11.1 %collective-permute-start.8 = (bf16[512,256]{1,0:T(8,128)(2,1)S(1)}, bf16[512,256]{1,0:T(8,128)(2,1)S(1)}, u32[]{:S(2)}, u32[]{:S(2)}) collective-permute-start(bf16[512,256]{1,0:T(8,128)(2,1)S(1)} %select_bitcast_fusion), channel_id=1, source_target_pairs={{0,192},{64,128},{128,64},{192,0},{1,193},{65,129},{129,65},{193,1... | collective-permute-start | bytes 786440 | tf_op jit(solution)/shard_map/ppermute | solution.py:450
  42.2 10.5 %collective-permute-start.7 = (bf16[512,256]{1,0:T(8,128)(2,1)S(1)}, bf16[512,256]{1,0:T(8,128)(2,1)S(1)}, u32[]{:S(2)}, u32[]{:S(2)}) collective-permute-start(bf16[512,256]{1,0:T(8,128)(2,1)S(1)} %select_bitcast_fusion), channel_id=1, source_target_pairs={{0,128},{64,192},{128,0},{192,64},{1,129},{65,193},{129,1},{193,65... | collective-permute-start | bytes 786440 | tf_op jit(solution)/shard_map/ppermute | solution.py:450
  44.6 8.4 %collective-permute-start.6 = (bf16[512,256]{1,0:T(8,128)(2,1)S(1)}, bf16[512,256]{1,0:T(8,128)(2,1)S(1)}, u32[]{:S(2)}, u32[]{:S(2)}) collective-permute-start(bf16[512,256]{1,0:T(8,128)(2,1)S(1)} %select_bitcast_fusion), channel_id=1, source_target_pairs={{0,64},{64,0},{128,192},{192,128},{1,65},{65,1},{129,193},{193,129... | collective-permute-start | bytes 786440 | tf_op jit(solution)/shard_map/ppermute | solution.py:450
  45.8 2.7 %copy-start.11 = (bf16[4,128,512]{2,1,0:T(8,128)(2,1)}, bf16[4,128,512]{2,1,0:T(8,128)(2,1)S(1)}, u32[]{:S(2)}) copy-start(bf16[4,128,512]{2,1,0:T(8,128)(2,1)S(1)} %collective-permute-done.inner) | copy-start | bytes 1572868
  48.5 0.8 copy-start.13
  53.0 43.6 %copy-start.14 = (bf16[4,128,512]{2,1,0:T(8,128)(2,1)S(1)}, bf16[4,128,512]{2,1,0:T(8,128)(2,1)}, u32[]{:S(2)}) copy-start(bf16[4,128,512]{2,1,0:T(8,128)(2,1)} %copy-done.13) | copy-start | bytes 1572868
  53.0 12.9 %collective-permute-start.11 = (bf16[512,256]{1,0:T(8,128)(2,1)S(1)}, bf16[512,256]{1,0:T(8,128)(2,1)S(1)}, u32[]{:S(2)}, u32[]{:S(2)}) collective-permute-start(bf16[512,256]{1,0:T(8,128)(2,1)S(1)} %get-tuple-element.71.refs_0_), channel_id=1, source_target_pairs={{0,6},{1,7},{2,4},{3,5},{4,2},{5,3},{6,0},{7,1},{8,14},{9,15},{10,... | collective-permute-start | bytes 786440 | tf_op jit(solution)/shard_map/ppermute | solution.py:454
  53.9 12.0 %collective-permute-start.10 = (bf16[512,256]{1,0:T(8,128)(2,1)S(1)}, bf16[512,256]{1,0:T(8,128)(2,1)S(1)}, u32[]{:S(2)}, u32[]{:S(2)}) collective-permute-start(bf16[512,256]{1,0:T(8,128)(2,1)S(1)} %get-tuple-element.71.refs_0_), channel_id=1, source_target_pairs={{0,4},{1,5},{2,6},{3,7},{4,0},{5,1},{6,2},{7,3},{8,12},{9,13},{10,... | collective-permute-start | bytes 786440 | tf_op jit(solution)/shard_map/ppermute | solution.py:454
  54.5 12.0 %collective-permute-start.9 = (bf16[512,256]{1,0:T(8,128)(2,1)S(1)}, bf16[512,256]{1,0:T(8,128)(2,1)S(1)}, u32[]{:S(2)}, u32[]{:S(2)}) collective-permute-start(bf16[512,256]{1,0:T(8,128)(2,1)S(1)} %get-tuple-element.71.refs_0_), channel_id=1, source_target_pairs={{0,2},{1,3},{2,0},{3,1},{4,6},{5,7},{6,4},{7,5},{8,10},{9,11},{10,... | collective-permute-start | bytes 786440 | tf_op jit(solution)/shard_map/ppermute | solution.py:454
  66.5 13.9 %collective-permute-start.14 = (bf16[512,256]{1,0:T(8,128)(2,1)S(1)}, bf16[512,256]{1,0:T(8,128)(2,1)S(1)}, u32[]{:S(2)}, u32[]{:S(2)}) collective-permute-start(bf16[512,256]{1,0:T(8,128)(2,1)S(1)} %get-tuple-element.49.refs_0_), channel_id=1, source_target_pairs={{0,6},{1,7},{2,4},{3,5},{4,2},{5,3},{6,0},{7,1},{8,14},{9,15},{10,... | collective-permute-start | bytes 786440 | tf_op jit(solution)/shard_map/ppermute | solution.py:454
  69.4 11.1 %collective-permute-start.13 = (bf16[512,256]{1,0:T(8,128)(2,1)S(1)}, bf16[512,256]{1,0:T(8,128)(2,1)S(1)}, u32[]{:S(2)}, u32[]{:S(2)}) collective-permute-start(bf16[512,256]{1,0:T(8,128)(2,1)S(1)} %get-tuple-element.49.refs_0_), channel_id=1, source_target_pairs={{0,4},{1,5},{2,6},{3,7},{4,0},{5,1},{6,2},{7,3},{8,12},{9,13},{10,... | collective-permute-start | bytes 786440 | tf_op jit(solution)/shard_map/ppermute | solution.py:454
  70.3 10.9 %collective-permute-start.12 = (bf16[512,256]{1,0:T(8,128)(2,1)S(1)}, bf16[512,256]{1,0:T(8,128)(2,1)S(1)}, u32[]{:S(2)}, u32[]{:S(2)}) collective-permute-start(bf16[512,256]{1,0:T(8,128)(2,1)S(1)} %get-tuple-element.49.refs_0_), channel_id=1, source_target_pairs={{0,2},{1,3},{2,0},{3,1},{4,6},{5,7},{6,4},{7,5},{8,10},{9,11},{10,... | collective-permute-start | bytes 786440 | tf_op jit(solution)/shard_map/ppermute | solution.py:454
  70.6 22.7 %collective-permute-start.3 = (bf16[3088,128]{1,0:T(8,128)(2,1)}, bf16[3088,128]{1,0:T(8,128)(2,1)S(1)}, u32[]{:S(2)}, u32[]{:S(2)}) collective-permute-start(bf16[3088,128]{1,0:T(8,128)(2,1)} %get-tuple-element.41), channel_id=1, source_target_pairs={{0,192},{64,128},{128,64},{192,0},{1,193},{65,129},{129,65},{193,1... | collective-permute-start | bytes 2371592 | tf_op jit(solution)/shard_map/ppermute | solution.py:450
  77.2 18.8 %collective-permute-start.2 = (bf16[3088,128]{1,0:T(8,128)(2,1)}, bf16[3088,128]{1,0:T(8,128)(2,1)S(1)}, u32[]{:S(2)}, u32[]{:S(2)}) collective-permute-start(bf16[3088,128]{1,0:T(8,128)(2,1)} %get-tuple-element.40.own), channel_id=1, source_target_pairs={{0,64},{64,0},{128,192},{192,128},{1,65},{65,1},{129,193},{193,129... | collective-permute-start | bytes 2371592 | tf_op jit(solution)/shard_map/ppermute | solution.py:450
  77.3 19.3 %copy-start.9 = (bf16[4,512,512]{2,1,0:T(8,128)(2,1)S(1)}, bf16[4,512,512]{2,1,0:T(8,128)(2,1)}, u32[]{:S(2)}) copy-start(bf16[4,512,512]{2,1,0:T(8,128)(2,1)} %samples.3) | copy-start | bytes 6291460
  77.4 19.2 %copy-start.2 = (bf16[1,1,512,512]{3,2,1,0:T(8,128)(2,1)S(1)}, bf16[1,1,512,512]{3,2,1,0:T(8,128)(2,1)}, u32[]{:S(2)}) copy-start(bf16[1,1,512,512]{3,2,1,0:T(8,128)(2,1)} %refs_0_.7) | copy-start | bytes 1572868
  77.4 19.1 %copy-start.4 = (bf16[1,1,512,512]{3,2,1,0:T(8,128)(2,1)S(1)}, bf16[1,1,512,512]{3,2,1,0:T(8,128)(2,1)}, u32[]{:S(2)}) copy-start(bf16[1,1,512,512]{3,2,1,0:T(8,128)(2,1)} %refs_1_.5) | copy-start | bytes 1572868
  77.4 19.1 %copy-start.6 = (bf16[1,1,512,512]{3,2,1,0:T(8,128)(2,1)S(1)}, bf16[1,1,512,512]{3,2,1,0:T(8,128)(2,1)}, u32[]{:S(2)}) copy-start(bf16[1,1,512,512]{3,2,1,0:T(8,128)(2,1)} %refs_2_.5) | copy-start | bytes 1572868
  77.4 19.1 %copy-start.8 = (bf16[1,1,512,512]{3,2,1,0:T(8,128)(2,1)S(1)}, bf16[1,1,512,512]{3,2,1,0:T(8,128)(2,1)}, u32[]{:S(2)}) copy-start(bf16[1,1,512,512]{3,2,1,0:T(8,128)(2,1)} %refs_3_.5) | copy-start | bytes 1572868
  77.4 19.1 %copy-start.10 = (bf16[1,4,6,128,128]{4,3,2,1,0:T(8,128)(2,1)S(1)}, bf16[1,4,6,128,128]{4,3,2,1,0:T(8,128)(2,1)}, u32[]{:S(2)}) copy-start(bf16[1,4,6,128,128]{4,3,2,1,0:T(8,128)(2,1)} %tiles.3) | copy-start | bytes 2359300
  77.4 19.1 %copy-start.12 = (bf16[4,128,512]{2,1,0:T(8,128)(2,1)S(1)}, bf16[4,128,512]{2,1,0:T(8,128)(2,1)}, u32[]{:S(2)}) copy-start(bf16[4,128,512]{2,1,0:T(8,128)(2,1)} %copy-done.11) | copy-start | bytes 1572868
  77.4 19.1 %copy-start.15 = (s32[1,4,6]{2,1,0:T(4,128)S(1)}, s32[1,4,6]{2,1,0:T(4,128)}, u32[]{:S(2)}) copy-start(s32[1,4,6]{2,1,0:T(4,128)} %src.3) | copy-start | bytes 292
  77.5 19.1 %copy-start.16 = (f32[1,1,512]{2,1,0:T(1,128)S(1)}, f32[1,1,512]{2,1,0:T(1,128)}, u32[]{:S(2)}) copy-start(f32[1,1,512]{2,1,0:T(1,128)} %gain.3) | copy-start | bytes 6148
  77.5 19.1 %copy-start.17 = (s32[1,4]{1,0:T(1,128)S(1)}, s32[1,4]{1,0:T(1,128)}, u32[]{:S(2)}) copy-start(s32[1,4]{1,0:T(1,128)} %cnt.3) | copy-start | bytes 52
  80.4 24.8 %collective-permute-start.19 = (bf16[4,512,256]{2,1,0:T(8,128)(2,1)S(1)}, bf16[4,512,256]{2,1,0:T(8,128)(2,1)S(1)}, u32[]{:S(2)}, u32[]{:S(2)}) collective-permute-start(bf16[4,512,256]{2,1,0:T(8,128)(2,1)S(1)} %joined.4.refs_4_), channel_id=1, source_target_pairs={{0,1},{1,0},{2,3},{3,2},{4,5},{5,4},{6,7},{7,6},{8,9},{9,8},{10,11... | collective-permute-start | bytes 3145736 | tf_op jit(solution)/shard_map/ppermute | solution.py:454
  81.3 33.6 %collective-permute-start.15 = (bf16[4,512,256]{2,1,0:T(8,128)(2,1)S(1)}, bf16[4,512,256]{2,1,0:T(8,128)(2,1)S(1)}, u32[]{:S(2)}, u32[]{:S(2)}) collective-permute-start(bf16[4,512,256]{2,1,0:T(8,128)(2,1)S(1)} %joined.3.refs_4_), channel_id=1, source_target_pairs={{0,1},{1,0},{2,3},{3,2},{4,5},{5,4},{6,7},{7,6},{8,9},{9,8},{10,11... | collective-permute-start | bytes 3145736 | tf_op jit(solution)/shard_map/ppermute | solution.py:454
  93.3 11.8 %collective-permute-start.5 = (bf16[1552,128]{1,0:T(8,128)(2,1)S(1)}, bf16[1552,128]{1,0:T(8,128)(2,1)S(1)}, u32[]{:S(2)}, u32[]{:S(2)}) collective-permute-start(bf16[1552,128]{1,0:T(8,128)(2,1)S(1)} %slice.9), channel_id=1, source_target_pairs={{0,64},{64,0},{128,192},{192,128},{1,65},{65,1},{129,193},{193,129... | collective-permute-start | bytes 1191944 | tf_op jit(solution)/shard_map/ppermute | solution.py:450
  96.1 9.1 %collective-permute-start.4 = (bf16[1536,128]{1,0:T(8,128)(2,1)S(1)}, bf16[1536,128]{1,0:T(8,128)(2,1)S(1)}, u32[]{:S(2)}, u32[]{:S(2)}) collective-permute-start(bf16[1536,128]{1,0:T(8,128)(2,1)S(1)} %slice.8), channel_id=1, source_target_pairs={{0,192},{64,128},{128,64},{192,0},{1,193},{65,129},{129,65},{193,1... | collective-permute-start | bytes 1179656 | tf_op jit(solution)/shard_map/ppermute | solution.py:450
  105.5 11.9 %copy-start = (bf16[3088,128]{1,0:T(8,128)(2,1)S(1)}, bf16[3088,128]{1,0:T(8,128)(2,1)}, u32[]{:S(2)}) copy-start(bf16[3088,128]{1,0:T(8,128)(2,1)} %get-tuple-element.40.own) | copy-start | bytes 2371588
  106.0 12.7 %collective-permute-start.20 = (bf16[128,512]{1,0:T(8,128)(2,1)S(1)}, bf16[128,512]{1,0:T(8,128)(2,1)S(1)}, u32[]{:S(2)}, u32[]{:S(2)}) collective-permute-start(bf16[128,512]{1,0:T(8,128)(2,1)S(1)} %get-tuple-element.55), channel_id=1, source_target_pairs={{0,1},{1,0},{2,3},{3,2},{4,5},{5,4},{6,7},{7,6},{8,9},{9,8},{10,11... | collective-permute-start | bytes 393224 | tf_op jit(solution)/shard_map/ppermute | solution.py:454
  106.1 12.6 %collective-permute-start.21 = (bf16[128,512]{1,0:T(8,128)(2,1)S(1)}, bf16[128,512]{1,0:T(8,128)(2,1)S(1)}, u32[]{:S(2)}, u32[]{:S(2)}) collective-permute-start(bf16[128,512]{1,0:T(8,128)(2,1)S(1)} %get-tuple-element.56), channel_id=1, source_target_pairs={{0,63},{1,2},{2,1},{3,4},{4,3},{5,6},{6,5},{7,8},{8,7},{9,10},{10,... | collective-permute-start | bytes 393224 | tf_op jit(solution)/shard_map/ppermute | solution.py:454
  114.9 7.6 %collective-permute-start.18 = (bf16[512,256]{1,0:T(8,128)(2,1)S(1)}, bf16[512,256]{1,0:T(8,128)(2,1)S(1)}, u32[]{:S(2)}, u32[]{:S(2)}) collective-permute-start(bf16[512,256]{1,0:T(8,128)(2,1)S(1)} %get-tuple-element.58.refs_0_), channel_id=1, source_target_pairs={{0,56},{1,57},{2,58},{3,59},{4,60},{5,61},{6,62},{7,63},{8,16},{9,... | collective-permute-start | bytes 786440 | tf_op jit(solution)/shard_map/ppermute | solution.py:454
  115.8 14.0 %collective-permute-start.17 = (bf16[512,256]{1,0:T(8,128)(2,1)S(1)}, bf16[512,256]{1,0:T(8,128)(2,1)S(1)}, u32[]{:S(2)}, u32[]{:S(2)}) collective-permute-start(bf16[512,256]{1,0:T(8,128)(2,1)S(1)} %get-tuple-element.58.refs_0_), channel_id=1, source_target_pairs={{0,16},{1,17},{2,18},{3,19},{4,20},{5,21},{6,22},{7,23},{8,24},{9,... | collective-permute-start | bytes 786440 | tf_op jit(solution)/shard_map/ppermute | solution.py:454
  115.8 14.0 %collective-permute-start.16 = (bf16[512,256]{1,0:T(8,128)(2,1)S(1)}, bf16[512,256]{1,0:T(8,128)(2,1)S(1)}, u32[]{:S(2)}, u32[]{:S(2)}) collective-permute-start(bf16[512,256]{1,0:T(8,128)(2,1)S(1)} %get-tuple-element.58.refs_0_), channel_id=1, source_target_pairs={{0,8},{1,9},{2,10},{3,11},{4,12},{5,13},{6,14},{7,15},{8,0},{9,1},... | collective-permute-start | bytes 786440 | tf_op jit(solution)/shard_map/ppermute | solution.py:454
  130.0 12.6 %collective-permute-start.22 = (bf16[4,512,256]{2,1,0:T(8,128)(2,1)S(1)}, bf16[4,512,256]{2,1,0:T(8,128)(2,1)S(1)}, u32[]{:S(2)}, u32[]{:S(2)}) collective-permute-start(bf16[4,512,256]{2,1,0:T(8,128)(2,1)S(1)} %joined.5.refs_4_), channel_id=1, source_target_pairs={{0,1},{1,0},{2,3},{3,2},{4,5},{5,4},{6,7},{7,6},{8,9},{9,8},{10,11... | collective-permute-start | bytes 3145736 | tf_op jit(solution)/shard_map/ppermute | solution.py:454
  131.0 7.7 %collective-permute-start.23 = (bf16[128,512]{1,0:T(8,128)(2,1)S(1)}, bf16[128,512]{1,0:T(8,128)(2,1)S(1)}, u32[]{:S(2)}, u32[]{:S(2)}) collective-permute-start(bf16[128,512]{1,0:T(8,128)(2,1)S(1)} %get-tuple-element.65), channel_id=1, source_target_pairs={{0,1},{1,0},{2,3},{3,2},{4,5},{5,4},{6,7},{7,6},{8,9},{9,8},{10,11... | collective-permute-start | bytes 393224 | tf_op jit(solution)/shard_map/ppermute | solution.py:454
  131.4 8.7 %collective-permute-start.24 = (bf16[128,512]{1,0:T(8,128)(2,1)S(1)}, bf16[128,512]{1,0:T(8,128)(2,1)S(1)}, u32[]{:S(2)}, u32[]{:S(2)}) collective-permute-start(bf16[128,512]{1,0:T(8,128)(2,1)S(1)} %get-tuple-element.66), channel_id=1, source_target_pairs={{0,63},{1,2},{2,1},{3,4},{4,3},{5,6},{6,5},{7,8},{8,7},{9,10},{10,... | collective-permute-start | bytes 393224 | tf_op jit(solution)/shard_map/ppermute | solution.py:454
  143.2 6.5 %collective-permute-start.25 = (bf16[128,512]{1,0:T(8,128)(2,1)S(1)}, bf16[128,512]{1,0:T(8,128)(2,1)S(1)}, u32[]{:S(2)}, u32[]{:S(2)}) collective-permute-start(bf16[128,512]{1,0:T(8,128)(2,1)S(1)} %get-tuple-element.68), channel_id=1, source_target_pairs={{0,1},{1,0},{2,3},{3,2},{4,5},{5,4},{6,7},{7,6},{8,9},{9,8},{10,11... | collective-permute-start | bytes 393224 | tf_op jit(solution)/shard_map/ppermute | solution.py:454
  143.3 7.8 %collective-permute-start.26 = (bf16[128,512]{1,0:T(8,128)(2,1)S(1)}, bf16[128,512]{1,0:T(8,128)(2,1)S(1)}, u32[]{:S(2)}, u32[]{:S(2)}) collective-permute-start(bf16[128,512]{1,0:T(8,128)(2,1)S(1)} %get-tuple-element.69), channel_id=1, source_target_pairs={{0,63},{1,2},{2,1},{3,4},{4,3},{5,6},{6,5},{7,8},{8,7},{9,10},{10,... | collective-permute-start | bytes 393224 | tf_op jit(solution)/shard_map/ppermute | solution.py:454

commit v5 on v4

--- a/solution.py
+++ b/solution.py
@@ -255,7 +255,7 @@
     )(*args)
 
 
-def copies(kernel_name, plan, shapes, *args, mib=4):
+def copies(kernel_name, plan, shapes, *args, mib=4, out=ANY):
     def kernel(*refs):
         ins, outs, sem = refs[: len(args)], refs[len(args) : -1], refs[-1]
         moves = [
@@ -270,7 +270,7 @@
         kernel,
         out_shape=[jax.ShapeDtypeStruct(shape, BF) for shape in shapes],
         in_specs=[ANY] * len(args),
-        out_specs=[ANY] * len(shapes),
+        out_specs=[out] * len(shapes),
         scratch_shapes=[pltpu.SemaphoreType.DMA((4,))],
         compiler_params=params(mib),
         cost_estimate=pl.CostEstimate(flops=0, bytes_accessed=2_000_000, transcendentals=0),
@@ -287,7 +287,7 @@
             (ins[0].at[:, pl.ds(pl.multiple_of(core * last, BLK), BLK)], outs[1]),
         ]
 
-    return copies("edges", plan, [(4, BLK, D)] * 2, samples, mib=60)
+    return copies("edges", plan, [(4, BLK, D)] * 2, samples, mib=60, out=VMEM)
 
 
 def joined(ring):
@@ -483,23 +483,26 @@
     def both(pieces):
         return pieces, over_dom(pieces, OTHER_CORE)
 
-    over_y, over_z = [by_y(x) for x in (1, 2, 3)], [Z_EVEN, Z_FAR, Z_ODD]
+    over_y = [by_y(x) for x in (1, 2, 3)]
     x1, x2, x3 = after((x1, x2, x3), own, own_far)
     ring1 = ring(jnp.where(p == 2, x3, jnp.where(p == 3, x2, x1)), over_y)
     then = jnp.where(p == 0, x2, jnp.where(p == 1, x3, x1))
     last = jnp.where(p == 0, x3, jnp.where(p == 1, x2, x1))
     ring2 = ring(after(then, ring1), over_y)
     stages = {1: both(joined(ring1)), 2: both(joined(ring2))}
-    ring3 = ring(after(last, near, far, stages[2]), over_z)
+    last = after(last, near, far)
+    ring3 = [last, over_dom(last, Z_EVEN), None, over_dom(last, Z_ODD)]
     h = arrived_call(h0, near, far, after(mixed_a, stages[2][0]), mixed_b)
     for section in range(1, SEG):
         w = weights_call(section, ws, stages[section])
         tiles, codes, gain = tiles_call(section, arrays)
         sender, inner, outer = sender_call(section, h, w)
         inner, outer = exchange(inner, outer)
+        if section == 1:
+            ring3[2] = over_dom(after(last, inner, outer), Z_FAR)
+        elif section == 2:
+            stages[3] = both(joined(after(ring3, inner, outer)))
         h = section_call(section, codes, gain, tiles, w, h, inner, outer, sender)
-        if section == 1:
-            stages[3] = both(joined(after(ring3, h)))
     return h[None]
 
 

time: 155 us -> 118 us (0.76)
  Pallas kernels: 51.6 us -> 20.9 us
  waiting for transfers between devices: 49.8 us -> 42.7 us
    pallas_call x4, Pallas kernels: 33.3 us -> 2.69 us  [copies(): pl.pallas_call(kernel, out_shape=[jax.ShapeDtypeStruct(shape, BF) for sha...]
    ppermute x7, waiting for transfers between devices: 22.6 us -> 12.7 us  [over_segments(): return lax.ppermute(value, 'segment', by_segment(x))]
    ppermute x20, waiting for transfers between devices: 27.2 us -> 30 us  [over_dom(): return lax.ppermute(value, 'dom', pairs)]
  transfers between devices with their start and end apart: 27 -> 27, of which waited for: 13 -> 12; matrix products, arithmetic and copies ran while one was open for 0% -> 0% of each run, Pallas kernels for 10% -> 12%
where the time goes in v5:
time: 118 us; the launch traced here: 116 us
  starting transfers between devices  51 us (43%)
  waiting for transfers between devices  42.7 us (36%)
  Pallas kernels  20.9 us (18%)
    ppermute x20, starting transfers between devices, over_dom(): return lax.ppermute(value, 'dom', pairs)  38.8 us
    ppermute x20, waiting for transfers between devices, over_dom(): return lax.ppermute(value, 'dom', pairs)  30 us
    ppermute x7, waiting for transfers between devices, over_segments(): return lax.ppermute(value, 'segment', by_segment(x))  12.7 us
    ppermute x7, starting transfers between devices, over_segments(): return lax.ppermute(value, 'segment', by_segment(x))  12.2 us
    pallas_call x3, Pallas kernels, section_call(): pl.pallas_call(section_kernel, out_shape=jax.ShapeDtypeStruct((BD * BLK,...  8.03 us
    pallas_call x2, Pallas kernels, first_call(): pl.pallas_call(functools.partial(first_kernel, order), out_shape=[jax.Sha...  4.05 us
    pallas_call x3, Pallas kernels, tiles_call(): pl.pallas_call(functools.partial(tiles_kernel, section), out_shape=[jax.S...  3.86 us
    pallas_call x4, Pallas kernels, copies(): pl.pallas_call(kernel, out_shape=[jax.ShapeDtypeStruct(shape, BF) for sha...  2.69 us
  transfers between devices with their start and end apart: 27, of which 12 were waited for; matrix products, arithmetic and copies ran while one was open for 0% of the time, Pallas kernels for 12%

profile of v5, /device:TPU:6, one launch (start us, length us, event | category | flops | bytes accessed | tf_op | source)
XLA Modules:
  0.0 116.2 jit_solution(16167246729743330613)
XLA Ops:
  0.0 0.0 copy-start.1
  0.0 2.3 %edges.1 = (bf16[4,128,512]{2,1,0:T(8,128)(2,1)}, bf16[4,128,512]{2,1,0:T(8,128)(2,1)}) custom-call(bf16[4,512,512]{2,1,0:T(8,128)(2,1)} %samples.3), custom_call_target="tpu_custom_call" | custom-call | bytes 2000000 | tf_op jit(solution)/shard_map/edges/pallas_call | solution.py:269
  2.4 0.1 collective-permute-start
  2.5 8.4 %collective-permute-start.1 = (bf16[4,128,512]{2,1,0:T(8,128)(2,1)}, bf16[4,128,512]{2,1,0:T(8,128)(2,1)S(1)}, u32[]{:S(2)}, u32[]{:S(2)}) collective-permute-start(bf16[4,128,512]{2,1,0:T(8,128)(2,1)} %get-tuple-element.40), channel_id=1, source_target_pairs={{0,63},{1,2},{2,1},{3,4},{4,3},{5,6},{6,5},{7,8},{8,7},{9,10},{10,... | collective-permute-start | bytes 1572872 | tf_op jit(solution)/shard_map/ppermute | solution.py:454
  10.9 0.1 select_bitcast_fusion
  11.1 0.6 collective-permute-start.8
  11.6 2.4 %collective-permute-start.7 = (bf16[512,256]{1,0:T(8,128)(2,1)S(1)}, bf16[512,256]{1,0:T(8,128)(2,1)S(1)}, u32[]{:S(2)}, u32[]{:S(2)}) collective-permute-start(bf16[512,256]{1,0:T(8,128)(2,1)S(1)} %select_bitcast_fusion), channel_id=1, source_target_pairs={{0,128},{64,192},{128,0},{192,64},{1,129},{65,193},{129,1},{193,65... | collective-permute-start | bytes 786440 | tf_op jit(solution)/shard_map/ppermute | solution.py:450
  14.0 1.2 %collective-permute-start.6 = (bf16[512,256]{1,0:T(8,128)(2,1)S(1)}, bf16[512,256]{1,0:T(8,128)(2,1)S(1)}, u32[]{:S(2)}, u32[]{:S(2)}) collective-permute-start(bf16[512,256]{1,0:T(8,128)(2,1)S(1)} %select_bitcast_fusion), channel_id=1, source_target_pairs={{0,64},{64,0},{128,192},{192,128},{1,65},{65,1},{129,193},{193,129... | collective-permute-start | bytes 786440 | tf_op jit(solution)/shard_map/ppermute | solution.py:450
  15.2 2.7 %collective-permute-done.1.outer = bf16[4,128,512]{2,1,0:T(8,128)(2,1)S(1)} collective-permute-done((bf16[4,128,512]{2,1,0:T(8,128)(2,1)}, bf16[4,128,512]{2,1,0:T(8,128)(2,1)S(1)}, u32[]{:S(2)}, u32[]{:S(2)}) %collective-permute-start.1) | collective-permute-done | bytes 524320 | tf_op jit(solution)/shard_map/ppermute | solution.py:454
  18.0 0.8 copy-done.13
  18.8 3.4 %first3.1 = (bf16[3088,128]{1,0:T(8,128)(2,1)}, bf16[3088,128]{1,0:T(8,128)(2,1)}) custom-call(s32[1,4,6]{2,1,0:T(4,128)} %src.3, s32[1,4]{1,0:T(1,128)} %cnt.3, f32[1,1,512]{2,1,0:T(1,128)} %gain.3, bf16[4,128,512]{2,1,0:T(8,128)(2,1)} %copy-done.11, bf16[4,128,512]{2,1,0:T(8,128)(2,1)} %copy-done.13, bf16[4,512,512]{2,1,0:T(8,128)(2,1)} %samples.3, ...), custom_call_target="tpu_custom_call" | custom-call | flops 6000000000 | bytes 4000000 | tf_op jit(solution)/shard_map/first3/pallas_call | solution.py:197
  22.2 0.2 collective-permute-done.6
  22.4 0.1 select_select_fusion
  22.5 0.9 collective-permute-start.12
  23.3 0.6 collective-permute-start.11
  24.0 2.7 %collective-permute-start.10 = (bf16[512,256]{1,0:T(8,128)(2,1)S(1)}, bf16[512,256]{1,0:T(8,128)(2,1)S(1)}, u32[]{:S(2)}, u32[]{:S(2)}) collective-permute-start(bf16[512,256]{1,0:T(8,128)(2,1)S(1)} %get-tuple-element.73.refs_0_), channel_id=1, source_target_pairs={{0,2},{1,3},{2,0},{3,1},{4,6},{5,7},{6,4},{7,5},{8,10},{9,11},{10,... | collective-permute-start | bytes 786440 | tf_op jit(solution)/shard_map/ppermute | solution.py:454
  26.6 8.7 %collective-permute-done.12.refs_3_ = bf16[512,256]{1,0:T(8,128)(2,1)S(1)} collective-permute-done((bf16[512,256]{1,0:T(8,128)(2,1)S(1)}, bf16[512,256]{1,0:T(8,128)(2,1)S(1)}, u32[]{:S(2)}, u32[]{:S(2)}) %collective-permute-start.12) | collective-permute-done | bytes 262176 | tf_op jit(solution)/shard_map/ppermute | solution.py:454
  35.4 0.6 collective-permute-done.10.refs_1_
  36.0 2.9 %collective-permute-start.15 = (bf16[512,256]{1,0:T(8,128)(2,1)S(1)}, bf16[512,256]{1,0:T(8,128)(2,1)S(1)}, u32[]{:S(2)}, u32[]{:S(2)}) collective-permute-start(bf16[512,256]{1,0:T(8,128)(2,1)S(1)} %get-tuple-element.51.refs_0_), channel_id=1, source_target_pairs={{0,6},{1,7},{2,4},{3,5},{4,2},{5,3},{6,0},{7,1},{8,14},{9,15},{10,... | collective-permute-start | bytes 786440 | tf_op jit(solution)/shard_map/ppermute | solution.py:454
  38.8 6.6 %collective-permute-start.3 = (bf16[3088,128]{1,0:T(8,128)(2,1)}, bf16[3088,128]{1,0:T(8,128)(2,1)S(1)}, u32[]{:S(2)}, u32[]{:S(2)}) collective-permute-start(bf16[3088,128]{1,0:T(8,128)(2,1)} %get-tuple-element.42), channel_id=1, source_target_pairs={{0,192},{64,128},{128,64},{192,0},{1,193},{65,129},{129,65},{193,1... | collective-permute-start | bytes 2371592 | tf_op jit(solution)/shard_map/ppermute | solution.py:450
  45.4 0.1 joined.4.refs_4_
  45.5 0.0 copy-start.2
  45.5 0.0 copy-start.4
  45.6 0.0 copy-start.10
  45.6 0.0 copy-start.12
  45.6 0.1 collective-permute-start.16
  45.7 0.4 collective-permute-start.14
  46.1 1.0 collective-permute-start.13
  47.1 9.3 %collective-permute-done.14.refs_2_ = bf16[512,256]{1,0:T(8,128)(2,1)S(1)} collective-permute-done((bf16[512,256]{1,0:T(8,128)(2,1)S(1)}, bf16[512,256]{1,0:T(8,128)(2,1)S(1)}, u32[]{:S(2)}, u32[]{:S(2)}) %collective-permute-start.14) | collective-permute-done | bytes 262176 | tf_op jit(solution)/shard_map/ppermute | solution.py:454
  56.4 2.9 %collective-permute-done.13.refs_1_ = bf16[512,256]{1,0:T(8,128)(2,1)S(1)} collective-permute-done((bf16[512,256]{1,0:T(8,128)(2,1)S(1)}, bf16[512,256]{1,0:T(8,128)(2,1)S(1)}, u32[]{:S(2)}, u32[]{:S(2)}) %collective-permute-start.13) | collective-permute-done | bytes 262176 | tf_op jit(solution)/shard_map/ppermute | solution.py:454
  59.3 0.1 joined.3.refs_4_
  59.5 0.1 collective-permute-start.21
  59.6 2.5 %collective-permute-done.3.far = bf16[3088,128]{1,0:T(8,128)(2,1)S(1)} collective-permute-done((bf16[3088,128]{1,0:T(8,128)(2,1)}, bf16[3088,128]{1,0:T(8,128)(2,1)S(1)}, u32[]{:S(2)}, u32[]{:S(2)}) %collective-permute-start.3) | collective-permute-done | bytes 790560 | tf_op jit(solution)/shard_map/ppermute | solution.py:450
  62.1 0.1 collective-permute-start.5
  62.2 1.7 %collective-permute-done.2.near = bf16[3088,128]{1,0:T(8,128)(2,1)S(1)} collective-permute-done((bf16[3088,128]{1,0:T(8,128)(2,1)}, bf16[3088,128]{1,0:T(8,128)(2,1)S(1)}, u32[]{:S(2)}, u32[]{:S(2)}) %collective-permute-start.2) | collective-permute-done | bytes 790560 | tf_op jit(solution)/shard_map/ppermute | solution.py:450
  64.0 1.3 %collective-permute-start.4 = (bf16[1536,128]{1,0:T(8,128)(2,1)S(1)}, bf16[1536,128]{1,0:T(8,128)(2,1)S(1)}, u32[]{:S(2)}, u32[]{:S(2)}) collective-permute-start(bf16[1536,128]{1,0:T(8,128)(2,1)S(1)} %slice.8), channel_id=1, source_target_pairs={{0,192},{64,128},{128,64},{192,0},{1,193},{65,129},{129,65},{193,1... | collective-permute-start | bytes 1179656 | tf_op jit(solution)/shard_map/ppermute | solution.py:450
  65.4 0.7 first1.1.h0
  66.0 8.2 %collective-permute-done.4.mixed_a = bf16[1536,128]{1,0:T(8,128)(2,1)S(1)} collective-permute-done((bf16[1536,128]{1,0:T(8,128)(2,1)S(1)}, bf16[1536,128]{1,0:T(8,128)(2,1)S(1)}, u32[]{:S(2)}, u32[]{:S(2)}) %collective-permute-start.4) | collective-permute-done | bytes 393248 | tf_op jit(solution)/shard_map/ppermute | solution.py:450
  74.3 0.1 arrived.1.h
  74.4 0.2 weights1.1.w
  74.6 0.5 sender1.1
  75.1 0.1 collective-permute-start.17
  75.2 8.2 %collective-permute-start.18 = (bf16[128,512]{1,0:T(8,128)(2,1)S(1)}, bf16[128,512]{1,0:T(8,128)(2,1)S(1)}, u32[]{:S(2)}, u32[]{:S(2)}) collective-permute-start(bf16[128,512]{1,0:T(8,128)(2,1)S(1)} %get-tuple-element.54), channel_id=1, source_target_pairs={{0,63},{1,2},{2,1},{3,4},{4,3},{5,6},{6,5},{7,8},{8,7},{9,10},{10,... | collective-permute-start | bytes 393224 | tf_op jit(solution)/shard_map/ppermute | solution.py:454
  83.5 1.1 collective-permute-start.20
  84.5 1.3 %tiles1.1 = (bf16[24,128,128]{2,1,0:T(8,128)(2,1)S(1)}, s32[8,128]{1,0:T(8,128)S(1)}, f32[1,512]{1,0:T(1,128)S(1)}) custom-call(bf16[3088,128]{1,0:T(8,128)(2,1)S(1)} %copy-done, bf16[3088,128]{1,0:T(8,128)(2,1)S(1)} %collective-permute-done.2.near, bf16[3088,128]{1,0:T(8,128)(2,1)S(1)} %collective-permute-done.3.far, ...), custom_call_target="tpu_custom_call" | custom-call | bytes 2000000 | tf_op jit(solution)/shard_map/tiles1/pallas_call | solution.py:374
  85.8 1.6 %collective-permute-done.18.outer = bf16[128,512]{1,0:T(8,128)(2,1)S(1)} collective-permute-done((bf16[128,512]{1,0:T(8,128)(2,1)S(1)}, bf16[128,512]{1,0:T(8,128)(2,1)S(1)}, u32[]{:S(2)}, u32[]{:S(2)}) %collective-permute-start.18) | collective-permute-done | bytes 131104 | tf_op jit(solution)/shard_map/ppermute | solution.py:454
  87.4 0.0 collective-permute-start.19
  87.4 2.4 %section1.1.h = bf16[512,512]{1,0:T(8,128)(2,1)S(1)} custom-call(s32[8,128]{1,0:T(8,128)S(1)} %get-tuple-element.56.codes, f32[1,512]{1,0:T(1,128)S(1)} %get-tuple-element.57.gain, bf16[24,128,128]{2,1,0:T(8,128)(2,1)S(1)} %get-tuple-element.58.tiles, bf16[4,512,512]{2,1,0:T(8,128)(2,1)S(1)} %weights1.1.w, bf16[512,512]{1,0:T(8,128)(2,1)S(1)} %arrived.1.h, ...), custom_call_target="tpu_custom_call" | custom-call | flops 1500000000 | bytes 4000000 | tf_op jit(solution)/shard_map/section1/pallas_call | solution.py:401
  89.8 0.2 weights2.1.w
  90.1 0.5 sender2.1
  90.6 0.3 collective-permute-start.22
  90.9 5.3 %collective-permute-start.23 = (bf16[128,512]{1,0:T(8,128)(2,1)S(1)}, bf16[128,512]{1,0:T(8,128)(2,1)S(1)}, u32[]{:S(2)}, u32[]{:S(2)}) collective-permute-start(bf16[128,512]{1,0:T(8,128)(2,1)S(1)} %get-tuple-element.61), channel_id=1, source_target_pairs={{0,63},{1,2},{2,1},{3,4},{4,3},{5,6},{6,5},{7,8},{8,7},{9,10},{10,... | collective-permute-start | bytes 393224 | tf_op jit(solution)/shard_map/ppermute | solution.py:454
  96.2 2.8 %collective-permute-done.19.refs_2_ = bf16[512,256]{1,0:T(8,128)(2,1)S(1)} collective-permute-done((bf16[512,256]{1,0:T(8,128)(2,1)S(1)}, bf16[512,256]{1,0:T(8,128)(2,1)S(1)}, u32[]{:S(2)}, u32[]{:S(2)}) %collective-permute-start.19) | collective-permute-done | bytes 262176 | tf_op jit(solution)/shard_map/ppermute | solution.py:454
  99.0 0.1 joined.5.refs_4_
  99.2 0.1 collective-permute-start.24
  99.3 1.3 %tiles2.1 = (bf16[24,128,128]{2,1,0:T(8,128)(2,1)S(1)}, s32[8,128]{1,0:T(8,128)S(1)}, f32[1,512]{1,0:T(1,128)S(1)}) custom-call(bf16[3088,128]{1,0:T(8,128)(2,1)S(1)} %copy-done, bf16[3088,128]{1,0:T(8,128)(2,1)S(1)} %collective-permute-done.2.near, bf16[3088,128]{1,0:T(8,128)(2,1)S(1)} %collective-permute-done.3.far, ...), custom_call_target="tpu_custom_call" | custom-call | bytes 2000000 | tf_op jit(solution)/shard_map/tiles2/pallas_call | solution.py:374
  100.6 2.4 %section2.1.h = bf16[512,512]{1,0:T(8,128)(2,1)S(1)} custom-call(s32[8,128]{1,0:T(8,128)S(1)} %get-tuple-element.66.codes, f32[1,512]{1,0:T(1,128)S(1)} %get-tuple-element.67.gain, bf16[24,128,128]{2,1,0:T(8,128)(2,1)S(1)} %get-tuple-element.68.tiles, bf16[4,512,512]{2,1,0:T(8,128)(2,1)S(1)} %weights2.1.w, bf16[512,512]{1,0:T(8,128)(2,1)S(1)} %section1.1.h, ...), custom_call_target="tpu_custom_call" | custom-call | flops 1500000000 | bytes 4000000 | tf_op jit(solution)/shard_map/section2/pallas_call | solution.py:401
  103.0 0.2 weights3.1.w
  103.2 0.5 sender3.1
  103.7 0.5 collective-permute-start.25
  104.3 6.1 %collective-permute-start.26 = (bf16[128,512]{1,0:T(8,128)(2,1)S(1)}, bf16[128,512]{1,0:T(8,128)(2,1)S(1)}, u32[]{:S(2)}, u32[]{:S(2)}) collective-permute-start(bf16[128,512]{1,0:T(8,128)(2,1)S(1)} %get-tuple-element.71), channel_id=1, source_target_pairs={{0,63},{1,2},{2,1},{3,4},{4,3},{5,6},{6,5},{7,8},{8,7},{9,10},{10,... | collective-permute-start | bytes 393224 | tf_op jit(solution)/shard_map/ppermute | solution.py:454
  110.3 1.3 %tiles3.1 = (bf16[24,128,128]{2,1,0:T(8,128)(2,1)S(1)}, s32[8,128]{1,0:T(8,128)S(1)}, f32[1,512]{1,0:T(1,128)S(1)}) custom-call(bf16[3088,128]{1,0:T(8,128)(2,1)S(1)} %copy-done, bf16[3088,128]{1,0:T(8,128)(2,1)S(1)} %collective-permute-done.2.near, bf16[3088,128]{1,0:T(8,128)(2,1)S(1)} %collective-permute-done.3.far, ...), custom_call_target="tpu_custom_call" | custom-call | bytes 2000000 | tf_op jit(solution)/shard_map/tiles3/pallas_call | solution.py:374
  111.6 1.4 %collective-permute-done.26.outer = bf16[128,512]{1,0:T(8,128)(2,1)S(1)} collective-permute-done((bf16[128,512]{1,0:T(8,128)(2,1)S(1)}, bf16[128,512]{1,0:T(8,128)(2,1)S(1)}, u32[]{:S(2)}, u32[]{:S(2)}) %collective-permute-start.26) | collective-permute-done | bytes 131104 | tf_op jit(solution)/shard_map/ppermute | solution.py:454
  113.0 3.2 %section3.1 = bf16[512,512]{1,0:T(8,128)(2,1)} custom-call(s32[8,128]{1,0:T(8,128)S(1)} %get-tuple-element.43.codes, f32[1,512]{1,0:T(1,128)S(1)} %get-tuple-element.44.gain, bf16[24,128,128]{2,1,0:T(8,128)(2,1)S(1)} %get-tuple-element.45.tiles, bf16[4,512,512]{2,1,0:T(8,128)(2,1)S(1)} %weights3.1.w, bf16[512,512]{1,0:T(8,128)(2,1)S(1)} %section2.1.h, ...), custom_call_target="tpu_custom_call" | custom-call | flops 1500000000 | bytes 4000000 | tf_op jit(solution)/shard_map/section3/pallas_call | solution.py:401
  (49 shorter events, 0.2 us)
Async XLA Ops:
  0.0 10.9 %copy-start.7 = (bf16[1,1,512,512]{3,2,1,0:T(8,128)(2,1)S(1)}, bf16[1,1,512,512]{3,2,1,0:T(8,128)(2,1)}, u32[]{:S(2)}) copy-start(bf16[1,1,512,512]{3,2,1,0:T(8,128)(2,1)} %refs_3_.5) | copy-start | bytes 1572868
  0.0 10.9 %copy-start.5 = (bf16[1,1,512,512]{3,2,1,0:T(8,128)(2,1)S(1)}, bf16[1,1,512,512]{3,2,1,0:T(8,128)(2,1)}, u32[]{:S(2)}) copy-start(bf16[1,1,512,512]{3,2,1,0:T(8,128)(2,1)} %refs_2_.5) | copy-start | bytes 1572868
  0.0 10.9 %copy-start.3 = (bf16[1,1,512,512]{3,2,1,0:T(8,128)(2,1)S(1)}, bf16[1,1,512,512]{3,2,1,0:T(8,128)(2,1)}, u32[]{:S(2)}) copy-start(bf16[1,1,512,512]{3,2,1,0:T(8,128)(2,1)} %refs_1_.5) | copy-start | bytes 1572868
  0.0 10.9 %copy-start.1 = (bf16[1,1,512,512]{3,2,1,0:T(8,128)(2,1)S(1)}, bf16[1,1,512,512]{3,2,1,0:T(8,128)(2,1)}, u32[]{:S(2)}) copy-start(bf16[1,1,512,512]{3,2,1,0:T(8,128)(2,1)} %refs_0_.7) | copy-start | bytes 1572868
  2.4 12.9 %collective-permute-start = (bf16[4,128,512]{2,1,0:T(8,128)(2,1)}, bf16[4,128,512]{2,1,0:T(8,128)(2,1)S(1)}, u32[]{:S(2)}, u32[]{:S(2)}) collective-permute-start(bf16[4,128,512]{2,1,0:T(8,128)(2,1)} %get-tuple-element.39), channel_id=1, source_target_pairs={{0,1},{1,0},{2,3},{3,2},{4,5},{5,4},{6,7},{7,6},{8,9},{9,8},{10,11... | collective-permute-start | bytes 1572872 | tf_op jit(solution)/shard_map/ppermute | solution.py:454
  2.5 15.5 %collective-permute-start.1 = (bf16[4,128,512]{2,1,0:T(8,128)(2,1)}, bf16[4,128,512]{2,1,0:T(8,128)(2,1)S(1)}, u32[]{:S(2)}, u32[]{:S(2)}) collective-permute-start(bf16[4,128,512]{2,1,0:T(8,128)(2,1)} %get-tuple-element.40), channel_id=1, source_target_pairs={{0,63},{1,2},{2,1},{3,4},{4,3},{5,6},{6,5},{7,8},{8,7},{9,10},{10,... | collective-permute-start | bytes 1572872 | tf_op jit(solution)/shard_map/ppermute | solution.py:454
  11.1 11.1 %collective-permute-start.8 = (bf16[512,256]{1,0:T(8,128)(2,1)S(1)}, bf16[512,256]{1,0:T(8,128)(2,1)S(1)}, u32[]{:S(2)}, u32[]{:S(2)}) collective-permute-start(bf16[512,256]{1,0:T(8,128)(2,1)S(1)} %select_bitcast_fusion), channel_id=1, source_target_pairs={{0,192},{64,128},{128,64},{192,0},{1,193},{65,129},{129,65},{193,1... | collective-permute-start | bytes 786440 | tf_op jit(solution)/shard_map/ppermute | solution.py:450
  11.6 10.5 %collective-permute-start.7 = (bf16[512,256]{1,0:T(8,128)(2,1)S(1)}, bf16[512,256]{1,0:T(8,128)(2,1)S(1)}, u32[]{:S(2)}, u32[]{:S(2)}) collective-permute-start(bf16[512,256]{1,0:T(8,128)(2,1)S(1)} %select_bitcast_fusion), channel_id=1, source_target_pairs={{0,128},{64,192},{128,0},{192,64},{1,129},{65,193},{129,1},{193,65... | collective-permute-start | bytes 786440 | tf_op jit(solution)/shard_map/ppermute | solution.py:450
  14.0 8.4 %collective-permute-start.6 = (bf16[512,256]{1,0:T(8,128)(2,1)S(1)}, bf16[512,256]{1,0:T(8,128)(2,1)S(1)}, u32[]{:S(2)}, u32[]{:S(2)}) collective-permute-start(bf16[512,256]{1,0:T(8,128)(2,1)S(1)} %select_bitcast_fusion), channel_id=1, source_target_pairs={{0,64},{64,0},{128,192},{192,128},{1,65},{65,1},{129,193},{193,129... | collective-permute-start | bytes 786440 | tf_op jit(solution)/shard_map/ppermute | solution.py:450
  15.2 2.7 %copy-start.11 = (bf16[4,128,512]{2,1,0:T(8,128)(2,1)}, bf16[4,128,512]{2,1,0:T(8,128)(2,1)S(1)}, u32[]{:S(2)}) copy-start(bf16[4,128,512]{2,1,0:T(8,128)(2,1)S(1)} %collective-permute-done.inner) | copy-start | bytes 1572868
  18.0 0.8 copy-start.13
  22.4 42.9 %copy-start.14 = (bf16[4,128,512]{2,1,0:T(8,128)(2,1)S(1)}, bf16[4,128,512]{2,1,0:T(8,128)(2,1)}, u32[]{:S(2)}) copy-start(bf16[4,128,512]{2,1,0:T(8,128)(2,1)} %copy-done.13) | copy-start | bytes 1572868
  22.5 12.9 %collective-permute-start.12 = (bf16[512,256]{1,0:T(8,128)(2,1)S(1)}, bf16[512,256]{1,0:T(8,128)(2,1)S(1)}, u32[]{:S(2)}, u32[]{:S(2)}) collective-permute-start(bf16[512,256]{1,0:T(8,128)(2,1)S(1)} %get-tuple-element.73.refs_0_), channel_id=1, source_target_pairs={{0,6},{1,7},{2,4},{3,5},{4,2},{5,3},{6,0},{7,1},{8,14},{9,15},{10,... | collective-permute-start | bytes 786440 | tf_op jit(solution)/shard_map/ppermute | solution.py:454
  23.3 12.0 %collective-permute-start.11 = (bf16[512,256]{1,0:T(8,128)(2,1)S(1)}, bf16[512,256]{1,0:T(8,128)(2,1)S(1)}, u32[]{:S(2)}, u32[]{:S(2)}) collective-permute-start(bf16[512,256]{1,0:T(8,128)(2,1)S(1)} %get-tuple-element.73.refs_0_), channel_id=1, source_target_pairs={{0,4},{1,5},{2,6},{3,7},{4,0},{5,1},{6,2},{7,3},{8,12},{9,13},{10,... | collective-permute-start | bytes 786440 | tf_op jit(solution)/shard_map/ppermute | solution.py:454
  24.0 12.0 %collective-permute-start.10 = (bf16[512,256]{1,0:T(8,128)(2,1)S(1)}, bf16[512,256]{1,0:T(8,128)(2,1)S(1)}, u32[]{:S(2)}, u32[]{:S(2)}) collective-permute-start(bf16[512,256]{1,0:T(8,128)(2,1)S(1)} %get-tuple-element.73.refs_0_), channel_id=1, source_target_pairs={{0,2},{1,3},{2,0},{3,1},{4,6},{5,7},{6,4},{7,5},{8,10},{9,11},{10,... | collective-permute-start | bytes 786440 | tf_op jit(solution)/shard_map/ppermute | solution.py:454
  36.0 10.2 %collective-permute-start.15 = (bf16[512,256]{1,0:T(8,128)(2,1)S(1)}, bf16[512,256]{1,0:T(8,128)(2,1)S(1)}, u32[]{:S(2)}, u32[]{:S(2)}) collective-permute-start(bf16[512,256]{1,0:T(8,128)(2,1)S(1)} %get-tuple-element.51.refs_0_), channel_id=1, source_target_pairs={{0,6},{1,7},{2,4},{3,5},{4,2},{5,3},{6,0},{7,1},{8,14},{9,15},{10,... | collective-permute-start | bytes 786440 | tf_op jit(solution)/shard_map/ppermute | solution.py:454
  38.8 23.3 %collective-permute-start.3 = (bf16[3088,128]{1,0:T(8,128)(2,1)}, bf16[3088,128]{1,0:T(8,128)(2,1)S(1)}, u32[]{:S(2)}, u32[]{:S(2)}) collective-permute-start(bf16[3088,128]{1,0:T(8,128)(2,1)} %get-tuple-element.42), channel_id=1, source_target_pairs={{0,192},{64,128},{128,64},{192,0},{1,193},{65,129},{129,65},{193,1... | collective-permute-start | bytes 2371592 | tf_op jit(solution)/shard_map/ppermute | solution.py:450
  45.4 18.6 %collective-permute-start.2 = (bf16[3088,128]{1,0:T(8,128)(2,1)}, bf16[3088,128]{1,0:T(8,128)(2,1)S(1)}, u32[]{:S(2)}, u32[]{:S(2)}) collective-permute-start(bf16[3088,128]{1,0:T(8,128)(2,1)} %get-tuple-element.41.own), channel_id=1, source_target_pairs={{0,64},{64,0},{128,192},{192,128},{1,65},{65,1},{129,193},{193,129... | collective-permute-start | bytes 2371592 | tf_op jit(solution)/shard_map/ppermute | solution.py:450
  45.4 19.9 %copy-start.9 = (bf16[4,512,512]{2,1,0:T(8,128)(2,1)S(1)}, bf16[4,512,512]{2,1,0:T(8,128)(2,1)}, u32[]{:S(2)}) copy-start(bf16[4,512,512]{2,1,0:T(8,128)(2,1)} %samples.3) | copy-start | bytes 6291460
  45.5 19.8 %copy-start.2 = (bf16[1,1,512,512]{3,2,1,0:T(8,128)(2,1)S(1)}, bf16[1,1,512,512]{3,2,1,0:T(8,128)(2,1)}, u32[]{:S(2)}) copy-start(bf16[1,1,512,512]{3,2,1,0:T(8,128)(2,1)} %refs_0_.7) | copy-start | bytes 1572868
  45.5 19.8 %copy-start.4 = (bf16[1,1,512,512]{3,2,1,0:T(8,128)(2,1)S(1)}, bf16[1,1,512,512]{3,2,1,0:T(8,128)(2,1)}, u32[]{:S(2)}) copy-start(bf16[1,1,512,512]{3,2,1,0:T(8,128)(2,1)} %refs_1_.5) | copy-start | bytes 1572868
  45.5 19.8 %copy-start.6 = (bf16[1,1,512,512]{3,2,1,0:T(8,128)(2,1)S(1)}, bf16[1,1,512,512]{3,2,1,0:T(8,128)(2,1)}, u32[]{:S(2)}) copy-start(bf16[1,1,512,512]{3,2,1,0:T(8,128)(2,1)} %refs_2_.5) | copy-start | bytes 1572868
  45.5 19.8 %copy-start.8 = (bf16[1,1,512,512]{3,2,1,0:T(8,128)(2,1)S(1)}, bf16[1,1,512,512]{3,2,1,0:T(8,128)(2,1)}, u32[]{:S(2)}) copy-start(bf16[1,1,512,512]{3,2,1,0:T(8,128)(2,1)} %refs_3_.5) | copy-start | bytes 1572868
  45.6 19.8 %copy-start.10 = (bf16[1,4,6,128,128]{4,3,2,1,0:T(8,128)(2,1)S(1)}, bf16[1,4,6,128,128]{4,3,2,1,0:T(8,128)(2,1)}, u32[]{:S(2)}) copy-start(bf16[1,4,6,128,128]{4,3,2,1,0:T(8,128)(2,1)} %tiles.3) | copy-start | bytes 2359300
  45.6 19.8 %copy-start.12 = (bf16[4,128,512]{2,1,0:T(8,128)(2,1)S(1)}, bf16[4,128,512]{2,1,0:T(8,128)(2,1)}, u32[]{:S(2)}) copy-start(bf16[4,128,512]{2,1,0:T(8,128)(2,1)} %copy-done.11) | copy-start | bytes 1572868
  45.6 19.8 %copy-start.15 = (s32[1,4,6]{2,1,0:T(4,128)S(1)}, s32[1,4,6]{2,1,0:T(4,128)}, u32[]{:S(2)}) copy-start(s32[1,4,6]{2,1,0:T(4,128)} %src.3) | copy-start | bytes 292
  45.6 19.8 %copy-start.16 = (f32[1,1,512]{2,1,0:T(1,128)S(1)}, f32[1,1,512]{2,1,0:T(1,128)}, u32[]{:S(2)}) copy-start(f32[1,1,512]{2,1,0:T(1,128)} %gain.3) | copy-start | bytes 6148
  45.6 19.8 %copy-start.17 = (s32[1,4]{1,0:T(1,128)S(1)}, s32[1,4]{1,0:T(1,128)}, u32[]{:S(2)}) copy-start(s32[1,4]{1,0:T(1,128)} %cnt.3) | copy-start | bytes 52
  45.6 28.8 %collective-permute-start.16 = (bf16[4,512,256]{2,1,0:T(8,128)(2,1)S(1)}, bf16[4,512,256]{2,1,0:T(8,128)(2,1)S(1)}, u32[]{:S(2)}, u32[]{:S(2)}) collective-permute-start(bf16[4,512,256]{2,1,0:T(8,128)(2,1)S(1)} %joined.4.refs_4_), channel_id=1, source_target_pairs={{0,1},{1,0},{2,3},{3,2},{4,5},{5,4},{6,7},{7,6},{8,9},{9,8},{10,11... | collective-permute-start | bytes 3145736 | tf_op jit(solution)/shard_map/ppermute | solution.py:454
  45.7 10.7 %collective-permute-start.14 = (bf16[512,256]{1,0:T(8,128)(2,1)S(1)}, bf16[512,256]{1,0:T(8,128)(2,1)S(1)}, u32[]{:S(2)}, u32[]{:S(2)}) collective-permute-start(bf16[512,256]{1,0:T(8,128)(2,1)S(1)} %get-tuple-element.51.refs_0_), channel_id=1, source_target_pairs={{0,4},{1,5},{2,6},{3,7},{4,0},{5,1},{6,2},{7,3},{8,12},{9,13},{10,... | collective-permute-start | bytes 786440 | tf_op jit(solution)/shard_map/ppermute | solution.py:454
  46.1 13.2 %collective-permute-start.13 = (bf16[512,256]{1,0:T(8,128)(2,1)S(1)}, bf16[512,256]{1,0:T(8,128)(2,1)S(1)}, u32[]{:S(2)}, u32[]{:S(2)}) collective-permute-start(bf16[512,256]{1,0:T(8,128)(2,1)S(1)} %get-tuple-element.51.refs_0_), channel_id=1, source_target_pairs={{0,2},{1,3},{2,0},{3,1},{4,6},{5,7},{6,4},{7,5},{8,10},{9,11},{10,... | collective-permute-start | bytes 786440 | tf_op jit(solution)/shard_map/ppermute | solution.py:454
  59.5 30.4 %collective-permute-start.21 = (bf16[4,512,256]{2,1,0:T(8,128)(2,1)S(1)}, bf16[4,512,256]{2,1,0:T(8,128)(2,1)S(1)}, u32[]{:S(2)}, u32[]{:S(2)}) collective-permute-start(bf16[4,512,256]{2,1,0:T(8,128)(2,1)S(1)} %joined.3.refs_4_), channel_id=1, source_target_pairs={{0,1},{1,0},{2,3},{3,2},{4,5},{5,4},{6,7},{7,6},{8,9},{9,8},{10,11... | collective-permute-start | bytes 3145736 | tf_op jit(solution)/shard_map/ppermute | solution.py:454
  62.1 12.2 %collective-permute-start.5 = (bf16[1552,128]{1,0:T(8,128)(2,1)S(1)}, bf16[1552,128]{1,0:T(8,128)(2,1)S(1)}, u32[]{:S(2)}, u32[]{:S(2)}) collective-permute-start(bf16[1552,128]{1,0:T(8,128)(2,1)S(1)} %slice.9), channel_id=1, source_target_pairs={{0,64},{64,0},{128,192},{192,128},{1,65},{65,1},{129,193},{193,129... | collective-permute-start | bytes 1191944 | tf_op jit(solution)/shard_map/ppermute | solution.py:450
  64.0 10.3 %collective-permute-start.4 = (bf16[1536,128]{1,0:T(8,128)(2,1)S(1)}, bf16[1536,128]{1,0:T(8,128)(2,1)S(1)}, u32[]{:S(2)}, u32[]{:S(2)}) collective-permute-start(bf16[1536,128]{1,0:T(8,128)(2,1)S(1)} %slice.8), channel_id=1, source_target_pairs={{0,192},{64,128},{128,64},{192,0},{1,193},{65,129},{129,65},{193,1... | collective-permute-start | bytes 1179656 | tf_op jit(solution)/shard_map/ppermute | solution.py:450
  74.6 9.9 %copy-start = (bf16[3088,128]{1,0:T(8,128)(2,1)S(1)}, bf16[3088,128]{1,0:T(8,128)(2,1)}, u32[]{:S(2)}) copy-start(bf16[3088,128]{1,0:T(8,128)(2,1)} %get-tuple-element.41.own) | copy-start | bytes 2371588
  75.1 10.7 %collective-permute-start.17 = (bf16[128,512]{1,0:T(8,128)(2,1)S(1)}, bf16[128,512]{1,0:T(8,128)(2,1)S(1)}, u32[]{:S(2)}, u32[]{:S(2)}) collective-permute-start(bf16[128,512]{1,0:T(8,128)(2,1)S(1)} %get-tuple-element.53), channel_id=1, source_target_pairs={{0,1},{1,0},{2,3},{3,2},{4,5},{5,4},{6,7},{7,6},{8,9},{9,8},{10,11... | collective-permute-start | bytes 393224 | tf_op jit(solution)/shard_map/ppermute | solution.py:454
  75.2 12.1 %collective-permute-start.18 = (bf16[128,512]{1,0:T(8,128)(2,1)S(1)}, bf16[128,512]{1,0:T(8,128)(2,1)S(1)}, u32[]{:S(2)}, u32[]{:S(2)}) collective-permute-start(bf16[128,512]{1,0:T(8,128)(2,1)S(1)} %get-tuple-element.54), channel_id=1, source_target_pairs={{0,63},{1,2},{2,1},{3,4},{4,3},{5,6},{6,5},{7,8},{8,7},{9,10},{10,... | collective-permute-start | bytes 393224 | tf_op jit(solution)/shard_map/ppermute | solution.py:454
  83.5 12.7 %collective-permute-start.20 = (bf16[512,256]{1,0:T(8,128)(2,1)S(1)}, bf16[512,256]{1,0:T(8,128)(2,1)S(1)}, u32[]{:S(2)}, u32[]{:S(2)}) collective-permute-start(bf16[512,256]{1,0:T(8,128)(2,1)S(1)} %get-tuple-element.62.refs_0_), channel_id=1, source_target_pairs={{0,56},{1,57},{2,58},{3,59},{4,60},{5,61},{6,62},{7,63},{8,16},{9,... | collective-permute-start | bytes 786440 | tf_op jit(solution)/shard_map/ppermute | solution.py:454
  84.5 11.7 %collective-permute-start.9 = (bf16[512,256]{1,0:T(8,128)(2,1)S(1)}, bf16[512,256]{1,0:T(8,128)(2,1)S(1)}, u32[]{:S(2)}, u32[]{:S(2)}) collective-permute-start(bf16[512,256]{1,0:T(8,128)(2,1)S(1)} %get-tuple-element.62.refs_0_), channel_id=1, source_target_pairs={{0,8},{1,9},{2,10},{3,11},{4,12},{5,13},{6,14},{7,15},{8,0},{9,1},... | collective-permute-start | bytes 786440 | tf_op jit(solution)/shard_map/ppermute | solution.py:454
  87.4 11.6 %collective-permute-start.19 = (bf16[512,256]{1,0:T(8,128)(2,1)S(1)}, bf16[512,256]{1,0:T(8,128)(2,1)S(1)}, u32[]{:S(2)}, u32[]{:S(2)}) collective-permute-start(bf16[512,256]{1,0:T(8,128)(2,1)S(1)} %get-tuple-element.62.refs_0_), channel_id=1, source_target_pairs={{0,16},{1,17},{2,18},{3,19},{4,20},{5,21},{6,22},{7,23},{8,24},{9,... | collective-permute-start | bytes 786440 | tf_op jit(solution)/shard_map/ppermute | solution.py:454
  90.6 8.4 %collective-permute-start.22 = (bf16[128,512]{1,0:T(8,128)(2,1)S(1)}, bf16[128,512]{1,0:T(8,128)(2,1)S(1)}, u32[]{:S(2)}, u32[]{:S(2)}) collective-permute-start(bf16[128,512]{1,0:T(8,128)(2,1)S(1)} %get-tuple-element.60), channel_id=1, source_target_pairs={{0,1},{1,0},{2,3},{3,2},{4,5},{5,4},{6,7},{7,6},{8,9},{9,8},{10,11... | collective-permute-start | bytes 393224 | tf_op jit(solution)/shard_map/ppermute | solution.py:454
  90.9 8.1 %collective-permute-start.23 = (bf16[128,512]{1,0:T(8,128)(2,1)S(1)}, bf16[128,512]{1,0:T(8,128)(2,1)S(1)}, u32[]{:S(2)}, u32[]{:S(2)}) collective-permute-start(bf16[128,512]{1,0:T(8,128)(2,1)S(1)} %get-tuple-element.61), channel_id=1, source_target_pairs={{0,63},{1,2},{2,1},{3,4},{4,3},{5,6},{6,5},{7,8},{8,7},{9,10},{10,... | collective-permute-start | bytes 393224 | tf_op jit(solution)/shard_map/ppermute | solution.py:454
  99.2 3.8 %collective-permute-start.24 = (bf16[4,512,256]{2,1,0:T(8,128)(2,1)S(1)}, bf16[4,512,256]{2,1,0:T(8,128)(2,1)S(1)}, u32[]{:S(2)}, u32[]{:S(2)}) collective-permute-start(bf16[4,512,256]{2,1,0:T(8,128)(2,1)S(1)} %joined.5.refs_4_), channel_id=1, source_target_pairs={{0,1},{1,0},{2,3},{3,2},{4,5},{5,4},{6,7},{7,6},{8,9},{9,8},{10,11... | collective-permute-start | bytes 3145736 | tf_op jit(solution)/shard_map/ppermute | solution.py:454
  103.7 7.9 %collective-permute-start.25 = (bf16[128,512]{1,0:T(8,128)(2,1)S(1)}, bf16[128,512]{1,0:T(8,128)(2,1)S(1)}, u32[]{:S(2)}, u32[]{:S(2)}) collective-permute-start(bf16[128,512]{1,0:T(8,128)(2,1)S(1)} %get-tuple-element.70), channel_id=1, source_target_pairs={{0,1},{1,0},{2,3},{3,2},{4,5},{5,4},{6,7},{7,6},{8,9},{9,8},{10,11... | collective-permute-start | bytes 393224 | tf_op jit(solution)/shard_map/ppermute | solution.py:454
  104.3 8.7 %collective-permute-start.26 = (bf16[128,512]{1,0:T(8,128)(2,1)S(1)}, bf16[128,512]{1,0:T(8,128)(2,1)S(1)}, u32[]{:S(2)}, u32[]{:S(2)}) collective-permute-start(bf16[128,512]{1,0:T(8,128)(2,1)S(1)} %get-tuple-element.71), channel_id=1, source_target_pairs={{0,63},{1,2},{2,1},{3,4},{4,3},{5,6},{6,5},{7,8},{8,7},{9,10},{10,... | collective-permute-start | bytes 393224 | tf_op jit(solution)/shard_map/ppermute | solution.py:454

commit v6 on v5

--- a/solution.py
+++ b/solution.py
@@ -489,19 +489,19 @@
     then = jnp.where(p == 0, x2, jnp.where(p == 1, x3, x1))
     last = jnp.where(p == 0, x3, jnp.where(p == 1, x2, x1))
     ring2 = ring(after(then, ring1), over_y)
-    stages = {1: both(joined(ring1)), 2: both(joined(ring2))}
-    last = after(last, near, far)
-    ring3 = [last, over_dom(last, Z_EVEN), None, over_dom(last, Z_ODD)]
-    h = arrived_call(h0, near, far, after(mixed_a, stages[2][0]), mixed_b)
+    last = after(last, ring1)
+    ring3 = [last, over_dom(last, Z_EVEN), over_dom(last, Z_FAR), over_dom(last, Z_ODD)]
+    stages, pieces2, pieces3 = {1: both(joined(ring1))}, joined(ring2), joined(ring3)
+    h = arrived_call(h0, near, far, after(mixed_a, pieces2, pieces3), mixed_b)
     for section in range(1, SEG):
         w = weights_call(section, ws, stages[section])
         tiles, codes, gain = tiles_call(section, arrays)
         sender, inner, outer = sender_call(section, h, w)
         inner, outer = exchange(inner, outer)
         if section == 1:
-            ring3[2] = over_dom(after(last, inner, outer), Z_FAR)
+            stages[2] = both(after(pieces2, inner, outer))
         elif section == 2:
-            stages[3] = both(joined(after(ring3, inner, outer)))
+            stages[3] = both(after(pieces3, inner, outer))
         h = section_call(section, codes, gain, tiles, w, h, inner, outer, sender)
     return h[None]
 

time: 118 us -> 123 us (1.042); the launches traced: 116 us -> 123 us
  starting transfers between devices: 51 us -> 57.5 us
  local copies, waits for them, and re-layouts: 0.93 us -> 3 us
  waiting for transfers between devices: 42.7 us -> 40.9 us
    ppermute x7, waiting for transfers between devices: 12.7 us -> 0.02 us  [over_segments(): return lax.ppermute(value, 'segment', by_segment(x))]
    ppermute x20, waiting for transfers between devices: 30 us -> 40.8 us  [over_dom(): return lax.ppermute(value, 'dom', pairs)]
    ppermute x20, starting transfers between devices: 38.8 us -> 44.7 us  [over_dom(): return lax.ppermute(value, 'dom', pairs)]
    unnamed x36, local copies, waits for them, and re-layouts: 0.88 us -> 2.95 us
  transfers between devices with their start and end apart: 27 -> 27, of which waited for: 12 -> 11; matrix products, arithmetic and copies ran while one was open for 0% -> 0% of each run, Pallas kernels for 12% -> 11%
where the time goes in v6:
time: 123 us
  starting transfers between devices  57.5 us (47%)
  waiting for transfers between devices  40.9 us (33%)
  Pallas kernels  20.9 us (17%)
  local copies, waits for them, and re-layouts  3 us (2%)
    ppermute x20, starting transfers between devices, over_dom(): return lax.ppermute(value, 'dom', pairs)  44.7 us
    ppermute x20, waiting for transfers between devices, over_dom(): return lax.ppermute(value, 'dom', pairs)  40.8 us
    ppermute x7, starting transfers between devices, over_segments(): return lax.ppermute(value, 'segment', by_segment(x))  12.8 us
    pallas_call x3, Pallas kernels, section_call(): pl.pallas_call(section_kernel, out_shape=jax.ShapeDtypeStruct((BD * BLK,...  8.03 us
    pallas_call x2, Pallas kernels, first_call(): pl.pallas_call(functools.partial(first_kernel, order), out_shape=[jax.Sha...  4.04 us
    pallas_call x3, Pallas kernels, tiles_call(): pl.pallas_call(functools.partial(tiles_kernel, section), out_shape=[jax.S...  3.81 us
    unnamed x36, local copies, waits for them, and re-layouts  2.95 us
    pallas_call x4, Pallas kernels, copies(): pl.pallas_call(kernel, out_shape=[jax.ShapeDtypeStruct(shape, BF) for sha...  2.69 us
  transfers between devices with their start and end apart: 27, of which 11 were waited for; matrix products, arithmetic and copies ran while one was open for 0% of the time, Pallas kernels for 11%

profile of v6, /device:TPU:6, one launch (start us, length us, event | category | flops | bytes accessed | tf_op | source)
XLA Modules:
  0.0 122.9 jit_solution(16572225831152749386)
XLA Ops:
  0.0 0.0 copy-start.1
  0.0 2.3 %edges.1 = (bf16[4,128,512]{2,1,0:T(8,128)(2,1)}, bf16[4,128,512]{2,1,0:T(8,128)(2,1)}) custom-call(bf16[4,512,512]{2,1,0:T(8,128)(2,1)} %samples.3), custom_call_target="tpu_custom_call" | custom-call | bytes 2000000 | tf_op jit(solution)/shard_map/edges/pallas_call | solution.py:269
  2.4 0.1 collective-permute-start
  2.5 8.4 %collective-permute-start.1 = (bf16[4,128,512]{2,1,0:T(8,128)(2,1)}, bf16[4,128,512]{2,1,0:T(8,128)(2,1)S(1)}, u32[]{:S(2)}, u32[]{:S(2)}) collective-permute-start(bf16[4,128,512]{2,1,0:T(8,128)(2,1)} %get-tuple-element.37), channel_id=1, source_target_pairs={{0,63},{1,2},{2,1},{3,4},{4,3},{5,6},{6,5},{7,8},{8,7},{9,10},{10,... | collective-permute-start | bytes 1572872 | tf_op jit(solution)/shard_map/ppermute | solution.py:454
  10.9 0.1 select_bitcast_fusion
  11.1 0.6 collective-permute-start.8
  11.6 2.4 %collective-permute-start.7 = (bf16[512,256]{1,0:T(8,128)(2,1)S(1)}, bf16[512,256]{1,0:T(8,128)(2,1)S(1)}, u32[]{:S(2)}, u32[]{:S(2)}) collective-permute-start(bf16[512,256]{1,0:T(8,128)(2,1)S(1)} %select_bitcast_fusion), channel_id=1, source_target_pairs={{0,128},{64,192},{128,0},{192,64},{1,129},{65,193},{129,1},{193,65... | collective-permute-start | bytes 786440 | tf_op jit(solution)/shard_map/ppermute | solution.py:450
  14.0 1.2 collective-permute-start.6
  15.2 2.7 %collective-permute-done.1.outer = bf16[4,128,512]{2,1,0:T(8,128)(2,1)S(1)} collective-permute-done((bf16[4,128,512]{2,1,0:T(8,128)(2,1)}, bf16[4,128,512]{2,1,0:T(8,128)(2,1)S(1)}, u32[]{:S(2)}, u32[]{:S(2)}) %collective-permute-start.1) | collective-permute-done | bytes 524320 | tf_op jit(solution)/shard_map/ppermute | solution.py:454
  18.0 0.8 copy-done.13
  18.8 3.4 %first3.1 = (bf16[3088,128]{1,0:T(8,128)(2,1)}, bf16[3088,128]{1,0:T(8,128)(2,1)}) custom-call(s32[1,4,6]{2,1,0:T(4,128)} %src.3, s32[1,4]{1,0:T(1,128)} %cnt.3, f32[1,1,512]{2,1,0:T(1,128)} %gain.3, bf16[4,128,512]{2,1,0:T(8,128)(2,1)} %copy-done.11, bf16[4,128,512]{2,1,0:T(8,128)(2,1)} %copy-done.13, bf16[4,512,512]{2,1,0:T(8,128)(2,1)} %samples.3, ...), custom_call_target="tpu_custom_call" | custom-call | flops 6000000000 | bytes 4000000 | tf_op jit(solution)/shard_map/first3/pallas_call | solution.py:197
  22.1 8.2 %collective-permute-start.3 = (bf16[3088,128]{1,0:T(8,128)(2,1)}, bf16[3088,128]{1,0:T(8,128)(2,1)S(1)}, u32[]{:S(2)}, u32[]{:S(2)}) collective-permute-start(bf16[3088,128]{1,0:T(8,128)(2,1)} %get-tuple-element.39), channel_id=1, source_target_pairs={{0,192},{64,128},{128,64},{192,0},{1,193},{65,129},{129,65},{193,1... | collective-permute-start | bytes 2371592 | tf_op jit(solution)/shard_map/ppermute | solution.py:450
  30.4 0.1 select_select_fusion
  30.5 0.0 copy-start.2
  30.5 0.0 copy-start.4
  30.5 0.0 copy-start.8
  30.5 0.0 copy-start.10
  30.6 0.0 copy-start.17
  30.6 0.1 collective-permute-start.11
  30.7 0.1 collective-permute-start.10
  30.8 4.0 %collective-permute-start.9 = (bf16[512,256]{1,0:T(8,128)(2,1)S(1)}, bf16[512,256]{1,0:T(8,128)(2,1)S(1)}, u32[]{:S(2)}, u32[]{:S(2)}) collective-permute-start(bf16[512,256]{1,0:T(8,128)(2,1)S(1)} %get-tuple-element.68.refs_0_), channel_id=1, source_target_pairs={{0,2},{1,3},{2,0},{3,1},{4,6},{5,7},{6,4},{7,5},{8,10},{9,11},{10,... | collective-permute-start | bytes 786440 | tf_op jit(solution)/shard_map/ppermute | solution.py:454
  34.8 7.1 %collective-permute-done.11.refs_3_ = bf16[512,256]{1,0:T(8,128)(2,1)S(1)} collective-permute-done((bf16[512,256]{1,0:T(8,128)(2,1)S(1)}, bf16[512,256]{1,0:T(8,128)(2,1)S(1)}, u32[]{:S(2)}, u32[]{:S(2)}) %collective-permute-start.11) | collective-permute-done | bytes 262176 | tf_op jit(solution)/shard_map/ppermute | solution.py:454
  41.9 0.6 collective-permute-done.9.refs_1_
  42.5 0.1 joined.4.refs_4_
  42.6 0.3 collective-permute-start.15
  42.9 6.6 %collective-permute-start.14 = (bf16[512,256]{1,0:T(8,128)(2,1)S(1)}, bf16[512,256]{1,0:T(8,128)(2,1)S(1)}, u32[]{:S(2)}, u32[]{:S(2)}) collective-permute-start(bf16[512,256]{1,0:T(8,128)(2,1)S(1)} %get-tuple-element.47.refs_0_), channel_id=1, source_target_pairs={{0,56},{1,57},{2,58},{3,59},{4,60},{5,61},{6,62},{7,63},{8,16},{9,... | collective-permute-start | bytes 786440 | tf_op jit(solution)/shard_map/ppermute | solution.py:454
  49.5 6.6 %collective-permute-done.14.refs_3_ = bf16[512,256]{1,0:T(8,128)(2,1)S(1)} collective-permute-done((bf16[512,256]{1,0:T(8,128)(2,1)S(1)}, bf16[512,256]{1,0:T(8,128)(2,1)S(1)}, u32[]{:S(2)}, u32[]{:S(2)}) %collective-permute-start.14) | collective-permute-done | bytes 262176 | tf_op jit(solution)/shard_map/ppermute | solution.py:454
  56.1 3.5 %collective-permute-start.12 = (bf16[512,256]{1,0:T(8,128)(2,1)S(1)}, bf16[512,256]{1,0:T(8,128)(2,1)S(1)}, u32[]{:S(2)}, u32[]{:S(2)}) collective-permute-start(bf16[512,256]{1,0:T(8,128)(2,1)S(1)} %get-tuple-element.47.refs_0_), channel_id=1, source_target_pairs={{0,8},{1,9},{2,10},{3,11},{4,12},{5,13},{6,14},{7,15},{8,0},{9,1},... | collective-permute-start | bytes 786440 | tf_op jit(solution)/shard_map/ppermute | solution.py:454
  59.6 1.6 %collective-permute-start.18 = (bf16[512,256]{1,0:T(8,128)(2,1)S(1)}, bf16[512,256]{1,0:T(8,128)(2,1)S(1)}, u32[]{:S(2)}, u32[]{:S(2)}) collective-permute-start(bf16[512,256]{1,0:T(8,128)(2,1)S(1)} %get-tuple-element.51.refs_0_), channel_id=1, source_target_pairs={{0,6},{1,7},{2,4},{3,5},{4,2},{5,3},{6,0},{7,1},{8,14},{9,15},{10,... | collective-permute-start | bytes 786440 | tf_op jit(solution)/shard_map/ppermute | solution.py:454
  61.2 0.1 collective-permute-start.5
  61.4 3.0 %collective-permute-done.13.refs_2_ = bf16[512,256]{1,0:T(8,128)(2,1)S(1)} collective-permute-done((bf16[512,256]{1,0:T(8,128)(2,1)S(1)}, bf16[512,256]{1,0:T(8,128)(2,1)S(1)}, u32[]{:S(2)}, u32[]{:S(2)}) %collective-permute-start.13) | collective-permute-done | bytes 262176 | tf_op jit(solution)/shard_map/ppermute | solution.py:454
  64.4 0.3 collective-permute-start.4
  64.7 5.2 %collective-permute-done.12.refs_1_ = bf16[512,256]{1,0:T(8,128)(2,1)S(1)} collective-permute-done((bf16[512,256]{1,0:T(8,128)(2,1)S(1)}, bf16[512,256]{1,0:T(8,128)(2,1)S(1)}, u32[]{:S(2)}, u32[]{:S(2)}) %collective-permute-start.12) | collective-permute-done | bytes 262176 | tf_op jit(solution)/shard_map/ppermute | solution.py:454
  69.9 0.9 collective-permute-start.17
  70.9 1.2 collective-permute-start.16
  72.1 1.0 copy-done.12
  73.2 1.0 copy-done.14
  74.2 0.7 first1.1.h0
  74.9 0.1 joined.3.refs_4_
  75.0 5.6 %collective-permute-done.17.refs_2_ = bf16[512,256]{1,0:T(8,128)(2,1)S(1)} collective-permute-done((bf16[512,256]{1,0:T(8,128)(2,1)S(1)}, bf16[512,256]{1,0:T(8,128)(2,1)S(1)}, u32[]{:S(2)}, u32[]{:S(2)}) %collective-permute-start.17) | collective-permute-done | bytes 262176 | tf_op jit(solution)/shard_map/ppermute | solution.py:454
  80.6 3.3 %collective-permute-done.16.refs_1_ = bf16[512,256]{1,0:T(8,128)(2,1)S(1)} collective-permute-done((bf16[512,256]{1,0:T(8,128)(2,1)S(1)}, bf16[512,256]{1,0:T(8,128)(2,1)S(1)}, u32[]{:S(2)}, u32[]{:S(2)}) %collective-permute-start.16) | collective-permute-done | bytes 262176 | tf_op jit(solution)/shard_map/ppermute | solution.py:454
  83.9 0.1 joined.5.refs_4_
  84.0 0.1 arrived.1.h
  84.2 0.2 weights1.1.w
  84.4 0.5 sender1.1
  84.9 0.1 collective-permute-start.19
  85.0 6.3 %collective-permute-start.20 = (bf16[128,512]{1,0:T(8,128)(2,1)S(1)}, bf16[128,512]{1,0:T(8,128)(2,1)S(1)}, u32[]{:S(2)}, u32[]{:S(2)}) collective-permute-start(bf16[128,512]{1,0:T(8,128)(2,1)S(1)} %get-tuple-element.54), channel_id=1, source_target_pairs={{0,63},{1,2},{2,1},{3,4},{4,3},{5,6},{6,5},{7,8},{8,7},{9,10},{10,... | collective-permute-start | bytes 393224 | tf_op jit(solution)/shard_map/ppermute | solution.py:454
  91.3 2.6 %collective-permute-done.20.outer = bf16[128,512]{1,0:T(8,128)(2,1)S(1)} collective-permute-done((bf16[128,512]{1,0:T(8,128)(2,1)S(1)}, bf16[128,512]{1,0:T(8,128)(2,1)S(1)}, u32[]{:S(2)}, u32[]{:S(2)}) %collective-permute-start.20) | collective-permute-done | bytes 131104 | tf_op jit(solution)/shard_map/ppermute | solution.py:454
  94.0 1.3 %tiles1.1 = (bf16[24,128,128]{2,1,0:T(8,128)(2,1)S(1)}, s32[8,128]{1,0:T(8,128)S(1)}, f32[1,512]{1,0:T(1,128)S(1)}) custom-call(bf16[3088,128]{1,0:T(8,128)(2,1)S(1)} %copy-done, bf16[3088,128]{1,0:T(8,128)(2,1)S(1)} %collective-permute-done.2.near, bf16[3088,128]{1,0:T(8,128)(2,1)S(1)} %collective-permute-done.3.far, ...), custom_call_target="tpu_custom_call" | custom-call | bytes 2000000 | tf_op jit(solution)/shard_map/tiles1/pallas_call | solution.py:374
  95.3 2.4 %section1.1.h = bf16[512,512]{1,0:T(8,128)(2,1)S(1)} custom-call(s32[8,128]{1,0:T(8,128)S(1)} %get-tuple-element.48.codes, f32[1,512]{1,0:T(1,128)S(1)} %get-tuple-element.49.gain, bf16[24,128,128]{2,1,0:T(8,128)(2,1)S(1)} %get-tuple-element.50.tiles, bf16[4,512,512]{2,1,0:T(8,128)(2,1)S(1)} %weights1.1.w, bf16[512,512]{1,0:T(8,128)(2,1)S(1)} %arrived.1.h, ...), custom_call_target="tpu_custom_call" | custom-call | flops 1500000000 | bytes 4000000 | tf_op jit(solution)/shard_map/section1/pallas_call | solution.py:401
  97.7 0.2 weights2.1.w
  97.9 0.5 sender2.1
  98.4 0.8 collective-permute-start.22
  99.2 5.1 %collective-permute-start.23 = (bf16[128,512]{1,0:T(8,128)(2,1)S(1)}, bf16[128,512]{1,0:T(8,128)(2,1)S(1)}, u32[]{:S(2)}, u32[]{:S(2)}) collective-permute-start(bf16[128,512]{1,0:T(8,128)(2,1)S(1)} %get-tuple-element.58), channel_id=1, source_target_pairs={{0,63},{1,2},{2,1},{3,4},{4,3},{5,6},{6,5},{7,8},{8,7},{9,10},{10,... | collective-permute-start | bytes 393224 | tf_op jit(solution)/shard_map/ppermute | solution.py:454
  104.3 2.6 %collective-permute-done.23.outer = bf16[128,512]{1,0:T(8,128)(2,1)S(1)} collective-permute-done((bf16[128,512]{1,0:T(8,128)(2,1)S(1)}, bf16[128,512]{1,0:T(8,128)(2,1)S(1)}, u32[]{:S(2)}, u32[]{:S(2)}) %collective-permute-start.23) | collective-permute-done | bytes 131104 | tf_op jit(solution)/shard_map/ppermute | solution.py:454
  106.9 1.3 %tiles2.1 = (bf16[24,128,128]{2,1,0:T(8,128)(2,1)S(1)}, s32[8,128]{1,0:T(8,128)S(1)}, f32[1,512]{1,0:T(1,128)S(1)}) custom-call(bf16[3088,128]{1,0:T(8,128)(2,1)S(1)} %copy-done, bf16[3088,128]{1,0:T(8,128)(2,1)S(1)} %collective-permute-done.2.near, bf16[3088,128]{1,0:T(8,128)(2,1)S(1)} %collective-permute-done.3.far, ...), custom_call_target="tpu_custom_call" | custom-call | bytes 2000000 | tf_op jit(solution)/shard_map/tiles2/pallas_call | solution.py:374
  108.2 2.4 %section2.1.h = bf16[512,512]{1,0:T(8,128)(2,1)S(1)} custom-call(s32[8,128]{1,0:T(8,128)S(1)} %get-tuple-element.60.codes, f32[1,512]{1,0:T(1,128)S(1)} %get-tuple-element.61.gain, bf16[24,128,128]{2,1,0:T(8,128)(2,1)S(1)} %get-tuple-element.62.tiles, bf16[4,512,512]{2,1,0:T(8,128)(2,1)S(1)} %weights2.1.w, bf16[512,512]{1,0:T(8,128)(2,1)S(1)} %section1.1.h, ...), custom_call_target="tpu_custom_call" | custom-call | flops 1500000000 | bytes 4000000 | tf_op jit(solution)/shard_map/section2/pallas_call | solution.py:401
  110.7 0.2 weights3.1.w
  110.9 0.5 sender3.1
  111.4 0.6 collective-permute-start.25
  112.0 5.1 %collective-permute-start.26 = (bf16[128,512]{1,0:T(8,128)(2,1)S(1)}, bf16[128,512]{1,0:T(8,128)(2,1)S(1)}, u32[]{:S(2)}, u32[]{:S(2)}) collective-permute-start(bf16[128,512]{1,0:T(8,128)(2,1)S(1)} %get-tuple-element.65), channel_id=1, source_target_pairs={{0,63},{1,2},{2,1},{3,4},{4,3},{5,6},{6,5},{7,8},{8,7},{9,10},{10,... | collective-permute-start | bytes 393224 | tf_op jit(solution)/shard_map/ppermute | solution.py:454
  117.0 1.3 %tiles3.1 = (bf16[24,128,128]{2,1,0:T(8,128)(2,1)S(1)}, s32[8,128]{1,0:T(8,128)S(1)}, f32[1,512]{1,0:T(1,128)S(1)}) custom-call(bf16[3088,128]{1,0:T(8,128)(2,1)S(1)} %copy-done, bf16[3088,128]{1,0:T(8,128)(2,1)S(1)} %collective-permute-done.2.near, bf16[3088,128]{1,0:T(8,128)(2,1)S(1)} %collective-permute-done.3.far, ...), custom_call_target="tpu_custom_call" | custom-call | bytes 2000000 | tf_op jit(solution)/shard_map/tiles3/pallas_call | solution.py:374
  118.3 1.4 %collective-permute-done.26.outer = bf16[128,512]{1,0:T(8,128)(2,1)S(1)} collective-permute-done((bf16[128,512]{1,0:T(8,128)(2,1)S(1)}, bf16[128,512]{1,0:T(8,128)(2,1)S(1)}, u32[]{:S(2)}, u32[]{:S(2)}) %collective-permute-start.26) | collective-permute-done | bytes 131104 | tf_op jit(solution)/shard_map/ppermute | solution.py:454
  119.7 3.2 %section3.1 = bf16[512,512]{1,0:T(8,128)(2,1)} custom-call(s32[8,128]{1,0:T(8,128)S(1)} %get-tuple-element.40.codes, f32[1,512]{1,0:T(1,128)S(1)} %get-tuple-element.41.gain, bf16[24,128,128]{2,1,0:T(8,128)(2,1)S(1)} %get-tuple-element.42.tiles, bf16[4,512,512]{2,1,0:T(8,128)(2,1)S(1)} %weights3.1.w, bf16[512,512]{1,0:T(8,128)(2,1)S(1)} %section2.1.h, ...), custom_call_target="tpu_custom_call" | custom-call | flops 1500000000 | bytes 4000000 | tf_op jit(solution)/shard_map/section3/pallas_call | solution.py:401
  (49 shorter events, 0.2 us)
Async XLA Ops:
  0.0 10.9 %copy-start.7 = (bf16[1,1,512,512]{3,2,1,0:T(8,128)(2,1)S(1)}, bf16[1,1,512,512]{3,2,1,0:T(8,128)(2,1)}, u32[]{:S(2)}) copy-start(bf16[1,1,512,512]{3,2,1,0:T(8,128)(2,1)} %refs_3_.5) | copy-start | bytes 1572868
  0.0 10.9 %copy-start.5 = (bf16[1,1,512,512]{3,2,1,0:T(8,128)(2,1)S(1)}, bf16[1,1,512,512]{3,2,1,0:T(8,128)(2,1)}, u32[]{:S(2)}) copy-start(bf16[1,1,512,512]{3,2,1,0:T(8,128)(2,1)} %refs_2_.5) | copy-start | bytes 1572868
  0.0 10.9 %copy-start.3 = (bf16[1,1,512,512]{3,2,1,0:T(8,128)(2,1)S(1)}, bf16[1,1,512,512]{3,2,1,0:T(8,128)(2,1)}, u32[]{:S(2)}) copy-start(bf16[1,1,512,512]{3,2,1,0:T(8,128)(2,1)} %refs_1_.5) | copy-start | bytes 1572868
  0.0 10.9 %copy-start.1 = (bf16[1,1,512,512]{3,2,1,0:T(8,128)(2,1)S(1)}, bf16[1,1,512,512]{3,2,1,0:T(8,128)(2,1)}, u32[]{:S(2)}) copy-start(bf16[1,1,512,512]{3,2,1,0:T(8,128)(2,1)} %refs_0_.7) | copy-start | bytes 1572868
  2.4 12.9 %collective-permute-start = (bf16[4,128,512]{2,1,0:T(8,128)(2,1)}, bf16[4,128,512]{2,1,0:T(8,128)(2,1)S(1)}, u32[]{:S(2)}, u32[]{:S(2)}) collective-permute-start(bf16[4,128,512]{2,1,0:T(8,128)(2,1)} %get-tuple-element.36), channel_id=1, source_target_pairs={{0,1},{1,0},{2,3},{3,2},{4,5},{5,4},{6,7},{7,6},{8,9},{9,8},{10,11... | collective-permute-start | bytes 1572872 | tf_op jit(solution)/shard_map/ppermute | solution.py:454
  2.5 15.5 %collective-permute-start.1 = (bf16[4,128,512]{2,1,0:T(8,128)(2,1)}, bf16[4,128,512]{2,1,0:T(8,128)(2,1)S(1)}, u32[]{:S(2)}, u32[]{:S(2)}) collective-permute-start(bf16[4,128,512]{2,1,0:T(8,128)(2,1)} %get-tuple-element.37), channel_id=1, source_target_pairs={{0,63},{1,2},{2,1},{3,4},{4,3},{5,6},{6,5},{7,8},{8,7},{9,10},{10,... | collective-permute-start | bytes 1572872 | tf_op jit(solution)/shard_map/ppermute | solution.py:454
  11.1 19.3 %collective-permute-start.8 = (bf16[512,256]{1,0:T(8,128)(2,1)S(1)}, bf16[512,256]{1,0:T(8,128)(2,1)S(1)}, u32[]{:S(2)}, u32[]{:S(2)}) collective-permute-start(bf16[512,256]{1,0:T(8,128)(2,1)S(1)} %select_bitcast_fusion), channel_id=1, source_target_pairs={{0,192},{64,128},{128,64},{192,0},{1,193},{65,129},{129,65},{193,1... | collective-permute-start | bytes 786440 | tf_op jit(solution)/shard_map/ppermute | solution.py:450
  11.6 18.8 %collective-permute-start.7 = (bf16[512,256]{1,0:T(8,128)(2,1)S(1)}, bf16[512,256]{1,0:T(8,128)(2,1)S(1)}, u32[]{:S(2)}, u32[]{:S(2)}) collective-permute-start(bf16[512,256]{1,0:T(8,128)(2,1)S(1)} %select_bitcast_fusion), channel_id=1, source_target_pairs={{0,128},{64,192},{128,0},{192,64},{1,129},{65,193},{129,1},{193,65... | collective-permute-start | bytes 786440 | tf_op jit(solution)/shard_map/ppermute | solution.py:450
  14.0 16.4 %collective-permute-start.6 = (bf16[512,256]{1,0:T(8,128)(2,1)S(1)}, bf16[512,256]{1,0:T(8,128)(2,1)S(1)}, u32[]{:S(2)}, u32[]{:S(2)}) collective-permute-start(bf16[512,256]{1,0:T(8,128)(2,1)S(1)} %select_bitcast_fusion), channel_id=1, source_target_pairs={{0,64},{64,0},{128,192},{192,128},{1,65},{65,1},{129,193},{193,129... | collective-permute-start | bytes 786440 | tf_op jit(solution)/shard_map/ppermute | solution.py:450
  15.2 2.7 %copy-start.11 = (bf16[4,128,512]{2,1,0:T(8,128)(2,1)}, bf16[4,128,512]{2,1,0:T(8,128)(2,1)S(1)}, u32[]{:S(2)}) copy-start(bf16[4,128,512]{2,1,0:T(8,128)(2,1)S(1)} %collective-permute-done.inner) | copy-start | bytes 1572868
  18.0 0.8 copy-start.13
  22.1 37.4 %collective-permute-start.3 = (bf16[3088,128]{1,0:T(8,128)(2,1)}, bf16[3088,128]{1,0:T(8,128)(2,1)S(1)}, u32[]{:S(2)}, u32[]{:S(2)}) collective-permute-start(bf16[3088,128]{1,0:T(8,128)(2,1)} %get-tuple-element.39), channel_id=1, source_target_pairs={{0,192},{64,128},{128,64},{192,0},{1,193},{65,129},{129,65},{193,1... | collective-permute-start | bytes 2371592 | tf_op jit(solution)/shard_map/ppermute | solution.py:450
  30.4 41.7 %copy-start.9 = (bf16[4,512,512]{2,1,0:T(8,128)(2,1)S(1)}, bf16[4,512,512]{2,1,0:T(8,128)(2,1)}, u32[]{:S(2)}) copy-start(bf16[4,512,512]{2,1,0:T(8,128)(2,1)} %samples.3) | copy-start | bytes 6291460
  30.5 41.6 %copy-start.2 = (bf16[1,1,512,512]{3,2,1,0:T(8,128)(2,1)S(1)}, bf16[1,1,512,512]{3,2,1,0:T(8,128)(2,1)}, u32[]{:S(2)}) copy-start(bf16[1,1,512,512]{3,2,1,0:T(8,128)(2,1)} %refs_0_.7) | copy-start | bytes 1572868
  30.5 41.6 %copy-start.4 = (bf16[1,1,512,512]{3,2,1,0:T(8,128)(2,1)S(1)}, bf16[1,1,512,512]{3,2,1,0:T(8,128)(2,1)}, u32[]{:S(2)}) copy-start(bf16[1,1,512,512]{3,2,1,0:T(8,128)(2,1)} %refs_1_.5) | copy-start | bytes 1572868
  30.5 41.6 %copy-start.6 = (bf16[1,1,512,512]{3,2,1,0:T(8,128)(2,1)S(1)}, bf16[1,1,512,512]{3,2,1,0:T(8,128)(2,1)}, u32[]{:S(2)}) copy-start(bf16[1,1,512,512]{3,2,1,0:T(8,128)(2,1)} %refs_2_.5) | copy-start | bytes 1572868
  30.5 41.6 %copy-start.8 = (bf16[1,1,512,512]{3,2,1,0:T(8,128)(2,1)S(1)}, bf16[1,1,512,512]{3,2,1,0:T(8,128)(2,1)}, u32[]{:S(2)}) copy-start(bf16[1,1,512,512]{3,2,1,0:T(8,128)(2,1)} %refs_3_.5) | copy-start | bytes 1572868
  30.5 41.6 %copy-start.10 = (bf16[1,4,6,128,128]{4,3,2,1,0:T(8,128)(2,1)S(1)}, bf16[1,4,6,128,128]{4,3,2,1,0:T(8,128)(2,1)}, u32[]{:S(2)}) copy-start(bf16[1,4,6,128,128]{4,3,2,1,0:T(8,128)(2,1)} %tiles.3) | copy-start | bytes 2359300
  30.5 41.6 %copy-start.15 = (s32[1,4,6]{2,1,0:T(4,128)S(1)}, s32[1,4,6]{2,1,0:T(4,128)}, u32[]{:S(2)}) copy-start(s32[1,4,6]{2,1,0:T(4,128)} %src.3) | copy-start | bytes 292
  30.6 41.6 %copy-start.16 = (f32[1,1,512]{2,1,0:T(1,128)S(1)}, f32[1,1,512]{2,1,0:T(1,128)}, u32[]{:S(2)}) copy-start(f32[1,1,512]{2,1,0:T(1,128)} %gain.3) | copy-start | bytes 6148
  30.6 41.6 %copy-start.17 = (s32[1,4]{1,0:T(1,128)S(1)}, s32[1,4]{1,0:T(1,128)}, u32[]{:S(2)}) copy-start(s32[1,4]{1,0:T(1,128)} %cnt.3) | copy-start | bytes 52
  30.6 11.3 %collective-permute-start.11 = (bf16[512,256]{1,0:T(8,128)(2,1)S(1)}, bf16[512,256]{1,0:T(8,128)(2,1)S(1)}, u32[]{:S(2)}, u32[]{:S(2)}) collective-permute-start(bf16[512,256]{1,0:T(8,128)(2,1)S(1)} %get-tuple-element.68.refs_0_), channel_id=1, source_target_pairs={{0,6},{1,7},{2,4},{3,5},{4,2},{5,3},{6,0},{7,1},{8,14},{9,15},{10,... | collective-permute-start | bytes 786440 | tf_op jit(solution)/shard_map/ppermute | solution.py:454
  30.7 11.2 %collective-permute-start.10 = (bf16[512,256]{1,0:T(8,128)(2,1)S(1)}, bf16[512,256]{1,0:T(8,128)(2,1)S(1)}, u32[]{:S(2)}, u32[]{:S(2)}) collective-permute-start(bf16[512,256]{1,0:T(8,128)(2,1)S(1)} %get-tuple-element.68.refs_0_), channel_id=1, source_target_pairs={{0,4},{1,5},{2,6},{3,7},{4,0},{5,1},{6,2},{7,3},{8,12},{9,13},{10,... | collective-permute-start | bytes 786440 | tf_op jit(solution)/shard_map/ppermute | solution.py:454
  30.8 11.7 %collective-permute-start.9 = (bf16[512,256]{1,0:T(8,128)(2,1)S(1)}, bf16[512,256]{1,0:T(8,128)(2,1)S(1)}, u32[]{:S(2)}, u32[]{:S(2)}) collective-permute-start(bf16[512,256]{1,0:T(8,128)(2,1)S(1)} %get-tuple-element.68.refs_0_), channel_id=1, source_target_pairs={{0,2},{1,3},{2,0},{3,1},{4,6},{5,7},{6,4},{7,5},{8,10},{9,11},{10,... | collective-permute-start | bytes 786440 | tf_op jit(solution)/shard_map/ppermute | solution.py:454
  34.8 26.5 %collective-permute-start.2 = (bf16[3088,128]{1,0:T(8,128)(2,1)}, bf16[3088,128]{1,0:T(8,128)(2,1)S(1)}, u32[]{:S(2)}, u32[]{:S(2)}) collective-permute-start(bf16[3088,128]{1,0:T(8,128)(2,1)} %get-tuple-element.38.own), channel_id=1, source_target_pairs={{0,64},{64,0},{128,192},{192,128},{1,65},{65,1},{129,193},{193,129... | collective-permute-start | bytes 2371592 | tf_op jit(solution)/shard_map/ppermute | solution.py:450
  42.6 41.6 %collective-permute-start.15 = (bf16[4,512,256]{2,1,0:T(8,128)(2,1)S(1)}, bf16[4,512,256]{2,1,0:T(8,128)(2,1)S(1)}, u32[]{:S(2)}, u32[]{:S(2)}) collective-permute-start(bf16[4,512,256]{2,1,0:T(8,128)(2,1)S(1)} %joined.4.refs_4_), channel_id=1, source_target_pairs={{0,1},{1,0},{2,3},{3,2},{4,5},{5,4},{6,7},{7,6},{8,9},{9,8},{10,11... | collective-permute-start | bytes 3145736 | tf_op jit(solution)/shard_map/ppermute | solution.py:454
  42.9 13.2 %collective-permute-start.14 = (bf16[512,256]{1,0:T(8,128)(2,1)S(1)}, bf16[512,256]{1,0:T(8,128)(2,1)S(1)}, u32[]{:S(2)}, u32[]{:S(2)}) collective-permute-start(bf16[512,256]{1,0:T(8,128)(2,1)S(1)} %get-tuple-element.47.refs_0_), channel_id=1, source_target_pairs={{0,56},{1,57},{2,58},{3,59},{4,60},{5,61},{6,62},{7,63},{8,16},{9,... | collective-permute-start | bytes 786440 | tf_op jit(solution)/shard_map/ppermute | solution.py:454
  49.5 15.0 %collective-permute-start.13 = (bf16[512,256]{1,0:T(8,128)(2,1)S(1)}, bf16[512,256]{1,0:T(8,128)(2,1)S(1)}, u32[]{:S(2)}, u32[]{:S(2)}) collective-permute-start(bf16[512,256]{1,0:T(8,128)(2,1)S(1)} %get-tuple-element.47.refs_0_), channel_id=1, source_target_pairs={{0,16},{1,17},{2,18},{3,19},{4,20},{5,21},{6,22},{7,23},{8,24},{9,... | collective-permute-start | bytes 786440 | tf_op jit(solution)/shard_map/ppermute | solution.py:454
  56.1 13.9 %collective-permute-start.12 = (bf16[512,256]{1,0:T(8,128)(2,1)S(1)}, bf16[512,256]{1,0:T(8,128)(2,1)S(1)}, u32[]{:S(2)}, u32[]{:S(2)}) collective-permute-start(bf16[512,256]{1,0:T(8,128)(2,1)S(1)} %get-tuple-element.47.refs_0_), channel_id=1, source_target_pairs={{0,8},{1,9},{2,10},{3,11},{4,12},{5,13},{6,14},{7,15},{8,0},{9,1},... | collective-permute-start | bytes 786440 | tf_op jit(solution)/shard_map/ppermute | solution.py:454
  59.6 11.3 %collective-permute-start.18 = (bf16[512,256]{1,0:T(8,128)(2,1)S(1)}, bf16[512,256]{1,0:T(8,128)(2,1)S(1)}, u32[]{:S(2)}, u32[]{:S(2)}) collective-permute-start(bf16[512,256]{1,0:T(8,128)(2,1)S(1)} %get-tuple-element.51.refs_0_), channel_id=1, source_target_pairs={{0,6},{1,7},{2,4},{3,5},{4,2},{5,3},{6,0},{7,1},{8,14},{9,15},{10,... | collective-permute-start | bytes 786440 | tf_op jit(solution)/shard_map/ppermute | solution.py:454
  61.2 22.8 %collective-permute-start.5 = (bf16[1552,128]{1,0:T(8,128)(2,1)S(1)}, bf16[1552,128]{1,0:T(8,128)(2,1)S(1)}, u32[]{:S(2)}, u32[]{:S(2)}) collective-permute-start(bf16[1552,128]{1,0:T(8,128)(2,1)S(1)} %slice.9), channel_id=1, source_target_pairs={{0,64},{64,0},{128,192},{192,128},{1,65},{65,1},{129,193},{193,129... | collective-permute-start | bytes 1191944 | tf_op jit(solution)/shard_map/ppermute | solution.py:450
  64.4 19.6 %collective-permute-start.4 = (bf16[1536,128]{1,0:T(8,128)(2,1)S(1)}, bf16[1536,128]{1,0:T(8,128)(2,1)S(1)}, u32[]{:S(2)}, u32[]{:S(2)}) collective-permute-start(bf16[1536,128]{1,0:T(8,128)(2,1)S(1)} %slice.8), channel_id=1, source_target_pairs={{0,192},{64,128},{128,64},{192,0},{1,193},{65,129},{129,65},{193,1... | collective-permute-start | bytes 1179656 | tf_op jit(solution)/shard_map/ppermute | solution.py:450
  69.9 10.7 %collective-permute-start.17 = (bf16[512,256]{1,0:T(8,128)(2,1)S(1)}, bf16[512,256]{1,0:T(8,128)(2,1)S(1)}, u32[]{:S(2)}, u32[]{:S(2)}) collective-permute-start(bf16[512,256]{1,0:T(8,128)(2,1)S(1)} %get-tuple-element.51.refs_0_), channel_id=1, source_target_pairs={{0,4},{1,5},{2,6},{3,7},{4,0},{5,1},{6,2},{7,3},{8,12},{9,13},{10,... | collective-permute-start | bytes 786440 | tf_op jit(solution)/shard_map/ppermute | solution.py:454
  70.9 13.0 %collective-permute-start.16 = (bf16[512,256]{1,0:T(8,128)(2,1)S(1)}, bf16[512,256]{1,0:T(8,128)(2,1)S(1)}, u32[]{:S(2)}, u32[]{:S(2)}) collective-permute-start(bf16[512,256]{1,0:T(8,128)(2,1)S(1)} %get-tuple-element.51.refs_0_), channel_id=1, source_target_pairs={{0,2},{1,3},{2,0},{3,1},{4,6},{5,7},{6,4},{7,5},{8,10},{9,11},{10,... | collective-permute-start | bytes 786440 | tf_op jit(solution)/shard_map/ppermute | solution.py:454
  72.1 1.0 copy-start.12
  73.2 1.0 copy-start.14
  84.4 9.6 %copy-start = (bf16[3088,128]{1,0:T(8,128)(2,1)S(1)}, bf16[3088,128]{1,0:T(8,128)(2,1)}, u32[]{:S(2)}) copy-start(bf16[3088,128]{1,0:T(8,128)(2,1)} %get-tuple-element.38.own) | copy-start | bytes 2371588
  84.9 6.4 %collective-permute-start.19 = (bf16[128,512]{1,0:T(8,128)(2,1)S(1)}, bf16[128,512]{1,0:T(8,128)(2,1)S(1)}, u32[]{:S(2)}, u32[]{:S(2)}) collective-permute-start(bf16[128,512]{1,0:T(8,128)(2,1)S(1)} %get-tuple-element.53), channel_id=1, source_target_pairs={{0,1},{1,0},{2,3},{3,2},{4,5},{5,4},{6,7},{7,6},{8,9},{9,8},{10,11... | collective-permute-start | bytes 393224 | tf_op jit(solution)/shard_map/ppermute | solution.py:454
  85.0 8.9 %collective-permute-start.20 = (bf16[128,512]{1,0:T(8,128)(2,1)S(1)}, bf16[128,512]{1,0:T(8,128)(2,1)S(1)}, u32[]{:S(2)}, u32[]{:S(2)}) collective-permute-start(bf16[128,512]{1,0:T(8,128)(2,1)S(1)} %get-tuple-element.54), channel_id=1, source_target_pairs={{0,63},{1,2},{2,1},{3,4},{4,3},{5,6},{6,5},{7,8},{8,7},{9,10},{10,... | collective-permute-start | bytes 393224 | tf_op jit(solution)/shard_map/ppermute | solution.py:454
  94.0 3.7 %collective-permute-start.21 = (bf16[4,512,256]{2,1,0:T(8,128)(2,1)S(1)}, bf16[4,512,256]{2,1,0:T(8,128)(2,1)S(1)}, u32[]{:S(2)}, u32[]{:S(2)}) collective-permute-start(bf16[4,512,256]{2,1,0:T(8,128)(2,1)S(1)} %joined.5.refs_4_), channel_id=1, source_target_pairs={{0,1},{1,0},{2,3},{3,2},{4,5},{5,4},{6,7},{7,6},{8,9},{9,8},{10,11... | collective-permute-start | bytes 3145736 | tf_op jit(solution)/shard_map/ppermute | solution.py:454
  98.4 5.9 %collective-permute-start.22 = (bf16[128,512]{1,0:T(8,128)(2,1)S(1)}, bf16[128,512]{1,0:T(8,128)(2,1)S(1)}, u32[]{:S(2)}, u32[]{:S(2)}) collective-permute-start(bf16[128,512]{1,0:T(8,128)(2,1)S(1)} %get-tuple-element.57), channel_id=1, source_target_pairs={{0,1},{1,0},{2,3},{3,2},{4,5},{5,4},{6,7},{7,6},{8,9},{9,8},{10,11... | collective-permute-start | bytes 393224 | tf_op jit(solution)/shard_map/ppermute | solution.py:454
  99.2 7.7 %collective-permute-start.23 = (bf16[128,512]{1,0:T(8,128)(2,1)S(1)}, bf16[128,512]{1,0:T(8,128)(2,1)S(1)}, u32[]{:S(2)}, u32[]{:S(2)}) collective-permute-start(bf16[128,512]{1,0:T(8,128)(2,1)S(1)} %get-tuple-element.58), channel_id=1, source_target_pairs={{0,63},{1,2},{2,1},{3,4},{4,3},{5,6},{6,5},{7,8},{8,7},{9,10},{10,... | collective-permute-start | bytes 393224 | tf_op jit(solution)/shard_map/ppermute | solution.py:454
  106.9 3.7 %collective-permute-start.24 = (bf16[4,512,256]{2,1,0:T(8,128)(2,1)S(1)}, bf16[4,512,256]{2,1,0:T(8,128)(2,1)S(1)}, u32[]{:S(2)}, u32[]{:S(2)}) collective-permute-start(bf16[4,512,256]{2,1,0:T(8,128)(2,1)S(1)} %joined.3.refs_4_), channel_id=1, source_target_pairs={{0,1},{1,0},{2,3},{3,2},{4,5},{5,4},{6,7},{7,6},{8,9},{9,8},{10,11... | collective-permute-start | bytes 3145736 | tf_op jit(solution)/shard_map/ppermute | solution.py:454
  111.4 6.9 %collective-permute-start.25 = (bf16[128,512]{1,0:T(8,128)(2,1)S(1)}, bf16[128,512]{1,0:T(8,128)(2,1)S(1)}, u32[]{:S(2)}, u32[]{:S(2)}) collective-permute-start(bf16[128,512]{1,0:T(8,128)(2,1)S(1)} %get-tuple-element.64), channel_id=1, source_target_pairs={{0,1},{1,0},{2,3},{3,2},{4,5},{5,4},{6,7},{7,6},{8,9},{9,8},{10,11... | collective-permute-start | bytes 393224 | tf_op jit(solution)/shard_map/ppermute | solution.py:454
  112.0 7.7 %collective-permute-start.26 = (bf16[128,512]{1,0:T(8,128)(2,1)S(1)}, bf16[128,512]{1,0:T(8,128)(2,1)S(1)}, u32[]{:S(2)}, u32[]{:S(2)}) collective-permute-start(bf16[128,512]{1,0:T(8,128)(2,1)S(1)} %get-tuple-element.65), channel_id=1, source_target_pairs={{0,63},{1,2},{2,1},{3,4},{4,3},{5,6},{6,5},{7,8},{8,7},{9,10},{10,... | collective-permute-start | bytes 393224 | tf_op jit(solution)/shard_map/ppermute | solution.py:454

commit v7 on v3

--- a/solution.py
+++ b/solution.py
@@ -476,12 +476,14 @@
 
     over_y, over_z = [by_y(x) for x in (1, 2, 3)], [Z_EVEN, Z_FAR, Z_ODD]
     x1, x2, x3 = after((x1, x2, x3), own, own_far)
-    ring1 = ring(jnp.where(p == 2, x3, jnp.where(p == 3, x2, x1)), over_y)
+    then = jnp.where(p == 2, x3, jnp.where(p == 3, x2, x1))
+    ring1 = [then] + [over_dom(then, route) for route in over_y]
     then = jnp.where(p == 0, x2, jnp.where(p == 1, x3, x1))
     last = jnp.where(p == 0, x3, jnp.where(p == 1, x2, x1))
-    then, last = after((then, last), near, far, ring1)
-    ring2, ring3 = ring(then, over_z), ring(last, over_y)
-    stages = {1: both(joined(ring1)), 2: both(joined(ring2))}
+    stages = {1: both(joined(ring1))}
+    then, last = after((then, last), near, far, stages[1])
+    ring2, ring3 = [then] + [over_dom(then, route) for route in over_z], ring(last, over_y)
+    stages[2] = both(joined(ring2))
     h = arrived_call(h0, near, far, mixed_a, mixed_b)
     for section in range(1, SEG):
         if section == 2:

time: 114 us -> 112 us (0.982)
  waiting for transfers between devices: 50.5 us -> 37.9 us
  starting transfers between devices: 37.6 us -> 48 us
    ppermute x20, waiting for transfers between devices: 44.2 us -> 24.9 us  [over_dom(): return lax.ppermute(value, 'dom', pairs)]
    ppermute x20, starting transfers between devices: 26 us -> 35.9 us  [over_dom(): return lax.ppermute(value, 'dom', pairs)]
    ppermute x7, waiting for transfers between devices: 6.24 us -> 13 us  [over_segments(): return lax.ppermute(value, 'segment', by_segment(x))]
  transfers between devices with their start and end apart: 27 -> 27, of which waited for: 13 -> 14; matrix products, arithmetic and copies ran while one was open for 0% -> 0% of each run, Pallas kernels for 13% -> 13%
where the time goes in v7:
time: 112 us
  starting transfers between devices  48 us (43%)
  waiting for transfers between devices  37.9 us (34%)
  Pallas kernels  18.8 us (17%)
  local copies, waits for them, and re-layouts  3.78 us (3%)
  other arithmetic  2.62 us (2%)
    ppermute x20, starting transfers between devices, over_dom(): return lax.ppermute(value, 'dom', pairs)  35.9 us
    ppermute x20, waiting for transfers between devices, over_dom(): return lax.ppermute(value, 'dom', pairs)  24.9 us
    ppermute x7, waiting for transfers between devices, over_segments(): return lax.ppermute(value, 'segment', by_segment(x))  13 us
    ppermute x7, starting transfers between devices, over_segments(): return lax.ppermute(value, 'segment', by_segment(x))  12.1 us
    pallas_call x3, Pallas kernels, section_call(): pl.pallas_call(section_kernel, out_shape=jax.ShapeDtypeStruct((BD * BLK,...  8.09 us
    pallas_call x2, Pallas kernels, first_call(): pl.pallas_call(functools.partial(first_kernel, order), out_shape=[jax.Sha...  4.04 us
    pallas_call x3, Pallas kernels, tiles_call(): pl.pallas_call(functools.partial(tiles_kernel, section), out_shape=[jax.S...  3.83 us
    unnamed x36, local copies, waits for them, and re-layouts  3.73 us
  transfers between devices with their start and end apart: 27, of which 14 were waited for; matrix products, arithmetic and copies ran while one was open for 0% of the time, Pallas kernels for 13%

profile of v7, /device:TPU:6, one launch (start us, length us, event | category | flops | bytes accessed | tf_op | source)
XLA Modules:
  0.0 111.6 jit_solution(5559582081418143275)
XLA Ops:
  0.0 2.4 %broadcast_select_fusion = (bf16[4,128,512]{2,1,0:T(8,128)(2,1)}, bf16[4,128,512]{2,1,0:T(8,128)(2,1)}) fusion(pred[]{:T(512)S(6)} %eq.25, bf16[4,512,512]{2,1,0:T(8,128)(2,1)} %samples.3), kind=kLoop, calls=%fused_computation | loop fusion | flops 524288 | bytes 2097153 | tf_op jit(solution)/shard_map/jit(_where)/select_n | solution.py:453
  2.4 7.7 %collective-permute-start.1 = (bf16[4,128,512]{2,1,0:T(8,128)(2,1)}, bf16[4,128,512]{2,1,0:T(8,128)(2,1)S(1)}, u32[]{:S(2)}, u32[]{:S(2)}) collective-permute-start(bf16[4,128,512]{2,1,0:T(8,128)(2,1)} %get-tuple-element.67), channel_id=1, source_target_pairs={{0,63},{1,2},{2,1},{3,4},{4,3},{5,6},{6,5},{7,8},{8,7},{9,10},{10,... | collective-permute-start | bytes 1572872 | tf_op jit(solution)/shard_map/ppermute | solution.py:442
  10.2 0.2 select_bitcast_fusion
  10.4 0.6 collective-permute-start.8
  10.9 2.4 %collective-permute-start.7 = (bf16[512,256]{1,0:T(8,128)(2,1)S(1)}, bf16[512,256]{1,0:T(8,128)(2,1)S(1)}, u32[]{:S(2)}, u32[]{:S(2)}) collective-permute-start(bf16[512,256]{1,0:T(8,128)(2,1)S(1)} %select_bitcast_fusion), channel_id=1, source_target_pairs={{0,128},{64,192},{128,0},{192,64},{1,129},{65,193},{129,1},{193,65... | collective-permute-start | bytes 786440 | tf_op jit(solution)/shard_map/ppermute | solution.py:438
  13.3 1.2 %collective-permute-start.6 = (bf16[512,256]{1,0:T(8,128)(2,1)S(1)}, bf16[512,256]{1,0:T(8,128)(2,1)S(1)}, u32[]{:S(2)}, u32[]{:S(2)}) collective-permute-start(bf16[512,256]{1,0:T(8,128)(2,1)S(1)} %select_bitcast_fusion), channel_id=1, source_target_pairs={{0,64},{64,0},{128,192},{192,128},{1,65},{65,1},{129,193},{193,129... | collective-permute-start | bytes 786440 | tf_op jit(solution)/shard_map/ppermute | solution.py:438
  14.5 2.7 %collective-permute-done.1.outer = bf16[4,128,512]{2,1,0:T(8,128)(2,1)S(1)} collective-permute-done((bf16[4,128,512]{2,1,0:T(8,128)(2,1)}, bf16[4,128,512]{2,1,0:T(8,128)(2,1)S(1)}, u32[]{:S(2)}, u32[]{:S(2)}) %collective-permute-start.1) | collective-permute-done | bytes 524320 | tf_op jit(solution)/shard_map/ppermute | solution.py:442
  17.2 0.8 copy-done.11
  18.0 0.8 copy-done.13
  18.8 3.4 %first3.1 = (bf16[3088,128]{1,0:T(8,128)(2,1)}, bf16[3088,128]{1,0:T(8,128)(2,1)}) custom-call(s32[1,4,6]{2,1,0:T(4,128)} %src.3, s32[1,4]{1,0:T(1,128)} %cnt.3, f32[1,1,512]{2,1,0:T(1,128)} %gain.3, bf16[4,128,512]{2,1,0:T(8,128)(2,1)} %copy-done.13, bf16[4,128,512]{2,1,0:T(8,128)(2,1)} %copy-done.11, bf16[4,512,512]{2,1,0:T(8,128)(2,1)} %samples.3, ...), custom_call_target="tpu_custom_call" | custom-call | flops 6000000000 | bytes 4000000 | tf_op jit(solution)/shard_map/first3/pallas_call | solution.py:197
  22.2 3.8 %collective-permute-done.8 = bf16[512,256]{1,0:T(8,128)(2,1)S(1)} collective-permute-done((bf16[512,256]{1,0:T(8,128)(2,1)S(1)}, bf16[512,256]{1,0:T(8,128)(2,1)S(1)}, u32[]{:S(2)}, u32[]{:S(2)}) %collective-permute-start.8) | collective-permute-done | bytes 262176 | tf_op jit(solution)/shard_map/ppermute | solution.py:438
  26.0 0.6 collective-permute-done.6
  26.6 0.1 select_select_fusion
  26.7 0.0 copy-start.2
  26.7 0.0 copy-start.8
  26.7 0.0 copy-start.10
  26.8 0.1 collective-permute-start.11
  26.9 0.1 collective-permute-start.10
  27.0 4.0 %collective-permute-start.9 = (bf16[512,256]{1,0:T(8,128)(2,1)S(1)}, bf16[512,256]{1,0:T(8,128)(2,1)S(1)}, u32[]{:S(2)}, u32[]{:S(2)}) collective-permute-start(bf16[512,256]{1,0:T(8,128)(2,1)S(1)} %get-tuple-element.69.refs_0_), channel_id=1, source_target_pairs={{0,2},{1,3},{2,0},{3,1},{4,6},{5,7},{6,4},{7,5},{8,10},{9,11},{10,... | collective-permute-start | bytes 786440 | tf_op jit(solution)/shard_map/ppermute | solution.py:442
  31.0 3.9 %collective-permute-start.3 = (bf16[3088,128]{1,0:T(8,128)(2,1)}, bf16[3088,128]{1,0:T(8,128)(2,1)S(1)}, u32[]{:S(2)}, u32[]{:S(2)}) collective-permute-start(bf16[3088,128]{1,0:T(8,128)(2,1)} %get-tuple-element.37), channel_id=1, source_target_pairs={{0,192},{64,128},{128,64},{192,0},{1,193},{65,129},{129,65},{193,1... | collective-permute-start | bytes 2371592 | tf_op jit(solution)/shard_map/ppermute | solution.py:438
  34.9 6.4 %collective-permute-done.11.refs_3_ = bf16[512,256]{1,0:T(8,128)(2,1)S(1)} collective-permute-done((bf16[512,256]{1,0:T(8,128)(2,1)S(1)}, bf16[512,256]{1,0:T(8,128)(2,1)S(1)}, u32[]{:S(2)}, u32[]{:S(2)}) %collective-permute-start.11) | collective-permute-done | bytes 262176 | tf_op jit(solution)/shard_map/ppermute | solution.py:442
  41.3 0.6 collective-permute-done.9.refs_1_
  41.9 0.2 joined.3.refs_4_
  42.1 0.3 collective-permute-start.12
  42.4 8.1 %collective-permute-done.3.far = bf16[3088,128]{1,0:T(8,128)(2,1)S(1)} collective-permute-done((bf16[3088,128]{1,0:T(8,128)(2,1)}, bf16[3088,128]{1,0:T(8,128)(2,1)S(1)}, u32[]{:S(2)}, u32[]{:S(2)}) %collective-permute-start.3) | collective-permute-done | bytes 790560 | tf_op jit(solution)/shard_map/ppermute | solution.py:438
  50.5 0.1 collective-permute-start.5
  50.6 0.1 collective-permute-done.2.near
  50.7 3.9 %collective-permute-start.4 = (bf16[1536,128]{1,0:T(8,128)(2,1)S(1)}, bf16[1536,128]{1,0:T(8,128)(2,1)S(1)}, u32[]{:S(2)}, u32[]{:S(2)}) collective-permute-start(bf16[1536,128]{1,0:T(8,128)(2,1)S(1)} %slice.16), channel_id=1, source_target_pairs={{0,192},{64,128},{128,64},{192,0},{1,193},{65,129},{129,65},{193,1... | collective-permute-start | bytes 1179656 | tf_op jit(solution)/shard_map/ppermute | solution.py:438
  54.7 3.8 %collective-permute-start.21 = (bf16[512,256]{1,0:T(8,128)(2,1)S(1)}, bf16[512,256]{1,0:T(8,128)(2,1)S(1)}, u32[]{:S(2)}, u32[]{:S(2)}) collective-permute-start(bf16[512,256]{1,0:T(8,128)(2,1)S(1)} %get-tuple-element.60.refs_0_), channel_id=1, source_target_pairs={{0,56},{1,57},{2,58},{3,59},{4,60},{5,61},{6,62},{7,63},{8,16},{9,... | collective-permute-start | bytes 786440 | tf_op jit(solution)/shard_map/ppermute | solution.py:442
  58.4 1.5 %collective-permute-start.19 = (bf16[512,256]{1,0:T(8,128)(2,1)S(1)}, bf16[512,256]{1,0:T(8,128)(2,1)S(1)}, u32[]{:S(2)}, u32[]{:S(2)}) collective-permute-start(bf16[512,256]{1,0:T(8,128)(2,1)S(1)} %get-tuple-element.60.refs_0_), channel_id=1, source_target_pairs={{0,8},{1,9},{2,10},{3,11},{4,12},{5,13},{6,14},{7,15},{8,0},{9,1},... | collective-permute-start | bytes 786440 | tf_op jit(solution)/shard_map/ppermute | solution.py:442
  60.0 0.4 collective-permute-done.4.mixed_a
  60.4 2.5 %collective-permute-start.14 = (bf16[512,256]{1,0:T(8,128)(2,1)S(1)}, bf16[512,256]{1,0:T(8,128)(2,1)S(1)}, u32[]{:S(2)}, u32[]{:S(2)}) collective-permute-start(bf16[512,256]{1,0:T(8,128)(2,1)S(1)} %get-tuple-element.53.refs_0_), channel_id=1, source_target_pairs={{0,6},{1,7},{2,4},{3,5},{4,2},{5,3},{6,0},{7,1},{8,14},{9,15},{10,... | collective-permute-start | bytes 786440 | tf_op jit(solution)/shard_map/ppermute | solution.py:442
  63.0 1.0 copy-done.12
  64.0 1.0 copy-done.14
  65.0 0.7 first1.1.h0
  65.7 0.1 arrived.1.h
  65.8 0.2 weights1.1.w
  66.1 4.9 %collective-permute-done.20.refs_2_ = bf16[512,256]{1,0:T(8,128)(2,1)S(1)} collective-permute-done((bf16[512,256]{1,0:T(8,128)(2,1)S(1)}, bf16[512,256]{1,0:T(8,128)(2,1)S(1)}, u32[]{:S(2)}, u32[]{:S(2)}) %collective-permute-start.20) | collective-permute-done | bytes 262176 | tf_op jit(solution)/shard_map/ppermute | solution.py:442
  71.0 0.3 collective-permute-done.19.refs_1_
  71.3 0.2 joined.5.refs_4_
  71.4 0.1 collective-permute-start.22
  71.5 0.5 sender1.1
  72.1 0.6 collective-permute-start.16
  72.6 7.3 %collective-permute-start.17 = (bf16[128,512]{1,0:T(8,128)(2,1)S(1)}, bf16[128,512]{1,0:T(8,128)(2,1)S(1)}, u32[]{:S(2)}, u32[]{:S(2)}) collective-permute-start(bf16[128,512]{1,0:T(8,128)(2,1)S(1)} %get-tuple-element.51), channel_id=1, source_target_pairs={{0,63},{1,2},{2,1},{3,4},{4,3},{5,6},{6,5},{7,8},{8,7},{9,10},{10,... | collective-permute-start | bytes 393224 | tf_op jit(solution)/shard_map/ppermute | solution.py:442
  79.9 1.3 %tiles1.1 = (bf16[24,128,128]{2,1,0:T(8,128)(2,1)S(1)}, s32[8,128]{1,0:T(8,128)S(1)}, f32[1,512]{1,0:T(1,128)S(1)}) custom-call(bf16[3088,128]{1,0:T(8,128)(2,1)S(1)} %copy-done, bf16[3088,128]{1,0:T(8,128)(2,1)S(1)} %collective-permute-done.2.near, bf16[3088,128]{1,0:T(8,128)(2,1)S(1)} %collective-permute-done.3.far, ...), custom_call_target="tpu_custom_call" | custom-call | bytes 2000000 | tf_op jit(solution)/shard_map/tiles1/pallas_call | solution.py:362
  81.3 2.5 %collective-permute-done.17.outer = bf16[128,512]{1,0:T(8,128)(2,1)S(1)} collective-permute-done((bf16[128,512]{1,0:T(8,128)(2,1)S(1)}, bf16[128,512]{1,0:T(8,128)(2,1)S(1)}, u32[]{:S(2)}, u32[]{:S(2)}) %collective-permute-start.17) | collective-permute-done | bytes 131104 | tf_op jit(solution)/shard_map/ppermute | solution.py:442
  83.7 2.4 %section1.1.h = bf16[512,512]{1,0:T(8,128)(2,1)S(1)} custom-call(s32[8,128]{1,0:T(8,128)S(1)} %get-tuple-element.47.codes, f32[1,512]{1,0:T(1,128)S(1)} %get-tuple-element.48.gain, bf16[24,128,128]{2,1,0:T(8,128)(2,1)S(1)} %get-tuple-element.49.tiles, bf16[4,512,512]{2,1,0:T(8,128)(2,1)S(1)} %weights1.1.w, bf16[512,512]{1,0:T(8,128)(2,1)S(1)} %arrived.1.h, ...), custom_call_target="tpu_custom_call" | custom-call | flops 1500000000 | bytes 4000000 | tf_op jit(solution)/shard_map/section1/pallas_call | solution.py:389
  86.2 1.6 %collective-permute-done.15.refs_2_ = bf16[512,256]{1,0:T(8,128)(2,1)S(1)} collective-permute-done((bf16[512,256]{1,0:T(8,128)(2,1)S(1)}, bf16[512,256]{1,0:T(8,128)(2,1)S(1)}, u32[]{:S(2)}, u32[]{:S(2)}) %collective-permute-start.15) | collective-permute-done | bytes 262176 | tf_op jit(solution)/shard_map/ppermute | solution.py:442
  87.8 0.2 joined.4.refs_4_
  88.0 0.3 collective-permute-start.18
  88.3 0.2 weights2.1.w
  88.5 0.5 sender2.1
  89.0 0.6 collective-permute-start.23
  89.6 3.5 %collective-permute-start.24 = (bf16[128,512]{1,0:T(8,128)(2,1)S(1)}, bf16[128,512]{1,0:T(8,128)(2,1)S(1)}, u32[]{:S(2)}, u32[]{:S(2)}) collective-permute-start(bf16[128,512]{1,0:T(8,128)(2,1)S(1)} %get-tuple-element.62), channel_id=1, source_target_pairs={{0,63},{1,2},{2,1},{3,4},{4,3},{5,6},{6,5},{7,8},{8,7},{9,10},{10,... | collective-permute-start | bytes 393224 | tf_op jit(solution)/shard_map/ppermute | solution.py:442
  93.1 1.3 %tiles2.1 = (bf16[24,128,128]{2,1,0:T(8,128)(2,1)S(1)}, s32[8,128]{1,0:T(8,128)S(1)}, f32[1,512]{1,0:T(1,128)S(1)}) custom-call(bf16[3088,128]{1,0:T(8,128)(2,1)S(1)} %copy-done, bf16[3088,128]{1,0:T(8,128)(2,1)S(1)} %collective-permute-done.2.near, bf16[3088,128]{1,0:T(8,128)(2,1)S(1)} %collective-permute-done.3.far, ...), custom_call_target="tpu_custom_call" | custom-call | bytes 2000000 | tf_op jit(solution)/shard_map/tiles2/pallas_call | solution.py:362
  94.4 2.9 %collective-permute-done.24.outer = bf16[128,512]{1,0:T(8,128)(2,1)S(1)} collective-permute-done((bf16[128,512]{1,0:T(8,128)(2,1)S(1)}, bf16[128,512]{1,0:T(8,128)(2,1)S(1)}, u32[]{:S(2)}, u32[]{:S(2)}) %collective-permute-start.24) | collective-permute-done | bytes 131104 | tf_op jit(solution)/shard_map/ppermute | solution.py:442
  97.3 2.4 %section2.1.h = bf16[512,512]{1,0:T(8,128)(2,1)S(1)} custom-call(s32[8,128]{1,0:T(8,128)S(1)} %get-tuple-element.57.codes, f32[1,512]{1,0:T(1,128)S(1)} %get-tuple-element.58.gain, bf16[24,128,128]{2,1,0:T(8,128)(2,1)S(1)} %get-tuple-element.59.tiles, bf16[4,512,512]{2,1,0:T(8,128)(2,1)S(1)} %weights2.1.w, bf16[512,512]{1,0:T(8,128)(2,1)S(1)} %section1.1.h, ...), custom_call_target="tpu_custom_call" | custom-call | flops 1500000000 | bytes 4000000 | tf_op jit(solution)/shard_map/section2/pallas_call | solution.py:389
  99.8 0.2 weights3.1.w
  100.0 0.5 sender3.1
  100.5 0.1 collective-permute-start.25
  100.6 3.6 %collective-permute-start.26 = (bf16[128,512]{1,0:T(8,128)(2,1)S(1)}, bf16[128,512]{1,0:T(8,128)(2,1)S(1)}, u32[]{:S(2)}, u32[]{:S(2)}) collective-permute-start(bf16[128,512]{1,0:T(8,128)(2,1)S(1)} %get-tuple-element.65), channel_id=1, source_target_pairs={{0,63},{1,2},{2,1},{3,4},{4,3},{5,6},{6,5},{7,8},{8,7},{9,10},{10,... | collective-permute-start | bytes 393224 | tf_op jit(solution)/shard_map/ppermute | solution.py:442
  104.2 1.3 %tiles3.1 = (bf16[24,128,128]{2,1,0:T(8,128)(2,1)S(1)}, s32[8,128]{1,0:T(8,128)S(1)}, f32[1,512]{1,0:T(1,128)S(1)}) custom-call(bf16[3088,128]{1,0:T(8,128)(2,1)S(1)} %copy-done, bf16[3088,128]{1,0:T(8,128)(2,1)S(1)} %collective-permute-done.2.near, bf16[3088,128]{1,0:T(8,128)(2,1)S(1)} %collective-permute-done.3.far, ...), custom_call_target="tpu_custom_call" | custom-call | bytes 2000000 | tf_op jit(solution)/shard_map/tiles3/pallas_call | solution.py:362
  105.4 3.0 %collective-permute-done.26.outer = bf16[128,512]{1,0:T(8,128)(2,1)S(1)} collective-permute-done((bf16[128,512]{1,0:T(8,128)(2,1)S(1)}, bf16[128,512]{1,0:T(8,128)(2,1)S(1)}, u32[]{:S(2)}, u32[]{:S(2)}) %collective-permute-start.26) | collective-permute-done | bytes 131104 | tf_op jit(solution)/shard_map/ppermute | solution.py:442
  108.4 3.2 %section3.1 = bf16[512,512]{1,0:T(8,128)(2,1)} custom-call(s32[8,128]{1,0:T(8,128)S(1)} %get-tuple-element.38.codes, f32[1,512]{1,0:T(1,128)S(1)} %get-tuple-element.39.gain, bf16[24,128,128]{2,1,0:T(8,128)(2,1)S(1)} %get-tuple-element.40.tiles, bf16[4,512,512]{2,1,0:T(8,128)(2,1)S(1)} %weights3.1.w, bf16[512,512]{1,0:T(8,128)(2,1)S(1)} %section2.1.h, ...), custom_call_target="tpu_custom_call" | custom-call | flops 1500000000 | bytes 4000000 | tf_op jit(solution)/shard_map/section3/pallas_call | solution.py:389
  (49 shorter events, 0.2 us)
Async XLA Ops:
  0.0 10.2 %copy-start.7 = (bf16[1,1,512,512]{3,2,1,0:T(8,128)(2,1)S(1)}, bf16[1,1,512,512]{3,2,1,0:T(8,128)(2,1)}, u32[]{:S(2)}) copy-start(bf16[1,1,512,512]{3,2,1,0:T(8,128)(2,1)} %refs_3_.5) | copy-start | bytes 1572868
  0.0 10.2 %copy-start.5 = (bf16[1,1,512,512]{3,2,1,0:T(8,128)(2,1)S(1)}, bf16[1,1,512,512]{3,2,1,0:T(8,128)(2,1)}, u32[]{:S(2)}) copy-start(bf16[1,1,512,512]{3,2,1,0:T(8,128)(2,1)} %refs_2_.5) | copy-start | bytes 1572868
  0.0 10.2 %copy-start.3 = (bf16[1,1,512,512]{3,2,1,0:T(8,128)(2,1)S(1)}, bf16[1,1,512,512]{3,2,1,0:T(8,128)(2,1)}, u32[]{:S(2)}) copy-start(bf16[1,1,512,512]{3,2,1,0:T(8,128)(2,1)} %refs_1_.5) | copy-start | bytes 1572868
  0.0 10.2 %copy-start.1 = (bf16[1,1,512,512]{3,2,1,0:T(8,128)(2,1)S(1)}, bf16[1,1,512,512]{3,2,1,0:T(8,128)(2,1)}, u32[]{:S(2)}) copy-start(bf16[1,1,512,512]{3,2,1,0:T(8,128)(2,1)} %refs_0_.5) | copy-start | bytes 1572868
  2.4 14.8 %collective-permute-start.1 = (bf16[4,128,512]{2,1,0:T(8,128)(2,1)}, bf16[4,128,512]{2,1,0:T(8,128)(2,1)S(1)}, u32[]{:S(2)}, u32[]{:S(2)}) collective-permute-start(bf16[4,128,512]{2,1,0:T(8,128)(2,1)} %get-tuple-element.67), channel_id=1, source_target_pairs={{0,63},{1,2},{2,1},{3,4},{4,3},{5,6},{6,5},{7,8},{8,7},{9,10},{10,... | collective-permute-start | bytes 1572872 | tf_op jit(solution)/shard_map/ppermute | solution.py:442
  10.2 7.1 %collective-permute-start = (bf16[4,128,512]{2,1,0:T(8,128)(2,1)}, bf16[4,128,512]{2,1,0:T(8,128)(2,1)S(1)}, u32[]{:S(2)}, u32[]{:S(2)}) collective-permute-start(bf16[4,128,512]{2,1,0:T(8,128)(2,1)} %get-tuple-element.68), channel_id=1, source_target_pairs={{0,1},{1,0},{2,3},{3,2},{4,5},{5,4},{6,7},{7,6},{8,9},{9,8},{10,11... | collective-permute-start | bytes 1572872 | tf_op jit(solution)/shard_map/ppermute | solution.py:442
  10.4 15.6 %collective-permute-start.8 = (bf16[512,256]{1,0:T(8,128)(2,1)S(1)}, bf16[512,256]{1,0:T(8,128)(2,1)S(1)}, u32[]{:S(2)}, u32[]{:S(2)}) collective-permute-start(bf16[512,256]{1,0:T(8,128)(2,1)S(1)} %select_bitcast_fusion), channel_id=1, source_target_pairs={{0,192},{64,128},{128,64},{192,0},{1,193},{65,129},{129,65},{193,1... | collective-permute-start | bytes 786440 | tf_op jit(solution)/shard_map/ppermute | solution.py:438
  10.9 15.1 %collective-permute-start.7 = (bf16[512,256]{1,0:T(8,128)(2,1)S(1)}, bf16[512,256]{1,0:T(8,128)(2,1)S(1)}, u32[]{:S(2)}, u32[]{:S(2)}) collective-permute-start(bf16[512,256]{1,0:T(8,128)(2,1)S(1)} %select_bitcast_fusion), channel_id=1, source_target_pairs={{0,128},{64,192},{128,0},{192,64},{1,129},{65,193},{129,1},{193,65... | collective-permute-start | bytes 786440 | tf_op jit(solution)/shard_map/ppermute | solution.py:438
  13.3 13.3 %collective-permute-start.6 = (bf16[512,256]{1,0:T(8,128)(2,1)S(1)}, bf16[512,256]{1,0:T(8,128)(2,1)S(1)}, u32[]{:S(2)}, u32[]{:S(2)}) collective-permute-start(bf16[512,256]{1,0:T(8,128)(2,1)S(1)} %select_bitcast_fusion), channel_id=1, source_target_pairs={{0,64},{64,0},{128,192},{192,128},{1,65},{65,1},{129,193},{193,129... | collective-permute-start | bytes 786440 | tf_op jit(solution)/shard_map/ppermute | solution.py:438
  17.2 0.8 copy-start.11
  18.0 0.8 copy-start.13
  26.6 36.3 %copy-start.9 = (bf16[4,512,512]{2,1,0:T(8,128)(2,1)S(1)}, bf16[4,512,512]{2,1,0:T(8,128)(2,1)}, u32[]{:S(2)}) copy-start(bf16[4,512,512]{2,1,0:T(8,128)(2,1)} %samples.3) | copy-start | bytes 6291460
  26.7 36.2 %copy-start.2 = (bf16[1,1,512,512]{3,2,1,0:T(8,128)(2,1)S(1)}, bf16[1,1,512,512]{3,2,1,0:T(8,128)(2,1)}, u32[]{:S(2)}) copy-start(bf16[1,1,512,512]{3,2,1,0:T(8,128)(2,1)} %refs_0_.5) | copy-start | bytes 1572868
  26.7 36.2 %copy-start.4 = (bf16[1,1,512,512]{3,2,1,0:T(8,128)(2,1)S(1)}, bf16[1,1,512,512]{3,2,1,0:T(8,128)(2,1)}, u32[]{:S(2)}) copy-start(bf16[1,1,512,512]{3,2,1,0:T(8,128)(2,1)} %refs_1_.5) | copy-start | bytes 1572868
  26.7 36.2 %copy-start.6 = (bf16[1,1,512,512]{3,2,1,0:T(8,128)(2,1)S(1)}, bf16[1,1,512,512]{3,2,1,0:T(8,128)(2,1)}, u32[]{:S(2)}) copy-start(bf16[1,1,512,512]{3,2,1,0:T(8,128)(2,1)} %refs_2_.5) | copy-start | bytes 1572868
  26.7 36.2 %copy-start.8 = (bf16[1,1,512,512]{3,2,1,0:T(8,128)(2,1)S(1)}, bf16[1,1,512,512]{3,2,1,0:T(8,128)(2,1)}, u32[]{:S(2)}) copy-start(bf16[1,1,512,512]{3,2,1,0:T(8,128)(2,1)} %refs_3_.5) | copy-start | bytes 1572868
  26.7 36.2 %copy-start.10 = (bf16[1,4,6,128,128]{4,3,2,1,0:T(8,128)(2,1)S(1)}, bf16[1,4,6,128,128]{4,3,2,1,0:T(8,128)(2,1)}, u32[]{:S(2)}) copy-start(bf16[1,4,6,128,128]{4,3,2,1,0:T(8,128)(2,1)} %tiles.3) | copy-start | bytes 2359300
  26.7 36.2 %copy-start.15 = (s32[1,4,6]{2,1,0:T(4,128)S(1)}, s32[1,4,6]{2,1,0:T(4,128)}, u32[]{:S(2)}) copy-start(s32[1,4,6]{2,1,0:T(4,128)} %src.3) | copy-start | bytes 292
  26.8 36.2 %copy-start.16 = (f32[1,1,512]{2,1,0:T(1,128)S(1)}, f32[1,1,512]{2,1,0:T(1,128)}, u32[]{:S(2)}) copy-start(f32[1,1,512]{2,1,0:T(1,128)} %gain.3) | copy-start | bytes 6148
  26.8 36.2 %copy-start.17 = (s32[1,4]{1,0:T(1,128)S(1)}, s32[1,4]{1,0:T(1,128)}, u32[]{:S(2)}) copy-start(s32[1,4]{1,0:T(1,128)} %cnt.3) | copy-start | bytes 52
  26.8 14.5 %collective-permute-start.11 = (bf16[512,256]{1,0:T(8,128)(2,1)S(1)}, bf16[512,256]{1,0:T(8,128)(2,1)S(1)}, u32[]{:S(2)}, u32[]{:S(2)}) collective-permute-start(bf16[512,256]{1,0:T(8,128)(2,1)S(1)} %get-tuple-element.69.refs_0_), channel_id=1, source_target_pairs={{0,6},{1,7},{2,4},{3,5},{4,2},{5,3},{6,0},{7,1},{8,14},{9,15},{10,... | collective-permute-start | bytes 786440 | tf_op jit(solution)/shard_map/ppermute | solution.py:442
  26.9 14.4 %collective-permute-start.10 = (bf16[512,256]{1,0:T(8,128)(2,1)S(1)}, bf16[512,256]{1,0:T(8,128)(2,1)S(1)}, u32[]{:S(2)}, u32[]{:S(2)}) collective-permute-start(bf16[512,256]{1,0:T(8,128)(2,1)S(1)} %get-tuple-element.69.refs_0_), channel_id=1, source_target_pairs={{0,4},{1,5},{2,6},{3,7},{4,0},{5,1},{6,2},{7,3},{8,12},{9,13},{10,... | collective-permute-start | bytes 786440 | tf_op jit(solution)/shard_map/ppermute | solution.py:442
  27.0 14.9 %collective-permute-start.9 = (bf16[512,256]{1,0:T(8,128)(2,1)S(1)}, bf16[512,256]{1,0:T(8,128)(2,1)S(1)}, u32[]{:S(2)}, u32[]{:S(2)}) collective-permute-start(bf16[512,256]{1,0:T(8,128)(2,1)S(1)} %get-tuple-element.69.refs_0_), channel_id=1, source_target_pairs={{0,2},{1,3},{2,0},{3,1},{4,6},{5,7},{6,4},{7,5},{8,10},{9,11},{10,... | collective-permute-start | bytes 786440 | tf_op jit(solution)/shard_map/ppermute | solution.py:442
  31.0 19.5 %collective-permute-start.3 = (bf16[3088,128]{1,0:T(8,128)(2,1)}, bf16[3088,128]{1,0:T(8,128)(2,1)S(1)}, u32[]{:S(2)}, u32[]{:S(2)}) collective-permute-start(bf16[3088,128]{1,0:T(8,128)(2,1)} %get-tuple-element.37), channel_id=1, source_target_pairs={{0,192},{64,128},{128,64},{192,0},{1,193},{65,129},{129,65},{193,1... | collective-permute-start | bytes 2371592 | tf_op jit(solution)/shard_map/ppermute | solution.py:438
  34.9 15.8 %collective-permute-start.2 = (bf16[3088,128]{1,0:T(8,128)(2,1)}, bf16[3088,128]{1,0:T(8,128)(2,1)S(1)}, u32[]{:S(2)}, u32[]{:S(2)}) collective-permute-start(bf16[3088,128]{1,0:T(8,128)(2,1)} %get-tuple-element.36.own), channel_id=1, source_target_pairs={{0,64},{64,0},{128,192},{192,128},{1,65},{65,1},{129,193},{193,129... | collective-permute-start | bytes 2371592 | tf_op jit(solution)/shard_map/ppermute | solution.py:438
  42.1 12.5 %collective-permute-start.12 = (bf16[4,512,256]{2,1,0:T(8,128)(2,1)S(1)}, bf16[4,512,256]{2,1,0:T(8,128)(2,1)S(1)}, u32[]{:S(2)}, u32[]{:S(2)}) collective-permute-start(bf16[4,512,256]{2,1,0:T(8,128)(2,1)S(1)} %joined.3.refs_4_), channel_id=1, source_target_pairs={{0,1},{1,0},{2,3},{3,2},{4,5},{5,4},{6,7},{7,6},{8,9},{9,8},{10,11... | collective-permute-start | bytes 3145736 | tf_op jit(solution)/shard_map/ppermute | solution.py:442
  50.5 12.4 %collective-permute-start.5 = (bf16[1552,128]{1,0:T(8,128)(2,1)S(1)}, bf16[1552,128]{1,0:T(8,128)(2,1)S(1)}, u32[]{:S(2)}, u32[]{:S(2)}) collective-permute-start(bf16[1552,128]{1,0:T(8,128)(2,1)S(1)} %slice.17), channel_id=1, source_target_pairs={{0,64},{64,0},{128,192},{192,128},{1,65},{65,1},{129,193},{193,129... | collective-permute-start | bytes 1191944 | tf_op jit(solution)/shard_map/ppermute | solution.py:438
  50.7 9.7 %collective-permute-start.4 = (bf16[1536,128]{1,0:T(8,128)(2,1)S(1)}, bf16[1536,128]{1,0:T(8,128)(2,1)S(1)}, u32[]{:S(2)}, u32[]{:S(2)}) collective-permute-start(bf16[1536,128]{1,0:T(8,128)(2,1)S(1)} %slice.16), channel_id=1, source_target_pairs={{0,192},{64,128},{128,64},{192,0},{1,193},{65,129},{129,65},{193,1... | collective-permute-start | bytes 1179656 | tf_op jit(solution)/shard_map/ppermute | solution.py:438
  54.7 11.4 %collective-permute-start.21 = (bf16[512,256]{1,0:T(8,128)(2,1)S(1)}, bf16[512,256]{1,0:T(8,128)(2,1)S(1)}, u32[]{:S(2)}, u32[]{:S(2)}) collective-permute-start(bf16[512,256]{1,0:T(8,128)(2,1)S(1)} %get-tuple-element.60.refs_0_), channel_id=1, source_target_pairs={{0,56},{1,57},{2,58},{3,59},{4,60},{5,61},{6,62},{7,63},{8,16},{9,... | collective-permute-start | bytes 786440 | tf_op jit(solution)/shard_map/ppermute | solution.py:442
  58.4 12.5 %collective-permute-start.20 = (bf16[512,256]{1,0:T(8,128)(2,1)S(1)}, bf16[512,256]{1,0:T(8,128)(2,1)S(1)}, u32[]{:S(2)}, u32[]{:S(2)}) collective-permute-start(bf16[512,256]{1,0:T(8,128)(2,1)S(1)} %get-tuple-element.60.refs_0_), channel_id=1, source_target_pairs={{0,16},{1,17},{2,18},{3,19},{4,20},{5,21},{6,22},{7,23},{8,24},{9,... | collective-permute-start | bytes 786440 | tf_op jit(solution)/shard_map/ppermute | solution.py:442
  58.4 12.8 %collective-permute-start.19 = (bf16[512,256]{1,0:T(8,128)(2,1)S(1)}, bf16[512,256]{1,0:T(8,128)(2,1)S(1)}, u32[]{:S(2)}, u32[]{:S(2)}) collective-permute-start(bf16[512,256]{1,0:T(8,128)(2,1)S(1)} %get-tuple-element.60.refs_0_), channel_id=1, source_target_pairs={{0,8},{1,9},{2,10},{3,11},{4,12},{5,13},{6,14},{7,15},{8,0},{9,1},... | collective-permute-start | bytes 786440 | tf_op jit(solution)/shard_map/ppermute | solution.py:442
  60.4 19.5 %collective-permute-start.14 = (bf16[512,256]{1,0:T(8,128)(2,1)S(1)}, bf16[512,256]{1,0:T(8,128)(2,1)S(1)}, u32[]{:S(2)}, u32[]{:S(2)}) collective-permute-start(bf16[512,256]{1,0:T(8,128)(2,1)S(1)} %get-tuple-element.53.refs_0_), channel_id=1, source_target_pairs={{0,6},{1,7},{2,4},{3,5},{4,2},{5,3},{6,0},{7,1},{8,14},{9,15},{10,... | collective-permute-start | bytes 786440 | tf_op jit(solution)/shard_map/ppermute | solution.py:442
  62.9 17.0 %collective-permute-start.13 = (bf16[512,256]{1,0:T(8,128)(2,1)S(1)}, bf16[512,256]{1,0:T(8,128)(2,1)S(1)}, u32[]{:S(2)}, u32[]{:S(2)}) collective-permute-start(bf16[512,256]{1,0:T(8,128)(2,1)S(1)} %get-tuple-element.53.refs_0_), channel_id=1, source_target_pairs={{0,2},{1,3},{2,0},{3,1},{4,6},{5,7},{6,4},{7,5},{8,10},{9,11},{10,... | collective-permute-start | bytes 786440 | tf_op jit(solution)/shard_map/ppermute | solution.py:442
  63.0 1.0 copy-start.12
  64.0 1.0 copy-start.14
  66.1 13.8 %copy-start = (bf16[3088,128]{1,0:T(8,128)(2,1)S(1)}, bf16[3088,128]{1,0:T(8,128)(2,1)}, u32[]{:S(2)}) copy-start(bf16[3088,128]{1,0:T(8,128)(2,1)} %get-tuple-element.36.own) | copy-start | bytes 2371588
  71.4 16.8 %collective-permute-start.22 = (bf16[4,512,256]{2,1,0:T(8,128)(2,1)S(1)}, bf16[4,512,256]{2,1,0:T(8,128)(2,1)S(1)}, u32[]{:S(2)}, u32[]{:S(2)}) collective-permute-start(bf16[4,512,256]{2,1,0:T(8,128)(2,1)S(1)} %joined.5.refs_4_), channel_id=1, source_target_pairs={{0,1},{1,0},{2,3},{3,2},{4,5},{5,4},{6,7},{7,6},{8,9},{9,8},{10,11... | collective-permute-start | bytes 3145736 | tf_op jit(solution)/shard_map/ppermute | solution.py:442
  72.1 9.2 %collective-permute-start.16 = (bf16[128,512]{1,0:T(8,128)(2,1)S(1)}, bf16[128,512]{1,0:T(8,128)(2,1)S(1)}, u32[]{:S(2)}, u32[]{:S(2)}) collective-permute-start(bf16[128,512]{1,0:T(8,128)(2,1)S(1)} %get-tuple-element.50), channel_id=1, source_target_pairs={{0,1},{1,0},{2,3},{3,2},{4,5},{5,4},{6,7},{7,6},{8,9},{9,8},{10,11... | collective-permute-start | bytes 393224 | tf_op jit(solution)/shard_map/ppermute | solution.py:442
  72.6 11.1 %collective-permute-start.17 = (bf16[128,512]{1,0:T(8,128)(2,1)S(1)}, bf16[128,512]{1,0:T(8,128)(2,1)S(1)}, u32[]{:S(2)}, u32[]{:S(2)}) collective-permute-start(bf16[128,512]{1,0:T(8,128)(2,1)S(1)} %get-tuple-element.51), channel_id=1, source_target_pairs={{0,63},{1,2},{2,1},{3,4},{4,3},{5,6},{6,5},{7,8},{8,7},{9,10},{10,... | collective-permute-start | bytes 393224 | tf_op jit(solution)/shard_map/ppermute | solution.py:442
  79.9 7.9 %collective-permute-start.15 = (bf16[512,256]{1,0:T(8,128)(2,1)S(1)}, bf16[512,256]{1,0:T(8,128)(2,1)S(1)}, u32[]{:S(2)}, u32[]{:S(2)}) collective-permute-start(bf16[512,256]{1,0:T(8,128)(2,1)S(1)} %get-tuple-element.53.refs_0_), channel_id=1, source_target_pairs={{0,4},{1,5},{2,6},{3,7},{4,0},{5,1},{6,2},{7,3},{8,12},{9,13},{10,... | collective-permute-start | bytes 786440 | tf_op jit(solution)/shard_map/ppermute | solution.py:442
  88.0 11.8 %collective-permute-start.18 = (bf16[4,512,256]{2,1,0:T(8,128)(2,1)S(1)}, bf16[4,512,256]{2,1,0:T(8,128)(2,1)S(1)}, u32[]{:S(2)}, u32[]{:S(2)}) collective-permute-start(bf16[4,512,256]{2,1,0:T(8,128)(2,1)S(1)} %joined.4.refs_4_), channel_id=1, source_target_pairs={{0,1},{1,0},{2,3},{3,2},{4,5},{5,4},{6,7},{7,6},{8,9},{9,8},{10,11... | collective-permute-start | bytes 3145736 | tf_op jit(solution)/shard_map/ppermute | solution.py:442
  89.0 5.3 %collective-permute-start.23 = (bf16[128,512]{1,0:T(8,128)(2,1)S(1)}, bf16[128,512]{1,0:T(8,128)(2,1)S(1)}, u32[]{:S(2)}, u32[]{:S(2)}) collective-permute-start(bf16[128,512]{1,0:T(8,128)(2,1)S(1)} %get-tuple-element.61), channel_id=1, source_target_pairs={{0,1},{1,0},{2,3},{3,2},{4,5},{5,4},{6,7},{7,6},{8,9},{9,8},{10,11... | collective-permute-start | bytes 393224 | tf_op jit(solution)/shard_map/ppermute | solution.py:442
  89.6 7.7 %collective-permute-start.24 = (bf16[128,512]{1,0:T(8,128)(2,1)S(1)}, bf16[128,512]{1,0:T(8,128)(2,1)S(1)}, u32[]{:S(2)}, u32[]{:S(2)}) collective-permute-start(bf16[128,512]{1,0:T(8,128)(2,1)S(1)} %get-tuple-element.62), channel_id=1, source_target_pairs={{0,63},{1,2},{2,1},{3,4},{4,3},{5,6},{6,5},{7,8},{8,7},{9,10},{10,... | collective-permute-start | bytes 393224 | tf_op jit(solution)/shard_map/ppermute | solution.py:442
  100.5 4.9 %collective-permute-start.25 = (bf16[128,512]{1,0:T(8,128)(2,1)S(1)}, bf16[128,512]{1,0:T(8,128)(2,1)S(1)}, u32[]{:S(2)}, u32[]{:S(2)}) collective-permute-start(bf16[128,512]{1,0:T(8,128)(2,1)S(1)} %get-tuple-element.64), channel_id=1, source_target_pairs={{0,1},{1,0},{2,3},{3,2},{4,5},{5,4},{6,7},{7,6},{8,9},{9,8},{10,11... | collective-permute-start | bytes 393224 | tf_op jit(solution)/shard_map/ppermute | solution.py:442
  100.6 7.8 %collective-permute-start.26 = (bf16[128,512]{1,0:T(8,128)(2,1)S(1)}, bf16[128,512]{1,0:T(8,128)(2,1)S(1)}, u32[]{:S(2)}, u32[]{:S(2)}) collective-permute-start(bf16[128,512]{1,0:T(8,128)(2,1)S(1)} %get-tuple-element.65), channel_id=1, source_target_pairs={{0,63},{1,2},{2,1},{3,4},{4,3},{5,6},{6,5},{7,8},{8,7},{9,10},{10,... | collective-permute-start | bytes 393224 | tf_op jit(solution)/shard_map/ppermute | solution.py:442

commit v8 on v7

--- a/solution.py
+++ b/solution.py
@@ -483,7 +483,6 @@
     stages = {1: both(joined(ring1))}
     then, last = after((then, last), near, far, stages[1])
     ring2, ring3 = [then] + [over_dom(then, route) for route in over_z], ring(last, over_y)
-    stages[2] = both(joined(ring2))
     h = arrived_call(h0, near, far, mixed_a, mixed_b)
     for section in range(1, SEG):
         if section == 2:
@@ -491,6 +490,8 @@
         w = weights_call(section, ws, stages[section])
         tiles, codes, gain = tiles_call(section, arrays)
         sender, inner, outer = sender_call(section, h, w)
+        if section == 1:
+            stages[2] = both(joined(after(ring2, sender)))
         inner, outer = exchange(inner, outer)
         h = section_call(section, codes, gain, tiles, w, h, inner, outer, sender)
     return h[None]

time: 112 us -> 112 us (level)
  no operation moved by 1% of the time
where the time goes in v8:
time: 112 us; the launch traced here: 111 us
  starting transfers between devices  47.9 us (43%)
  waiting for transfers between devices  37.4 us (33%)
  Pallas kernels  18.8 us (17%)
  local copies, waits for them, and re-layouts  3.78 us (3%)
  other arithmetic  2.62 us (2%)
    ppermute x20, starting transfers between devices, over_dom(): return lax.ppermute(value, 'dom', pairs)  35.8 us
    ppermute x20, waiting for transfers between devices, over_dom(): return lax.ppermute(value, 'dom', pairs)  24.5 us
    ppermute x7, waiting for transfers between devices, over_segments(): return lax.ppermute(value, 'segment', by_segment(x))  13 us
    ppermute x7, starting transfers between devices, over_segments(): return lax.ppermute(value, 'segment', by_segment(x))  12.1 us
    pallas_call x3, Pallas kernels, section_call(): pl.pallas_call(section_kernel, out_shape=jax.ShapeDtypeStruct((BD * BLK,...  8.09 us
    pallas_call x2, Pallas kernels, first_call(): pl.pallas_call(functools.partial(first_kernel, order), out_shape=[jax.Sha...  4.04 us
    pallas_call x3, Pallas kernels, tiles_call(): pl.pallas_call(functools.partial(tiles_kernel, section), out_shape=[jax.S...  3.83 us
    unnamed x36, local copies, waits for them, and re-layouts  3.73 us
  transfers between devices with their start and end apart: 27, of which 14 were waited for; matrix products, arithmetic and copies ran while one was open for 0% of the time, Pallas kernels for 13%

profile of v8, /device:TPU:6, one launch (start us, length us, event | category | flops | bytes accessed | tf_op | source)
XLA Modules:
  0.0 111.0 jit_solution(10225299466189551377)
XLA Ops:
  0.0 0.0 copy-start.1
  0.0 2.4 %broadcast_select_fusion = (bf16[4,128,512]{2,1,0:T(8,128)(2,1)}, bf16[4,128,512]{2,1,0:T(8,128)(2,1)}) fusion(pred[]{:T(512)S(6)} %eq.25, bf16[4,512,512]{2,1,0:T(8,128)(2,1)} %samples.3), kind=kLoop, calls=%fused_computation | loop fusion | flops 524288 | bytes 2097153 | tf_op jit(solution)/shard_map/jit(_where)/select_n | solution.py:453
  2.4 7.7 %collective-permute-start.1 = (bf16[4,128,512]{2,1,0:T(8,128)(2,1)}, bf16[4,128,512]{2,1,0:T(8,128)(2,1)S(1)}, u32[]{:S(2)}, u32[]{:S(2)}) collective-permute-start(bf16[4,128,512]{2,1,0:T(8,128)(2,1)} %get-tuple-element.75), channel_id=1, source_target_pairs={{0,63},{1,2},{2,1},{3,4},{4,3},{5,6},{6,5},{7,8},{8,7},{9,10},{10,... | collective-permute-start | bytes 1572872 | tf_op jit(solution)/shard_map/ppermute | solution.py:442
  10.2 0.2 select_bitcast_fusion
  10.4 0.6 collective-permute-start.8
  10.9 2.4 %collective-permute-start.7 = (bf16[512,256]{1,0:T(8,128)(2,1)S(1)}, bf16[512,256]{1,0:T(8,128)(2,1)S(1)}, u32[]{:S(2)}, u32[]{:S(2)}) collective-permute-start(bf16[512,256]{1,0:T(8,128)(2,1)S(1)} %select_bitcast_fusion), channel_id=1, source_target_pairs={{0,128},{64,192},{128,0},{192,64},{1,129},{65,193},{129,1},{193,65... | collective-permute-start | bytes 786440 | tf_op jit(solution)/shard_map/ppermute | solution.py:438
  13.3 1.2 %collective-permute-start.6 = (bf16[512,256]{1,0:T(8,128)(2,1)S(1)}, bf16[512,256]{1,0:T(8,128)(2,1)S(1)}, u32[]{:S(2)}, u32[]{:S(2)}) collective-permute-start(bf16[512,256]{1,0:T(8,128)(2,1)S(1)} %select_bitcast_fusion), channel_id=1, source_target_pairs={{0,64},{64,0},{128,192},{192,128},{1,65},{65,1},{129,193},{193,129... | collective-permute-start | bytes 786440 | tf_op jit(solution)/shard_map/ppermute | solution.py:438
  14.5 2.7 %collective-permute-done.1.outer = bf16[4,128,512]{2,1,0:T(8,128)(2,1)S(1)} collective-permute-done((bf16[4,128,512]{2,1,0:T(8,128)(2,1)}, bf16[4,128,512]{2,1,0:T(8,128)(2,1)S(1)}, u32[]{:S(2)}, u32[]{:S(2)}) %collective-permute-start.1) | collective-permute-done | bytes 524320 | tf_op jit(solution)/shard_map/ppermute | solution.py:442
  17.2 0.8 copy-done.11
  18.0 0.8 copy-done.13
  18.8 3.4 %first3.1 = (bf16[3088,128]{1,0:T(8,128)(2,1)}, bf16[3088,128]{1,0:T(8,128)(2,1)}) custom-call(s32[1,4,6]{2,1,0:T(4,128)} %src.3, s32[1,4]{1,0:T(1,128)} %cnt.3, f32[1,1,512]{2,1,0:T(1,128)} %gain.3, bf16[4,128,512]{2,1,0:T(8,128)(2,1)} %copy-done.13, bf16[4,128,512]{2,1,0:T(8,128)(2,1)} %copy-done.11, bf16[4,512,512]{2,1,0:T(8,128)(2,1)} %samples.3, ...), custom_call_target="tpu_custom_call" | custom-call | flops 6000000000 | bytes 4000000 | tf_op jit(solution)/shard_map/first3/pallas_call | solution.py:197
  22.2 3.8 %collective-permute-done.8 = bf16[512,256]{1,0:T(8,128)(2,1)S(1)} collective-permute-done((bf16[512,256]{1,0:T(8,128)(2,1)S(1)}, bf16[512,256]{1,0:T(8,128)(2,1)S(1)}, u32[]{:S(2)}, u32[]{:S(2)}) %collective-permute-start.8) | collective-permute-done | bytes 262176 | tf_op jit(solution)/shard_map/ppermute | solution.py:438
  26.0 0.6 collective-permute-done.6
  26.6 0.1 select_select_fusion
  26.7 0.0 copy-start.2
  26.7 0.0 copy-start.4
  26.8 0.1 collective-permute-start.11
  26.9 0.1 collective-permute-start.10
  27.0 4.0 %collective-permute-start.9 = (bf16[512,256]{1,0:T(8,128)(2,1)S(1)}, bf16[512,256]{1,0:T(8,128)(2,1)S(1)}, u32[]{:S(2)}, u32[]{:S(2)}) collective-permute-start(bf16[512,256]{1,0:T(8,128)(2,1)S(1)} %get-tuple-element.77.refs_0_), channel_id=1, source_target_pairs={{0,2},{1,3},{2,0},{3,1},{4,6},{5,7},{6,4},{7,5},{8,10},{9,11},{10,... | collective-permute-start | bytes 786440 | tf_op jit(solution)/shard_map/ppermute | solution.py:442
  31.0 3.9 %collective-permute-start.3 = (bf16[3088,128]{1,0:T(8,128)(2,1)}, bf16[3088,128]{1,0:T(8,128)(2,1)S(1)}, u32[]{:S(2)}, u32[]{:S(2)}) collective-permute-start(bf16[3088,128]{1,0:T(8,128)(2,1)} %get-tuple-element.41), channel_id=1, source_target_pairs={{0,192},{64,128},{128,64},{192,0},{1,193},{65,129},{129,65},{193,1... | collective-permute-start | bytes 2371592 | tf_op jit(solution)/shard_map/ppermute | solution.py:438
  34.9 6.4 %collective-permute-done.11.refs_3_ = bf16[512,256]{1,0:T(8,128)(2,1)S(1)} collective-permute-done((bf16[512,256]{1,0:T(8,128)(2,1)S(1)}, bf16[512,256]{1,0:T(8,128)(2,1)S(1)}, u32[]{:S(2)}, u32[]{:S(2)}) %collective-permute-start.11) | collective-permute-done | bytes 262176 | tf_op jit(solution)/shard_map/ppermute | solution.py:442
  41.3 0.6 collective-permute-done.9.refs_1_
  41.9 0.2 joined.3.refs_4_
  42.1 0.3 collective-permute-start.12
  42.4 8.1 %collective-permute-done.3.far = bf16[3088,128]{1,0:T(8,128)(2,1)S(1)} collective-permute-done((bf16[3088,128]{1,0:T(8,128)(2,1)}, bf16[3088,128]{1,0:T(8,128)(2,1)S(1)}, u32[]{:S(2)}, u32[]{:S(2)}) %collective-permute-start.3) | collective-permute-done | bytes 790560 | tf_op jit(solution)/shard_map/ppermute | solution.py:438
  50.5 0.1 collective-permute-start.5
  50.6 0.1 collective-permute-done.2.near
  50.7 3.9 %collective-permute-start.4 = (bf16[1536,128]{1,0:T(8,128)(2,1)S(1)}, bf16[1536,128]{1,0:T(8,128)(2,1)S(1)}, u32[]{:S(2)}, u32[]{:S(2)}) collective-permute-start(bf16[1536,128]{1,0:T(8,128)(2,1)S(1)} %slice.16), channel_id=1, source_target_pairs={{0,192},{64,128},{128,64},{192,0},{1,193},{65,129},{129,65},{193,1... | collective-permute-start | bytes 1179656 | tf_op jit(solution)/shard_map/ppermute | solution.py:438
  54.7 3.8 %collective-permute-start.21 = (bf16[512,256]{1,0:T(8,128)(2,1)S(1)}, bf16[512,256]{1,0:T(8,128)(2,1)S(1)}, u32[]{:S(2)}, u32[]{:S(2)}) collective-permute-start(bf16[512,256]{1,0:T(8,128)(2,1)S(1)} %get-tuple-element.65.refs_0_), channel_id=1, source_target_pairs={{0,56},{1,57},{2,58},{3,59},{4,60},{5,61},{6,62},{7,63},{8,16},{9,... | collective-permute-start | bytes 786440 | tf_op jit(solution)/shard_map/ppermute | solution.py:442
  58.4 1.5 %collective-permute-start.19 = (bf16[512,256]{1,0:T(8,128)(2,1)S(1)}, bf16[512,256]{1,0:T(8,128)(2,1)S(1)}, u32[]{:S(2)}, u32[]{:S(2)}) collective-permute-start(bf16[512,256]{1,0:T(8,128)(2,1)S(1)} %get-tuple-element.65.refs_0_), channel_id=1, source_target_pairs={{0,8},{1,9},{2,10},{3,11},{4,12},{5,13},{6,14},{7,15},{8,0},{9,1},... | collective-permute-start | bytes 786440 | tf_op jit(solution)/shard_map/ppermute | solution.py:442
  60.0 0.4 collective-permute-done.4.mixed_a
  60.4 2.5 %collective-permute-start.14 = (bf16[512,256]{1,0:T(8,128)(2,1)S(1)}, bf16[512,256]{1,0:T(8,128)(2,1)S(1)}, u32[]{:S(2)}, u32[]{:S(2)}) collective-permute-start(bf16[512,256]{1,0:T(8,128)(2,1)S(1)} %get-tuple-element.57.refs_0_), channel_id=1, source_target_pairs={{0,6},{1,7},{2,4},{3,5},{4,2},{5,3},{6,0},{7,1},{8,14},{9,15},{10,... | collective-permute-start | bytes 786440 | tf_op jit(solution)/shard_map/ppermute | solution.py:442
  63.0 1.0 copy-done.12
  64.0 1.0 copy-done.14
  65.0 0.7 first1.1.h0
  65.7 0.1 arrived.1.h
  65.8 0.2 weights1.1.w
  66.1 0.5 sender1.1
  66.6 4.4 %collective-permute-done.20.refs_2_ = bf16[512,256]{1,0:T(8,128)(2,1)S(1)} collective-permute-done((bf16[512,256]{1,0:T(8,128)(2,1)S(1)}, bf16[512,256]{1,0:T(8,128)(2,1)S(1)}, u32[]{:S(2)}, u32[]{:S(2)}) %collective-permute-start.20) | collective-permute-done | bytes 262176 | tf_op jit(solution)/shard_map/ppermute | solution.py:442
  71.0 0.3 collective-permute-done.19.refs_1_
  71.3 0.2 joined.5.refs_4_
  71.4 0.1 collective-permute-start.22
  71.5 0.5 collective-permute-start.16
  72.0 7.3 %collective-permute-start.17 = (bf16[128,512]{1,0:T(8,128)(2,1)S(1)}, bf16[128,512]{1,0:T(8,128)(2,1)S(1)}, u32[]{:S(2)}, u32[]{:S(2)}) collective-permute-start(bf16[128,512]{1,0:T(8,128)(2,1)S(1)} %get-tuple-element.55), channel_id=1, source_target_pairs={{0,63},{1,2},{2,1},{3,4},{4,3},{5,6},{6,5},{7,8},{8,7},{9,10},{10,... | collective-permute-start | bytes 393224 | tf_op jit(solution)/shard_map/ppermute | solution.py:442
  79.3 1.3 %tiles1.1 = (bf16[24,128,128]{2,1,0:T(8,128)(2,1)S(1)}, s32[8,128]{1,0:T(8,128)S(1)}, f32[1,512]{1,0:T(1,128)S(1)}) custom-call(bf16[3088,128]{1,0:T(8,128)(2,1)S(1)} %copy-done, bf16[3088,128]{1,0:T(8,128)(2,1)S(1)} %collective-permute-done.2.near, bf16[3088,128]{1,0:T(8,128)(2,1)S(1)} %collective-permute-done.3.far, ...), custom_call_target="tpu_custom_call" | custom-call | bytes 2000000 | tf_op jit(solution)/shard_map/tiles1/pallas_call | solution.py:362
  80.7 2.5 %collective-permute-done.17.outer = bf16[128,512]{1,0:T(8,128)(2,1)S(1)} collective-permute-done((bf16[128,512]{1,0:T(8,128)(2,1)S(1)}, bf16[128,512]{1,0:T(8,128)(2,1)S(1)}, u32[]{:S(2)}, u32[]{:S(2)}) %collective-permute-start.17) | collective-permute-done | bytes 131104 | tf_op jit(solution)/shard_map/ppermute | solution.py:442
  83.2 2.4 %section1.1.h = bf16[512,512]{1,0:T(8,128)(2,1)S(1)} custom-call(s32[8,128]{1,0:T(8,128)S(1)} %get-tuple-element.51.codes, f32[1,512]{1,0:T(1,128)S(1)} %get-tuple-element.52.gain, bf16[24,128,128]{2,1,0:T(8,128)(2,1)S(1)} %get-tuple-element.53.tiles, bf16[4,512,512]{2,1,0:T(8,128)(2,1)S(1)} %weights1.1.w, bf16[512,512]{1,0:T(8,128)(2,1)S(1)} %arrived.1.h, ...), custom_call_target="tpu_custom_call" | custom-call | flops 1500000000 | bytes 4000000 | tf_op jit(solution)/shard_map/section1/pallas_call | solution.py:389
  85.6 1.6 %collective-permute-done.15.refs_2_ = bf16[512,256]{1,0:T(8,128)(2,1)S(1)} collective-permute-done((bf16[512,256]{1,0:T(8,128)(2,1)S(1)}, bf16[512,256]{1,0:T(8,128)(2,1)S(1)}, u32[]{:S(2)}, u32[]{:S(2)}) %collective-permute-start.15) | collective-permute-done | bytes 262176 | tf_op jit(solution)/shard_map/ppermute | solution.py:442
  87.2 0.2 joined.4.refs_4_
  87.4 0.3 collective-permute-start.18
  87.7 0.2 weights2.1.w
  87.9 0.5 sender2.1
  88.5 0.6 collective-permute-start.23
  89.0 3.5 %collective-permute-start.24 = (bf16[128,512]{1,0:T(8,128)(2,1)S(1)}, bf16[128,512]{1,0:T(8,128)(2,1)S(1)}, u32[]{:S(2)}, u32[]{:S(2)}) collective-permute-start(bf16[128,512]{1,0:T(8,128)(2,1)S(1)} %get-tuple-element.70), channel_id=1, source_target_pairs={{0,63},{1,2},{2,1},{3,4},{4,3},{5,6},{6,5},{7,8},{8,7},{9,10},{10,... | collective-permute-start | bytes 393224 | tf_op jit(solution)/shard_map/ppermute | solution.py:442
  92.5 1.3 %tiles2.1 = (bf16[24,128,128]{2,1,0:T(8,128)(2,1)S(1)}, s32[8,128]{1,0:T(8,128)S(1)}, f32[1,512]{1,0:T(1,128)S(1)}) custom-call(bf16[3088,128]{1,0:T(8,128)(2,1)S(1)} %copy-done, bf16[3088,128]{1,0:T(8,128)(2,1)S(1)} %collective-permute-done.2.near, bf16[3088,128]{1,0:T(8,128)(2,1)S(1)} %collective-permute-done.3.far, ...), custom_call_target="tpu_custom_call" | custom-call | bytes 2000000 | tf_op jit(solution)/shard_map/tiles2/pallas_call | solution.py:362
  93.8 3.0 %collective-permute-done.24.outer = bf16[128,512]{1,0:T(8,128)(2,1)S(1)} collective-permute-done((bf16[128,512]{1,0:T(8,128)(2,1)S(1)}, bf16[128,512]{1,0:T(8,128)(2,1)S(1)}, u32[]{:S(2)}, u32[]{:S(2)}) %collective-permute-start.24) | collective-permute-done | bytes 131104 | tf_op jit(solution)/shard_map/ppermute | solution.py:442
  96.7 2.4 %section2.1.h = bf16[512,512]{1,0:T(8,128)(2,1)S(1)} custom-call(s32[8,128]{1,0:T(8,128)S(1)} %get-tuple-element.61.codes, f32[1,512]{1,0:T(1,128)S(1)} %get-tuple-element.62.gain, bf16[24,128,128]{2,1,0:T(8,128)(2,1)S(1)} %get-tuple-element.63.tiles, bf16[4,512,512]{2,1,0:T(8,128)(2,1)S(1)} %weights2.1.w, bf16[512,512]{1,0:T(8,128)(2,1)S(1)} %section1.1.h, ...), custom_call_target="tpu_custom_call" | custom-call | flops 1500000000 | bytes 4000000 | tf_op jit(solution)/shard_map/section2/pallas_call | solution.py:389
  99.2 0.2 weights3.1.w
  99.4 0.5 sender3.1
  99.9 0.1 collective-permute-start.25
  100.0 3.6 %collective-permute-start.26 = (bf16[128,512]{1,0:T(8,128)(2,1)S(1)}, bf16[128,512]{1,0:T(8,128)(2,1)S(1)}, u32[]{:S(2)}, u32[]{:S(2)}) collective-permute-start(bf16[128,512]{1,0:T(8,128)(2,1)S(1)} %get-tuple-element.73), channel_id=1, source_target_pairs={{0,63},{1,2},{2,1},{3,4},{4,3},{5,6},{6,5},{7,8},{8,7},{9,10},{10,... | collective-permute-start | bytes 393224 | tf_op jit(solution)/shard_map/ppermute | solution.py:442
  103.6 1.3 %tiles3.1 = (bf16[24,128,128]{2,1,0:T(8,128)(2,1)S(1)}, s32[8,128]{1,0:T(8,128)S(1)}, f32[1,512]{1,0:T(1,128)S(1)}) custom-call(bf16[3088,128]{1,0:T(8,128)(2,1)S(1)} %copy-done, bf16[3088,128]{1,0:T(8,128)(2,1)S(1)} %collective-permute-done.2.near, bf16[3088,128]{1,0:T(8,128)(2,1)S(1)} %collective-permute-done.3.far, ...), custom_call_target="tpu_custom_call" | custom-call | bytes 2000000 | tf_op jit(solution)/shard_map/tiles3/pallas_call | solution.py:362
  104.8 3.0 %collective-permute-done.26.outer = bf16[128,512]{1,0:T(8,128)(2,1)S(1)} collective-permute-done((bf16[128,512]{1,0:T(8,128)(2,1)S(1)}, bf16[128,512]{1,0:T(8,128)(2,1)S(1)}, u32[]{:S(2)}, u32[]{:S(2)}) %collective-permute-start.26) | collective-permute-done | bytes 131104 | tf_op jit(solution)/shard_map/ppermute | solution.py:442
  107.8 3.3 %section3.1 = bf16[512,512]{1,0:T(8,128)(2,1)} custom-call(s32[8,128]{1,0:T(8,128)S(1)} %get-tuple-element.42.codes, f32[1,512]{1,0:T(1,128)S(1)} %get-tuple-element.43.gain, bf16[24,128,128]{2,1,0:T(8,128)(2,1)S(1)} %get-tuple-element.44.tiles, bf16[4,512,512]{2,1,0:T(8,128)(2,1)S(1)} %weights3.1.w, bf16[512,512]{1,0:T(8,128)(2,1)S(1)} %section2.1.h, ...), custom_call_target="tpu_custom_call" | custom-call | flops 1500000000 | bytes 4000000 | tf_op jit(solution)/shard_map/section3/pallas_call | solution.py:389
  (49 shorter events, 0.2 us)
Async XLA Ops:
  0.0 10.2 %copy-start.7 = (bf16[1,1,512,512]{3,2,1,0:T(8,128)(2,1)S(1)}, bf16[1,1,512,512]{3,2,1,0:T(8,128)(2,1)}, u32[]{:S(2)}) copy-start(bf16[1,1,512,512]{3,2,1,0:T(8,128)(2,1)} %refs_3_.5) | copy-start | bytes 1572868
  0.0 10.2 %copy-start.5 = (bf16[1,1,512,512]{3,2,1,0:T(8,128)(2,1)S(1)}, bf16[1,1,512,512]{3,2,1,0:T(8,128)(2,1)}, u32[]{:S(2)}) copy-start(bf16[1,1,512,512]{3,2,1,0:T(8,128)(2,1)} %refs_2_.5) | copy-start | bytes 1572868
  0.0 10.2 %copy-start.3 = (bf16[1,1,512,512]{3,2,1,0:T(8,128)(2,1)S(1)}, bf16[1,1,512,512]{3,2,1,0:T(8,128)(2,1)}, u32[]{:S(2)}) copy-start(bf16[1,1,512,512]{3,2,1,0:T(8,128)(2,1)} %refs_1_.5) | copy-start | bytes 1572868
  0.0 10.2 %copy-start.1 = (bf16[1,1,512,512]{3,2,1,0:T(8,128)(2,1)S(1)}, bf16[1,1,512,512]{3,2,1,0:T(8,128)(2,1)}, u32[]{:S(2)}) copy-start(bf16[1,1,512,512]{3,2,1,0:T(8,128)(2,1)} %refs_0_.5) | copy-start | bytes 1572868
  2.4 14.8 %collective-permute-start.1 = (bf16[4,128,512]{2,1,0:T(8,128)(2,1)}, bf16[4,128,512]{2,1,0:T(8,128)(2,1)S(1)}, u32[]{:S(2)}, u32[]{:S(2)}) collective-permute-start(bf16[4,128,512]{2,1,0:T(8,128)(2,1)} %get-tuple-element.75), channel_id=1, source_target_pairs={{0,63},{1,2},{2,1},{3,4},{4,3},{5,6},{6,5},{7,8},{8,7},{9,10},{10,... | collective-permute-start | bytes 1572872 | tf_op jit(solution)/shard_map/ppermute | solution.py:442
  10.2 7.1 %collective-permute-start = (bf16[4,128,512]{2,1,0:T(8,128)(2,1)}, bf16[4,128,512]{2,1,0:T(8,128)(2,1)S(1)}, u32[]{:S(2)}, u32[]{:S(2)}) collective-permute-start(bf16[4,128,512]{2,1,0:T(8,128)(2,1)} %get-tuple-element.76), channel_id=1, source_target_pairs={{0,1},{1,0},{2,3},{3,2},{4,5},{5,4},{6,7},{7,6},{8,9},{9,8},{10,11... | collective-permute-start | bytes 1572872 | tf_op jit(solution)/shard_map/ppermute | solution.py:442
  10.4 15.6 %collective-permute-start.8 = (bf16[512,256]{1,0:T(8,128)(2,1)S(1)}, bf16[512,256]{1,0:T(8,128)(2,1)S(1)}, u32[]{:S(2)}, u32[]{:S(2)}) collective-permute-start(bf16[512,256]{1,0:T(8,128)(2,1)S(1)} %select_bitcast_fusion), channel_id=1, source_target_pairs={{0,192},{64,128},{128,64},{192,0},{1,193},{65,129},{129,65},{193,1... | collective-permute-start | bytes 786440 | tf_op jit(solution)/shard_map/ppermute | solution.py:438
  10.9 15.1 %collective-permute-start.7 = (bf16[512,256]{1,0:T(8,128)(2,1)S(1)}, bf16[512,256]{1,0:T(8,128)(2,1)S(1)}, u32[]{:S(2)}, u32[]{:S(2)}) collective-permute-start(bf16[512,256]{1,0:T(8,128)(2,1)S(1)} %select_bitcast_fusion), channel_id=1, source_target_pairs={{0,128},{64,192},{128,0},{192,64},{1,129},{65,193},{129,1},{193,65... | collective-permute-start | bytes 786440 | tf_op jit(solution)/shard_map/ppermute | solution.py:438
  13.3 13.3 %collective-permute-start.6 = (bf16[512,256]{1,0:T(8,128)(2,1)S(1)}, bf16[512,256]{1,0:T(8,128)(2,1)S(1)}, u32[]{:S(2)}, u32[]{:S(2)}) collective-permute-start(bf16[512,256]{1,0:T(8,128)(2,1)S(1)} %select_bitcast_fusion), channel_id=1, source_target_pairs={{0,64},{64,0},{128,192},{192,128},{1,65},{65,1},{129,193},{193,129... | collective-permute-start | bytes 786440 | tf_op jit(solution)/shard_map/ppermute | solution.py:438
  17.2 0.8 copy-start.11
  18.0 0.8 copy-start.13
  26.6 36.3 %copy-start.9 = (bf16[4,512,512]{2,1,0:T(8,128)(2,1)S(1)}, bf16[4,512,512]{2,1,0:T(8,128)(2,1)}, u32[]{:S(2)}) copy-start(bf16[4,512,512]{2,1,0:T(8,128)(2,1)} %samples.3) | copy-start | bytes 6291460
  26.7 36.2 %copy-start.2 = (bf16[1,1,512,512]{3,2,1,0:T(8,128)(2,1)S(1)}, bf16[1,1,512,512]{3,2,1,0:T(8,128)(2,1)}, u32[]{:S(2)}) copy-start(bf16[1,1,512,512]{3,2,1,0:T(8,128)(2,1)} %refs_0_.5) | copy-start | bytes 1572868
  26.7 36.2 %copy-start.4 = (bf16[1,1,512,512]{3,2,1,0:T(8,128)(2,1)S(1)}, bf16[1,1,512,512]{3,2,1,0:T(8,128)(2,1)}, u32[]{:S(2)}) copy-start(bf16[1,1,512,512]{3,2,1,0:T(8,128)(2,1)} %refs_1_.5) | copy-start | bytes 1572868
  26.7 36.2 %copy-start.6 = (bf16[1,1,512,512]{3,2,1,0:T(8,128)(2,1)S(1)}, bf16[1,1,512,512]{3,2,1,0:T(8,128)(2,1)}, u32[]{:S(2)}) copy-start(bf16[1,1,512,512]{3,2,1,0:T(8,128)(2,1)} %refs_2_.5) | copy-start | bytes 1572868
  26.7 36.2 %copy-start.8 = (bf16[1,1,512,512]{3,2,1,0:T(8,128)(2,1)S(1)}, bf16[1,1,512,512]{3,2,1,0:T(8,128)(2,1)}, u32[]{:S(2)}) copy-start(bf16[1,1,512,512]{3,2,1,0:T(8,128)(2,1)} %refs_3_.5) | copy-start | bytes 1572868
  26.7 36.2 %copy-start.10 = (bf16[1,4,6,128,128]{4,3,2,1,0:T(8,128)(2,1)S(1)}, bf16[1,4,6,128,128]{4,3,2,1,0:T(8,128)(2,1)}, u32[]{:S(2)}) copy-start(bf16[1,4,6,128,128]{4,3,2,1,0:T(8,128)(2,1)} %tiles.3) | copy-start | bytes 2359300
  26.7 36.2 %copy-start.15 = (s32[1,4,6]{2,1,0:T(4,128)S(1)}, s32[1,4,6]{2,1,0:T(4,128)}, u32[]{:S(2)}) copy-start(s32[1,4,6]{2,1,0:T(4,128)} %src.3) | copy-start | bytes 292
  26.8 36.2 %copy-start.16 = (f32[1,1,512]{2,1,0:T(1,128)S(1)}, f32[1,1,512]{2,1,0:T(1,128)}, u32[]{:S(2)}) copy-start(f32[1,1,512]{2,1,0:T(1,128)} %gain.3) | copy-start | bytes 6148
  26.8 36.2 %copy-start.17 = (s32[1,4]{1,0:T(1,128)S(1)}, s32[1,4]{1,0:T(1,128)}, u32[]{:S(2)}) copy-start(s32[1,4]{1,0:T(1,128)} %cnt.3) | copy-start | bytes 52
  26.8 14.5 %collective-permute-start.11 = (bf16[512,256]{1,0:T(8,128)(2,1)S(1)}, bf16[512,256]{1,0:T(8,128)(2,1)S(1)}, u32[]{:S(2)}, u32[]{:S(2)}) collective-permute-start(bf16[512,256]{1,0:T(8,128)(2,1)S(1)} %get-tuple-element.77.refs_0_), channel_id=1, source_target_pairs={{0,6},{1,7},{2,4},{3,5},{4,2},{5,3},{6,0},{7,1},{8,14},{9,15},{10,... | collective-permute-start | bytes 786440 | tf_op jit(solution)/shard_map/ppermute | solution.py:442
  26.9 14.4 %collective-permute-start.10 = (bf16[512,256]{1,0:T(8,128)(2,1)S(1)}, bf16[512,256]{1,0:T(8,128)(2,1)S(1)}, u32[]{:S(2)}, u32[]{:S(2)}) collective-permute-start(bf16[512,256]{1,0:T(8,128)(2,1)S(1)} %get-tuple-element.77.refs_0_), channel_id=1, source_target_pairs={{0,4},{1,5},{2,6},{3,7},{4,0},{5,1},{6,2},{7,3},{8,12},{9,13},{10,... | collective-permute-start | bytes 786440 | tf_op jit(solution)/shard_map/ppermute | solution.py:442
  27.0 14.9 %collective-permute-start.9 = (bf16[512,256]{1,0:T(8,128)(2,1)S(1)}, bf16[512,256]{1,0:T(8,128)(2,1)S(1)}, u32[]{:S(2)}, u32[]{:S(2)}) collective-permute-start(bf16[512,256]{1,0:T(8,128)(2,1)S(1)} %get-tuple-element.77.refs_0_), channel_id=1, source_target_pairs={{0,2},{1,3},{2,0},{3,1},{4,6},{5,7},{6,4},{7,5},{8,10},{9,11},{10,... | collective-permute-start | bytes 786440 | tf_op jit(solution)/shard_map/ppermute | solution.py:442
  31.0 19.5 %collective-permute-start.3 = (bf16[3088,128]{1,0:T(8,128)(2,1)}, bf16[3088,128]{1,0:T(8,128)(2,1)S(1)}, u32[]{:S(2)}, u32[]{:S(2)}) collective-permute-start(bf16[3088,128]{1,0:T(8,128)(2,1)} %get-tuple-element.41), channel_id=1, source_target_pairs={{0,192},{64,128},{128,64},{192,0},{1,193},{65,129},{129,65},{193,1... | collective-permute-start | bytes 2371592 | tf_op jit(solution)/shard_map/ppermute | solution.py:438
  34.9 15.8 %collective-permute-start.2 = (bf16[3088,128]{1,0:T(8,128)(2,1)}, bf16[3088,128]{1,0:T(8,128)(2,1)S(1)}, u32[]{:S(2)}, u32[]{:S(2)}) collective-permute-start(bf16[3088,128]{1,0:T(8,128)(2,1)} %get-tuple-element.40.own), channel_id=1, source_target_pairs={{0,64},{64,0},{128,192},{192,128},{1,65},{65,1},{129,193},{193,129... | collective-permute-start | bytes 2371592 | tf_op jit(solution)/shard_map/ppermute | solution.py:438
  42.1 12.5 %collective-permute-start.12 = (bf16[4,512,256]{2,1,0:T(8,128)(2,1)S(1)}, bf16[4,512,256]{2,1,0:T(8,128)(2,1)S(1)}, u32[]{:S(2)}, u32[]{:S(2)}) collective-permute-start(bf16[4,512,256]{2,1,0:T(8,128)(2,1)S(1)} %joined.3.refs_4_), channel_id=1, source_target_pairs={{0,1},{1,0},{2,3},{3,2},{4,5},{5,4},{6,7},{7,6},{8,9},{9,8},{10,11... | collective-permute-start | bytes 3145736 | tf_op jit(solution)/shard_map/ppermute | solution.py:442
  50.5 12.4 %collective-permute-start.5 = (bf16[1552,128]{1,0:T(8,128)(2,1)S(1)}, bf16[1552,128]{1,0:T(8,128)(2,1)S(1)}, u32[]{:S(2)}, u32[]{:S(2)}) collective-permute-start(bf16[1552,128]{1,0:T(8,128)(2,1)S(1)} %slice.17), channel_id=1, source_target_pairs={{0,64},{64,0},{128,192},{192,128},{1,65},{65,1},{129,193},{193,129... | collective-permute-start | bytes 1191944 | tf_op jit(solution)/shard_map/ppermute | solution.py:438
  50.7 9.7 %collective-permute-start.4 = (bf16[1536,128]{1,0:T(8,128)(2,1)S(1)}, bf16[1536,128]{1,0:T(8,128)(2,1)S(1)}, u32[]{:S(2)}, u32[]{:S(2)}) collective-permute-start(bf16[1536,128]{1,0:T(8,128)(2,1)S(1)} %slice.16), channel_id=1, source_target_pairs={{0,192},{64,128},{128,64},{192,0},{1,193},{65,129},{129,65},{193,1... | collective-permute-start | bytes 1179656 | tf_op jit(solution)/shard_map/ppermute | solution.py:438
  54.7 11.9 %collective-permute-start.21 = (bf16[512,256]{1,0:T(8,128)(2,1)S(1)}, bf16[512,256]{1,0:T(8,128)(2,1)S(1)}, u32[]{:S(2)}, u32[]{:S(2)}) collective-permute-start(bf16[512,256]{1,0:T(8,128)(2,1)S(1)} %get-tuple-element.65.refs_0_), channel_id=1, source_target_pairs={{0,56},{1,57},{2,58},{3,59},{4,60},{5,61},{6,62},{7,63},{8,16},{9,... | collective-permute-start | bytes 786440 | tf_op jit(solution)/shard_map/ppermute | solution.py:442
  58.4 12.5 %collective-permute-start.20 = (bf16[512,256]{1,0:T(8,128)(2,1)S(1)}, bf16[512,256]{1,0:T(8,128)(2,1)S(1)}, u32[]{:S(2)}, u32[]{:S(2)}) collective-permute-start(bf16[512,256]{1,0:T(8,128)(2,1)S(1)} %get-tuple-element.65.refs_0_), channel_id=1, source_target_pairs={{0,16},{1,17},{2,18},{3,19},{4,20},{5,21},{6,22},{7,23},{8,24},{9,... | collective-permute-start | bytes 786440 | tf_op jit(solution)/shard_map/ppermute | solution.py:442
  58.4 12.8 %collective-permute-start.19 = (bf16[512,256]{1,0:T(8,128)(2,1)S(1)}, bf16[512,256]{1,0:T(8,128)(2,1)S(1)}, u32[]{:S(2)}, u32[]{:S(2)}) collective-permute-start(bf16[512,256]{1,0:T(8,128)(2,1)S(1)} %get-tuple-element.65.refs_0_), channel_id=1, source_target_pairs={{0,8},{1,9},{2,10},{3,11},{4,12},{5,13},{6,14},{7,15},{8,0},{9,1},... | collective-permute-start | bytes 786440 | tf_op jit(solution)/shard_map/ppermute | solution.py:442
  60.4 18.9 %collective-permute-start.14 = (bf16[512,256]{1,0:T(8,128)(2,1)S(1)}, bf16[512,256]{1,0:T(8,128)(2,1)S(1)}, u32[]{:S(2)}, u32[]{:S(2)}) collective-permute-start(bf16[512,256]{1,0:T(8,128)(2,1)S(1)} %get-tuple-element.57.refs_0_), channel_id=1, source_target_pairs={{0,6},{1,7},{2,4},{3,5},{4,2},{5,3},{6,0},{7,1},{8,14},{9,15},{10,... | collective-permute-start | bytes 786440 | tf_op jit(solution)/shard_map/ppermute | solution.py:442
  62.9 16.4 %collective-permute-start.13 = (bf16[512,256]{1,0:T(8,128)(2,1)S(1)}, bf16[512,256]{1,0:T(8,128)(2,1)S(1)}, u32[]{:S(2)}, u32[]{:S(2)}) collective-permute-start(bf16[512,256]{1,0:T(8,128)(2,1)S(1)} %get-tuple-element.57.refs_0_), channel_id=1, source_target_pairs={{0,2},{1,3},{2,0},{3,1},{4,6},{5,7},{6,4},{7,5},{8,10},{9,11},{10,... | collective-permute-start | bytes 786440 | tf_op jit(solution)/shard_map/ppermute | solution.py:442
  63.0 1.0 copy-start.12
  64.0 1.0 copy-start.14
  66.1 13.2 %copy-start = (bf16[3088,128]{1,0:T(8,128)(2,1)S(1)}, bf16[3088,128]{1,0:T(8,128)(2,1)}, u32[]{:S(2)}) copy-start(bf16[3088,128]{1,0:T(8,128)(2,1)} %get-tuple-element.40.own) | copy-start | bytes 2371588
  71.4 16.3 %collective-permute-start.22 = (bf16[4,512,256]{2,1,0:T(8,128)(2,1)S(1)}, bf16[4,512,256]{2,1,0:T(8,128)(2,1)S(1)}, u32[]{:S(2)}, u32[]{:S(2)}) collective-permute-start(bf16[4,512,256]{2,1,0:T(8,128)(2,1)S(1)} %joined.5.refs_4_), channel_id=1, source_target_pairs={{0,1},{1,0},{2,3},{3,2},{4,5},{5,4},{6,7},{7,6},{8,9},{9,8},{10,11... | collective-permute-start | bytes 3145736 | tf_op jit(solution)/shard_map/ppermute | solution.py:442
  71.5 9.1 %collective-permute-start.16 = (bf16[128,512]{1,0:T(8,128)(2,1)S(1)}, bf16[128,512]{1,0:T(8,128)(2,1)S(1)}, u32[]{:S(2)}, u32[]{:S(2)}) collective-permute-start(bf16[128,512]{1,0:T(8,128)(2,1)S(1)} %get-tuple-element.54), channel_id=1, source_target_pairs={{0,1},{1,0},{2,3},{3,2},{4,5},{5,4},{6,7},{7,6},{8,9},{9,8},{10,11... | collective-permute-start | bytes 393224 | tf_op jit(solution)/shard_map/ppermute | solution.py:442
  72.0 11.1 %collective-permute-start.17 = (bf16[128,512]{1,0:T(8,128)(2,1)S(1)}, bf16[128,512]{1,0:T(8,128)(2,1)S(1)}, u32[]{:S(2)}, u32[]{:S(2)}) collective-permute-start(bf16[128,512]{1,0:T(8,128)(2,1)S(1)} %get-tuple-element.55), channel_id=1, source_target_pairs={{0,63},{1,2},{2,1},{3,4},{4,3},{5,6},{6,5},{7,8},{8,7},{9,10},{10,... | collective-permute-start | bytes 393224 | tf_op jit(solution)/shard_map/ppermute | solution.py:442
  79.3 7.9 %collective-permute-start.15 = (bf16[512,256]{1,0:T(8,128)(2,1)S(1)}, bf16[512,256]{1,0:T(8,128)(2,1)S(1)}, u32[]{:S(2)}, u32[]{:S(2)}) collective-permute-start(bf16[512,256]{1,0:T(8,128)(2,1)S(1)} %get-tuple-element.57.refs_0_), channel_id=1, source_target_pairs={{0,4},{1,5},{2,6},{3,7},{4,0},{5,1},{6,2},{7,3},{8,12},{9,13},{10,... | collective-permute-start | bytes 786440 | tf_op jit(solution)/shard_map/ppermute | solution.py:442
  87.4 11.8 %collective-permute-start.18 = (bf16[4,512,256]{2,1,0:T(8,128)(2,1)S(1)}, bf16[4,512,256]{2,1,0:T(8,128)(2,1)S(1)}, u32[]{:S(2)}, u32[]{:S(2)}) collective-permute-start(bf16[4,512,256]{2,1,0:T(8,128)(2,1)S(1)} %joined.4.refs_4_), channel_id=1, source_target_pairs={{0,1},{1,0},{2,3},{3,2},{4,5},{5,4},{6,7},{7,6},{8,9},{9,8},{10,11... | collective-permute-start | bytes 3145736 | tf_op jit(solution)/shard_map/ppermute | solution.py:442
  88.5 5.3 %collective-permute-start.23 = (bf16[128,512]{1,0:T(8,128)(2,1)S(1)}, bf16[128,512]{1,0:T(8,128)(2,1)S(1)}, u32[]{:S(2)}, u32[]{:S(2)}) collective-permute-start(bf16[128,512]{1,0:T(8,128)(2,1)S(1)} %get-tuple-element.69), channel_id=1, source_target_pairs={{0,1},{1,0},{2,3},{3,2},{4,5},{5,4},{6,7},{7,6},{8,9},{9,8},{10,11... | collective-permute-start | bytes 393224 | tf_op jit(solution)/shard_map/ppermute | solution.py:442
  89.0 7.7 %collective-permute-start.24 = (bf16[128,512]{1,0:T(8,128)(2,1)S(1)}, bf16[128,512]{1,0:T(8,128)(2,1)S(1)}, u32[]{:S(2)}, u32[]{:S(2)}) collective-permute-start(bf16[128,512]{1,0:T(8,128)(2,1)S(1)} %get-tuple-element.70), channel_id=1, source_target_pairs={{0,63},{1,2},{2,1},{3,4},{4,3},{5,6},{6,5},{7,8},{8,7},{9,10},{10,... | collective-permute-start | bytes 393224 | tf_op jit(solution)/shard_map/ppermute | solution.py:442
  99.9 4.9 %collective-permute-start.25 = (bf16[128,512]{1,0:T(8,128)(2,1)S(1)}, bf16[128,512]{1,0:T(8,128)(2,1)S(1)}, u32[]{:S(2)}, u32[]{:S(2)}) collective-permute-start(bf16[128,512]{1,0:T(8,128)(2,1)S(1)} %get-tuple-element.72), channel_id=1, source_target_pairs={{0,1},{1,0},{2,3},{3,2},{4,5},{5,4},{6,7},{7,6},{8,9},{9,8},{10,11... | collective-permute-start | bytes 393224 | tf_op jit(solution)/shard_map/ppermute | solution.py:442
  100.0 7.8 %collective-permute-start.26 = (bf16[128,512]{1,0:T(8,128)(2,1)S(1)}, bf16[128,512]{1,0:T(8,128)(2,1)S(1)}, u32[]{:S(2)}, u32[]{:S(2)}) collective-permute-start(bf16[128,512]{1,0:T(8,128)(2,1)S(1)} %get-tuple-element.73), channel_id=1, source_target_pairs={{0,63},{1,2},{2,1},{3,4},{4,3},{5,6},{6,5},{7,8},{8,7},{9,10},{10,... | collective-permute-start | bytes 393224 | tf_op jit(solution)/shard_map/ppermute | solution.py:442
